TPU v7x, 32 devices: a whole 2x2x4 slice. The times are simulated.
32 devices in a mesh: dp: 4 (over y, x), seq: 2 (over core), tensor: 4 (over z).
Axes of the slice: x: 2, y: 2, z: 4, core: 2. Of those that a mesh axis runs over, the one named last changes fastest.
Arguments:
- tokens: bfloat16 [4, 2048, 1536], P('dp', 'seq'), may hold values from -6 to 6
- positions: int32 [3, 4, 2048], P(None, 'dp', 'seq'), may hold values from 0 to 100, as said below
- time_emb: float32 [4, 6, 1536], P('dp'), may hold values from -4 to 4
- modulation: float32 [6, 1536], replicated, may hold values from -4 to 4
- context: bfloat16 [512, 1536], replicated, may hold values from -6 to 6
- adapter_index: int32 [4], P('dp'), may hold values from 0 to 7
- self_qkv: bfloat16 [3, 1536, 1536], P(None, None, 'tensor'), may hold values from -0.15625 to 0.15625
- self_bias: bfloat16 [3, 1536], P(None, 'tensor'), may hold values from -2 to 2
- self_gain: bfloat16 [2, 1536], P(None, 'tensor'), may hold values from 0.25 to 1.75
- self_out: bfloat16 [1536, 1536], P('tensor'), may hold values from -2.5 to 2.5
- cross_qkv: bfloat16 [3, 1536, 1536], P(None, None, 'tensor'), may hold values from -0.15625 to 0.15625
- cross_bias: bfloat16 [3, 1536], P(None, 'tensor'), may hold values from -2 to 2
- cross_gain: bfloat16 [2, 1536], P(None, 'tensor'), may hold values from 0.25 to 1.75
- cross_out: bfloat16 [1536, 1536], P('tensor'), may hold values from -2.5 to 2.5
- cross_norm_gain: float32 [1536], replicated, may hold values from 0.25 to 1.75
- cross_norm_bias: float32 [1536], replicated, may hold values from -2 to 2
- ffn_in: bfloat16 [1536, 8960], P(None, 'tensor'), may hold values from -0.15625 to 0.15625
- ffn_bias: bfloat16 [8960], P('tensor'), may hold values from -2 to 2
- ffn_out: bfloat16 [8960, 1536], P('tensor'), may hold values from -0.0625 to 0.0625
- out_bias: bfloat16 [3, 1536], replicated, may hold values from -2 to 2
- col_down: bfloat16 [8, 6, 1536, 16], replicated, may hold values from -0.15625 to 0.15625
- col_up: bfloat16 [8, 6, 16, 1536], P(None, None, None, 'tensor'), may hold values from -0.75 to 0.75
- ffn1_down: bfloat16 [8, 1536, 16], replicated, may hold values from -0.15625 to 0.15625
- ffn1_up: bfloat16 [8, 16, 8960], P(None, None, 'tensor'), may hold values from -0.75 to 0.75
- row_down: bfloat16 [8, 2, 1536, 16], P(None, None, 'tensor'), may hold values from -1.25 to 1.25
- row_up: bfloat16 [8, 2, 16, 1536], replicated, may hold values from -0.75 to 0.75
- ffn2_down: bfloat16 [8, 8960, 16], P(None, 'tensor'), may hold values from -0.0625 to 0.0625
- ffn2_up: bfloat16 [8, 16, 1536], replicated, may hold values from -0.75 to 0.75
- out_grad: bfloat16 [4, 2048, 1536], P('dp', 'seq'), may hold values from -6 to 6
Outputs:
- output: bfloat16 [4, 2048, 1536], P('dp', 'seq')
- input_grad: bfloat16 [4, 2048, 1536], P('dp', 'seq')
- context_grad: float32 [512, 1536], replicated
- col_down_grad: float32 [8, 6, 1536, 16], replicated
- col_up_grad: float32 [8, 6, 16, 1536], P(None, None, None, 'tensor')
- ffn1_down_grad: float32 [8, 1536, 16], replicated
- ffn1_up_grad: float32 [8, 16, 8960], P(None, None, 'tensor')
- row_down_grad: float32 [8, 2, 1536, 16], P(None, None, 'tensor')
- row_up_grad: float32 [8, 2, 16, 1536], replicated
- ffn2_down_grad: float32 [8, 8960, 16], P(None, 'tensor')
- ffn2_up_grad: float32 [8, 16, 1536], replicated
Inputs may be any that keep to these rules, and one draw needn't show every extreme that they name: positions[0], positions[1], positions[2] are a token's frame, row and column in its latent's grid of 2 x 32 x 32 (tokens in the order frame, row, column), each times a stride of 1 to 3 plus an offset of 0 to 7, stride and offset fixed for a latent and a component.
All inputs are finite; a program needn't handle non-finite values.
Results may differ from a plain program's by a relative error of at most 0.025.
Values may be sent and summed in bfloat16 or wider, within the bound.
No kernel may reach another device: no remote copies, remote signals or barrier semaphores. Data moves between devices by JAX's collectives and lax.ppermute only.
A program may use at most 256 MiB of HBM per device.

v0:
```python
import jax
import jax.numpy as jnp
from jax import lax
from jax.sharding import PartitionSpec as P

D = 1536
HEAD_DIM = 128


epsilon = 1e-06


def normalize(values):
    centered = values - jnp.mean(values, axis=-1, keepdims=True)
    inverse = lax.rsqrt(jnp.mean(centered * centered, axis=-1, keepdims=True) + epsilon)
    return (centered * inverse, inverse)


def normalize_back(normed, inverse, upstream):
    return inverse * (
        upstream
        - jnp.mean(upstream, axis=-1, keepdims=True)
        - normed * jnp.mean(upstream * normed, axis=-1, keepdims=True)
    )


def norm_back(pre_values, inverse, gain_row, upstream, stat_total):
    cubed = inverse * inverse * inverse
    return (
        inverse[:, None] * gain_row * upstream
        - pre_values * cubed[:, None] * stat_total[:, None] / D
    )


def rope_angles(grid_pos, head_width):
    one_sixth = head_width // 6
    pair_counts = [(head_width - 4 * one_sixth) // 2, one_sixth, one_sixth]
    pieces = []
    for component in range(3):
        pair_count = pair_counts[component]
        frequency = 1.0 / 10000.0 ** (jnp.arange(pair_count, dtype=jnp.float32) / pair_count)
        pieces.append(grid_pos[component].astype(jnp.float32)[:, None] * frequency[None, :])
    return jnp.concatenate(pieces, axis=1)


def rotate(values, angles):
    full_shape = values.shape
    paired = values.reshape(full_shape[0], full_shape[1], full_shape[2] // 2, 2)
    cosine = jnp.cos(angles)[:, None, :]
    sine_part = jnp.sin(angles)[:, None, :]
    even_part = paired[..., 0]
    odd_part = paired[..., 1]
    turned = jnp.stack(
        [even_part * cosine - odd_part * sine_part, even_part * sine_part + odd_part * cosine],
        axis=-1,
    )
    return turned.reshape(full_shape)


def select_slot(table, index):
    return lax.dynamic_index_in_dim(table, index, 0, keepdims=False)


def spread_slot(gradient, index, slot_count):
    hits = (jnp.arange(slot_count) == index).astype(jnp.float32)
    return hits.reshape((slot_count,) + (1,) * gradient.ndim) * gradient[None]


def columns_forward(inputs, weights, biases, downs, ups):
    latent = jnp.einsum("td,jdr->jtr", inputs, downs, preferred_element_type=jnp.float32).astype(
        jnp.bfloat16
    )
    projected = jnp.einsum("td,jdc->jtc", inputs, weights, preferred_element_type=jnp.float32)
    projected = projected + jnp.einsum(
        "jtr,jrc->jtc", latent, ups, preferred_element_type=jnp.float32
    )
    return (projected + biases.astype(jnp.float32)[:, None, :], latent)


def columns_backward(inputs, weights, downs, ups, latent, upstream):
    grad_up = jnp.einsum("jtr,jtc->jrc", latent, upstream, preferred_element_type=jnp.float32)
    grad_latent = jnp.einsum(
        "jtc,jrc->jtr", upstream, ups, preferred_element_type=jnp.float32
    ).astype(jnp.bfloat16)
    grad_down = jnp.einsum("td,jtr->jdr", inputs, grad_latent, preferred_element_type=jnp.float32)
    grad_inputs = jnp.einsum("jtc,jdc->td", upstream, weights, preferred_element_type=jnp.float32)
    grad_inputs = grad_inputs + jnp.einsum(
        "jtr,jdr->td", grad_latent, downs, preferred_element_type=jnp.float32
    )
    return (grad_inputs, grad_down, grad_up)


def rows_forward(inputs, weight, down, up):
    latent = jnp.dot(inputs, down, preferred_element_type=jnp.float32).astype(jnp.bfloat16)
    partial_value = jnp.dot(inputs, weight, preferred_element_type=jnp.float32) + jnp.dot(
        latent, up, preferred_element_type=jnp.float32
    )
    return (partial_value, latent)


def rows_backward(inputs, weight, down, up, latent, upstream):
    grad_up = jnp.einsum("tr,td->rd", latent, upstream, preferred_element_type=jnp.float32)
    grad_latent = jnp.einsum("td,rd->tr", upstream, up, preferred_element_type=jnp.float32).astype(
        jnp.bfloat16
    )
    grad_down = jnp.einsum("tc,tr->cr", inputs, grad_latent, preferred_element_type=jnp.float32)
    grad_inputs = jnp.einsum("td,cd->tc", upstream, weight, preferred_element_type=jnp.float32)
    grad_inputs = grad_inputs + jnp.einsum(
        "tr,cr->tc", grad_latent, down, preferred_element_type=jnp.float32
    )
    return (grad_inputs, grad_down, grad_up)


def attend_forward(queries, key_rows, value_rows):
    score_scale = HEAD_DIM ** (-0.5)
    length, head_count, width = queries.shape
    stride = min(512, length)

    def one_block(query_block):
        scores = (
            jnp.einsum("qhd,khd->hqk", query_block, key_rows, preferred_element_type=jnp.float32)
            * score_scale
        )
        highest_score = jnp.max(scores, axis=-1, keepdims=True)
        expanded = jnp.exp(scores - highest_score)
        totals = jnp.sum(expanded, axis=-1, keepdims=True)
        weights = (expanded / totals).astype(jnp.bfloat16)
        mixed = jnp.einsum("hqk,khd->qhd", weights, value_rows, preferred_element_type=jnp.float32)
        return (mixed, (highest_score + jnp.log(totals))[..., 0])

    mixed, logsum = lax.map(one_block, queries.reshape(length // stride, stride, head_count, width))
    return (mixed.reshape(length, head_count, width), logsum)


def attend_backward(queries, key_rows, value_rows, logsum, grad_out):
    score_scale = HEAD_DIM ** (-0.5)
    length, head_count, width = queries.shape
    stride = min(512, length)
    count = length // stride

    def one_block(carry, entry):
        acc_keys, acc_values = carry
        query_block, logsum_block, grad_block = entry
        scores = (
            jnp.einsum("qhd,khd->hqk", query_block, key_rows, preferred_element_type=jnp.float32)
            * score_scale
        )
        probs = jnp.exp(scores - logsum_block[..., None])
        grad_probs = jnp.einsum(
            "qhd,khd->hqk", grad_block, value_rows, preferred_element_type=jnp.float32
        )
        delta = jnp.sum(grad_probs * probs, axis=-1, keepdims=True)
        grad_scores = (probs * (grad_probs - delta)).astype(jnp.bfloat16)
        grad_query = (
            jnp.einsum("hqk,khd->qhd", grad_scores, key_rows, preferred_element_type=jnp.float32)
            * score_scale
        )
        grad_keys = (
            jnp.einsum("hqk,qhd->khd", grad_scores, query_block, preferred_element_type=jnp.float32)
            * score_scale
        )
        grad_values = jnp.einsum(
            "hqk,qhd->khd",
            probs.astype(jnp.bfloat16),
            grad_block,
            preferred_element_type=jnp.float32,
        )
        return ((acc_keys + grad_keys, acc_values + grad_values), grad_query)

    zeros = jnp.zeros(key_rows.shape, jnp.float32)
    entries = (
        queries.reshape(count, stride, head_count, width),
        logsum,
        grad_out.reshape(count, stride, head_count, width),
    )
    (grad_keys, grad_values), grad_query = lax.scan(one_block, (zeros, zeros), entries)
    return (grad_query.reshape(length, head_count, width), grad_keys, grad_values)


def square_totals(first, second):
    return lax.psum((first, second), "tensor")


def norm_totals(first, second):
    return lax.psum((first, second), "tensor")


def branch_total(partial_value):
    return lax.psum(partial_value.astype(jnp.bfloat16), "tensor").astype(jnp.float32)


def input_total(partial_value):
    return lax.psum(partial_value.astype(jnp.bfloat16), "tensor").astype(jnp.float32)


def per_device(
    tokens,
    positions,
    time_emb,
    modulation,
    context,
    adapter_index,
    self_qkv,
    self_bias,
    self_gain,
    self_out,
    cross_qkv,
    cross_bias,
    cross_gain,
    cross_out,
    cross_norm_gain,
    cross_norm_bias,
    ffn_in,
    ffn_bias,
    ffn_out,
    out_bias,
    col_down,
    col_up,
    ffn1_down,
    ffn1_up,
    row_down,
    row_up,
    ffn2_down,
    ffn2_up,
    out_grad,
):
    token_count = tokens.shape[1]
    context_count = context.shape[0]
    col_width = self_qkv.shape[2]
    head_count = col_width // HEAD_DIM
    slot_count = col_down.shape[0]
    index = adapter_index[0]
    seq_share = 1.0 / lax.axis_size("seq")
    inputs = tokens[0].astype(jnp.float32)
    modes = modulation + time_emb[0]
    downs = select_slot(col_down, index)
    ups = select_slot(col_up, index)
    row_downs = select_slot(row_down, index)
    row_ups = select_slot(row_up, index)
    first_down = select_slot(ffn1_down, index)
    first_up = select_slot(ffn1_up, index)
    second_down = select_slot(ffn2_down, index)
    second_up = select_slot(ffn2_up, index)
    angles = rope_angles(positions[:, 0, :], HEAD_DIM)
    gains_self = self_gain.astype(jnp.float32)
    gains_cross = cross_gain.astype(jnp.float32)
    biases_out = out_bias.astype(jnp.float32)
    normed_one, inverse_one = normalize(inputs)
    hidden_one = (normed_one * (1.0 + modes[1]) + modes[0]).astype(jnp.bfloat16)
    self_pre, self_latent = columns_forward(hidden_one, self_qkv, self_bias, downs[0:3], ups[0:3])
    square_q, square_k = square_totals(
        jnp.sum(self_pre[0] * self_pre[0], axis=-1), jnp.sum(self_pre[1] * self_pre[1], axis=-1)
    )
    inverse_q = lax.rsqrt(square_q / D + epsilon)
    inverse_k = lax.rsqrt(square_k / D + epsilon)
    query_rot = rotate(
        (self_pre[0] * inverse_q[:, None] * gains_self[0]).reshape(
            token_count, head_count, HEAD_DIM
        ),
        angles,
    ).astype(jnp.bfloat16)
    key_rot = rotate(
        (self_pre[1] * inverse_k[:, None] * gains_self[1]).reshape(
            token_count, head_count, HEAD_DIM
        ),
        angles,
    ).astype(jnp.bfloat16)
    value_self = self_pre[2].astype(jnp.bfloat16).reshape(token_count, head_count, HEAD_DIM)
    key_all, value_all = (
        lax.all_gather(key_rot, "seq", axis=0, tiled=True),
        lax.all_gather(value_self, "seq", axis=0, tiled=True),
    )
    attn_self, logsum_self = attend_forward(query_rot, key_all, value_all)
    mixed_self = attn_self.reshape(token_count, col_width).astype(jnp.bfloat16)
    partial_self, latent_self_out = rows_forward(mixed_self, self_out, row_downs[0], row_ups[0])
    after_self = inputs + (branch_total(partial_self) + biases_out[0]) * modes[2]
    normed_three, inverse_three = normalize(after_self)
    hidden_three = (normed_three * cross_norm_gain + cross_norm_bias).astype(jnp.bfloat16)
    query_pre_c, latent_cq = columns_forward(
        hidden_three, cross_qkv[0:1], cross_bias[0:1], downs[3:4], ups[3:4]
    )
    context_pre, latent_ckv = columns_forward(
        context, cross_qkv[1:3], cross_bias[1:3], downs[4:6], ups[4:6]
    )
    pre_qc = query_pre_c[0]
    pre_kc = context_pre[0]
    square_qc, square_kc = square_totals(
        jnp.sum(pre_qc * pre_qc, axis=-1), jnp.sum(pre_kc * pre_kc, axis=-1)
    )
    inverse_qc = lax.rsqrt(square_qc / D + epsilon)
    inverse_kc = lax.rsqrt(square_kc / D + epsilon)
    query_cross = (
        (pre_qc * inverse_qc[:, None] * gains_cross[0])
        .astype(jnp.bfloat16)
        .reshape(token_count, head_count, HEAD_DIM)
    )
    key_cross = (
        (pre_kc * inverse_kc[:, None] * gains_cross[1])
        .astype(jnp.bfloat16)
        .reshape(context_count, head_count, HEAD_DIM)
    )
    value_cross = context_pre[1].astype(jnp.bfloat16).reshape(context_count, head_count, HEAD_DIM)
    attn_cross, logsum_cross = attend_forward(query_cross, key_cross, value_cross)
    mixed_cross = attn_cross.reshape(token_count, col_width).astype(jnp.bfloat16)
    partial_cross, latent_cross_out = rows_forward(mixed_cross, cross_out, row_downs[1], row_ups[1])
    after_cross = after_self + branch_total(partial_cross) + biases_out[1]
    normed_two, inverse_two = normalize(after_cross)
    hidden_two = (normed_two * (1.0 + modes[4]) + modes[3]).astype(jnp.bfloat16)
    feed_pre, latent_first = columns_forward(
        hidden_two, ffn_in[None], ffn_bias[None], first_down[None], first_up[None]
    )
    gelu_in = feed_pre[0]
    gated = jax.nn.gelu(gelu_in, approximate=True).astype(jnp.bfloat16)
    partial_feed, latent_second = rows_forward(gated, ffn_out, second_down, second_up)
    result = after_cross + (branch_total(partial_feed) + biases_out[2]) * modes[5]
    grad_result = out_grad[0].astype(jnp.float32)
    grad_feed = (grad_result * modes[5]).astype(jnp.bfloat16)
    grad_gated, grad_second_down, grad_second_up = rows_backward(
        gated, ffn_out, second_down, second_up, latent_second, grad_feed
    )
    gelu_value, gelu_pull = jax.vjp(lambda values: jax.nn.gelu(values, approximate=True), gelu_in)
    grad_gelu_in = gelu_pull(grad_gated)[0].astype(jnp.bfloat16)
    grad_hidden_two, grad_first_down, grad_first_up = columns_backward(
        hidden_two, ffn_in[None], first_down[None], first_up[None], latent_first, grad_gelu_in[None]
    )
    total_two = input_total(grad_hidden_two)
    grad_after_cross = grad_result + normalize_back(
        normed_two, inverse_two, total_two * (1.0 + modes[4])
    )
    first_up_grad = spread_slot(grad_first_up[0], index, slot_count)
    second_down_grad = spread_slot(grad_second_down, index, slot_count)
    first_down_grad = spread_slot(grad_first_down[0], index, slot_count)
    second_up_grad = spread_slot(grad_second_up, index, slot_count)
    grad_cross_out = grad_after_cross.astype(jnp.bfloat16)
    grad_mixed_c, grad_rdown_c, grad_rup_c = rows_backward(
        mixed_cross, cross_out, row_downs[1], row_ups[1], latent_cross_out, grad_cross_out
    )
    grad_attn_c = grad_mixed_c.astype(jnp.bfloat16).reshape(token_count, head_count, HEAD_DIM)
    grad_qc, grad_kc, grad_vc = attend_backward(
        query_cross, key_cross, value_cross, logsum_cross, grad_attn_c
    )
    grad_kc, grad_vc = (
        lax.psum(grad_kc.astype(jnp.bfloat16), "seq").astype(jnp.float32),
        lax.psum(grad_vc.astype(jnp.bfloat16), "seq").astype(jnp.float32),
    )
    flat_qc = grad_qc.reshape(token_count, col_width)
    flat_kc = grad_kc.reshape(context_count, col_width)
    stat_qc, stat_kc = norm_totals(
        jnp.sum(flat_qc * gains_cross[0] * pre_qc, axis=-1),
        jnp.sum(flat_kc * gains_cross[1] * pre_kc, axis=-1),
    )
    grad_pre_qc = norm_back(pre_qc, inverse_qc, gains_cross[0], flat_qc, stat_qc).astype(
        jnp.bfloat16
    )
    grad_pre_kc = norm_back(pre_kc, inverse_kc, gains_cross[1], flat_kc, stat_kc).astype(
        jnp.bfloat16
    )
    grad_pre_vc = grad_vc.reshape(context_count, col_width).astype(jnp.bfloat16)
    grad_hidden_three, grad_down_cq, grad_up_cq = columns_backward(
        hidden_three, cross_qkv[0:1], downs[3:4], ups[3:4], latent_cq, grad_pre_qc[None]
    )
    grad_context, grad_down_ckv, grad_up_ckv = columns_backward(
        context,
        cross_qkv[1:3],
        downs[4:6],
        ups[4:6],
        latent_ckv,
        jnp.stack([grad_pre_kc, grad_pre_vc]),
    )
    context_grad = lax.psum(grad_context, ("dp", "tensor"))
    total_three = input_total(grad_hidden_three)
    grad_after_self = grad_after_cross + normalize_back(
        normed_three, inverse_three, total_three * cross_norm_gain
    )
    cross_up_grad = spread_slot(
        jnp.concatenate([grad_up_cq, grad_up_ckv * seq_share], axis=0), index, slot_count
    )
    cross_rdown_grad = spread_slot(grad_rdown_c, index, slot_count)
    cross_down_grad = spread_slot(
        jnp.concatenate([grad_down_cq, grad_down_ckv * seq_share], axis=0), index, slot_count
    )
    cross_rup_grad = spread_slot(grad_rup_c, index, slot_count)
    grad_self_out = (grad_after_self * modes[2]).astype(jnp.bfloat16)
    grad_mixed_s, grad_rdown_s, grad_rup_s = rows_backward(
        mixed_self, self_out, row_downs[0], row_ups[0], latent_self_out, grad_self_out
    )
    grad_attn_s = grad_mixed_s.astype(jnp.bfloat16).reshape(token_count, head_count, HEAD_DIM)
    grad_query_rot, grad_key_all, grad_value_all = attend_backward(
        query_rot, key_all, value_all, logsum_self, grad_attn_s
    )
    grad_key_rot, grad_value_self = (
        lax.psum_scatter(
            grad_key_all.astype(jnp.bfloat16), "seq", scatter_dimension=0, tiled=True
        ).astype(jnp.float32),
        lax.psum_scatter(
            grad_value_all.astype(jnp.bfloat16), "seq", scatter_dimension=0, tiled=True
        ).astype(jnp.float32),
    )
    flat_q = rotate(grad_query_rot, -angles).reshape(token_count, col_width)
    flat_k = rotate(grad_key_rot, -angles).reshape(token_count, col_width)
    stat_q, stat_k = norm_totals(
        jnp.sum(flat_q * gains_self[0] * self_pre[0], axis=-1),
        jnp.sum(flat_k * gains_self[1] * self_pre[1], axis=-1),
    )
    grad_pre_q = norm_back(self_pre[0], inverse_q, gains_self[0], flat_q, stat_q).astype(
        jnp.bfloat16
    )
    grad_pre_k = norm_back(self_pre[1], inverse_k, gains_self[1], flat_k, stat_k).astype(
        jnp.bfloat16
    )
    grad_pre_v = grad_value_self.reshape(token_count, col_width).astype(jnp.bfloat16)
    grad_hidden_one, grad_down_self, grad_up_self = columns_backward(
        hidden_one,
        self_qkv,
        downs[0:3],
        ups[0:3],
        self_latent,
        jnp.stack([grad_pre_q, grad_pre_k, grad_pre_v]),
    )
    total_one = input_total(grad_hidden_one)
    grad_inputs = grad_after_self + normalize_back(
        normed_one, inverse_one, total_one * (1.0 + modes[1])
    )
    self_up_grad = spread_slot(grad_up_self, index, slot_count)
    self_rdown_grad = spread_slot(grad_rdown_s, index, slot_count)
    self_down_grad = spread_slot(grad_down_self, index, slot_count)
    self_rup_grad = spread_slot(grad_rup_s, index, slot_count)
    col_up_grad = jnp.concatenate([self_up_grad, cross_up_grad], axis=1)
    row_down_grad = jnp.stack([self_rdown_grad, cross_rdown_grad], axis=1)
    col_down_grad = jnp.concatenate([self_down_grad, cross_down_grad], axis=1)
    row_up_grad = jnp.stack([self_rup_grad, cross_rup_grad], axis=1)
    col_up_grad, first_up_grad, row_down_grad, second_down_grad = (
        lax.psum(col_up_grad.astype(jnp.bfloat16), ("dp", "seq")).astype(jnp.float32),
        lax.psum(first_up_grad.astype(jnp.bfloat16), ("dp", "seq")).astype(jnp.float32),
        lax.psum(row_down_grad.astype(jnp.bfloat16), ("dp", "seq")).astype(jnp.float32),
        lax.psum(second_down_grad.astype(jnp.bfloat16), ("dp", "seq")).astype(jnp.float32),
    )
    col_down_grad, first_down_grad, row_up_grad, second_up_grad = lax.psum(
        (col_down_grad, first_down_grad, row_up_grad, second_up_grad), ("dp", "seq", "tensor")
    )
    return (
        result.astype(jnp.bfloat16)[None],
        grad_inputs.astype(jnp.bfloat16)[None],
        context_grad,
        col_down_grad,
        col_up_grad,
        first_down_grad,
        first_up_grad,
        row_down_grad,
        row_up_grad,
        second_down_grad,
        second_up_grad,
    )


def solution(mesh):
    placed = (
        P("dp", "seq", None),
        P(None, "dp", "seq"),
        P("dp", None, None),
        P(),
        P(),
        P("dp"),
        P(None, None, "tensor"),
        P(None, "tensor"),
        P(None, "tensor"),
        P("tensor", None),
        P(None, None, "tensor"),
        P(None, "tensor"),
        P(None, "tensor"),
        P("tensor", None),
        P(),
        P(),
        P(None, "tensor"),
        P("tensor"),
        P("tensor", None),
        P(),
        P(),
        P(None, None, None, "tensor"),
        P(),
        P(None, None, "tensor"),
        P(None, None, "tensor", None),
        P(),
        P(None, "tensor", None),
        P(),
        P("dp", "seq", None),
    )
    return jax.shard_map(
        per_device,
        mesh=mesh,
        in_specs=placed,
        out_specs=(
            P("dp", "seq", None),
            P("dp", "seq", None),
            P(),
            P(),
            P(None, None, None, "tensor"),
            P(),
            P(None, None, "tensor"),
            P(None, None, "tensor", None),
            P(),
            P(None, "tensor", None),
            P(),
        ),
        check_vma=False,
    )
```

profile of v0, /device:TPU:9, one launch (start us, length us, event | category | flops | bytes accessed | tf_op | source)
XLA Modules:
  0.0 1690.6 jit_solution(4883182369540955361)
XLA Ops:
  19.8 4.2 fusion.116
  36.7 7.5 all-reduce.3
  51.9 4.9 subtract_convert_fusion.3
  67.7 4.0 pad_maximum_fusion.5
  71.7 3.7 convert_element_type.382
  81.0 8.3 all-gather.5.cloned.1.call-done
  90.3 21.5 %while.54 = (s32[]{:T(128)}, bf16[2,512,3,128]{3,1,2,0:T(8,128)(2,1)}, f32[2,3,512]{2,1,0:T(4,128)S(1)}, bf16[2,512,3,128]{3,1,2,0:T(8,128)(2,1)}, bf16[2048,3,1...) while((s32[]{:T(128)}, bf16[2,512,3,128]{3,1,2,0:T(8,128)(2,1)}, ...), condition=%wide.region_9.10_spmd, body=%wide.region_6.9_spmd.sunk | while | flops 1638922752 | bytes 54716596 | solution.py:131
  96.2 3.9 fusion.366
  106.9 3.9 fusion.366
  142.9 99.2 %all-reduce.17.cloned.1.call-done = bf16[1024,1536]{1,0:T(8,128)(2,1)} async-done(((bf16[1024,1536]{1,0:T(8,128)(2,1)}), bf16[1024,1536]{1,0:T(8,128)(2,1)}) %all-reduce.17.cloned.1.call-update) | async-done | bytes 3145744 | tf_op jit(solution)/shard_map/psum | solution.py:189
  242.2 4.3 fusion.175
  254.7 4.5 fusion.144
  259.2 9.8 all-reduce.2
  276.3 3.6 copy.80
  286.1 10.0 while.55
  311.8 12.1 fusion.133
  323.9 103.4 %all-reduce.19.cloned.1.call-done = bf16[1024,1536]{1,0:T(8,128)(2,1)} async-done(((bf16[1024,1536]{1,0:T(8,128)(2,1)}), bf16[1024,1536]{1,0:T(8,128)(2,1)}) %all-reduce.19.cloned.1.call-update) | async-done | bytes 3145744 | tf_op jit(solution)/shard_map/psum | solution.py:189
  427.3 5.7 fusion.242
  439.4 9.8 fusion.246
  449.3 9.3 fusion.88
  458.6 10.7 fusion.76
  471.0 7.8 fusion.248
  482.6 120.0 %all-reduce.21.cloned.1.call-done = bf16[1024,1536]{1,0:T(8,128)(2,1)} async-done(((bf16[1024,1536]{1,0:T(8,128)(2,1)}), bf16[1024,1536]{1,0:T(8,128)(2,1)}) %all-reduce.21.cloned.1.call-update) | async-done | bytes 3145744 | tf_op jit(solution)/shard_map/psum | solution.py:193
  602.6 4.9 fusion.115
  608.3 4.4 fusion.91
  626.1 54.1 %while.56 = (s32[]{:T(128)}, f32[512,3,128]{0,2,1:T(8,128)}, f32[512,3,128]{0,2,1:T(8,128)}, f32[2,512,3,128]{1,0,3,2:T(2,128)}, bf16[2,512,3,128]{3,1,2,0:T(8,1...) while((s32[]{:T(128)}, f32[512,3,128]{0,2,1:T(8,128)}, ...), condition=%wide.region_30.31_spmd.clone, body=%wide.region_28.30_spmd.clone.sunk | while | flops 1017248256 | bytes 55490932 | solution.py:176
  638.1 15.0 dynamic_update_slice.36
  665.1 15.0 dynamic_update_slice.36
  680.1 3.8 reshape_reshape.31
  686.7 9.5 psum.183
  706.2 4.3 fusion.250
  710.5 3.7 fusion.254
  716.9 109.6 %all-reduce.23.cloned.1.call-done = bf16[1024,1536]{1,0:T(8,128)(2,1)} async-done(((bf16[1024,1536]{1,0:T(8,128)(2,1)}), bf16[1024,1536]{1,0:T(8,128)(2,1)}) %all-reduce.23.cloned.1.call-update) | async-done | bytes 3145744 | tf_op jit(solution)/shard_map/psum | solution.py:193
  826.5 6.2 fusion.114
  833.0 7.3 multiply_convert_fusion.2
  853.4 92.1 %while.57 = (s32[]{:T(128)}, f32[2048,3,128]{0,2,1:T(8,128)}, f32[2048,3,128]{0,2,1:T(8,128)}, f32[2,512,3,128]{1,0,3,2:T(2,128)}, bf16[2,512,3,128]{3,1,2,0:T(8...) while((s32[]{:T(128)}, f32[2048,3,128]{0,2,1:T(8,128)}, ...), condition=%wide.region_38.39_spmd.clone, body=%wide.region_36.38_spmd.clone.sunk | while | flops 4068407808 | bytes 136100112 | solution.py:176
  857.0 4.0 bitcast_add_fusion.11
  861.0 6.3 multiply_reduce_fusion.15
  867.3 6.6 multiply_convert_fusion.14
  882.8 15.0 dynamic_update_slice.37
  901.3 5.5 bitcast_add_fusion.11
  906.8 6.3 multiply_reduce_fusion.15
  913.1 6.6 multiply_convert_fusion.14
  922.4 5.1 bitcast_add_fusion.10
  930.5 15.0 dynamic_update_slice.37
  951.2 7.9 fusion.162
  959.1 10.0 fusion.247
  972.5 5.6 add_convert_fusion.3
  982.1 4.4 reshape_reshape.34
  992.5 6.2 multiply_subtract_fusion.1
  1007.5 3.9 pad_maximum_fusion.2
  1017.8 3.8 fusion.149
  1021.7 14.2 all-reduce.1
  1035.9 4.7 subtract_convert_fusion.1
  1044.5 4.7 fusion.176
  1051.3 8.3 fusion.112
  1065.6 4.2 fusion.228
  1087.6 28.0 %all-reduce.29.cloned.1.call-done = (bf16[8,6,16,384]{3,2,1,0:T(8,128)(2,1)}, bf16[8,16,2240]{2,1,0:T(8,128)(2,1)}, bf16[8,2,384,16]{2,3,1,0:T(8,128)(2,1)}, bf16[8,2240,16]{1,2,0:T(8,128)(2,1)}) async-done(((bf16[8,6,16,384]{3,2,1,0:T(8,128)(2,1)}, bf16[8,16,2240]{2,1,0:T(8,128)(2,1)}, bf16[8,2,384,16]{2,3,1,0:T(8,128)(2,1)}, bf16[8,2240,16]{1,2,0:T(8,128)(2,1)}), (bf16[8,6,16,384]{3,2,1,0:T(8,128)(2,1)}, ...) | async-done | bytes 1933328 | tf_op jit(solution)/shard_map/psum | solution.py:433
  1122.8 217.4 %all-reduce.31.cloned.1.call-done = (bf16[1024,1536]{1,0:T(8,128)(2,1)}, bf16[1024,1536]{1,0:T(8,128)(2,1)}) async-done(((bf16[1024,1536]{1,0:T(8,128)(2,1)}, bf16[1024,1536]{1,0:T(8,128)(2,1)}), (bf16[1024,1536]{1,0:T(8,128)(2,1)}, bf16[1024,1536]{1,0:T(8,128)(2,1)})) %all-reduce.31.cloned.1.call-update) | async-done | bytes 6291472 | tf_op jit(solution)/shard_map/psum | solution.py:189
  1340.2 4.2 fusion.113
  1344.4 6.6 fusion.121
  1354.7 138.7 %all-reduce.25.cloned.1.call-done = f32[512,1536]{1,0:T(8,128)} async-done(((f32[512,1536]{1,0:T(8,128)}), f32[512,1536]{1,0:T(8,128)}) %all-reduce.25.cloned.1.call-update) | async-done | bytes 3145744 | tf_op jit(solution)/shard_map/psum | solution.py:370
  1493.4 181.2 %all-reduce.27.cloned.1.call-done = (f32[8,6,1536,16]{2,3,1,0:T(8,128)}, f32[8,1536,16]{1,2,0:T(8,128)}, f32[8,2,16,1536]{3,2,1,0:T(8,128)}, f32[8,16,1536]{2,1,0:T(8,128)}) async-done(((f32[8,6,1536,16]{2,3,1,0:T(8,128)}, f32[8,1536,16]{1,2,0:T(8,128)}, f32[8,2,16,1536]{3,2,1,0:T(8,128)}, f32[8,16,1536]{2,1,0:T(8,128)}), (f32[8,6,1536,16]{2,3,1,0:T(8,128)}, f32[8,1536,16]{1,2,0:T(8,128)}, ...) | async-done | bytes 7864336 | tf_op jit(solution)/shard_map/psum | solution.py:438
  1674.6 3.9 copy.222
  (593 shorter events, 320.8 us)
Async XLA Ops:
  7.2 12.5 copy-start
  7.2 71.3 %all-gather.3.cloned.1.call-start = ((), (), s32[]{:S(2)}) async-start(), calls=%async_computation.2 | async-start | bytes 2359296 | tf_op jit(solution)/shard_map/all_gather | solution.py:270
  11.6 8.0 copy-start.112
  12.6 7.1 copy-start.121
  13.9 5.7 copy-start.102
  27.1 8.2 copy-start.134
  27.1 8.2 copy-start.135
  44.3 6.9 copy-start.48
  44.3 6.9 copy-start.67
  44.9 7.0 copy-start.116
  44.9 7.0 copy-start.118
  62.4 26.9 %all-gather.5.cloned.1.call-start = ((), (), s32[]{:S(2)}) async-start(), calls=%async_computation.3 | async-start | bytes 2359296 | tf_op jit(solution)/shard_map/all_gather | solution.py:271
  67.2 175.0 %all-reduce.17.cloned.1.call-start = ((), (), s32[]{:S(2)}) async-start(), calls=%async_computation.4 | async-start | bytes 6291456 | tf_op jit(solution)/shard_map/psum | solution.py:189
  111.7 7.2 copy-start.84
  122.5 304.8 %all-reduce.19.cloned.1.call-start = ((), (), s32[]{:S(2)}) async-start(), calls=%async_computation.5 | async-start | bytes 6291456 | tf_op jit(solution)/shard_map/psum | solution.py:189
  130.0 112.2 %copy-start.66 = (f32[1536]{0:T(1024)S(1)}, f32[1536]{0:T(1024)}, u32[]{:S(2)}) copy-start(f32[1536]{0:T(1024)} %get-tuple-element.312) | copy-start | bytes 18436
  251.2 8.0 copy-start.22
  306.9 295.7 %all-reduce.21.cloned.1.call-start = ((), (), s32[]{:S(2)}) async-start(), calls=%async_computation.6 | async-start | bytes 6291456 | tf_op jit(solution)/shard_map/psum | solution.py:193
  433.1 6.3 slice-start.4
  439.4 9.8 copy-start.89
  439.4 9.8 copy-start.138
  449.3 9.3 copy-start.124
  469.3 9.6 copy-start.30
  471.0 7.9 copy-start.74
  482.4 344.1 %all-reduce.23.cloned.1.call-start = ((), (), s32[]{:S(2)}) async-start(), calls=%async_computation.7 | async-start | bytes 6291456 | tf_op jit(solution)/shard_map/psum | solution.py:193
  602.6 5.6 copy-start.93
  602.6 5.6 copy-start.99
  602.6 5.6 copy-start.111
  706.1 273.9 %all-reduce.33.cloned.1.call-start = ((), (), s32[]{:S(2)}) async-start(), calls=%async_computation.14 | async-start | bytes 1572864 | tf_op jit(solution)/shard_map/psum | solution.py:343
  706.2 8.0 copy-start.128
  716.8 272.7 %reduce-scatter.3.cloned.1.call-start = ((), (), s32[]{:S(2)}) async-start(), calls=%async_computation.8 | async-start | bytes 2359296 | tf_op jit(solution)/shard_map/reduce_scatter | solution.py:392
  826.5 6.2 copy-start.5
  826.5 6.2 copy-start.11
  826.5 6.5 copy-start.43
  826.5 6.5 copy-start.97
  826.5 6.5 copy-start.107
  826.5 6.5 copy-start.109
  846.3 7.1 copy-start.85
  867.3 6.6 copy-start.1
  913.1 6.6 copy-start.1
  948.8 91.8 %reduce-scatter.5.cloned.1.call-start = ((), (), s32[]{:S(2)}) async-start(), calls=%async_computation.9 | async-start | bytes 2359296 | tf_op jit(solution)/shard_map/reduce_scatter | solution.py:395
  949.1 9.9 slice-start.2
  949.1 9.9 slice-start.6
  951.1 7.9 slice-start.3
  951.2 7.9 slice-start.7
  972.4 7.6 copy-start.126
  972.4 143.2 %all-reduce.29.cloned.1.call-start = ((), (), s32[]{:S(2)}) async-start(), calls=%async_computation.12 | async-start | bytes 3932160 | tf_op jit(solution)/shard_map/psum | solution.py:433
  972.5 5.7 copy-start.34
  972.5 5.7 copy-start.83
  972.5 6.6 copy-start.46
  972.5 6.6 copy-start.81
  1017.8 18.0 %copy-start.117 = (f32[1024]{0:T(1024)S(1)}, f32[1024]{0:T(1024)}, u32[]{:S(2)}) copy-start(f32[1024]{0:T(1024)} %copy-done.116) | copy-start | bytes 12292
  1017.8 18.0 %copy-start.119 = (f32[1024]{0:T(1024)S(1)}, f32[1024]{0:T(1024)}, u32[]{:S(2)}) copy-start(f32[1024]{0:T(1024)} %copy-done.118) | copy-start | bytes 12292
  1044.4 5.7 copy-start.100
  1051.3 288.9 %all-reduce.31.cloned.1.call-start = ((), (), s32[]{:S(2)}) async-start(), calls=%async_computation.13 | async-start | bytes 12582912 | tf_op jit(solution)/shard_map/psum | solution.py:189
  1059.6 433.8 %all-reduce.25.cloned.1.call-start = ((), (), s32[]{:S(2)}) async-start(), calls=%async_computation.10 | async-start | bytes 6291456 | tf_op jit(solution)/shard_map/psum | solution.py:370
  1076.2 598.3 %all-reduce.27.cloned.1.call-start = ((), (), s32[]{:S(2)}) async-start(), calls=%async_computation.11 | async-start | bytes 15728640 | tf_op jit(solution)/shard_map/psum | solution.py:438
  1115.6 6.1 copy-start.64
  1340.2 10.9 slice-start
  1344.4 6.7 copy-start.7
  1344.4 6.7 slice-start.1
  1344.4 6.7 copy-start.42
  1344.4 6.7 copy-start.114
  1344.4 6.7 copy-start.123
  (129 other events, 344.5 us)
Sparse Core Ops, SparseCore 0:
  62.6 13.5 all-gather.2
  78.3 10.9 all-gather.4
  122.6 119.4 all-reduce.16
  307.0 120.2 all-reduce.18
  482.5 120.0 all-reduce.20
  706.2 120.2 all-reduce.22
  829.4 20.9 all-reduce.32
  949.0 10.8 reduce-scatter.2
  972.5 11.0 reduce-scatter.4
  1051.4 64.1 all-reduce.28
  1118.7 221.3 all-reduce.30
  1346.5 146.8 all-reduce.24
  1500.7 173.8 all-reduce.26
where the time goes:
time: 1710 us; the launch traced here: 1690 us
  waiting for transfers between devices  1010 us (59%)
  matrix products  260 us (15%)
  local copies, waits for them, and re-layouts  196 us (11%)
  other arithmetic  169 us (10%)
  blocking collectives  41 us (2%)
    psum x3, waiting for transfers between devices, branch_total(): lax.psum(partial_value.astype(jnp.bfloat16), 'tensor').astype(jnp.float32)  420 us
    psum x2, waiting for transfers between devices, input_total(): lax.psum(partial_value.astype(jnp.bfloat16), 'tensor').astype(jnp.float32)  230 us
    psum x1, waiting for transfers between devices, per_device(): lax.psum((col_down_grad, first_down_grad, row_up_grad, second_up_grad), (...  181 us
    psum x1, waiting for transfers between devices, per_device(): context_grad = lax.psum(grad_context, ('dp', 'tensor'))  139 us
    dynamic_update_slice x8, local copies, waits for them, and re-layouts, attend_forward(): lax.map(one_block, queries.reshape(length // stride, stride, head_count,...  72.1 us
  transfers between devices with their start and end apart: 13, of which 9 were waited for; matrix products, arithmetic and copies ran while one was open for 19% of the time, Pallas kernels for 0%

commit v1 on v0

v1 whole, which is shorter than its diff:
```python
import functools
import math

import jax
import jax.numpy as jnp
import numpy as np
from jax import lax
from jax.experimental import pallas as pl
from jax.experimental.pallas import tpu as pltpu
from jax.sharding import PartitionSpec as P

F32 = jnp.float32
BF16 = jnp.bfloat16
HEAD_DIM = 128
EPS = 1e-06
LOG2E = 1.4426950408889634
SCALE = HEAD_DIM ** (-0.5)
VMEM_LIMIT = 58 * 1024 * 1024
GELU_C = math.sqrt(2.0 / math.pi)
M0, M1, M2, M3, M4, M5, B0, B1, B2, CG, CB = range(11)
AT_T, AT_S, ADAPTER, PART, SLOTS = range(5)


def nn(left, right):
    return jnp.dot(left, right, preferred_element_type=F32)


def nt(left, right):
    return lax.dot_general(left, right, (((1,), (1,)), ((), ())), preferred_element_type=F32)


def row_total(values):
    ones = jnp.ones((8, values.shape[1]), BF16)
    high = values.astype(BF16)
    return nt(ones, high) + nt(ones, (values - high.astype(F32)).astype(BF16))


def mean(values):
    return jnp.mean(values, axis=-1, keepdims=True)


def normalize(values):
    centered = values - mean(values)
    inverse = lax.rsqrt(mean(centered * centered) + EPS)
    return centered * inverse, inverse


def normalize_back(normed, inverse, upstream):
    return inverse * (upstream - mean(upstream) - normed * mean(upstream * normed))


def pair_swap(values):
    width = values.shape[1]
    lane = lax.broadcasted_iota(jnp.int32, values.shape, 1)
    return jnp.where(lane % 2 == 0, pltpu.roll(values, width - 1, 1), pltpu.roll(values, 1, 1))


def rope(values, cosine, sine):
    return values * cosine + pair_swap(values) * sine


def rope_back(values, cosine, sine):
    return values * cosine - pair_swap(values) * sine


def heads_of(array, count):
    return [array[:, h * HEAD_DIM : (h + 1) * HEAD_DIM] for h in range(count)]


def whole(shape):
    return pl.BlockSpec(shape, lambda *_: (0,) * len(shape))


def run_kernel(body, meta, ins, outs, grid=(1,), scratch=(), us=1.0, aliases=None, after=()):
    count = len(ins)
    ins = list(ins) + [(a, pl.BlockSpec(memory_space=pl.ANY)) for a in after]
    arrays = [a for a, _ in ins]
    moved = sum(math.prod(a.shape) * a.dtype.itemsize for a in arrays[:count]) + sum(
        math.prod(s.shape) * s.dtype.itemsize for s, _ in outs
    )

    def reading(meta_ref, *refs):
        return body(meta_ref, *refs[:count], *refs[len(arrays) :])

    return pl.pallas_call(
        reading,
        grid_spec=pltpu.PrefetchScalarGridSpec(
            num_scalar_prefetch=1,
            grid=grid,
            in_specs=[s for _, s in ins],
            out_specs=[s for _, s in outs],
            scratch_shapes=list(scratch),
        ),
        out_shape=[s for s, _ in outs],
        input_output_aliases=aliases or {},
        compiler_params=pltpu.CompilerParams(vmem_limit_bytes=VMEM_LIMIT),
        cost_estimate=pl.CostEstimate(
            flops=int(us * 1.15e9), bytes_accessed=int(min(moved, us * 2e6)), transcendentals=0
        ),
    )(meta, *arrays)


def sds(shape, dtype):
    return jax.ShapeDtypeStruct(shape, dtype)


def qkv_kernel(head_count, meta, tok, mod, emb, b_out, cg, cb, w, up, dn, bias, gain, cos, sin, ctx_ssq, *outs):
    y1, lat_t, pre_q, pre_k, raw_q, kv, ssq, vec, up_s = outs
    width = head_count * HEAD_DIM
    rank = up.shape[2]
    modes = mod[...] + emb[...]

    @pl.when(pl.program_id(0) == 0)
    def _():
        row = lax.broadcasted_iota(jnp.int32, modes.shape, 0)
        rows = [modes + jnp.where((row == 1) | (row == 4), 1.0, 0.0), b_out[...].astype(F32), cg[...], cb[...]]
        vec[...] = jnp.concatenate(rows + [jnp.zeros((5, modes.shape[1]), F32)], axis=0)
        up_s[...] = jnp.zeros_like(up_s)
        for j in range(3):
            up_s[j * rank : (j + 1) * rank, j * width : (j + 1) * width] = up[0, j]

    normed, _ = normalize(tok[...].astype(F32))
    y = (normed * (1.0 + modes[1:2, :]) + modes[0:1, :]).astype(BF16)
    y1[...] = y
    down = jnp.concatenate([dn[0, j] for j in range(3)], axis=0)
    lat = nt(y, down).astype(BF16)
    lat_t[...] = nt(down, y).astype(BF16)
    totals = []
    for j in range(3):
        lanes = slice(j * width, (j + 1) * width)
        u = nn(y, w[j]) + nn(lat, up_s[:, lanes]) + bias[j : j + 1, :].astype(F32)
        if j == 2:
            kv[:, width:] = u.astype(BF16)
            continue
        (pre_q, pre_k)[j][...] = u.astype(BF16)
        totals.append(row_total(u * u))
        scaled = u * gain[j : j + 1, :].astype(F32)
        for h in range(head_count):
            lanes = slice(h * HEAD_DIM, (h + 1) * HEAD_DIM)
            (raw_q, kv)[j][:, lanes] = rope(scaled[:, lanes], cos[...], sin[...]).astype(BF16)
    row = lax.broadcasted_iota(jnp.int32, totals[0].shape, 0)
    ssq[...] = jnp.where(row == 0, totals[0], jnp.where(row == 1, totals[1], ctx_ssq[...]))


def attention_kernel(groups, meta, raw_q, st, st_own, st_sib, k_own, k_sib, v_own, v_sib, *outs):
    blocks, out, lse, kn, vt = outs[:groups], outs[groups], outs[groups + 1], outs[groups + 2], outs[groups + 3]
    count = k_own.shape[0]
    step = pl.program_id(1)

    @pl.when(step == 0)
    def _():
        for at, (k, s, v) in enumerate(((k_own, st_own, v_own), (k_sib, st_sib, v_sib))):
            rows = slice(at * count, (at + 1) * count)
            kn[rows, :] = (k[...].astype(F32) * s[...].T[:, 1:2]).astype(BF16)
            vt[:, rows] = v[...].astype(F32).T.astype(BF16)

    q = (raw_q[...].astype(F32) * (st[...].T[:, 0:1] * (SCALE * LOG2E))).astype(BF16)
    scores = nt(kn[...], q)
    highest = jnp.max(scores, axis=0, keepdims=True)
    e = jnp.exp2(scores - highest)
    total = jnp.sum(e, axis=0, keepdims=True)
    mixed = (nn(vt[...], e.astype(BF16)) / total).T.astype(BF16)
    out[...] = mixed
    for r in range(groups):

        @pl.when(step == r)
        def _(r=r):
            blocks[r][...] = mixed

    lse[...] = jnp.broadcast_to(highest + jnp.log2(total), lse.shape)


def attention_back_kernel(groups, first, meta, raw_q, st, st_own, st_sib, k_own, k_sib, v_own, v_sib, out, lse, *rest):
    grads, rest = rest[:groups], rest[groups:]
    if not first:
        stat_in, cross_in = rest[:2]
        rest = rest[2:]
    dq, dkv_own, dkv_sib, stat, cross, kn, knt, vn, dk_acc, dv_acc, g_s = rest
    count = k_own.shape[0]
    size = raw_q.shape[0]
    step = pl.program_id(0)

    @pl.when(step == 0)
    def _():
        for at, (k, s, v) in enumerate(((k_own, st_own, v_own), (k_sib, st_sib, v_sib))):
            rows = slice(at * count, (at + 1) * count)
            scaled = k[...].astype(F32) * s[...].T[:, 1:2]
            kn[rows, :] = scaled.astype(BF16)
            knt[:, rows] = scaled.T.astype(BF16)
            vn[rows, :] = v[...]
        dk_acc[...] = jnp.zeros_like(dk_acc)
        dv_acc[...] = jnp.zeros_like(dv_acc)
        stat[...] = jnp.zeros_like(stat) if first else stat_in[...]
        cross[...] = jnp.zeros_like(cross) if first else cross_in[...]

    for r in range(groups):

        @pl.when(step == r)
        def _(r=r):
            g_s[...] = grads[r][...]

    raw = raw_q[...].astype(F32)
    q = (raw * (st[...].T[:, 0:1] * (SCALE * LOG2E))).astype(BF16)
    g = g_s[...]
    delta = row_total(g.astype(F32) * out[...].astype(F32))[0:1, :]
    p = jnp.exp2(nt(kn[...], q) - lse[0:1, :])
    dv_acc[...] += nn(p.astype(BF16), g)
    ds = (p * (nt(vn[...], g) - delta)).astype(BF16)
    dk_acc[...] += nn(ds, q)
    dqs = nn(knt[...], ds).T * SCALE
    dq[...] = dqs
    lanes = pl.ds(pl.multiple_of(lax.rem(meta[AT_T] + step, groups) * size, size), size)
    total = row_total(dqs * raw)
    stat[:, lanes] += jnp.where(lax.broadcasted_iota(jnp.int32, total.shape, 0) == 0, total, 0.0)

    @pl.when(step == pl.num_programs(0) - 1)
    def _():
        for at, (k, dkv, sums) in enumerate(((k_own, dkv_own, stat), (k_sib, dkv_sib, cross))):
            rows = slice(at * count, (at + 1) * count)
            dk = dk_acc[rows, :] * (1.0 / LOG2E)
            dkv[:, :HEAD_DIM] = dk.astype(dkv.dtype)
            dkv[:, HEAD_DIM:] = dv_acc[rows, :].astype(dkv.dtype)
            all_k = row_total(dk * k[...].astype(F32))
            sums[...] += jnp.where(lax.broadcasted_iota(jnp.int32, all_k.shape, 0) == 1, all_k, 0.0)


def qkv_back_kernel(head_count, at, meta, *refs):
    n = head_count
    dq, dkv, dkv_in = (refs[j * n : (j + 1) * n] for j in range(3))
    refs = refs[3 * n :]
    pre_q, pre_k, st, st_back, gain_in, cos, sin, w, up_in, dn_in, tok, vec, y1, lat_t, dx1 = refs[:15]
    packed_in = refs[15] if at else None
    part, packed, up = refs[-3:]
    inverse, cubed = st[...].T, st_back[...].T
    c, s = cos[...], sin[...]
    width = n * HEAD_DIM
    rank = up_in.shape[2]
    d = tok.shape[1]
    gain = gain_in[...].astype(F32)
    up[...] = jnp.zeros_like(up)
    for j in range(3):
        up[j * rank : (j + 1) * rank, j * width : (j + 1) * width] = up_in[0, j]
    dn = jnp.concatenate([dn_in[0, j] for j in range(3)], axis=0)
    dk = [a[:, :HEAD_DIM] + b[:, :HEAD_DIM].astype(F32) for a, b in zip(dkv, dkv_in)]
    dv = [a[:, HEAD_DIM:] + b[:, HEAD_DIM:].astype(F32) for a, b in zip(dkv, dkv_in)]
    grads = [
        jnp.concatenate([rope_back(ref[...], c, s) for ref in dq], axis=1),
        jnp.concatenate([rope_back(a, c, s) for a in dk], axis=1),
        jnp.concatenate(dv, axis=1).astype(BF16),
    ]
    for j, pre in enumerate((pre_q, pre_k)):
        grads[j] = (
            inverse[:, j : j + 1] * gain[j : j + 1, :] * grads[j] - pre[...].astype(F32) * cubed[:, j : j + 1]
        ).astype(BF16)
    joined = jnp.concatenate(grads, axis=1)
    d_lat = nt(joined, up[...]).astype(BF16)
    d_lat_t = nt(up[...], joined).astype(BF16)
    total = nn(d_lat, dn)
    for j in range(3):
        total = total + nt(grads[j], w[j])
    normed, inverse = normalize(tok[...].astype(F32))
    back = normalize_back(normed, inverse, total * vec[M1 : M1 + 1, :])
    own = (meta[0] == at).astype(F32)
    part[...] = (back + dx1[...] * own).astype(part.dtype)
    g_dn = nn(d_lat_t, y1[...])
    for j in range(3):
        rows = slice(j * rank, (j + 1) * rank)
        g_up = nn(lat_t[rows, :], grads[j])
        for start, g in ((j * d, g_dn[rows, :]), (3 * d + j * width, g_up)):
            lanes = slice(start, start + g.shape[1])
            packed[:, lanes] = g + packed_in[:, lanes] if at else g


def context_kernel(groups, meta, ctx, w, up, dn, bias, gain, up_q, down_row, pre, low, ssq, lat_t):
    key = meta[AT_S] == 0
    c = ctx[...]
    count = c.shape[0]
    rank, width = up.shape[2:]
    lat = nt(c, dn[0, 0]).astype(BF16)
    lat_t[...] = nt(dn[0, 0], c).astype(BF16)
    b, g = bias[...].astype(F32), gain[...].astype(F32)
    u = nn(c, w[0]) + nn(lat, up[0, 0]) + jnp.where(key, b[1:2, :], b[2:3, :])
    pre[...] = u
    low[:count, :] = (u * jnp.where(key, g[1:2, :], 1.0)).astype(BF16)
    low[count : count + rank, :] = up_q[0, 0]
    low[count + rank : count + 2 * rank, :] = down_row[0, 0]
    low[count + 2 * rank : count + 3 * rank, :] = down_row[0, 1]
    row = lax.broadcasted_iota(jnp.int32, (rank, width), 0)
    low[count + 3 * rank :, :] = jnp.where(row == 0, b[0:1, :], jnp.where(row == 1, g[0:1, :], 0.0)).astype(BF16)
    total = row_total(u * u)
    share, block = count // groups, ssq.shape[1] // groups
    ssq[...] = jnp.zeros_like(ssq)
    for j in range(groups):
        ssq[:, j * block : j * block + share] = total[:, j * share : (j + 1) * share]


def context_row(groups, count, rows):
    share, block = count // groups, rows.shape[1] // groups
    return jnp.concatenate([rows[2:3, j * block : j * block + share] for j in range(groups)], axis=1)


def context_back_kernel(meta, ctx, w, up_in, dn_in, lat_t, grad, out, g_up, g_dn):
    g = grad[...]
    up, dn = up_in[0, 0], dn_in[0, 0]
    d_lat = nt(g, up).astype(BF16)
    d_lat_t = nt(up, g).astype(BF16)
    out[...] = nt(g, w[0]) + nn(d_lat, dn)
    g_up[...] = nn(lat_t[...], g)
    g_dn[...] = nn(d_lat_t, ctx[...])


def pack_kernel(meta, wo, wq, wc, out):
    rows, width = wo.shape[0], wq.shape[2]
    out[:rows, :] = wo[...]
    for j in range(out.shape[1] // width):
        out[rows : 2 * rows, j * width : (j + 1) * width] = wq[0, j * rows : (j + 1) * rows, :]
    out[2 * rows :, :] = wc[...]


def stack_kernel(meta, *refs):
    for j, ref in enumerate(refs[:-1]):
        refs[-1][j] = ref[...]


def start_copies(meta, plan, refs, targets, sems):
    copies = [[] for _ in targets]
    at = 0
    for source, weight, first, rows, slot, inner, size in plan:
        target = targets[weight]
        width = target.shape[2]
        sides = refs[source].shape[2] // width
        for j in range(sides):
            start = pl.multiple_of(meta[slot] * (size * sides) + (j * size + inner), 16)
            copies[weight].append(
                pltpu.make_async_copy(
                    refs[source].at[:, pl.ds(first, rows), pl.ds(j * width, width)],
                    target.at[:, pl.ds(start, rows), :],
                    sems.at[at],
                )
            )
            at += 1
    for weight in copies:
        for copy in weight:
            copy.start()
    return copies


def finish(copies):
    for copy in copies:
        copy.wait()


def cross_kernel(groups, head_count, plan, meta, *refs):
    n = groups * head_count
    os_first, os_rest, refs = refs[:groups], refs[groups : 2 * groups], refs[2 * groups :]
    tok, vec, up, dn3 = refs[:4]
    ctx, refs = refs[4], refs[5:]
    st_own, st_sib, wo_own, wq_own, wc_own = refs[:5]
    k = 1 + max(entry[0] for entry in plan)
    sources, refs = refs[5 : 5 + k], refs[5 + k :]
    y2, x2, x1, y3, qn, qc, oc, os_all, lse, lats = refs[:10]
    wo, wq, wc, sems = refs[10:]
    copies = start_copies(meta, plan, sources, (wo, wq, wc), sems)
    dn3 = dn3[0, 0]
    rank = dn3.shape[0]
    ctx_len = ctx.shape[2] - 4 * rank
    group = [lax.rem(meta[AT_T] + groups - r, groups) for r in range(groups)]
    small = jnp.concatenate([ctx[0, group[r], ctx_len:, :] for r in range(groups)], axis=1)
    first = meta[AT_S] == 0
    key_row = context_row(groups, ctx_len, jnp.where(first, st_own[...], st_sib[...]))
    ctx_inverse = jnp.broadcast_to(key_row, (8, ctx_len)).T[:, 0:1]
    width = head_count * HEAD_DIM
    for r in range(groups):
        middle = r * width + os_first[r].shape[1]
        os_all[:, r * width : middle] = os_first[r][...]
        os_all[:, middle : (r + 1) * width] = os_rest[r][...]
    os_v = os_all[...]
    down0, down1 = small[rank : 2 * rank, :], small[2 * rank : 3 * rank, :]
    lat = nt(os_v, down0).astype(BF16)
    lats[0:rank, :] = nt(down0, os_v).astype(BF16)
    total = nn(lat, up[0, 0])
    finish(copies[0])
    for r in range(groups):
        total = total + nn(os_v[:, r * width : (r + 1) * width], wo[r - 1] if r else wo_own[...])
    x1_v = tok[...].astype(F32) + (total + vec[B0 : B0 + 1, :]) * vec[M2 : M2 + 1, :]
    x1[...] = x1_v
    normed, _ = normalize(x1_v)
    y3_v = (normed * vec[CG : CG + 1, :] + vec[CB : CB + 1, :]).astype(BF16)
    y3[...] = y3_v
    lat = nt(y3_v, dn3).astype(BF16)
    lats[2 * rank : 3 * rank, :] = nt(dn3, y3_v).astype(BF16)
    finish(copies[1])
    q = nn(lat, small[0:rank, :]) + small[3 * rank : 3 * rank + 1, :].astype(F32)
    q = q + jnp.concatenate([nn(y3_v, wq[r - 1] if r else wq_own[0]) for r in range(groups)], axis=1)
    qc[...] = q
    inverse = lax.rsqrt(mean(q * q) + EPS)
    gain = small[3 * rank + 1 : 3 * rank + 2, :].astype(F32)
    qn[...] = (q * (inverse * (SCALE * LOG2E)) * gain).astype(BF16)
    for j in range(n):
        r, lanes = j // head_count, slice((j % head_count) * HEAD_DIM, (j % head_count + 1) * HEAD_DIM)
        keys = (ctx[0, group[r], :ctx_len, lanes].astype(F32) * ctx_inverse).astype(BF16)
        values = ctx[1, group[r], :ctx_len, lanes]
        scores = nt(keys, qn[:, j * HEAD_DIM : (j + 1) * HEAD_DIM])
        highest = jnp.max(scores, axis=0, keepdims=True)
        e = jnp.exp2(scores - highest)
        sums = jnp.sum(e, axis=0, keepdims=True)
        mixed = nn(values.astype(F32).T.astype(BF16), e.astype(BF16)) / sums
        oc[:, j * HEAD_DIM : (j + 1) * HEAD_DIM] = mixed.T.astype(BF16)
        lse[j : j + 1, :] = highest + jnp.log2(sums)
    oc_v = oc[...]
    lat = nt(oc_v, down1).astype(BF16)
    lats[rank : 2 * rank, :] = nt(down1, oc_v).astype(BF16)
    total = nn(lat, up[0, 1])
    finish(copies[2])
    for r in range(groups):
        total = total + nn(oc_v[:, r * width : (r + 1) * width], wc[r - 1] if r else wc_own[...])
    x2_v = x1_v + total + vec[B1 : B1 + 1, :]
    x2[...] = x2_v
    normed, _ = normalize(x2_v)
    y2[...] = (normed * vec[M4 : M4 + 1, :] + vec[M3 : M3 + 1, :]).astype(BF16)


def cross_back_kernel(groups, head_count, plan, meta, *refs):
    n = groups * head_count
    dy_own, dy_in, og, x2, x1, y3, qn, qc, oc, os_all, lse, lats, vec, up, dn3 = refs[:15]
    ctx, refs = refs[15], refs[16:]
    st_own, st_sib, wo_own, wq_own, wc_own = refs[:5]
    k = 1 + max(entry[0] for entry in plan)
    sources, refs = refs[5 : 5 + k], refs[5 + k :]
    dos_first, dos_rest, refs = refs[:groups], refs[groups : 2 * groups], refs[2 * groups :]
    dx1, g_own, g_oth, g_up, g_split, g_dn, wo, wq, wc, dq_s, sems = refs
    copies = start_copies(meta, plan, sources, (wo, wq, wc), sems)
    dn3 = dn3[0, 0]
    rank = dn3.shape[0]
    ctx_len = ctx.shape[2] - 4 * rank
    group = [lax.rem(meta[AT_T] + groups - r, groups) for r in range(groups)]
    small = jnp.concatenate([ctx[0, group[r], ctx_len:, :] for r in range(groups)], axis=1)
    first = meta[AT_S] == 0
    key_row = context_row(groups, ctx_len, jnp.where(first, st_own[...], st_sib[...]))
    ctx_inverse = jnp.broadcast_to(key_row, (8, ctx_len)).T[:, 0:1]
    width = head_count * HEAD_DIM
    down0, down1 = small[rank : 2 * rank, :], small[2 * rank : 3 * rank, :]
    normed, inverse = normalize(x2[...])
    dn = (dy_own[...] + dy_in[...].astype(F32)) * vec[M4 : M4 + 1, :]
    dx2 = og[...].astype(F32) + normalize_back(normed, inverse, dn)
    grad = dx2.astype(BF16)
    d_lat = nt(grad, up[0, 1]).astype(BF16)
    d_lat_t = nt(up[0, 1], grad).astype(BF16)
    oc_v = oc[...]
    g_up[rank : 2 * rank, :] = nn(lats[rank : 2 * rank, :], grad)
    split = nn(d_lat_t, oc_v)
    for r in range(groups):
        g_split[r, 2 * rank : 3 * rank, :] = split[:, r * width : (r + 1) * width]
    finish(copies[2])
    d_oc = nn(d_lat, down1) + jnp.concatenate(
        [nt(grad, wc[r - 1] if r else wc_own[...]) for r in range(groups)], axis=1
    )
    d_oc = d_oc.astype(BF16)
    for j in range(n):
        r, lanes = j // head_count, slice((j % head_count) * HEAD_DIM, (j % head_count + 1) * HEAD_DIM)
        head = slice(j * HEAD_DIM, (j + 1) * HEAD_DIM)
        keys = (ctx[0, group[r], :ctx_len, lanes].astype(F32) * ctx_inverse).astype(BF16)
        values = ctx[1, group[r], :ctx_len, lanes]
        q, g = qn[:, head], d_oc[:, head]
        delta = row_total(g.astype(F32) * oc_v[:, head].astype(F32))[0:1, :]
        p = jnp.exp2(nt(keys, q) - lse[j : j + 1, :])
        dv = nn(p.astype(BF16), g)
        ds = (p * (nt(values, g) - delta)).astype(BF16)
        dk = nn(ds, q) * (1.0 / LOG2E)
        dq_s[:, head] = nn(keys.astype(F32).T.astype(BF16), ds).T * SCALE
        g_own[r, :, lanes] = jnp.where(first, dk, dv).astype(BF16)
        g_oth[r, :, lanes] = jnp.where(first, dv, dk).astype(BF16)
    q = qc[...]
    inverse = lax.rsqrt(mean(q * q) + EPS)
    gain = small[3 * rank + 1 : 3 * rank + 2, :].astype(F32)
    scaled = dq_s[...] * gain
    stat = mean(scaled * q)
    dqc = (inverse * scaled - q * (inverse * inverse * inverse * stat)).astype(BF16)
    up_q = small[0:rank, :]
    d_lat = nt(dqc, up_q).astype(BF16)
    d_lat_t = nt(up_q, dqc).astype(BF16)
    split = nn(lats[2 * rank : 3 * rank, :], dqc)
    for r in range(groups):
        g_split[r, 0:rank, :] = split[:, r * width : (r + 1) * width]
    g_dn[...] = nn(d_lat_t, y3[...])
    dy3 = nn(d_lat, dn3)
    finish(copies[1])
    for r in range(groups):
        part = dqc[:, r * width : (r + 1) * width]
        dy3 = dy3 + nt(part, wq[r - 1] if r else wq_own[0])
    normed, inverse = normalize(x1[...])
    dx1_v = dx2 + normalize_back(normed, inverse, dy3 * vec[CG : CG + 1, :])
    dx1[...] = dx1_v
    grad = (dx1_v * vec[M2 : M2 + 1, :]).astype(BF16)
    d_lat = nt(grad, up[0, 0]).astype(BF16)
    d_lat_t = nt(up[0, 0], grad).astype(BF16)
    g_up[0:rank, :] = nn(lats[0:rank, :], grad)
    split = nn(d_lat_t, os_all[...])
    for r in range(groups):
        g_split[r, rank : 2 * rank, :] = split[:, r * width : (r + 1) * width]
    finish(copies[0])
    low = nn(d_lat, down0)
    for r in range(groups):
        block = nt(grad, wo[r - 1] if r else wo_own[...]) + low[:, r * width : (r + 1) * width]
        dos_first[r][...] = block[:, :HEAD_DIM].astype(BF16)
        dos_rest[r][...] = block[:, HEAD_DIM:].astype(BF16)


def feed_kernel(tiles, first, meta, *refs):
    y2, og, vec, bias, dn1, up1, dn2, up2, w1_h, w2_h = refs[:10]
    if first:
        x2 = refs[10]
    else:
        acc = refs[10:14]
    refs = refs[11:] if first else refs[15:]
    dn1, up1, dn2, up2 = dn1.at[0], up1.at[0], dn2.at[0], up2.at[0]
    out, dy, g_up1, g_dn1, g_up2, g_dn2, w1, w2, sems = refs
    copies = []
    for at, (start, size) in enumerate(tiles):
        rows = pl.ds(start, size)
        pair = [
            pltpu.make_async_copy(h.at[rows, :], v.at[rows, :], sems.at[j, at])
            for j, (h, v) in enumerate(((w1_h, w1), (w2_h, w2)))
        ]
        for copy in pair:
            copy.start()
        copies.append(pair)
    y = y2[...]
    dff = (og[...].astype(F32) * vec[M5 : M5 + 1, :]).astype(BF16)
    lat = nt(y, dn1[...]).astype(BF16)
    lat_t = nt(dn1[...], y).astype(BF16)
    drl = nt(dff, up2[...]).astype(BF16)
    drl_t = nt(up2[...], dff).astype(BF16)
    part = grad = rl = rl_t = d_lat = d_lat_t = 0.0
    for (start, size), pair in zip(tiles, copies):
        cols = slice(start, start + size)
        finish(pair)
        h = nt(y, w1[cols, :]) + nn(lat, up1[:, cols]) + bias[:, cols]
        du = nt(dff, w2[cols, :]) + nn(drl, dn2[:, cols])
        sq = h * h
        t = jnp.tanh(GELU_C * h * (1.0 + 0.044715 * sq))
        act = (0.5 * h * (1.0 + t)).astype(BF16)
        slope = 0.5 * (1.0 + t) + (0.5 * GELU_C) * h * (1.0 - t * t) * (1.0 + (3.0 * 0.044715) * sq)
        dh = (du * slope).astype(BF16)
        part = part + nn(act, w2[cols, :])
        grad = grad + nn(dh, w1[cols, :])
        rl = rl + nt(act, dn2[:, cols])
        rl_t = rl_t + nt(dn2[:, cols], act)
        d_lat = d_lat + nt(dh, up1[:, cols])
        d_lat_t = d_lat_t + nt(up1[:, cols], dh)
        new_up1, new_dn2 = nn(lat_t, dh), nn(drl_t, act)
        g_up1[:, cols] = new_up1 if first else new_up1 + acc[0][:, cols]
        g_dn2[:, cols] = new_dn2 if first else new_dn2 + acc[3][:, cols]
    part = part + nn(rl.astype(BF16), up2[...])
    grad = grad + nn(d_lat.astype(BF16), dn1[...])
    new_dn1, new_up2 = nn(d_lat_t.astype(BF16), y), nn(rl_t.astype(BF16), dff)
    g_dn1[...] = new_dn1 if first else new_dn1 + acc[1][...]
    g_up2[...] = new_up2 if first else new_up2 + acc[2][...]
    part = part * vec[M5 : M5 + 1, :]
    if first:
        part = part + x2[...] + vec[B2 : B2 + 1, :] * vec[M5 : M5 + 1, :]
    out[...] = part.astype(out.dtype)
    dy[...] = grad.astype(dy.dtype)


def shift(count, step):
    return [(a, (a + step) % count) for a in range(count)]


def flip(count, step):
    return [(a, a ^ step) for a in range(count)]


def powers(count):
    return [1 << j for j in range(count.bit_length() - 1)]


def send(values, axis, pairs):
    return jax.tree.map(lambda v: lax.ppermute(v, axis, pairs), values)


def ring_pieces(own, axis):
    count = lax.axis_size(axis)
    pieces = [own]
    for _ in range(count - 1):
        pieces.append(send(pieces[-1], axis, shift(count, 1)))
    return pieces


def ring_total(parts, axis):
    count = lax.axis_size(axis)
    moving = parts[1]
    for r in range(2, count):
        moving = send(moving, axis, shift(count, 1))
        moving = (moving.astype(F32) + parts[r].astype(F32)).astype(BF16)
    return parts[0], send(moving, axis, shift(count, 1))


def gather_direct(own, axis):
    count = lax.axis_size(axis)
    return [own] + [send(own, axis, shift(count, r)) for r in range(1, count)]


def scatter_direct(parts, axis):
    count = lax.axis_size(axis)
    return parts[0].astype(F32) + sum(
        send(parts[r].astype(BF16), axis, shift(count, -r)).astype(F32) for r in range(1, count)
    )


def gather_flipped(own, axis):
    count = lax.axis_size(axis)
    return [own] + [send(own, axis, flip(count, j)) for j in range(1, count)]


def total_flipped(own, axis):
    terms = [v.astype(F32) for v in gather_flipped(own, axis)]
    while len(terms) > 1:
        terms = [terms[j] + terms[j + 1] for j in range(0, len(terms), 2)]
    return terms[0]


def halves(values, axis):
    half = values.shape[0] // 2
    low, high = values[:half], values[half:]
    upper = lax.axis_index(axis) == 1
    return jnp.where(upper, high, low), jnp.where(upper, low, high)


def pair_scatter(values):
    kept, sent = halves(values, "seq")
    return kept + send(sent.astype(BF16), "seq", flip(2, 1)).astype(F32)


def pair_gather(values, dim):
    other = send(values, "seq", flip(2, 1))
    upper = lax.axis_index("seq") == 1
    return jnp.concatenate([jnp.where(upper, other, values), jnp.where(upper, values, other)], axis=dim)


def place_blocks(blocks, axis):
    size = blocks[0].shape[0]
    out = jnp.zeros((size * len(blocks),) + blocks[0].shape[1:], blocks[0].dtype)
    index = lax.axis_index(axis)
    for j, block in enumerate(blocks):
        out = lax.dynamic_update_slice_in_dim(out, block, (index ^ j) * size, 0)
    return out


def total_twice(values, axis):
    for step in powers(lax.axis_size(axis)):
        values = values + send(values, axis, flip(lax.axis_size(axis), step))
    return values


class Chains:
    def __init__(self):
        self.chains, self.values, self.results = [], [], {}

    def add(self, chain):
        self.chains.append(chain)
        self.values.append(None)
        return len(self.chains) - 1

    def start(self, at):
        self.advance(at)

    def advance(self, at):
        try:
            self.values[at] = self.chains[at].send(self.values[at])
        except StopIteration as end:
            self.results[at] = end.value

    def step(self, skip=()):
        for at in range(len(self.chains)):
            if at not in self.results and at not in skip:
                self.advance(at)

    def live(self):
        return len(self.results) < len(self.chains)

    def done(self, at):
        return at in self.results

    def result(self, at):
        return self.results[at]

    def arrived(self):
        live = [self.values[at] for at in range(len(self.chains)) if at not in self.results]
        return jax.tree.leaves(live)

    def put(self, leaves):
        places = [at for at in range(len(self.chains)) if at not in self.results]
        structure = jax.tree.structure([self.values[at] for at in places])
        for at, value in zip(places, jax.tree.unflatten(structure, leaves)):
            self.values[at] = value


def seal(*values):
    return list(lax.optimization_barrier(values)) if values else []


def ring_steps(parts, axis):
    count = lax.axis_size(axis)
    moving = parts[1].astype(BF16)
    for r in range(2, count + 1):
        moving = yield send(moving, axis, shift(count, 1))
        if r < count:
            moving = (moving.astype(F32) + parts[r].astype(F32)).astype(BF16)
    return parts[0].astype(F32) + moving.astype(F32)


class Line:
    def __init__(self):
        self.parts, self.acc, self.total, self.out, self.at, self.moving = [], [], [], [], 0, []
        index = lax.axis_index("tensor")
        self.inner = (index == 1) | (index == 2)

    def add(self, part):
        self.parts.append(part)

    def send(self):
        inward = self.parts[self.at] if self.at < len(self.parts) else None
        outward = self.total[self.at - 2] if 0 <= self.at - 2 < len(self.total) else None
        across = self.acc[self.at - 1] if 0 <= self.at - 1 < len(self.acc) else None
        pairs = [(0, 1), (3, 2)] * (inward is not None) + [(1, 0), (2, 3)] * (outward is not None)
        if inward is None or outward is None:
            mine = outward if inward is None else inward
        else:
            mine = jnp.where(self.inner, outward, inward)
        self.moving = [send(mine, "tensor", pairs)] if pairs else []
        self.shape = (inward is not None, across is not None, outward is not None)
        if across is not None:
            self.moving.append(send(across, "tensor", [(1, 2), (2, 1)]))

    def receive(self, moving):
        inward, across, outward = self.shape
        moving = list(moving)
        add_low = lambda a, b: (a.astype(F32) + b.astype(F32)).astype(BF16)
        if inward or outward:
            first = moving.pop(0)
        if inward:
            self.acc.append(add_low(self.parts[self.at], first))
        if across:
            self.total.append(add_low(self.acc[self.at - 1], moving.pop(0)))
        if outward:
            self.out.append(jnp.where(self.inner, self.total[self.at - 2], first))
        self.at += 1
        self.moving = []

    def live(self):
        return len(self.out) < len(self.parts)


def adapter_steps(value, shared):
    groups, dp = lax.axis_size("tensor"), lax.axis_size("dp")
    pair, upper = flip(2, 1), lax.axis_index("seq") == 1
    kept, sent = halves(value, "seq")
    other = yield send(sent.astype(BF16), "seq", pair)
    value = kept + other.astype(F32)
    own, rest = value[:, :shared].astype(BF16), value[:, shared:].astype(BF16)
    for step in powers(groups):
        other = yield send(own, "tensor", flip(groups, step))
        own = (own.astype(F32) + other.astype(F32)).astype(BF16)
    value = jnp.concatenate([own, rest], axis=1)[None]
    for step in powers(dp):
        other = yield send(value, "dp", flip(dp, step))
        value = jnp.concatenate([value, other])
    other = yield send(value, "seq", pair)
    return jnp.concatenate([jnp.where(upper, other, value), jnp.where(upper, value, other)], axis=1)


def context_grad_steps(value):
    groups, dp = lax.axis_size("tensor"), lax.axis_size("dp")
    at_dp = lax.axis_index("dp")
    pair, second = flip(2, 1), lax.axis_index("seq") == 1
    kept, sent = halves(value, "seq")
    other = yield send(sent.astype(BF16), "seq", pair)
    value = kept + other.astype(F32)
    rows = value.shape[0] // dp
    parts = [lax.dynamic_slice_in_dim(value, (at_dp ^ j) * rows, rows, 0) for j in range(dp)]
    others = yield tuple(send(parts[j].astype(BF16), "dp", flip(dp, j)) for j in range(1, dp))
    value = (parts[0] + sum(other.astype(F32) for other in others)).astype(BF16)
    for step in powers(groups):
        other = yield send(value, "tensor", flip(groups, step))
        value = (value.astype(F32) + other.astype(F32)).astype(BF16)
    for step in powers(dp):
        other = yield send(value, "dp", flip(dp, step))
        upper = (at_dp & step) != 0
        value = jnp.concatenate([jnp.where(upper, other, value), jnp.where(upper, value, other)])
    other = yield send(value, "seq", pair)
    return jnp.concatenate([jnp.where(second, other, value), jnp.where(second, value, other)])


def weight_share():
    return 4 if lax.axis_size("dp") == 4 else 1


def weight_plan(rows, count):
    share, seq = weight_share(), lax.axis_size("seq")
    d, s = lax.axis_index("dp"), lax.axis_index("seq")
    slots = [(s ^ a) * share + ((d ^ b) if share > 1 else 0) for a in range(seq) for b in range(share)]
    total = rows * count
    cut = far_cut(total)
    half = [(0, 0, total, 0)]
    if share > 1:
        half += [(1, 0, total, 1), (2, 0, total, 2), (3, 0, cut, 3), (4, cut, total - cut, 3)]
    spans = half + [(len(half) + a, b, c, share + e) for a, b, c, e in half]
    plan = []
    for source, start, size, slot in spans:
        for weight in range(count):
            low, high = max(start, weight * rows), min(start + size, (weight + 1) * rows)
            if low < high:
                plan.append((source, weight, low - start, high - low, SLOTS + slot, low - weight * rows, rows))
    return plan, slots


def far_cut(total):
    return (total // 2 + 15) // 16 * 16


def rope_tables(grid_pos):
    sixth = HEAD_DIM // 6
    counts = [(HEAD_DIM - 4 * sixth) // 2, sixth, sixth]
    table = np.zeros((3, HEAD_DIM), np.float32)
    lane = 0
    for component, count in enumerate(counts):
        for pair in range(count):
            table[component, lane : lane + 2] = 10000.0 ** (-pair / count)
            lane += 2
    positions = grid_pos.astype(F32)
    angles = sum(positions[c][:, None] * table[c][None, :] for c in range(3))
    sign = np.where(np.arange(HEAD_DIM) % 2 == 0, -1.0, 1.0).astype(np.float32)
    return jnp.cos(angles), jnp.sin(angles) * sign[None, :]


def select_slot(table, index):
    return lax.dynamic_index_in_dim(table, index, 0, keepdims=False)


def spread(gradients, indices, slot_count):
    hits = (jnp.arange(slot_count)[:, None] == indices[None, :]).astype(F32)
    out = 0.0
    for latent in range(gradients.shape[0]):
        shape = (slot_count,) + (1,) * (gradients.ndim - 1)
        out = out + hits[:, latent].reshape(shape) * gradients[latent].astype(F32)[None]
    return out


def eight_rows(rows):
    return jnp.concatenate([jnp.stack(rows), jnp.zeros((8 - len(rows), rows[0].shape[0]), F32)])


def per_device(
    tokens,
    positions,
    time_emb,
    modulation,
    context,
    adapter_index,
    self_qkv,
    self_bias,
    self_gain,
    self_out,
    cross_qkv,
    cross_bias,
    cross_gain,
    cross_out,
    cross_norm_gain,
    cross_norm_bias,
    ffn_in,
    ffn_bias,
    ffn_out,
    out_bias,
    col_down,
    col_up,
    ffn1_down,
    ffn1_up,
    row_down,
    row_up,
    ffn2_down,
    ffn2_up,
    out_grad,
):
    groups = lax.axis_size("tensor")
    seq = lax.axis_size("seq")
    i, s = lax.axis_index("tensor"), lax.axis_index("seq")
    tl, d = tokens.shape[1:]
    tc = tl // groups
    ctx_len = context.shape[0]
    width = self_qkv.shape[2]
    hc = width // HEAD_DIM
    ff = ffn_in.shape[1]
    slots, rank = col_down.shape[0], col_down.shape[3]
    share = weight_share()
    slice_rows = width // (share * seq)
    plan, slot_list = weight_plan(slice_rows, 3)
    part_at = s * share + (lax.axis_index("dp") if share > 1 else 0)
    meta = jnp.stack([jnp.asarray(v, jnp.int32) for v in [i, s, adapter_index[0], part_at] + slot_list])
    tok, og = tokens[0], out_grad[0]
    block = pl.BlockSpec
    hbm = pl.BlockSpec(memory_space=pl.ANY)
    pair = flip(seq, 1)

    def table(array, *place, rows=1):
        if not place:
            return (array, block((1,) + array.shape[1:], lambda *a: (a[-1][ADAPTER],) + (0,) * (array.ndim - 1)))
        return (
            array,
            block(
                (1, rows) + array.shape[2:],
                lambda *a: (a[-1][ADAPTER], place[0](a[-1]) if callable(place[0]) else place[0], 0, 0),
            ),
        )

    col_dn, row_dn = jnp.swapaxes(col_down, 2, 3), jnp.swapaxes(row_down, 2, 3)
    feed_tables = [
        table(jnp.swapaxes(ffn1_down, 1, 2)),
        table(ffn1_up),
        table(jnp.swapaxes(ffn2_down, 1, 2)),
        table(ffn2_up),
    ]

    shard_at = lambda b, m: (m[PART], 0)
    (slices,) = run_kernel(
        pack_kernel,
        meta,
        [
            (self_out, block((slice_rows, d), shard_at)),
            (cross_qkv, block((1, slice_rows * groups, width), lambda b, m: (0, m[PART], 0))),
            (cross_out, block((slice_rows, d), shard_at)),
        ],
        [(sds((3 * slice_rows, d), BF16), whole((3 * slice_rows, d)))],
        us=1.5,
    )
    by_group = gather_direct(slices, "tensor")[1:]

    is_key = s == 0
    ctx_w = (cross_qkv, block((1, d, width), lambda b, m: (1 + m[AT_S], 0, 0)))
    ctx_up, ctx_dn = table(col_up, lambda m: 4 + m[AT_S]), table(col_dn, lambda m: 4 + m[AT_S])
    low_rows = ctx_len + 4 * rank
    ctx_pre, ctx_low, ctx_ssq, ctx_lat_t = run_kernel(
        functools.partial(context_kernel, groups),
        meta,
        [
            (context, whole(context.shape)),
            ctx_w,
            ctx_up,
            ctx_dn,
            (cross_bias, whole(cross_bias.shape)),
            (cross_gain, whole(cross_gain.shape)),
            table(col_up, 3),
            table(row_dn, 0, rows=2),
        ],
        [
            (sds((ctx_len, width), F32), whole((ctx_len, width))),
            (sds((low_rows, width), BF16), whole((low_rows, width))),
            (sds((8, tl), F32), whole((8, tl))),
            (sds((rank, ctx_len), BF16), whole((rank, ctx_len))),
        ],
        us=6,
        after=[slices],
    )
    cos, sin = rope_tables(positions[:, 0, :])
    rows_d = block((tc, d), lambda b, m: (b, 0))
    rows_w = block((tc, width), lambda b, m: (b, 0))
    rows_h = block((tc, HEAD_DIM), lambda b, m: (b, 0))
    lanes_8 = block((8, tc), lambda b, m: (0, b))
    self_tables = [table(col_up, 0, rows=3), table(col_dn, 0, rows=3)]
    y1, lat_t, pre_q, pre_k, raw_q, kv, ssq, vec = run_kernel(
        functools.partial(qkv_kernel, hc),
        meta,
        [
            (tok, rows_d),
            (modulation, whole(modulation.shape)),
            (time_emb[0], whole(modulation.shape)),
            (out_bias, whole(out_bias.shape)),
            (cross_norm_gain[None], whole((1, d))),
            (cross_norm_bias[None], whole((1, d))),
            (self_qkv, whole(self_qkv.shape)),
        ]
        + self_tables
        + [
            (self_bias, whole(self_bias.shape)),
            (self_gain, whole(self_gain.shape)),
            (cos, rows_h),
            (sin, rows_h),
            (ctx_ssq, lanes_8),
        ],
        [
            (sds((tl, d), BF16), rows_d),
            (sds((3 * rank, tl), BF16), block((3 * rank, tc), lambda b, m: (0, b))),
            (sds((tl, width), BF16), rows_w),
            (sds((tl, width), BF16), rows_w),
            (sds((tl, width), BF16), rows_w),
            (sds((tl, 2 * width), BF16), block((tc, 2 * width), lambda b, m: (b, 0))),
            (sds((8, tl), F32), lanes_8),
            (sds((16, d), F32), whole((16, d))),
        ],
        grid=(groups,),
        scratch=[pltpu.VMEM((3 * rank, 3 * width), BF16)],
        us=15,
    )
    kv_sib = send(kv, "seq", pair)
    *first_steps, last_step = powers(groups)
    for step in first_steps:
        ssq = ssq + send(ssq, "tensor", flip(groups, step))
    ssq, *by_group = seal(ssq, *by_group)
    (by_group,) = run_kernel(
        stack_kernel,
        meta,
        [(a, whole(a.shape)) for a in by_group],
        [(sds((groups - 1,) + slices.shape, BF16), whole((groups - 1,) + slices.shape))],
        us=2,
    )
    ssq, by_group = seal(ssq, by_group)
    along = [send(by_group, "dp", flip(share, 1)), send(by_group, "dp", flip(share, 2))] if share > 1 else []
    st_own = lax.rsqrt((ssq + send(ssq, "tensor", flip(groups, last_step))) / d + EPS)
    st_sib = send(st_own, "seq", pair)
    ctx_low, _ = seal(ctx_low, st_own)
    ctx_all = lax.all_gather(ctx_low, ("seq", "tensor"))
    ctx_all = ctx_all.reshape((seq, groups) + ctx_all.shape[1:])

    all_8 = whole((8, tl))
    turned = lambda r, m: lax.rem(m[AT_T] + r, groups)
    parts = [(0, hc - 1), (hc - 1, 1)]
    mixed, lses, os_pieces = [], [], []
    for first, count in parts:
        kv_at = lambda lane: block((tl, HEAD_DIM), lambda h, r, m: (0, lane + h))
        own_rows = block((tc, HEAD_DIM), lambda h, r, m: (0, h))
        *blocks, out, lse = run_kernel(
            functools.partial(attention_kernel, groups),
            meta,
            [
                (raw_q, block((tc, HEAD_DIM), lambda h, r, m, first=first: (turned(r, m), first + h))),
                (st_own, block((8, tc), lambda h, r, m: (0, turned(r, m)))),
                (st_own, all_8),
                (st_sib, all_8),
                (kv, kv_at(first)),
                (kv_sib, kv_at(first)),
                (kv, kv_at(hc + first)),
                (kv_sib, kv_at(hc + first)),
            ],
            [(sds((tc, count * HEAD_DIM), BF16), own_rows)] * groups
            + [
                (sds((tl, count * HEAD_DIM), BF16), block((tc, HEAD_DIM), lambda h, r, m: (r, h))),
                (sds((8 * count, tl), F32), block((8, tc), lambda h, r, m: (h, r))),
            ],
            grid=(count, groups),
            scratch=[pltpu.VMEM((2 * tl, HEAD_DIM), BF16), pltpu.VMEM((HEAD_DIM, 2 * tl), BF16)],
            us=9.5 * count,
            after=[by_group] if first == 0 else [out],
        )
        mixed.append(out)
        lses.append(lse)
        if first:
            blocks[0], *late = seal(blocks[0], *along, *os_pieces)
            along, os_pieces = late[: len(along)], late[len(along) :]
        os_pieces += [send(a, "tensor", shift(groups, r)) if r else a for r, a in enumerate(blocks)]
    weight_parts = [by_group] + along
    if share > 1:
        middle = far_cut(by_group.shape[1])
        weight_parts += [
            send(along[1][:, :middle], "dp", flip(share, 1)),
            send(along[0][:, middle:], "dp", flip(share, 2)),
        ]
    near = seal(*os_pieces[-groups + 1 :], *weight_parts)
    os_pieces[-groups + 1 :], weight_parts = near[: groups - 1], near[groups - 1 :]
    weight_parts = weight_parts + [send(p, "seq", pair) for p in weight_parts]

    vspec = whole(vec.shape)
    own_block = block((tc, d), lambda b, m: (m[AT_T], 0))
    weight_scratch = [
        pltpu.VMEM((groups - 1, width, d), BF16),
        pltpu.VMEM((groups - 1, d, width), BF16),
        pltpu.VMEM((groups - 1, width, d), BF16),
    ]
    sems = pltpu.SemaphoreType.DMA((len(plan) * groups,))
    shared = [
        table(row_up),
        table(col_dn, 3),
        (ctx_all, whole(ctx_all.shape)),
        (st_own, all_8),
        (st_sib, all_8),
        (self_out, whole(self_out.shape)),
        (cross_qkv, block((1, d, width), lambda b, m: (0, 0, 0))),
        (cross_out, whole(cross_out.shape)),
    ] + [(p, hbm) for p in weight_parts]
    whole_of = lambda shape, dtype: (sds(shape, dtype), whole(shape))
    y2, x2, x1, y3, qn, qc, oc, os_all, lse_c, lats = run_kernel(
        functools.partial(cross_kernel, groups, hc, plan),
        meta,
        [(p, whole(p.shape)) for p in os_pieces] + [(tok, own_block), (vec, vspec)] + shared,
        [
            whole_of((tc, d), BF16),
            whole_of((tc, d), F32),
            whole_of((tc, d), F32),
            whole_of((tc, d), BF16),
            whole_of((tc, d), BF16),
            whole_of((tc, d), F32),
            whole_of((tc, d), BF16),
            whole_of((tc, d), BF16),
            whole_of((16, tc), F32),
            whole_of((3 * rank, tc), BF16),
        ],
        scratch=weight_scratch + [sems],
        us=20,
    )

    tiles = [(a, min(768, ff - a)) for a in range(0, ff, 768)]
    w1t = ffn_in.T
    y2_pieces = ring_pieces(y2, "tensor")
    feed_bias = ffn_bias.astype(F32)[None]
    feed_out, dys, acc = None, [], None
    for r in range(groups):
        place = block((tc, d), lambda b, m, r=r: (lax.rem(m[AT_T] + groups - r, groups), 0))
        ins = [(y2_pieces[r], whole((tc, d))), (og, place), (vec, vspec), (feed_bias, whole(feed_bias.shape))]
        ins += feed_tables + [(w1t, hbm), (ffn_out, hbm)]
        if r == 0:
            ins += [(x2, whole((tc, d)))]
        else:
            ins += [(a, whole(a.shape)) for a in acc] + [(feed_out, hbm)]
        feed_out, dy, *acc = run_kernel(
            functools.partial(feed_kernel, tiles, r == 0),
            meta,
            ins,
            [(sds((tl, d), BF16), place), whole_of((tc, d), F32 if r == 0 else BF16)]
            + [whole_of((rank, n), F32) for n in (ff, d, d, ff)],
            scratch=[pltpu.VMEM((ff, d), BF16), pltpu.VMEM((ff, d), BF16), pltpu.SemaphoreType.DMA((2, len(tiles)))],
            us=18,
            aliases={15: 0} if r else None,
        )
        dys.append(dy)
    g_up1, g_dn1, g_up2, g_dn2 = acc

    dy_own, dy_in = ring_total(dys, "tensor")
    feed_out, dy_in = seal(feed_out, dy_in)
    line = Line() if groups == 4 else None
    if line:
        for r in range(groups):
            line.add(feed_out[r * tc : (r + 1) * tc])
        line.send()
    else:
        result = lax.psum(feed_out, "tensor")
    *dos, dx1, g_own, g_oth, g_rup, g_split, g_cqdn = run_kernel(
        functools.partial(cross_back_kernel, groups, hc, plan),
        meta,
        [(dy_own, whole((tc, d))), (dy_in, whole((tc, d))), (og, own_block)]
        + [(a, whole(a.shape)) for a in (x2, x1, y3, qn, qc, oc, os_all, lse_c, lats)]
        + [(vec, vspec)]
        + shared,
        [whole_of((tc, HEAD_DIM), BF16)] * groups
        + [whole_of((tc, width - HEAD_DIM), BF16)] * groups
        + [
            whole_of((tc, d), F32),
            whole_of((groups, ctx_len, width), BF16),
            whole_of((groups, ctx_len, width), BF16),
            whole_of((2 * rank, d), F32),
            whole_of((groups, 3 * rank, width), F32),
            whole_of((rank, d), F32),
        ],
        scratch=weight_scratch + [pltpu.VMEM((tc, d), F32), sems],
        us=26,
    )

    back_shift = lambda arrays: [send(a, "tensor", shift(groups, -r)) if r else a for r, a in enumerate(arrays)]
    moving = lambda: line.moving if line else []
    chains = Chains()
    dos[0], g_oth, g_cqdn, *tied = seal(dos[0], g_oth, g_cqdn, *moving())
    if line:
        line.receive(tied)
    dos_first = back_shift(dos[:groups])
    packed = jnp.concatenate([g_cqdn, g_dn1, g_rup[:rank], g_rup[rank:], g_up2, g_up1, g_dn2], axis=1)
    early_at = chains.add(adapter_steps(packed, 5 * d))
    g_oth = send(g_oth, "seq", pair)
    chains.step()
    g_oth, *dos_first = seal(g_oth, *dos_first)
    to_group = jnp.concatenate([g_own.astype(F32) + g_oth.astype(F32), g_split], axis=1)
    dos_rest = back_shift(dos[groups:])
    group_at = chains.add(ring_steps([to_group[r] for r in range(groups)], "tensor"))
    chains.step()

    back, dkv_in = [], []
    for h in range(hc):
        of, at = (0, h) if h < parts[1][0] else (1, h - parts[1][0])
        grads = dos_first if h == 0 else dos_rest
        lane = 0 if h == 0 else h - 1
        kv_at = lambda lane: block((tl, HEAD_DIM), lambda r, m: (0, lane))
        if h:
            tied = seal(*dos_rest, *chains.arrived(), *back[-1][:1])
            dos_rest = tied[: len(dos_rest)]
            chains.put(tied[len(dos_rest) : -1])
            dkv_in.append(send(back[-1][2], "seq", pair))
            if h == 1:
                chains.step([early_at])
                if line:
                    line.send()
            else:
                chains.step()
            grads = dos_rest
        back.append(
            run_kernel(
                functools.partial(attention_back_kernel, groups, h == 0),
                meta,
                [
                    (raw_q, block((tc, HEAD_DIM), lambda r, m, h=h: (turned(r, m), h))),
                    (st_own, block((8, tc), lambda r, m: (0, turned(r, m)))),
                    (st_own, all_8),
                    (st_sib, all_8),
                    (kv, kv_at(h)),
                    (kv_sib, kv_at(h)),
                    (kv, kv_at(hc + h)),
                    (kv_sib, kv_at(hc + h)),
                    (mixed[of], block((tc, HEAD_DIM), lambda r, m, at=at: (r, at))),
                    (lses[of], block((8, tc), lambda r, m, at=at: (at, r))),
                ]
                + [(g, block((tc, HEAD_DIM), lambda r, m, lane=lane: (0, lane))) for g in grads]
                + ([(a, all_8) for a in back[-1][3:]] if h else []),
                [
                    (sds((tl, HEAD_DIM), F32), block((tc, HEAD_DIM), lambda r, m: (turned(r, m), 0))),
                    whole_of((tl, 2 * HEAD_DIM), F32),
                    whole_of((tl, 2 * HEAD_DIM), BF16),
                    whole_of((8, tl), F32),
                    whole_of((8, tl), F32),
                ],
                grid=(groups,),
                scratch=[
                    pltpu.VMEM((2 * tl, HEAD_DIM), BF16),
                    pltpu.VMEM((HEAD_DIM, 2 * tl), BF16),
                    pltpu.VMEM((2 * tl, HEAD_DIM), BF16),
                    pltpu.VMEM((2 * tl, HEAD_DIM), F32),
                    pltpu.VMEM((2 * tl, HEAD_DIM), F32),
                    pltpu.VMEM((tc, HEAD_DIM), BF16),
                ],
                us=12.5,
                after=list(tied[-1:]) if h else [],
            )
        )
    dq, dkv, dkv_out = zip(*[b[:3] for b in back])
    stat, cross = back[-1][3:]
    stat, cross, *tied = seal(stat, cross, *chains.arrived(), *moving())
    count = len(chains.arrived())
    chains.put(tied[:count])
    if line:
        line.receive(tied[count:])
    cross = send(cross, "seq", pair)
    dkv_in.append(send(dkv_out[-1], "seq", pair))
    chains.step([early_at])
    to_group = chains.result(group_at)
    g_ctx, split = to_group[:ctx_len], to_group[ctx_len:]
    ctx_gain = jnp.where(is_key, cross_gain[1:2].astype(F32), 1.0)
    ctx_stat = jnp.sum(g_ctx * ctx_gain * ctx_pre, axis=1)
    stat = stat + cross
    for step in powers(groups):
        other, ctx_other, *tied = seal(*send((stat, ctx_stat), "tensor", flip(groups, step)), *chains.arrived())
        chains.put(tied)
        stat, ctx_stat = stat + other, ctx_stat + ctx_other
    if line:
        line.send()
    chains.step()
    st_back = st_own * st_own * st_own * stat / d

    ctx_inverse = jnp.concatenate([st_own[2, j * tc : j * tc + ctx_len // groups] for j in range(groups)])
    ctx_cubed = ctx_inverse * ctx_inverse * ctx_inverse * ctx_stat / d
    d_key = ctx_inverse[:, None] * ctx_gain * g_ctx - ctx_pre * ctx_cubed[:, None]
    d_ctx = jnp.where(is_key, d_key, g_ctx).astype(BF16)
    ctx_part, g_ctx_up, g_ctx_dn = run_kernel(
        context_back_kernel,
        meta,
        [
            (context, whole(context.shape)),
            ctx_w,
            ctx_up,
            ctx_dn,
            (ctx_lat_t, whole(ctx_lat_t.shape)),
            (d_ctx, whole(d_ctx.shape)),
        ],
        [whole_of((ctx_len, d), F32), whole_of((rank, width), F32), whole_of((rank, d), F32)],
        us=6,
    )

    q_parts, late = [], None
    for r in range(groups):
        in_d = block((tc, d), lambda b, m, r=r: (r, 0))
        in_w = block((tc, width), lambda b, m, r=r: (r, 0))
        in_h = block((tc, HEAD_DIM), lambda b, m, r=r: (r, 0))
        in_2h = block((tc, 2 * HEAD_DIM), lambda b, m, r=r: (r, 0))
        in_8 = block((8, tc), lambda b, m, r=r: (0, r))
        size = (rank, 3 * (d + width))
        part, late = run_kernel(
            functools.partial(qkv_back_kernel, hc, r),
            meta,
            [(a, in_h) for a in dq]
            + [(a, in_2h) for a in list(dkv) + dkv_in]
            + [
                (pre_q, in_w),
                (pre_k, in_w),
                (st_own, in_8),
                (st_back, in_8),
                (self_gain, whole(self_gain.shape)),
                (cos, in_h),
                (sin, in_h),
                (self_qkv, whole(self_qkv.shape)),
            ]
            + self_tables
            + [
                (tok, in_d),
                (vec, vspec),
                (y1, in_d),
                (lat_t, block((3 * rank, tc), lambda b, m, r=r: (0, r))),
                (dx1, whole((tc, d))),
            ]
            + ([(late, whole(size))] if r else []),
            [whole_of((tc, d), BF16), whole_of(size, F32)],
            scratch=[pltpu.VMEM((3 * rank, 3 * width), BF16)],
            us=8.5,
        )
        q_parts.append(part)
        if line:
            line.add(part)
        if r != 1:
            late, *tied = seal(late, *chains.arrived(), *moving())
            count = len(chains.arrived())
            chains.put(tied[:count])
            if r == 0:
                ctx_at = chains.add(context_grad_steps(ctx_part))
            chains.step()
            if line:
                line.receive(tied[count:])
                line.send()
    pick = lambda g: [jnp.where(is_key, g, 0.0), jnp.where(is_key, 0.0, g)]
    late = jnp.concatenate(
        [late[:, : 3 * d]]
        + pick(g_ctx_dn)
        + [late[:, 3 * d :], split[:rank]]
        + pick(g_ctx_up)
        + [split[rank : 2 * rank], split[2 * rank :]]
        + [jnp.broadcast_to(adapter_index[0].astype(F32) / seq, (rank, HEAD_DIM))],
        axis=1,
    )
    late_at = chains.add(adapter_steps(late, 5 * d))
    chains.start(late_at)
    while chains.live() or (line and line.live()):
        tied = seal(*chains.arrived(), *(line.moving if line else []))
        count = len(chains.arrived())
        chains.put(tied[:count])
        chains.step()
        if line and line.moving:
            line.receive(tied[count:])
            if line.live():
                line.send()
    early, late, context_grad = chains.result(early_at), chains.result(late_at), chains.result(ctx_at).astype(F32)
    if line:
        result, input_grad = jnp.concatenate(line.out[:groups]), jnp.concatenate(line.out[groups:])
    else:
        input_grad = lax.psum(jnp.concatenate(q_parts), "tensor")

    indices = jnp.round(late[:, 0, -1].astype(F32)).astype(jnp.int32)
    early, late = spread(early, indices, slots), spread(late[:, :, :-HEAD_DIM], indices, slots)
    cut = lambda grads, start, size, count: [
        grads[:, :, start + j * size : start + (j + 1) * size] for j in range(count)
    ]
    wide, feed = cut(early, 0, d, 5), cut(early, 5 * d, ff, 2)
    wide_late, narrow = cut(late, 0, d, 5), cut(late, 5 * d, width, 8)
    swap = lambda a: jnp.swapaxes(a, -1, -2)
    return (
        result[None],
        input_grad[None],
        context_grad,
        swap(jnp.stack(wide_late[:3] + wide[:1] + wide_late[3:], axis=1)),
        jnp.stack(narrow[:6], axis=1),
        swap(wide[1]),
        feed[0],
        swap(jnp.stack(narrow[6:], axis=1)),
        jnp.stack(wide[2:4], axis=1),
        swap(feed[1]),
        wide[4],
    )


def solution(mesh):
    placed = (
        P("dp", "seq", None),
        P(None, "dp", "seq"),
        P("dp", None, None),
        P(),
        P(),
        P("dp"),
        P(None, None, "tensor"),
        P(None, "tensor"),
        P(None, "tensor"),
        P("tensor", None),
        P(None, None, "tensor"),
        P(None, "tensor"),
        P(None, "tensor"),
        P("tensor", None),
        P(),
        P(),
        P(None, "tensor"),
        P("tensor"),
        P("tensor", None),
        P(),
        P(),
        P(None, None, None, "tensor"),
        P(),
        P(None, None, "tensor"),
        P(None, None, "tensor", None),
        P(),
        P(None, "tensor", None),
        P(),
        P("dp", "seq", None),
    )
    return jax.shard_map(
        per_device,
        mesh=mesh,
        in_specs=placed,
        out_specs=(
            P("dp", "seq", None),
            P("dp", "seq", None),
            P(),
            P(),
            P(None, None, None, "tensor"),
            P(),
            P(None, None, "tensor"),
            P(None, None, "tensor", None),
            P(),
            P(None, "tensor", None),
            P(),
        ),
        check_vma=False,
    )
```

time: 1710 us -> 651 us (0.38)
  waiting for transfers between devices: 1010 us -> 173 us
  matrix products: 260 us -> 0 us
  Pallas kernels: 0 us -> 253 us
  local copies, waits for them, and re-layouts: 196 us -> 26.5 us
  other arithmetic: 169 us -> 57.2 us
  starting transfers between devices: 1.75 us -> 112 us
  blocking collectives: 41 us -> 0 us
    psum x9 -> x0, waiting for transfers between devices: 997 us -> none  [the longest x3 420 us: branch_total(): lax.psum(partial_value.astype(jnp.bfloat16), 'tensor').astype(jnp.float32)]
    dot_general x84 -> x0, matrix products: 260 us -> none  [the longest x4 22.5 us: columns_backward(): jnp.einsum('jtc,jdc->td', upstream, weights, preferred_element_type=jnp.f...]
    pallas_call x0 -> x20, Pallas kernels: none -> 253 us  [run_kernel(): pl.pallas_call(reading, grid_spec=pltpu.PrefetchScalarGridSpec(num_scalar...]
    ppermute x0 -> x85, waiting for transfers between devices: none -> 173 us  [send(): return jax.tree.map(lambda v: lax.ppermute(v, axis, pairs), values)]
    ppermute x0 -> x85, starting transfers between devices: none -> 112 us  [send(): return jax.tree.map(lambda v: lax.ppermute(v, axis, pairs), values)]
    dynamic_update_slice x8 -> x0, local copies, waits for them, and re-layouts: 72.1 us -> none  [attend_forward(): lax.map(one_block, queries.reshape(length // stride, stride, head_count,...]
    reduce_sum x18 -> x1, other arithmetic: 46.1 us -> 0.19 us  [per_device(): ctx_stat = jnp.sum(g_ctx * ctx_gain * ctx_pre, axis=1)]
    psum x4 -> x0, blocking collectives: 41 us -> none  [the longest x2 23.7 us: norm_totals(): return lax.psum((first, second), 'tensor')]
  transfers between devices with their start and end apart: 13 -> 86, of which waited for: 9 -> 32; matrix products, arithmetic and copies ran while one was open for 19% -> 9% of each run, Pallas kernels for 0% -> 36%
where the time goes in v1:
time: 651 us; the launch traced here: 639 us
  Pallas kernels  253 us (39%)
  waiting for transfers between devices  173 us (27%)
  starting transfers between devices  112 us (17%)
  other arithmetic  57.2 us (9%)
  local copies, waits for them, and re-layouts  26.5 us (4%)
  between operations  16.7 us (3%)
    pallas_call x20, Pallas kernels, run_kernel(): pl.pallas_call(reading, grid_spec=pltpu.PrefetchScalarGridSpec(num_scalar...  253 us
    ppermute x85, waiting for transfers between devices, send(): return jax.tree.map(lambda v: lax.ppermute(v, axis, pairs), values)  173 us
    ppermute x85, starting transfers between devices, send(): return jax.tree.map(lambda v: lax.ppermute(v, axis, pairs), values)  112 us
    unnamed x174, local copies, waits for them, and re-layouts  13.1 us
  transfers between devices with their start and end apart: 86, of which 32 were waited for; matrix products, arithmetic and copies ran while one was open for 9% of the time, Pallas kernels for 36%

profile of v1, /device:TPU:9, one launch (start us, length us, event | category | flops | bytes accessed | tf_op | source)
XLA Modules:
  0.0 639.1 jit_solution(8680894550017142779)
XLA Ops:
  8.5 2.6 shard_map.392.refs_8_
  16.9 5.6 shard_map.393
  22.5 3.3 sine_multiply_fusion
  25.7 15.7 %shard_map.394 = (bf16[1024,1536]{1,0:T(8,128)(2,1)}, bf16[48,1024]{1,0:T(8,128)(2,1)}, bf16[1024,384]{1,0:T(8,128)(2,1)}, bf16[1024,384]{1,0:T(8,128)(2,1)}, bf...) custom-call(s32[12]{0:T(128)} %stack.104.meta_ref, ...), custom_call_target="tpu_custom_call" | custom-call | flops 17250000896 | bytes 18121472 | tf_op jit(solution)/shard_map/pallas_call | solution.py:85
  47.0 3.1 collective-permute-done.2.refs_1_
  50.1 2.7 collective-permute-done.3.refs_2_
  53.6 3.1 shard_map.395.refs_8_.refs_18_.refs_21_
  56.7 3.7 collective-permute-start.4
  66.2 16.9 %shard_map.396 = (bf16[256,256]{1,0:T(8,128)(2,1)}, bf16[256,256]{1,0:T(8,128)(2,1)}, bf16[256,256]{1,0:T(8,128)(2,1)}, bf16[256,256]{1,0:T(8,128)(2,1)}, bf16[1024,256]{1,0:T(8,128)(2,1)}, /*index=5*/f32[16,1024]{1,0:T(8,128)}) custom-call(s32[12]{0:T(128)} %stack.104.meta_ref, bf16[1024,384]{1,0:T(8,128)(2,1)} %get-tuple-element.204.refs_0_, ...), custom_call_target="tpu_custom_call" | custom-call | flops 21849999360 | bytes 8290304 | tf_op jit(solution)/shard_map/pallas_call | solution.py:85
  87.2 9.6 %shard_map.397 = (bf16[256,128]{1,0:T(8,128)(2,1)}, bf16[256,128]{1,0:T(8,128)(2,1)}, bf16[256,128]{1,0:T(8,128)(2,1)}, bf16[256,128]{1,0:T(8,128)(2,1)}, bf16[1024,128]{1,0:T(8,128)(2,1)}, /*index=5*/f32[8,1024]{1,0:T(8,128)}) custom-call(s32[12]{0:T(128)} %stack.104.meta_ref, bf16[1024,384]{1,0:T(8,128)(2,1)} %get-tuple-element.204.refs_0_, ...), custom_call_target="tpu_custom_call" | custom-call | flops 10924999680 | bytes 7733248 | tf_op jit(solution)/shard_map/pallas_call | solution.py:85
  96.9 12.8 %collective-permute-done.10.refs_2_ = bf16[256,256]{1,0:T(8,128)(2,1)S(1)} collective-permute-done((bf16[256,256]{1,0:T(8,128)(2,1)}, bf16[256,256]{1,0:T(8,128)(2,1)S(1)}, u32[]{:S(2)}, u32[]{:S(2)}) %collective-permute-start.10) | collective-permute-done | bytes 131104 | tf_op jit(solution)/shard_map/ppermute | solution.py:579
  109.7 2.6 collective-permute-done.11.refs_3_
  118.3 2.9 collective-permute-done.14.refs_7_
  121.2 5.3 collective-permute-done.16.refs_22_.refs_25_
  126.5 3.6 collective-permute-done.15.refs_21_.refs_24_
  133.1 6.7 %collective-permute-done.21.refs_27_.refs_30_ = bf16[3,64,1536]{2,1,0:T(8,128)(2,1)S(1)} collective-permute-done((bf16[3,64,1536]{2,1,0:T(8,128)(2,1)S(1)}, bf16[3,64,1536]{2,1,0:T(8,128)(2,1)S(1)}, u32[]{:S(2)}, u32[]{:S(2)}) %collective-permute-start.21) | collective-permute-done | bytes 589856 | tf_op jit(solution)/shard_map/ppermute | solution.py:579
  142.6 21.6 %shard_map.398 = (bf16[256,1536]{1,0:T(8,128)(2,1)}, f32[256,1536]{1,0:T(8,128)}, f32[256,1536]{1,0:T(8,128)}, bf16[256,1536]{1,0:T(8,128)(2,1)}, bf16[256,1536]...) custom-call(s32[12]{0:T(128)} %stack.104.meta_ref, ...), custom_call_target="tpu_custom_call" | custom-call | flops 23000000512 | bytes 35987456 | tf_op jit(solution)/shard_map/pallas_call | solution.py:85
  164.4 18.6 %shard_map.399 = (bf16[1024,1536]{1,0:T(8,128)(2,1)}, f32[256,1536]{1,0:T(8,128)}, f32[16,2240]{1,0:T(8,128)}, f32[16,1536]{1,0:T(8,128)}, f32[16,1536]{1,0:T(8,128)}, /*index=5*/f32[16,2240]{1,0:T(8,128)}) custom-call(s32[12]{0:T(128)} %stack.104.meta_ref, bf16[256,1536]{1,0:T(8,128)(2,1)} %get-tuple-element.240.refs_0_, bf16[1024,1536]{1,0:T(8,128)(2,1)} %bitcast.181, ...), custom_call_target="tpu_custom_call" | custom-call | flops 20700000256 | bytes 26510080 | tf_op jit(solution)/shard_map/pallas_call | solution.py:85
  184.2 17.9 %shard_map.400 = (bf16[1024,1536]{1,0:T(8,128)(2,1)}, bf16[256,1536]{1,0:T(8,128)(2,1)}, f32[16,2240]{1,0:T(8,128)}, f32[16,1536]{1,0:T(8,128)}, f32[16,1536]{1,0:T(8,128)}, /*index=5*/f32[16,2240]{1,0:T(8,128)}) custom-call(s32[12]{0:T(128)} %stack.104.meta_ref, bf16[256,1536]{1,0:T(8,128)(2,1)} %copy-done.54, ...), custom_call_target="tpu_custom_call", output_to_operand_aliasing={{0}: (15, {})} | custom-call | flops 20700000256 | bytes 27779840 | tf_op jit(solution)/shard_map/pallas_call | solution.py:85
  202.7 2.8 collective-permute-start.24
  205.5 17.9 %shard_map.401 = (bf16[1024,1536]{1,0:T(8,128)(2,1)}, bf16[256,1536]{1,0:T(8,128)(2,1)}, f32[16,2240]{1,0:T(8,128)}, f32[16,1536]{1,0:T(8,128)}, f32[16,1536]{1,0:T(8,128)}, /*index=5*/f32[16,2240]{1,0:T(8,128)}) custom-call(s32[12]{0:T(128)} %stack.104.meta_ref, bf16[256,1536]{1,0:T(8,128)(2,1)} %copy-done.52, ...), custom_call_target="tpu_custom_call", output_to_operand_aliasing={{0}: (15, {})} | custom-call | flops 20700000256 | bytes 27779840 | tf_op jit(solution)/shard_map/pallas_call | solution.py:85
  225.7 11.5 %collective-permute-done.24.refs_0_ = bf16[256,1536]{1,0:T(8,128)(2,1)S(1)} collective-permute-done((bf16[256,1536]{1,0:T(8,128)(2,1)S(1)}, bf16[256,1536]{1,0:T(8,128)(2,1)S(1)}, u32[]{:S(2)}, u32[]{:S(2)}) %collective-permute-start.24) | collective-permute-done | bytes 786464 | tf_op jit(solution)/shard_map/ppermute | solution.py:579
  238.0 17.9 %shard_map.402 = (bf16[1024,1536]{1,0:T(8,128)(2,1)}, bf16[256,1536]{1,0:T(8,128)(2,1)}, f32[16,2240]{1,0:T(8,128)}, f32[16,1536]{1,0:T(8,128)}, f32[16,1536]{1,0:T(8,128)}, /*index=5*/f32[16,2240]{1,0:T(8,128)}) custom-call(s32[12]{0:T(128)} %stack.104.meta_ref, bf16[256,1536]{1,0:T(8,128)(2,1)} %copy-done.53, ...), custom_call_target="tpu_custom_call", output_to_operand_aliasing={{0}: (15, {})} | custom-call | flops 20700000256 | bytes 27779840 | tf_op jit(solution)/shard_map/pallas_call | solution.py:85
  259.6 14.9 %collective-permute-done.27.refs_1_ = bf16[256,1536]{1,0:T(8,128)(2,1)S(1)} collective-permute-done((bf16[256,1536]{1,0:T(8,128)(2,1)S(1)}, bf16[256,1536]{1,0:T(8,128)(2,1)S(1)}, u32[]{:S(2)}, u32[]{:S(2)}) %collective-permute-start.27) | collective-permute-done | bytes 786464 | tf_op jit(solution)/shard_map/ppermute | solution.py:579
  274.6 2.7 fusion.52
  278.8 27.9 %shard_map.403 = (bf16[256,128]{1,0:T(8,128)(2,1)}, bf16[256,128]{1,0:T(8,128)(2,1)}, bf16[256,128]{1,0:T(8,128)(2,1)}, bf16[256,128]{1,0:T(8,128)(2,1)}, bf16[2...) custom-call(s32[12]{0:T(128)} %stack.104.meta_ref, ...), custom_call_target="tpu_custom_call" | custom-call | flops 29899999232 | bytes 42868736 | tf_op jit(solution)/shard_map/pallas_call | solution.py:85
  306.7 3.1 collective-permute-start.35
  313.4 5.5 collective-permute-start.32
  321.3 2.7 collective-permute-start.30
  328.0 12.5 %shard_map.404 = (f32[1024,128]{1,0:T(8,128)}, f32[1024,256]{1,0:T(8,128)}, bf16[1024,256]{1,0:T(8,128)(2,1)}, f32[8,1024]{1,0:T(8,128)}, f32[8,1024]{1,0:T(8,128)}) custom-call(s32[12]{0:T(128)} %stack.104.meta_ref, bf16[1024,384]{1,0:T(8,128)(2,1)} %get-tuple-element.204.refs_0_, f32[8,1024]{1,0:T(8,128)} %copy-done.24, f32[8,1024]{1,0:T(8,128)} %copy-done.24, ...), custom_call_target="tpu_custom_call" | custom-call | flops 14375000064 | bytes 10190848 | tf_op jit(solution)/shard_map/pallas_call | solution.py:85
  341.8 2.4 collective-permute-start.43
  349.0 12.5 %shard_map.405 = (f32[1024,128]{1,0:T(8,128)}, f32[1024,256]{1,0:T(8,128)}, bf16[1024,256]{1,0:T(8,128)(2,1)}, f32[8,1024]{1,0:T(8,128)}, f32[8,1024]{1,0:T(8,128)}) custom-call(s32[12]{0:T(128)} %stack.104.meta_ref, bf16[1024,384]{1,0:T(8,128)(2,1)} %get-tuple-element.204.refs_0_, f32[8,1024]{1,0:T(8,128)} %copy-done.24, f32[8,1024]{1,0:T(8,128)} %copy-done.24, ...), custom_call_target="tpu_custom_call" | custom-call | flops 14375000064 | bytes 10518528 | tf_op jit(solution)/shard_map/pallas_call | solution.py:85
  361.4 8.2 %collective-permute-done.39 = bf16[560,384]{1,0:T(8,128)(2,1)} collective-permute-done((bf16[560,384]{1,0:T(8,128)(2,1)}, bf16[560,384]{1,0:T(8,128)(2,1)}, u32[]{:S(2)}, u32[]{:S(2)}) %collective-permute-start.39) | collective-permute-done | bytes 430112 | tf_op jit(solution)/shard_map/ppermute | solution.py:579
  372.5 3.2 collective-permute-start.41
  375.7 12.5 %shard_map.406 = (f32[1024,128]{1,0:T(8,128)}, f32[1024,256]{1,0:T(8,128)}, bf16[1024,256]{1,0:T(8,128)(2,1)}, f32[8,1024]{1,0:T(8,128)}, f32[8,1024]{1,0:T(8,128)}) custom-call(s32[12]{0:T(128)} %stack.104.meta_ref, bf16[1024,384]{1,0:T(8,128)(2,1)} %get-tuple-element.204.refs_0_, f32[8,1024]{1,0:T(8,128)} %copy-done.24, f32[8,1024]{1,0:T(8,128)} %copy-done.24, ...), custom_call_target="tpu_custom_call" | custom-call | flops 14375000064 | bytes 10223616 | tf_op jit(solution)/shard_map/pallas_call | solution.py:85
  388.2 2.5 collective-permute-start.45
  399.0 3.1 collective-permute-done.51
  407.1 5.7 shard_map.410
  412.8 2.9 select_convert_fusion
  416.0 3.0 collective-permute-start.56
  419.0 8.8 %shard_map.407 = (bf16[256,1536]{1,0:T(8,128)(2,1)}, f32[16,5760]{1,0:T(8,128)}) custom-call(s32[12]{0:T(128)} %stack.104.meta_ref, f32[1024,128]{1,0:T(8,128)} %get-tuple-element.310.refs_16_.refs_0_, f32[1024,128]{1,0:T(8,128)} %get-tuple-element.318.refs_16_.refs_1_, f32[1024,128]{1,0:T(8,128)} %get-tuple-element.324.refs_2_, ...), custom_call_target="tpu_custom_call" | custom-call | flops 9774999552 | bytes 17000000 | tf_op jit(solution)/shard_map/pallas_call | solution.py:85
  434.4 3.9 collective-permute-start.58
  438.2 8.6 %shard_map.408 = (bf16[256,1536]{1,0:T(8,128)(2,1)}, f32[16,5760]{1,0:T(8,128)}) custom-call(s32[12]{0:T(128)} %stack.104.meta_ref, f32[1024,128]{1,0:T(8,128)} %get-tuple-element.310.refs_16_.refs_0_, f32[1024,128]{1,0:T(8,128)} %get-tuple-element.318.refs_16_.refs_1_, f32[1024,128]{1,0:T(8,128)} %get-tuple-element.324.refs_2_, ...), custom_call_target="tpu_custom_call" | custom-call | flops 9774999552 | bytes 17000000 | tf_op jit(solution)/shard_map/pallas_call | solution.py:85
  446.9 8.6 %shard_map.409 = (bf16[256,1536]{1,0:T(8,128)(2,1)}, f32[16,5760]{1,0:T(8,128)}) custom-call(s32[12]{0:T(128)} %stack.104.meta_ref, f32[1024,128]{1,0:T(8,128)} %get-tuple-element.310.refs_16_.refs_0_, f32[1024,128]{1,0:T(8,128)} %get-tuple-element.318.refs_16_.refs_1_, f32[1024,128]{1,0:T(8,128)} %get-tuple-element.324.refs_2_, ...), custom_call_target="tpu_custom_call" | custom-call | flops 9774999552 | bytes 17000000 | tf_op jit(solution)/shard_map/pallas_call | solution.py:85
  455.5 2.5 broadcast_select_fusion.14
  464.4 2.5 broadcast_select_fusion.11
  468.3 3.2 collective-permute-start.64
  471.5 8.6 %shard_map.411 = (bf16[256,1536]{1,0:T(8,128)(2,1)}, f32[16,5760]{1,0:T(8,128)}) custom-call(s32[12]{0:T(128)} %stack.104.meta_ref, f32[1024,128]{1,0:T(8,128)} %get-tuple-element.310.refs_16_.refs_0_, f32[1024,128]{1,0:T(8,128)} %get-tuple-element.318.refs_16_.refs_1_, f32[1024,128]{1,0:T(8,128)} %get-tuple-element.324.refs_2_, ...), custom_call_target="tpu_custom_call" | custom-call | flops 9774999552 | bytes 17000000 | tf_op jit(solution)/shard_map/pallas_call | solution.py:85
  482.9 3.4 collective-permute-done.62
  495.2 3.5 collective-permute-start.68
  502.0 9.9 %collective-permute-done.67 = bf16[256,1536]{1,0:T(8,128)(2,1)S(1)} collective-permute-done((bf16[256,1536]{1,0:T(8,128)(2,1)S(1)}, bf16[256,1536]{1,0:T(8,128)(2,1)S(1)}, u32[]{:S(2)}, u32[]{:S(2)}) %collective-permute-start.67) | collective-permute-done | bytes 786464 | tf_op jit(solution)/shard_map/ppermute | solution.py:579
  512.0 3.9 collective-permute-done.68
  516.1 2.6 collective-permute-start.70
  519.3 2.3 collective-permute-start.72
  525.0 16.8 %collective-permute-done.71 = bf16[256,1536]{1,0:T(8,128)(2,1)S(1)} collective-permute-done((bf16[256,1536]{1,0:T(8,128)(2,1)S(1)}, bf16[256,1536]{1,0:T(8,128)(2,1)S(1)}, u32[]{:S(2)}, u32[]{:S(2)}) %collective-permute-start.71) | collective-permute-done | bytes 786464 | tf_op jit(solution)/shard_map/ppermute | solution.py:579
  546.0 19.7 %collective-permute-done.74 = bf16[8,7680]{1,0:T(8,128)(2,1)S(1)} collective-permute-done((bf16[8,7680]{1,0:T(8,128)(2,1)S(1)}, bf16[8,7680]{1,0:T(8,128)(2,1)S(1)}, u32[]{:S(2)}, u32[]{:S(2)}) %collective-permute-start.74) | collective-permute-done | bytes 122912 | tf_op jit(solution)/shard_map/ppermute | solution.py:579
  567.3 5.0 collective-permute-start.79
  575.2 3.9 collective-permute-done.78
  579.1 6.3 collective-permute-done.79
  585.4 4.1 collective-permute-done.80
  589.7 5.0 collective-permute-start.81
  596.6 9.5 %collective-permute-done.82 = bf16[2,8,10880]{2,1,0:T(8,128)(2,1)S(1)} collective-permute-done((bf16[2,8,10880]{2,1,0:T(8,128)(2,1)S(1)}, bf16[2,8,10880]{2,1,0:T(8,128)(2,1)S(1)}, u32[]{:S(2)}, u32[]{:S(2)}) %collective-permute-start.82) | collective-permute-done | bytes 348192 | tf_op jit(solution)/shard_map/ppermute | solution.py:579
  606.1 7.2 %collective-permute-done.83 = bf16[256,1536]{1,0:T(8,128)(2,1)S(1)} collective-permute-done((bf16[256,1536]{1,0:T(8,128)(2,1)S(1)}, bf16[256,1536]{1,0:T(8,128)(2,1)S(1)}, u32[]{:S(2)}, u32[]{:S(2)}) %collective-permute-start.83) | collective-permute-done | bytes 786464 | tf_op jit(solution)/shard_map/ppermute | solution.py:579
  625.7 2.6 copy.51
  (411 shorter events, 136.1 us)
Async XLA Ops:
  7.2 135.3 %all-gather.3.cloned.1.call-start = ((), (), s32[]{:S(2)}) async-start(), calls=%async_computation | async-start | bytes 3981312 | tf_op jit(solution)/shard_map/all_gather | solution.py:1021
  11.2 35.9 %collective-permute-start.1 = (bf16[144,1536]{1,0:T(8,128)(2,1)}, bf16[144,1536]{1,0:T(8,128)(2,1)S(1)}, u32[]{:S(2)}, u32[]{:S(2)}) collective-permute-start(bf16[144,1536]{1,0:T(8,128)(2,1)} %shard_map.392.refs_8_), channel_id=1, source_target_pairs={{0,1},{1,2},{2,3},{3,0},{4,5},{5,6},{6,7},{7,4},{8,9},{9,10},{10,1... | collective-permute-start | bytes 1327112 | tf_op jit(solution)/shard_map/ppermute | solution.py:579
  12.5 37.6 %collective-permute-start.2 = (bf16[144,1536]{1,0:T(8,128)(2,1)}, bf16[144,1536]{1,0:T(8,128)(2,1)S(1)}, u32[]{:S(2)}, u32[]{:S(2)}) collective-permute-start(bf16[144,1536]{1,0:T(8,128)(2,1)} %shard_map.392.refs_8_), channel_id=1, source_target_pairs={{0,2},{1,3},{2,0},{3,1},{4,6},{5,7},{6,4},{7,5},{8,10},{9,11},{10,... | collective-permute-start | bytes 1327112 | tf_op jit(solution)/shard_map/ppermute | solution.py:579
  13.5 39.3 %collective-permute-start.3 = (bf16[144,1536]{1,0:T(8,128)(2,1)}, bf16[144,1536]{1,0:T(8,128)(2,1)S(1)}, u32[]{:S(2)}, u32[]{:S(2)}) collective-permute-start(bf16[144,1536]{1,0:T(8,128)(2,1)} %shard_map.392.refs_8_), channel_id=1, source_target_pairs={{0,3},{1,0},{2,1},{3,2},{4,7},{5,4},{6,5},{7,6},{8,11},{9,8},{10,9... | collective-permute-start | bytes 1327112 | tf_op jit(solution)/shard_map/ppermute | solution.py:579
  41.4 24.2 %collective-permute-start.6 = (bf16[1024,768]{1,0:T(8,128)(2,1)}, bf16[1024,768]{1,0:T(8,128)(2,1)}, u32[]{:S(2)}, u32[]{:S(2)}) collective-permute-start(bf16[1024,768]{1,0:T(8,128)(2,1)} %get-tuple-element.211.refs_4_.refs_6_), channel_id=1, source_target_pairs={{0,4},{4,0},{1,5},{5,1},{2,6},{6,2},{3,7},{7,3},{8,12},{12,8},{9,1... | collective-permute-start | bytes 4718600 | tf_op jit(solution)/shard_map/ppermute | solution.py:579
  63.1 49.3 %collective-permute-start.7 = (bf16[3,144,1536]{2,1,0:T(8,128)(2,1)}, bf16[3,144,1536]{2,1,0:T(8,128)(2,1)S(1)}, u32[]{:S(2)}, u32[]{:S(2)}) collective-permute-start(bf16[3,144,1536]{2,1,0:T(8,128)(2,1)} %shard_map.395.refs_8_.refs_18_.refs_21_), channel_id=1, source_target_pairs={{0,8},{8,0},{16,24},{24,16},{1,9},{9,1},{17,25},{25,17},{2,10},{10... | collective-permute-start | bytes 3981320 | tf_op jit(solution)/shard_map/ppermute | solution.py:579
  64.3 48.0 %collective-permute-start.8 = (bf16[3,144,1536]{2,1,0:T(8,128)(2,1)}, bf16[3,144,1536]{2,1,0:T(8,128)(2,1)S(1)}, u32[]{:S(2)}, u32[]{:S(2)}) collective-permute-start(bf16[3,144,1536]{2,1,0:T(8,128)(2,1)} %shard_map.395.refs_8_.refs_18_.refs_21_), channel_id=1, source_target_pairs={{0,16},{8,24},{16,0},{24,8},{1,17},{9,25},{17,1},{25,9},{2,18},{10... | collective-permute-start | bytes 3981320 | tf_op jit(solution)/shard_map/ppermute | solution.py:579
  83.1 13.8 %collective-permute-start.9 = (bf16[256,256]{1,0:T(8,128)(2,1)}, bf16[256,256]{1,0:T(8,128)(2,1)S(1)}, u32[]{:S(2)}, u32[]{:S(2)}) collective-permute-start(bf16[256,256]{1,0:T(8,128)(2,1)} %get-tuple-element.216), channel_id=1, source_target_pairs={{0,1},{1,2},{2,3},{3,0},{4,5},{5,6},{6,7},{7,4},{8,9},{9,10},{10,1... | collective-permute-start | bytes 393224 | tf_op jit(solution)/shard_map/ppermute | solution.py:579
  84.1 25.7 %collective-permute-start.10 = (bf16[256,256]{1,0:T(8,128)(2,1)}, bf16[256,256]{1,0:T(8,128)(2,1)S(1)}, u32[]{:S(2)}, u32[]{:S(2)}) collective-permute-start(bf16[256,256]{1,0:T(8,128)(2,1)} %get-tuple-element.217), channel_id=1, source_target_pairs={{0,2},{1,3},{2,0},{3,1},{4,6},{5,7},{6,4},{7,5},{8,10},{9,11},{10,... | collective-permute-start | bytes 393224 | tf_op jit(solution)/shard_map/ppermute | solution.py:579
  85.8 26.6 %collective-permute-start.11 = (bf16[256,256]{1,0:T(8,128)(2,1)}, bf16[256,256]{1,0:T(8,128)(2,1)S(1)}, u32[]{:S(2)}, u32[]{:S(2)}) collective-permute-start(bf16[256,256]{1,0:T(8,128)(2,1)} %get-tuple-element.218), channel_id=1, source_target_pairs={{0,3},{1,0},{2,1},{3,2},{4,7},{5,4},{6,5},{7,6},{8,11},{9,8},{10,9... | collective-permute-start | bytes 393224 | tf_op jit(solution)/shard_map/ppermute | solution.py:579
  112.5 17.6 %collective-permute-start.15 = (bf16[3,80,1536]{2,1,0:T(8,128)(2,1)S(1)}, bf16[3,80,1536]{2,1,0:T(8,128)(2,1)S(1)}, u32[]{:S(2)}, u32[]{:S(2)}) collective-permute-start(bf16[3,80,1536]{2,1,0:T(8,128)(2,1)S(1)} %slice.231), channel_id=1, source_target_pairs={{0,8},{8,0},{16,24},{24,16},{1,9},{9,1},{17,25},{25,17},{2,10},{10... | collective-permute-start | bytes 2211848 | tf_op jit(solution)/shard_map/ppermute | solution.py:579
  112.8 13.7 %collective-permute-start.16 = (bf16[3,64,1536]{2,1,0:T(8,128)(2,1)S(1)}, bf16[3,64,1536]{2,1,0:T(8,128)(2,1)S(1)}, u32[]{:S(2)}, u32[]{:S(2)}) collective-permute-start(bf16[3,64,1536]{2,1,0:T(8,128)(2,1)S(1)} %slice.232), channel_id=1, source_target_pairs={{0,16},{8,24},{16,0},{24,8},{1,17},{9,25},{17,1},{25,9},{2,18},{10... | collective-permute-start | bytes 1769480 | tf_op jit(solution)/shard_map/ppermute | solution.py:579
  131.5 11.0 %collective-permute-start.19 = (bf16[3,144,1536]{2,1,0:T(8,128)(2,1)S(1)}, bf16[3,144,1536]{2,1,0:T(8,128)(2,1)}, u32[]{:S(2)}, u32[]{:S(2)}) collective-permute-start(bf16[3,144,1536]{2,1,0:T(8,128)(2,1)S(1)} %collective-permute-done.8.refs_20_.refs_23_), channel_id=1, source_target_pairs={{0,4},{4,0},{1,5},{5,1},{2,6},{6,2},{3,7},{7,3},{8,12},{12,8},{9,1... | collective-permute-start | bytes 3981320 | tf_op jit(solution)/shard_map/ppermute | solution.py:579
  164.1 19.2 %collective-permute-start.22 = (bf16[256,1536]{1,0:T(8,128)(2,1)}, bf16[256,1536]{1,0:T(8,128)(2,1)S(1)}, u32[]{:S(2)}, u32[]{:S(2)}) collective-permute-start(bf16[256,1536]{1,0:T(8,128)(2,1)} %get-tuple-element.240.refs_0_), channel_id=1, source_target_pairs={{0,1},{1,2},{2,3},{3,0},{4,5},{5,6},{6,7},{7,4},{8,9},{9,10},{10,1... | collective-permute-start | bytes 2359304 | tf_op jit(solution)/shard_map/ppermute | solution.py:579
  183.3 19.3 %collective-permute-start.23 = (bf16[256,1536]{1,0:T(8,128)(2,1)S(1)}, bf16[256,1536]{1,0:T(8,128)(2,1)S(1)}, u32[]{:S(2)}, u32[]{:S(2)}) collective-permute-start(bf16[256,1536]{1,0:T(8,128)(2,1)S(1)} %collective-permute-done.22.refs_0_), channel_id=1, source_target_pairs={{0,1},{1,2},{2,3},{3,0},{4,5},{5,6},{6,7},{7,4},{8,9},{9,10},{10,1... | collective-permute-start | bytes 2359304 | tf_op jit(solution)/shard_map/ppermute | solution.py:579
  202.2 21.3 %collective-permute-start.25 = (bf16[256,1536]{1,0:T(8,128)(2,1)}, bf16[256,1536]{1,0:T(8,128)(2,1)S(1)}, u32[]{:S(2)}, u32[]{:S(2)}) collective-permute-start(bf16[256,1536]{1,0:T(8,128)(2,1)} %get-tuple-element.258), channel_id=1, source_target_pairs={{0,1},{1,2},{2,3},{3,0},{4,5},{5,6},{6,7},{7,4},{8,9},{9,10},{10,1... | collective-permute-start | bytes 2359304 | tf_op jit(solution)/shard_map/ppermute | solution.py:579
  202.7 34.4 %collective-permute-start.24 = (bf16[256,1536]{1,0:T(8,128)(2,1)S(1)}, bf16[256,1536]{1,0:T(8,128)(2,1)S(1)}, u32[]{:S(2)}, u32[]{:S(2)}) collective-permute-start(bf16[256,1536]{1,0:T(8,128)(2,1)S(1)} %collective-permute-done.23.refs_0_), channel_id=1, source_target_pairs={{0,1},{1,2},{2,3},{3,0},{4,5},{5,6},{6,7},{7,4},{8,9},{9,10},{10,1... | collective-permute-start | bytes 2359304 | tf_op jit(solution)/shard_map/ppermute | solution.py:579
  224.8 31.1 %collective-permute-start.26 = (bf16[256,1536]{1,0:T(8,128)(2,1)S(1)}, bf16[256,1536]{1,0:T(8,128)(2,1)S(1)}, u32[]{:S(2)}, u32[]{:S(2)}) collective-permute-start(bf16[256,1536]{1,0:T(8,128)(2,1)S(1)} %add_convert_fusion.17), channel_id=1, source_target_pairs={{0,1},{1,2},{2,3},{3,0},{4,5},{5,6},{6,7},{7,4},{8,9},{9,10},{10,1... | collective-permute-start | bytes 2359304 | tf_op jit(solution)/shard_map/ppermute | solution.py:579
  257.3 17.3 %collective-permute-start.27 = (bf16[256,1536]{1,0:T(8,128)(2,1)S(1)}, bf16[256,1536]{1,0:T(8,128)(2,1)S(1)}, u32[]{:S(2)}, u32[]{:S(2)}) collective-permute-start(bf16[256,1536]{1,0:T(8,128)(2,1)S(1)} %add_convert_fusion.16), channel_id=1, source_target_pairs={{0,1},{1,2},{2,3},{3,0},{4,5},{5,6},{6,7},{7,4},{8,9},{9,10},{10,1... | collective-permute-start | bytes 2359304 | tf_op jit(solution)/shard_map/ppermute | solution.py:579
  277.3 35.0 %collective-permute-start.28 = (bf16[256,1536]{1,0:T(8,128)(2,1)S(1)}, bf16[256,1536]{1,0:T(8,128)(2,1)S(1)}, u32[]{:S(2)}, u32[]{:S(2)}) collective-permute-start(bf16[256,1536]{1,0:T(8,128)(2,1)S(1)} %get-tuple-element.426), channel_id=1, source_target_pairs={{0,1},{3,2},{4,5},{7,6},{8,9},{11,10},{12,13},{15,14},{16,17},{19,... | collective-permute-start | bytes 2359304 | tf_op jit(solution)/shard_map/ppermute | solution.py:579
  306.7 14.6 %collective-permute-start.35 = (bf16[256,128]{1,0:T(8,128)(2,1)}, bf16[256,128]{1,0:T(8,128)(2,1)S(1)}, u32[]{:S(2)}, u32[]{:S(2)}) collective-permute-start(bf16[256,128]{1,0:T(8,128)(2,1)} %get-tuple-element.291), channel_id=1, source_target_pairs={{0,3},{1,0},{2,1},{3,2},{4,7},{5,4},{6,5},{7,6},{8,11},{9,8},{10,9... | collective-permute-start | bytes 196616 | tf_op jit(solution)/shard_map/ppermute | solution.py:579
  309.8 14.2 %collective-permute-start.36 = (bf16[256,128]{1,0:T(8,128)(2,1)}, bf16[256,128]{1,0:T(8,128)(2,1)S(1)}, u32[]{:S(2)}, u32[]{:S(2)}) collective-permute-start(bf16[256,128]{1,0:T(8,128)(2,1)} %get-tuple-element.292), channel_id=1, source_target_pairs={{0,2},{1,3},{2,0},{3,1},{4,6},{5,7},{6,4},{7,5},{8,10},{9,11},{10,... | collective-permute-start | bytes 196616 | tf_op jit(solution)/shard_map/ppermute | solution.py:579
  309.8 14.8 %collective-permute-start.37 = (bf16[256,128]{1,0:T(8,128)(2,1)}, bf16[256,128]{1,0:T(8,128)(2,1)S(1)}, u32[]{:S(2)}, u32[]{:S(2)}) collective-permute-start(bf16[256,128]{1,0:T(8,128)(2,1)} %get-tuple-element.293), channel_id=1, source_target_pairs={{0,1},{1,2},{2,3},{3,0},{4,5},{5,6},{6,7},{7,4},{8,9},{9,10},{10,1... | collective-permute-start | bytes 196616 | tf_op jit(solution)/shard_map/ppermute | solution.py:579
  311.1 29.4 %collective-permute-start.29 = (bf16[256,256]{1,0:T(8,128)(2,1)}, bf16[256,256]{1,0:T(8,128)(2,1)S(1)}, u32[]{:S(2)}, u32[]{:S(2)}) collective-permute-start(bf16[256,256]{1,0:T(8,128)(2,1)} %get-tuple-element.279), channel_id=1, source_target_pairs={{0,3},{1,0},{2,1},{3,2},{4,7},{5,4},{6,5},{7,6},{8,11},{9,8},{10,9... | collective-permute-start | bytes 393224 | tf_op jit(solution)/shard_map/ppermute | solution.py:579
  321.3 20.5 %collective-permute-start.30 = (bf16[256,256]{1,0:T(8,128)(2,1)S(1)}, bf16[256,256]{1,0:T(8,128)(2,1)}, u32[]{:S(2)}, u32[]{:S(2)}) collective-permute-start(bf16[256,256]{1,0:T(8,128)(2,1)S(1)} %copy-done.63), channel_id=1, source_target_pairs={{0,2},{1,3},{2,0},{3,1},{4,6},{5,7},{6,4},{7,5},{8,10},{9,11},{10,... | collective-permute-start | bytes 393224 | tf_op jit(solution)/shard_map/ppermute | solution.py:579
  324.0 20.2 %collective-permute-start.31 = (bf16[256,256]{1,0:T(8,128)(2,1)}, bf16[256,256]{1,0:T(8,128)(2,1)}, u32[]{:S(2)}, u32[]{:S(2)}) collective-permute-start(bf16[256,256]{1,0:T(8,128)(2,1)} %get-tuple-element.281), channel_id=1, source_target_pairs={{0,1},{1,2},{2,3},{3,0},{4,5},{5,6},{6,7},{7,4},{8,9},{9,10},{10,1... | collective-permute-start | bytes 393224 | tf_op jit(solution)/shard_map/ppermute | solution.py:579
  324.6 20.6 %collective-permute-start.33 = (bf16[8,7680]{1,0:T(8,128)(2,1)}, bf16[8,7680]{1,0:T(8,128)(2,1)S(1)}, u32[]{:S(2)}, u32[]{:S(2)}) collective-permute-start(bf16[8,7680]{1,0:T(8,128)(2,1)} %slice.302), channel_id=1, source_target_pairs={{0,1},{1,0},{2,3},{3,2},{4,5},{5,4},{6,7},{7,6},{8,9},{9,8},{10,11... | collective-permute-start | bytes 368648 | tf_op jit(solution)/shard_map/ppermute | solution.py:579
  327.3 18.0 %collective-permute-start.38 = (bf16[560,384]{1,0:T(8,128)(2,1)}, bf16[560,384]{1,0:T(8,128)(2,1)}, u32[]{:S(2)}, u32[]{:S(2)}) collective-permute-start(bf16[560,384]{1,0:T(8,128)(2,1)} %fusion.19), channel_id=1, source_target_pairs={{0,1},{1,2},{2,3},{3,0},{4,5},{5,6},{6,7},{7,4},{8,9},{9,10},{10,1... | collective-permute-start | bytes 1290248 | tf_op jit(solution)/shard_map/ppermute | solution.py:579
  340.5 47.7 %collective-permute-start.42 = (bf16[256,1536]{1,0:T(8,128)(2,1)}, bf16[256,1536]{1,0:T(8,128)(2,1)S(1)}, u32[]{:S(2)}, u32[]{:S(2)}) collective-permute-start(bf16[256,1536]{1,0:T(8,128)(2,1)} %get-tuple-element.425), channel_id=1, source_target_pairs={{0,1},{3,2},{4,5},{7,6},{8,9},{11,10},{12,13},{15,14},{16,17},{19,... | collective-permute-start | bytes 2359304 | tf_op jit(solution)/shard_map/ppermute | solution.py:579
  341.8 48.9 %collective-permute-start.43 = (bf16[256,1536]{1,0:T(8,128)(2,1)S(1)}, bf16[256,1536]{1,0:T(8,128)(2,1)S(1)}, u32[]{:S(2)}, u32[]{:S(2)}) collective-permute-start(bf16[256,1536]{1,0:T(8,128)(2,1)S(1)} %add_convert_fusion.15), channel_id=1, source_target_pairs={{1,2},{2,1},{5,6},{6,5},{9,10},{10,9},{13,14},{14,13},{17,18},{18,... | collective-permute-start | bytes 2359304 | tf_op jit(solution)/shard_map/ppermute | solution.py:579
  344.2 71.5 %collective-permute-start.44 = (bf16[1024,256]{1,0:T(8,128)(2,1)}, bf16[1024,256]{1,0:T(8,128)(2,1)}, u32[]{:S(2)}, u32[]{:S(2)}) collective-permute-start(bf16[1024,256]{1,0:T(8,128)(2,1)} %get-tuple-element.328), channel_id=1, source_target_pairs={{0,4},{4,0},{1,5},{5,1},{2,6},{6,2},{3,7},{7,3},{8,12},{12,8},{9,1... | collective-permute-start | bytes 1572872 | tf_op jit(solution)/shard_map/ppermute | solution.py:579
  347.2 22.4 %collective-permute-start.39 = (bf16[560,384]{1,0:T(8,128)(2,1)}, bf16[560,384]{1,0:T(8,128)(2,1)}, u32[]{:S(2)}, u32[]{:S(2)}) collective-permute-start(bf16[560,384]{1,0:T(8,128)(2,1)} %fusion.9), channel_id=1, source_target_pairs={{0,1},{1,2},{2,3},{3,0},{4,5},{5,6},{6,7},{7,4},{8,9},{9,10},{10,1... | collective-permute-start | bytes 1290248 | tf_op jit(solution)/shard_map/ppermute | solution.py:579
  370.6 20.2 %collective-permute-start.40 = (bf16[8,7680]{1,0:T(8,128)(2,1)S(1)}, bf16[8,7680]{1,0:T(8,128)(2,1)S(1)}, u32[]{:S(2)}, u32[]{:S(2)}) collective-permute-start(bf16[8,7680]{1,0:T(8,128)(2,1)S(1)} %add_convert_fusion.26), channel_id=1, source_target_pairs={{0,2},{1,3},{2,0},{3,1},{4,6},{5,7},{6,4},{7,5},{8,10},{9,11},{10,... | collective-permute-start | bytes 368648 | tf_op jit(solution)/shard_map/ppermute | solution.py:579
  372.5 18.3 %collective-permute-start.41 = (bf16[560,384]{1,0:T(8,128)(2,1)}, bf16[560,384]{1,0:T(8,128)(2,1)}, u32[]{:S(2)}, u32[]{:S(2)}) collective-permute-start(bf16[560,384]{1,0:T(8,128)(2,1)} %fusion.3), channel_id=1, source_target_pairs={{0,1},{1,2},{2,3},{3,0},{4,5},{5,6},{6,7},{7,4},{8,9},{9,10},{10,1... | collective-permute-start | bytes 1290248 | tf_op jit(solution)/shard_map/ppermute | solution.py:579
  388.2 27.7 %collective-permute-start.45 = (bf16[1024,256]{1,0:T(8,128)(2,1)}, bf16[1024,256]{1,0:T(8,128)(2,1)}, u32[]{:S(2)}, u32[]{:S(2)}) collective-permute-start(bf16[1024,256]{1,0:T(8,128)(2,1)} %get-tuple-element.329), channel_id=1, source_target_pairs={{0,4},{4,0},{1,5},{5,1},{2,6},{6,2},{3,7},{7,3},{8,12},{12,8},{9,1... | collective-permute-start | bytes 1572872 | tf_op jit(solution)/shard_map/ppermute | solution.py:579
  390.7 28.3 %collective-permute-start.46 = (bf16[1024,256]{1,0:T(8,128)(2,1)}, bf16[1024,256]{1,0:T(8,128)(2,1)}, u32[]{:S(2)}, u32[]{:S(2)}) collective-permute-start(bf16[1024,256]{1,0:T(8,128)(2,1)} %get-tuple-element.330), channel_id=1, source_target_pairs={{0,4},{4,0},{1,5},{5,1},{2,6},{6,2},{3,7},{7,3},{8,12},{12,8},{9,1... | collective-permute-start | bytes 1572872 | tf_op jit(solution)/shard_map/ppermute | solution.py:579
  402.1 25.7 %collective-permute-start.53 = (bf16[256,1536]{1,0:T(8,128)(2,1)}, bf16[256,1536]{1,0:T(8,128)(2,1)}, u32[]{:S(2)}, u32[]{:S(2)}) collective-permute-start(bf16[256,1536]{1,0:T(8,128)(2,1)} %broadcast_select_fusion.15), channel_id=1, source_target_pairs={{0,1},{3,2},{1,0},{2,3},{4,5},{7,6},{5,4},{6,7},{8,9},{11,10},{9,8... | collective-permute-start | bytes 2359304 | tf_op jit(solution)/shard_map/ppermute | solution.py:579
  403.4 24.4 %collective-permute-start.54 = (bf16[256,1536]{1,0:T(8,128)(2,1)S(1)}, bf16[256,1536]{1,0:T(8,128)(2,1)}, u32[]{:S(2)}, u32[]{:S(2)}) collective-permute-start(bf16[256,1536]{1,0:T(8,128)(2,1)S(1)} %add_convert_fusion.13), channel_id=1, source_target_pairs={{1,2},{2,1},{5,6},{6,5},{9,10},{10,9},{13,14},{14,13},{17,18},{18,... | collective-permute-start | bytes 2359304 | tf_op jit(solution)/shard_map/ppermute | solution.py:579
  415.7 12.0 %collective-permute-start.52 = (bf16[1,8,12160]{2,1,0:T(8,128)(2,1)S(1)}, bf16[1,8,12160]{2,1,0:T(8,128)(2,1)S(1)}, u32[]{:S(2)}, u32[]{:S(2)}) collective-permute-start(bf16[1,8,12160]{2,1,0:T(8,128)(2,1)S(1)} %maximum_bitcast_fusion.6), channel_id=1, source_target_pairs={{0,8},{8,0},{16,24},{24,16},{1,9},{9,1},{17,25},{25,17},{2,10},{10... | collective-permute-start | bytes 583688 | tf_op jit(solution)/shard_map/ppermute | solution.py:579
  416.0 42.0 %collective-permute-start.56 = (bf16[256,1536]{1,0:T(8,128)(2,1)}, bf16[256,1536]{1,0:T(8,128)(2,1)}, u32[]{:S(2)}, u32[]{:S(2)}) collective-permute-start(bf16[256,1536]{1,0:T(8,128)(2,1)} %select_convert_fusion), channel_id=1, source_target_pairs={{0,4},{4,0},{1,5},{5,1},{2,6},{6,2},{3,7},{7,3},{8,12},{12,8},{9,1... | collective-permute-start | bytes 2359304 | tf_op jit(solution)/shard_map/ppermute | solution.py:579
  428.6 29.4 %collective-permute-start.55 = (bf16[2,8,12160]{2,1,0:T(8,128)(2,1)}, bf16[2,8,12160]{2,1,0:T(8,128)(2,1)}, u32[]{:S(2)}, u32[]{:S(2)}) collective-permute-start(bf16[2,8,12160]{2,1,0:T(8,128)(2,1)} %pad_maximum_fusion.7), channel_id=1, source_target_pairs={{0,16},{8,24},{16,0},{24,8},{1,17},{9,25},{17,1},{25,9},{2,18},{10... | collective-permute-start | bytes 1167368 | tf_op jit(solution)/shard_map/ppermute | solution.py:579
  432.2 25.9 %collective-permute-start.57 = (bf16[256,1536]{1,0:T(8,128)(2,1)}, bf16[256,1536]{1,0:T(8,128)(2,1)}, u32[]{:S(2)}, u32[]{:S(2)}) collective-permute-start(bf16[256,1536]{1,0:T(8,128)(2,1)} %broadcast_select_fusion.13), channel_id=1, source_target_pairs={{0,1},{3,2},{1,0},{2,3},{4,5},{7,6},{5,4},{6,7},{8,9},{11,10},{9,8... | collective-permute-start | bytes 2359304 | tf_op jit(solution)/shard_map/ppermute | solution.py:579
  434.4 23.6 %collective-permute-start.58 = (bf16[256,1536]{1,0:T(8,128)(2,1)}, bf16[256,1536]{1,0:T(8,128)(2,1)}, u32[]{:S(2)}, u32[]{:S(2)}) collective-permute-start(bf16[256,1536]{1,0:T(8,128)(2,1)} %add_convert_fusion.11), channel_id=1, source_target_pairs={{1,2},{2,1},{5,6},{6,5},{9,10},{10,9},{13,14},{14,13},{17,18},{18,... | collective-permute-start | bytes 2359304 | tf_op jit(solution)/shard_map/ppermute | solution.py:579
  460.0 26.4 %collective-permute-start.59 = (bf16[4,8,12160]{2,1,0:T(8,128)(2,1)}, bf16[4,8,12160]{2,1,0:T(8,128)(2,1)}, u32[]{:S(2)}, u32[]{:S(2)}) collective-permute-start(bf16[4,8,12160]{2,1,0:T(8,128)(2,1)} %pad_maximum_fusion.3), channel_id=1, source_target_pairs={{0,4},{4,0},{1,5},{5,1},{2,6},{6,2},{3,7},{7,3},{8,12},{12,8},{9,1... | collective-permute-start | bytes 2334728 | tf_op jit(solution)/shard_map/ppermute | solution.py:579
  462.9 17.2 %collective-permute-start.60 = (bf16[64,1536]{1,0:T(8,128)(2,1)}, bf16[64,1536]{1,0:T(8,128)(2,1)}, u32[]{:S(2)}, u32[]{:S(2)}) collective-permute-start(bf16[64,1536]{1,0:T(8,128)(2,1)} %get-tuple-element.431), channel_id=1, source_target_pairs={{0,8},{8,0},{16,24},{24,16},{1,9},{9,1},{17,25},{25,17},{2,10},{10... | collective-permute-start | bytes 589832 | tf_op jit(solution)/shard_map/ppermute | solution.py:579
  463.1 19.9 %collective-permute-start.61 = (bf16[64,1536]{1,0:T(8,128)(2,1)}, bf16[64,1536]{1,0:T(8,128)(2,1)}, u32[]{:S(2)}, u32[]{:S(2)}) collective-permute-start(bf16[64,1536]{1,0:T(8,128)(2,1)} %get-tuple-element.430), channel_id=1, source_target_pairs={{0,16},{8,24},{16,0},{24,8},{1,17},{9,25},{17,1},{25,9},{2,18},{10... | collective-permute-start | bytes 589832 | tf_op jit(solution)/shard_map/ppermute | solution.py:579
  466.9 19.5 %collective-permute-start.63 = (bf16[256,1536]{1,0:T(8,128)(2,1)}, bf16[256,1536]{1,0:T(8,128)(2,1)}, u32[]{:S(2)}, u32[]{:S(2)}) collective-permute-start(bf16[256,1536]{1,0:T(8,128)(2,1)} %broadcast_select_fusion.11), channel_id=1, source_target_pairs={{0,1},{3,2},{1,0},{2,3},{4,5},{7,6},{5,4},{6,7},{8,9},{11,10},{9,8... | collective-permute-start | bytes 2359304 | tf_op jit(solution)/shard_map/ppermute | solution.py:579
  468.3 20.4 %collective-permute-start.64 = (bf16[256,1536]{1,0:T(8,128)(2,1)S(1)}, bf16[256,1536]{1,0:T(8,128)(2,1)S(1)}, u32[]{:S(2)}, u32[]{:S(2)}) collective-permute-start(bf16[256,1536]{1,0:T(8,128)(2,1)S(1)} %add_convert_fusion.9), channel_id=1, source_target_pairs={{1,2},{2,1},{5,6},{6,5},{9,10},{10,9},{13,14},{14,13},{17,18},{18,... | collective-permute-start | bytes 2359304 | tf_op jit(solution)/shard_map/ppermute | solution.py:579
  490.0 12.1 %collective-permute-start.65 = (bf16[64,1536]{1,0:T(8,128)(2,1)S(1)}, bf16[64,1536]{1,0:T(8,128)(2,1)S(1)}, u32[]{:S(2)}, u32[]{:S(2)}) collective-permute-start(bf16[64,1536]{1,0:T(8,128)(2,1)S(1)} %add_convert_fusion.20), channel_id=1, source_target_pairs={{0,1},{1,0},{2,3},{3,2},{4,5},{5,4},{6,7},{7,6},{8,9},{9,8},{10,11... | collective-permute-start | bytes 589832 | tf_op jit(solution)/shard_map/ppermute | solution.py:579
  490.3 11.7 %collective-permute-start.66 = (bf16[8,10880]{1,0:T(8,128)(2,1)S(1)}, bf16[8,10880]{1,0:T(8,128)(2,1)S(1)}, u32[]{:S(2)}, u32[]{:S(2)}) collective-permute-start(bf16[8,10880]{1,0:T(8,128)(2,1)S(1)} %select_convert_fusion.3), channel_id=1, source_target_pairs={{0,4},{4,0},{1,5},{5,1},{2,6},{6,2},{3,7},{7,3},{8,12},{12,8},{9,1... | collective-permute-start | bytes 522248 | tf_op jit(solution)/shard_map/ppermute | solution.py:579
  492.1 19.9 %collective-permute-start.67 = (bf16[256,1536]{1,0:T(8,128)(2,1)S(1)}, bf16[256,1536]{1,0:T(8,128)(2,1)S(1)}, u32[]{:S(2)}, u32[]{:S(2)}) collective-permute-start(bf16[256,1536]{1,0:T(8,128)(2,1)S(1)} %broadcast_select_fusion.9), channel_id=1, source_target_pairs={{0,1},{3,2},{1,0},{2,3},{4,5},{7,6},{5,4},{6,7},{8,9},{11,10},{9,8... | collective-permute-start | bytes 2359304 | tf_op jit(solution)/shard_map/ppermute | solution.py:579
  495.2 20.7 %collective-permute-start.68 = (bf16[256,1536]{1,0:T(8,128)(2,1)S(1)}, bf16[256,1536]{1,0:T(8,128)(2,1)S(1)}, u32[]{:S(2)}, u32[]{:S(2)}) collective-permute-start(bf16[256,1536]{1,0:T(8,128)(2,1)S(1)} %add_convert_fusion.7), channel_id=1, source_target_pairs={{1,2},{2,1},{5,6},{6,5},{9,10},{10,9},{13,14},{14,13},{17,18},{18,... | collective-permute-start | bytes 2359304 | tf_op jit(solution)/shard_map/ppermute | solution.py:579
  519.0 22.9 %collective-permute-start.71 = (bf16[256,1536]{1,0:T(8,128)(2,1)S(1)}, bf16[256,1536]{1,0:T(8,128)(2,1)S(1)}, u32[]{:S(2)}, u32[]{:S(2)}) collective-permute-start(bf16[256,1536]{1,0:T(8,128)(2,1)S(1)} %broadcast_select_fusion.7), channel_id=1, source_target_pairs={{0,1},{3,2},{1,0},{2,3},{4,5},{7,6},{5,4},{6,7},{8,9},{11,10},{9,8... | collective-permute-start | bytes 2359304 | tf_op jit(solution)/shard_map/ppermute | solution.py:579
  519.3 23.4 %collective-permute-start.72 = (bf16[256,1536]{1,0:T(8,128)(2,1)S(1)}, bf16[256,1536]{1,0:T(8,128)(2,1)S(1)}, u32[]{:S(2)}, u32[]{:S(2)}) collective-permute-start(bf16[256,1536]{1,0:T(8,128)(2,1)S(1)} %add_convert_fusion.5), channel_id=1, source_target_pairs={{1,2},{2,1},{5,6},{6,5},{9,10},{10,9},{13,14},{14,13},{17,18},{18,... | collective-permute-start | bytes 2359304 | tf_op jit(solution)/shard_map/ppermute | solution.py:579
  542.7 22.9 %collective-permute-start.73 = (bf16[64,1536]{1,0:T(8,128)(2,1)S(1)}, bf16[64,1536]{1,0:T(8,128)(2,1)S(1)}, u32[]{:S(2)}, u32[]{:S(2)}) collective-permute-start(bf16[64,1536]{1,0:T(8,128)(2,1)S(1)} %add_convert_fusion.18), channel_id=1, source_target_pairs={{0,8},{8,0},{16,24},{24,16},{1,9},{9,1},{17,25},{25,17},{2,10},{10... | collective-permute-start | bytes 589832 | tf_op jit(solution)/shard_map/ppermute | solution.py:579
  543.3 22.3 %collective-permute-start.75 = (bf16[256,1536]{1,0:T(8,128)(2,1)S(1)}, bf16[256,1536]{1,0:T(8,128)(2,1)S(1)}, u32[]{:S(2)}, u32[]{:S(2)}) collective-permute-start(bf16[256,1536]{1,0:T(8,128)(2,1)S(1)} %broadcast_select_fusion.5), channel_id=1, source_target_pairs={{0,1},{3,2},{1,0},{2,3},{4,5},{7,6},{5,4},{6,7},{8,9},{11,10},{9,8... | collective-permute-start | bytes 2359304 | tf_op jit(solution)/shard_map/ppermute | solution.py:579
  543.6 22.0 %collective-permute-start.76 = (bf16[256,1536]{1,0:T(8,128)(2,1)S(1)}, bf16[256,1536]{1,0:T(8,128)(2,1)S(1)}, u32[]{:S(2)}, u32[]{:S(2)}) collective-permute-start(bf16[256,1536]{1,0:T(8,128)(2,1)S(1)} %add_convert_fusion.3), channel_id=1, source_target_pairs={{1,2},{2,1},{5,6},{6,5},{9,10},{10,9},{13,14},{14,13},{17,18},{18,... | collective-permute-start | bytes 2359304 | tf_op jit(solution)/shard_map/ppermute | solution.py:579
  545.6 20.0 %collective-permute-start.74 = (bf16[8,7680]{1,0:T(8,128)(2,1)S(1)}, bf16[8,7680]{1,0:T(8,128)(2,1)S(1)}, u32[]{:S(2)}, u32[]{:S(2)}) collective-permute-start(bf16[8,7680]{1,0:T(8,128)(2,1)S(1)} %add_convert_fusion.24), channel_id=1, source_target_pairs={{0,2},{1,3},{2,0},{3,1},{4,6},{5,7},{6,4},{7,5},{8,10},{9,11},{10,... | collective-permute-start | bytes 368648 | tf_op jit(solution)/shard_map/ppermute | solution.py:579
  565.7 13.3 %collective-permute-start.77 = (bf16[128,1536]{1,0:T(8,128)(2,1)S(1)}, bf16[128,1536]{1,0:T(8,128)(2,1)S(1)}, u32[]{:S(2)}, u32[]{:S(2)}) collective-permute-start(bf16[128,1536]{1,0:T(8,128)(2,1)S(1)} %pad_maximum_fusion.5), channel_id=1, source_target_pairs={{0,16},{8,24},{16,0},{24,8},{1,17},{9,25},{17,1},{25,9},{2,18},{10... | collective-permute-start | bytes 1179656 | tf_op jit(solution)/shard_map/ppermute | solution.py:579
  567.3 18.0 %collective-permute-start.79 = (bf16[256,1536]{1,0:T(8,128)(2,1)S(1)}, bf16[256,1536]{1,0:T(8,128)(2,1)S(1)}, u32[]{:S(2)}, u32[]{:S(2)}) collective-permute-start(bf16[256,1536]{1,0:T(8,128)(2,1)S(1)} %add_convert_fusion.2), channel_id=1, source_target_pairs={{1,0},{2,3},{5,4},{6,7},{9,8},{10,11},{13,12},{14,15},{17,16},{18,... | collective-permute-start | bytes 2359304 | tf_op jit(solution)/shard_map/ppermute | solution.py:579
  572.5 17.0 %collective-permute-start.80 = (bf16[256,1536]{1,0:T(8,128)(2,1)S(1)}, bf16[256,1536]{1,0:T(8,128)(2,1)S(1)}, u32[]{:S(2)}, u32[]{:S(2)}) collective-permute-start(bf16[256,1536]{1,0:T(8,128)(2,1)S(1)} %add_convert_fusion.1), channel_id=1, source_target_pairs={{1,2},{2,1},{5,6},{6,5},{9,10},{10,9},{13,14},{14,13},{17,18},{18,... | collective-permute-start | bytes 2359304 | tf_op jit(solution)/shard_map/ppermute | solution.py:579
  589.7 16.4 %collective-permute-start.81 = (bf16[256,1536]{1,0:T(8,128)(2,1)S(1)}, bf16[256,1536]{1,0:T(8,128)(2,1)S(1)}, u32[]{:S(2)}, u32[]{:S(2)}) collective-permute-start(bf16[256,1536]{1,0:T(8,128)(2,1)S(1)} %pad_maximum_fusion.2), channel_id=1, source_target_pairs={{0,4},{4,0},{1,5},{5,1},{2,6},{6,2},{3,7},{7,3},{8,12},{12,8},{9,1... | collective-permute-start | bytes 2359304 | tf_op jit(solution)/shard_map/ppermute | solution.py:579
  594.9 18.4 %collective-permute-start.83 = (bf16[256,1536]{1,0:T(8,128)(2,1)S(1)}, bf16[256,1536]{1,0:T(8,128)(2,1)S(1)}, u32[]{:S(2)}, u32[]{:S(2)}) collective-permute-start(bf16[256,1536]{1,0:T(8,128)(2,1)S(1)} %add_convert_fusion), channel_id=1, source_target_pairs={{1,0},{2,3},{5,4},{6,7},{9,8},{10,11},{13,12},{14,15},{17,16},{18,... | collective-permute-start | bytes 2359304 | tf_op jit(solution)/shard_map/ppermute | solution.py:579
  596.3 9.8 %collective-permute-start.82 = (bf16[2,8,10880]{2,1,0:T(8,128)(2,1)S(1)}, bf16[2,8,10880]{2,1,0:T(8,128)(2,1)S(1)}, u32[]{:S(2)}, u32[]{:S(2)}) collective-permute-start(bf16[2,8,10880]{2,1,0:T(8,128)(2,1)S(1)} %pad_maximum_fusion.8), channel_id=1, source_target_pairs={{0,16},{8,24},{16,0},{24,8},{1,17},{9,25},{17,1},{25,9},{2,18},{10... | collective-permute-start | bytes 1044488 | tf_op jit(solution)/shard_map/ppermute | solution.py:579
  (101 other events, 1149.1 us)
Sparse Core Ops, SparseCore 0:
  61.9 51.3 all-gather.2

commit v2 on v1

--- a/solution.py
+++ b/solution.py
@@ -224,13 +224,21 @@
             sums[...] += jnp.where(lax.broadcasted_iota(jnp.int32, all_k.shape, 0) == 1, all_k, 0.0)
 
 
-def qkv_back_kernel(head_count, at, meta, *refs):
+def qkv_back_kernel(head_count, call, meta, *refs):
     n = head_count
     dq, dkv, dkv_in = (refs[j * n : (j + 1) * n] for j in range(3))
     refs = refs[3 * n :]
     pre_q, pre_k, st, st_back, gain_in, cos, sin, w, up_in, dn_in, tok, vec, y1, lat_t, dx1 = refs[:15]
-    packed_in = refs[15] if at else None
-    part, packed, up = refs[-3:]
+    packed_in = refs[15] if call else None
+    part, packed, up, w_s, sem = refs[-5:]
+    step = pl.program_id(0)
+    fetch = pltpu.make_async_copy(w, w_s, sem)
+
+    @pl.when(step == 0)
+    def _():
+        fetch.start()
+        packed[...] = packed_in[...] if call else jnp.zeros_like(packed)
+
     inverse, cubed = st[...].T, st_back[...].T
     c, s = cos[...], sin[...]
     width = n * HEAD_DIM
@@ -256,11 +264,16 @@
     d_lat = nt(joined, up[...]).astype(BF16)
     d_lat_t = nt(up[...], joined).astype(BF16)
     total = nn(d_lat, dn)
+
+    @pl.when(step == 0)
+    def _():
+        fetch.wait()
+
     for j in range(3):
-        total = total + nt(grads[j], w[j])
+        total = total + nt(grads[j], w_s[j])
     normed, inverse = normalize(tok[...].astype(F32))
     back = normalize_back(normed, inverse, total * vec[M1 : M1 + 1, :])
-    own = (meta[0] == at).astype(F32)
+    own = (meta[AT_T] == call * pl.num_programs(0) + step).astype(F32)
     part[...] = (back + dx1[...] * own).astype(part.dtype)
     g_dn = nn(d_lat_t, y1[...])
     for j in range(3):
@@ -268,7 +281,7 @@
         g_up = nn(lat_t[rows, :], grads[j])
         for start, g in ((j * d, g_dn[rows, :]), (3 * d + j * width, g_up)):
             lanes = slice(start, start + g.shape[1])
-            packed[:, lanes] = g + packed_in[:, lanes] if at else g
+            packed[:, lanes] += g
 
 
 def context_kernel(groups, meta, ctx, w, up, dn, bias, gain, up_q, down_row, pre, low, ssq, lat_t):
@@ -322,7 +335,7 @@
         refs[-1][j] = ref[...]
 
 
-def start_copies(meta, plan, refs, targets, sems):
+def start_copies(meta, plan, refs, targets, sems, own):
     copies = [[] for _ in targets]
     at = 0
     for source, weight, first, rows, slot, inner, size in plan:
@@ -334,11 +347,14 @@
             copies[weight].append(
                 pltpu.make_async_copy(
                     refs[source].at[:, pl.ds(first, rows), pl.ds(j * width, width)],
-                    target.at[:, pl.ds(start, rows), :],
+                    target.at[pl.ds(target.shape[0] - refs[source].shape[0], refs[source].shape[0]), pl.ds(start, rows), :],
                     sems.at[at],
                 )
             )
             at += 1
+    for weight, shard in own.items():
+        copies[weight].append(pltpu.make_async_copy(shard, targets[weight].at[0], sems.at[at]))
+        at += 1
     for weight in copies:
         for copy in weight:
             copy.start()
@@ -354,18 +370,18 @@
     n = groups * head_count
     os_first, os_rest, refs = refs[:groups], refs[groups : 2 * groups], refs[2 * groups :]
     tok, vec, up, dn3 = refs[:4]
-    ctx, refs = refs[4], refs[5:]
+    ctx_own, ctx_sib, refs = refs[4 : 4 + groups], refs[4 + groups : 4 + 2 * groups], refs[4 + 2 * groups :]
     st_own, st_sib, wo_own, wq_own, wc_own = refs[:5]
     k = 1 + max(entry[0] for entry in plan)
     sources, refs = refs[5 : 5 + k], refs[5 + k :]
     y2, x2, x1, y3, qn, qc, oc, os_all, lse, lats = refs[:10]
     wo, wq, wc, sems = refs[10:]
-    copies = start_copies(meta, plan, sources, (wo, wq, wc), sems)
+    copies = start_copies(meta, plan, sources, (wo, wq, wc), sems, {0: wo_own, 2: wc_own})
+    full = lambda weight: weight[...].reshape(weight.shape[0] * weight.shape[1], weight.shape[2])
     dn3 = dn3[0, 0]
     rank = dn3.shape[0]
-    ctx_len = ctx.shape[2] - 4 * rank
-    group = [lax.rem(meta[AT_T] + groups - r, groups) for r in range(groups)]
-    small = jnp.concatenate([ctx[0, group[r], ctx_len:, :] for r in range(groups)], axis=1)
+    ctx_len = ctx_own[0].shape[0] - 4 * rank
+    small = jnp.concatenate([ctx_own[r][ctx_len:, :] for r in range(groups)], axis=1)
     first = meta[AT_S] == 0
     key_row = context_row(groups, ctx_len, jnp.where(first, st_own[...], st_sib[...]))
     ctx_inverse = jnp.broadcast_to(key_row, (8, ctx_len)).T[:, 0:1]
@@ -380,8 +396,7 @@
     lats[0:rank, :] = nt(down0, os_v).astype(BF16)
     total = nn(lat, up[0, 0])
     finish(copies[0])
-    for r in range(groups):
-        total = total + nn(os_v[:, r * width : (r + 1) * width], wo[r - 1] if r else wo_own[...])
+    total = total + nn(os_v, full(wo))
     x1_v = tok[...].astype(F32) + (total + vec[B0 : B0 + 1, :]) * vec[M2 : M2 + 1, :]
     x1[...] = x1_v
     normed, _ = normalize(x1_v)
@@ -398,8 +413,9 @@
     qn[...] = (q * (inverse * (SCALE * LOG2E)) * gain).astype(BF16)
     for j in range(n):
         r, lanes = j // head_count, slice((j % head_count) * HEAD_DIM, (j % head_count + 1) * HEAD_DIM)
-        keys = (ctx[0, group[r], :ctx_len, lanes].astype(F32) * ctx_inverse).astype(BF16)
-        values = ctx[1, group[r], :ctx_len, lanes]
+        a, b = ctx_own[r][:ctx_len, lanes], ctx_sib[r][:ctx_len, lanes]
+        keys, values = jnp.where(first, a, b), jnp.where(first, b, a)
+        keys = (keys.astype(F32) * ctx_inverse).astype(BF16)
         scores = nt(keys, qn[:, j * HEAD_DIM : (j + 1) * HEAD_DIM])
         highest = jnp.max(scores, axis=0, keepdims=True)
         e = jnp.exp2(scores - highest)
@@ -412,8 +428,7 @@
     lats[rank : 2 * rank, :] = nt(down1, oc_v).astype(BF16)
     total = nn(lat, up[0, 1])
     finish(copies[2])
-    for r in range(groups):
-        total = total + nn(oc_v[:, r * width : (r + 1) * width], wc[r - 1] if r else wc_own[...])
+    total = total + nn(oc_v, full(wc))
     x2_v = x1_v + total + vec[B1 : B1 + 1, :]
     x2[...] = x2_v
     normed, _ = normalize(x2_v)
@@ -423,18 +438,18 @@
 def cross_back_kernel(groups, head_count, plan, meta, *refs):
     n = groups * head_count
     dy_own, dy_in, og, x2, x1, y3, qn, qc, oc, os_all, lse, lats, vec, up, dn3 = refs[:15]
-    ctx, refs = refs[15], refs[16:]
+    ctx_own, ctx_sib, refs = refs[15 : 15 + groups], refs[15 + groups : 15 + 2 * groups], refs[15 + 2 * groups :]
     st_own, st_sib, wo_own, wq_own, wc_own = refs[:5]
     k = 1 + max(entry[0] for entry in plan)
     sources, refs = refs[5 : 5 + k], refs[5 + k :]
     dos_first, dos_rest, refs = refs[:groups], refs[groups : 2 * groups], refs[2 * groups :]
     dx1, g_own, g_oth, g_up, g_split, g_dn, wo, wq, wc, dq_s, sems = refs
-    copies = start_copies(meta, plan, sources, (wo, wq, wc), sems)
+    copies = start_copies(meta, plan, sources, (wo, wq, wc), sems, {0: wo_own, 2: wc_own})
+    full = lambda weight: weight[...].reshape(weight.shape[0] * weight.shape[1], weight.shape[2])
     dn3 = dn3[0, 0]
     rank = dn3.shape[0]
-    ctx_len = ctx.shape[2] - 4 * rank
-    group = [lax.rem(meta[AT_T] + groups - r, groups) for r in range(groups)]
-    small = jnp.concatenate([ctx[0, group[r], ctx_len:, :] for r in range(groups)], axis=1)
+    ctx_len = ctx_own[0].shape[0] - 4 * rank
+    small = jnp.concatenate([ctx_own[r][ctx_len:, :] for r in range(groups)], axis=1)
     first = meta[AT_S] == 0
     key_row = context_row(groups, ctx_len, jnp.where(first, st_own[...], st_sib[...]))
     ctx_inverse = jnp.broadcast_to(key_row, (8, ctx_len)).T[:, 0:1]
@@ -452,15 +467,14 @@
     for r in range(groups):
         g_split[r, 2 * rank : 3 * rank, :] = split[:, r * width : (r + 1) * width]
     finish(copies[2])
-    d_oc = nn(d_lat, down1) + jnp.concatenate(
-        [nt(grad, wc[r - 1] if r else wc_own[...]) for r in range(groups)], axis=1
-    )
+    d_oc = nn(d_lat, down1) + nt(grad, full(wc))
     d_oc = d_oc.astype(BF16)
     for j in range(n):
         r, lanes = j // head_count, slice((j % head_count) * HEAD_DIM, (j % head_count + 1) * HEAD_DIM)
         head = slice(j * HEAD_DIM, (j + 1) * HEAD_DIM)
-        keys = (ctx[0, group[r], :ctx_len, lanes].astype(F32) * ctx_inverse).astype(BF16)
-        values = ctx[1, group[r], :ctx_len, lanes]
+        a, b = ctx_own[r][:ctx_len, lanes], ctx_sib[r][:ctx_len, lanes]
+        keys, values = jnp.where(first, a, b), jnp.where(first, b, a)
+        keys = (keys.astype(F32) * ctx_inverse).astype(BF16)
         q, g = qn[:, head], d_oc[:, head]
         delta = row_total(g.astype(F32) * oc_v[:, head].astype(F32))[0:1, :]
         p = jnp.exp2(nt(keys, q) - lse[j : j + 1, :])
@@ -499,9 +513,9 @@
     for r in range(groups):
         g_split[r, rank : 2 * rank, :] = split[:, r * width : (r + 1) * width]
     finish(copies[0])
-    low = nn(d_lat, down0)
+    d_os = nn(d_lat, down0) + nt(grad, full(wo))
     for r in range(groups):
-        block = nt(grad, wo[r - 1] if r else wo_own[...]) + low[:, r * width : (r + 1) * width]
+        block = d_os[:, r * width : (r + 1) * width]
         dos_first[r][...] = block[:, :HEAD_DIM].astype(BF16)
         dos_rest[r][...] = block[:, HEAD_DIM:].astype(BF16)
 
@@ -710,46 +724,105 @@
     return parts[0].astype(F32) + moving.astype(F32)
 
 
+def line_kernel(shape, meta, *refs):
+    inward, across, outward, both = shape
+    inner = (meta[AT_T] == 1) | (meta[AT_T] == 2)
+    count = (inward or outward) + inward + 2 * across + outward + both
+    ins, outs = list(refs[:count]), list(refs[count:])
+    add = lambda a, b: (a[...].astype(F32) + b[...].astype(F32)).astype(BF16)
+    if inward or outward:
+        first = ins.pop(0)
+    if inward:
+        outs.pop(0)[...] = add(ins.pop(0), first)
+    if across:
+        total = add(ins.pop(0), ins.pop(0))
+        outs.pop(0)[...] = jnp.where(inner, total, ins.pop(0)[...]) if both else total
+    if outward:
+        outs.pop(0)[...] = jnp.where(inner, ins.pop(0)[...], first[...])
+
+
 class Line:
-    def __init__(self):
-        self.parts, self.acc, self.total, self.out, self.at, self.moving = [], [], [], [], 0, []
-        index = lax.axis_index("tensor")
-        self.inner = (index == 1) | (index == 2)
-
-    def add(self, part):
-        self.parts.append(part)
-
-    def send(self):
-        inward = self.parts[self.at] if self.at < len(self.parts) else None
-        outward = self.total[self.at - 2] if 0 <= self.at - 2 < len(self.total) else None
-        across = self.acc[self.at - 1] if 0 <= self.at - 1 < len(self.acc) else None
-        pairs = [(0, 1), (3, 2)] * (inward is not None) + [(1, 0), (2, 3)] * (outward is not None)
-        if inward is None or outward is None:
-            mine = outward if inward is None else inward
+    def __init__(self, meta, size):
+        self.meta, self.size = meta, size
+        self.parts, self.targets, self.outs = [], [], {}
+        self.acc, self.total, self.at, self.moving = {}, {}, 0, []
+
+    def add(self, array, block, target, out_block):
+        self.parts.append((array, block))
+        self.targets.append((target, out_block))
+
+    def start(self):
+        array, block = self.parts[self.at] if self.at < len(self.parts) else (None, None)
+        inward, outward = array is not None, self.at - 2 in self.total
+        pairs = [(0, 1), (3, 2)] * inward + [(1, 0), (2, 3)] * outward
+        if inward and outward:
+            mine = self.total[self.at - 2]
+        elif inward:
+            mine = array[block * self.size : (block + 1) * self.size]
         else:
-            mine = jnp.where(self.inner, outward, inward)
+            mine = self.total.get(self.at - 2)
         self.moving = [send(mine, "tensor", pairs)] if pairs else []
-        self.shape = (inward is not None, across is not None, outward is not None)
-        if across is not None:
-            self.moving.append(send(across, "tensor", [(1, 2), (2, 1)]))
-
-    def receive(self, moving):
+        across = self.at - 1 in self.acc
+        if across:
+            self.moving.append(send(self.acc[self.at - 1], "tensor", [(1, 2), (2, 1)]))
+        self.shape = (inward, across, outward)
+
+    def advance(self, moving):
         inward, across, outward = self.shape
-        moving = list(moving)
-        add_low = lambda a, b: (a.astype(F32) + b.astype(F32)).astype(BF16)
-        if inward or outward:
-            first = moving.pop(0)
+        moving, at = list(moving), self.at
+        first = moving.pop(0) if inward or outward else None
+        second = moving.pop(0) if across else None
+        both = across and at + 1 < len(self.parts)
+        grid = 4
+        rows = lambda block: pl.BlockSpec((self.size // grid, width), lambda b, m: (block * grid + b, 0))
+        width = (second if first is None else first).shape[1]
+        kind = sds((self.size, width), BF16)
+        ins, outs, aliases = [], [], None
+        if first is not None:
+            ins.append((first, rows(0)))
         if inward:
-            self.acc.append(add_low(self.parts[self.at], first))
+            array, block = self.parts[at]
+            ins.append((array, rows(block)))
+            outs.append((kind, rows(0)))
         if across:
-            self.total.append(add_low(self.acc[self.at - 1], moving.pop(0)))
+            ins += [(self.acc[at - 1], rows(0)), (second, rows(0))]
+            outs.append((kind, rows(0)))
+        if both:
+            array, block = self.parts[at + 1]
+            ins.append((array, rows(block)))
         if outward:
-            self.out.append(jnp.where(self.inner, self.total[self.at - 2], first))
-        self.at += 1
-        self.moving = []
+            ins.append((self.total[at - 2], rows(0)))
+        count = len(ins)
+        if outward:
+            target, block = self.targets[at - 2]
+            length = self.size * sum(t == target for t, _ in self.targets)
+            outs.append((sds((length, width), BF16), rows(block)))
+            if target in self.outs:
+                ins.append((self.outs[target], pl.BlockSpec(memory_space=pl.ANY)))
+                aliases = {count + 1: len(outs) - 1}
+
+        def body(meta, *refs):
+            line_kernel((inward, across, outward, both), meta, *refs[:count], *refs[len(ins) :])
+
+        results = list(run_kernel(body, self.meta, ins, outs, grid=(grid,), us=3, aliases=aliases))
+        if inward:
+            self.acc[at] = results.pop(0)
+        if across:
+            self.total[at - 1] = results.pop(0)
+        if outward:
+            self.outs[self.targets[at - 2][0]] = results.pop(0)
+        self.at, self.moving = at + 1, []
+        if self.live():
+            self.start()
 
     def live(self):
-        return len(self.out) < len(self.parts)
+        return self.at < len(self.parts) + 2
+
+
+def total_steps(value, axis):
+    for step in powers(lax.axis_size(axis)):
+        value = value + (yield send(value, axis, flip(lax.axis_size(axis), step)))
+    return value
 
 
 def adapter_steps(value, shared):
@@ -1017,9 +1090,10 @@
     along = [send(by_group, "dp", flip(share, 1)), send(by_group, "dp", flip(share, 2))] if share > 1 else []
     st_own = lax.rsqrt((ssq + send(ssq, "tensor", flip(groups, last_step))) / d + EPS)
     st_sib = send(st_own, "seq", pair)
+    by_group_sib = send(by_group, "seq", pair)
+    st_sib, by_group_sib = seal(st_sib, by_group_sib)
     ctx_low, _ = seal(ctx_low, st_own)
-    ctx_all = lax.all_gather(ctx_low, ("seq", "tensor"))
-    ctx_all = ctx_all.reshape((seq, groups) + ctx_all.shape[1:])
+    ctx_pieces = [ctx_low, send(ctx_low, "tensor", shift(groups, 1))]
 
     all_8 = whole((8, tl))
     turned = lambda r, m: lax.rem(m[AT_T] + r, groups)
@@ -1054,8 +1128,12 @@
         mixed.append(out)
         lses.append(lse)
         if first:
-            blocks[0], *late = seal(blocks[0], *along, *os_pieces)
-            along, os_pieces = late[: len(along)], late[len(along) :]
+            blocks[0], ctx_pieces[-1], *along = seal(blocks[0], ctx_pieces[-1], *along)
+            ctx_pieces.append(send(ctx_pieces[-1], "tensor", shift(groups, 1)))
+            blocks[1], *os_pieces = seal(blocks[1], *os_pieces)
+        else:
+            blocks[0], ctx_pieces[-1] = seal(blocks[0], ctx_pieces[-1])
+            ctx_pieces.append(send(ctx_pieces[-1], "tensor", shift(groups, 1)))
         os_pieces += [send(a, "tensor", shift(groups, r)) if r else a for r, a in enumerate(blocks)]
     weight_parts = [by_group] + along
     if share > 1:
@@ -1066,25 +1144,26 @@
         ]
     near = seal(*os_pieces[-groups + 1 :], *weight_parts)
     os_pieces[-groups + 1 :], weight_parts = near[: groups - 1], near[groups - 1 :]
-    weight_parts = weight_parts + [send(p, "seq", pair) for p in weight_parts]
+    weight_parts = weight_parts + [by_group_sib] + [send(p, "seq", pair) for p in weight_parts[1:]]
+    ctx_sib = [send(p, "seq", pair) for p in ctx_pieces]
 
     vspec = whole(vec.shape)
     own_block = block((tc, d), lambda b, m: (m[AT_T], 0))
     weight_scratch = [
-        pltpu.VMEM((groups - 1, width, d), BF16),
+        pltpu.VMEM((groups, width, d), BF16),
         pltpu.VMEM((groups - 1, d, width), BF16),
-        pltpu.VMEM((groups - 1, width, d), BF16),
+        pltpu.VMEM((groups, width, d), BF16),
     ]
-    sems = pltpu.SemaphoreType.DMA((len(plan) * groups,))
+    sems = pltpu.SemaphoreType.DMA((len(plan) * groups + 2,))
     shared = [
         table(row_up),
         table(col_dn, 3),
-        (ctx_all, whole(ctx_all.shape)),
+        *[(p, whole(p.shape)) for p in ctx_pieces + ctx_sib],
         (st_own, all_8),
         (st_sib, all_8),
-        (self_out, whole(self_out.shape)),
+        (self_out, hbm),
         (cross_qkv, block((1, d, width), lambda b, m: (0, 0, 0))),
-        (cross_out, whole(cross_out.shape)),
+        (cross_out, hbm),
     ] + [(p, hbm) for p in weight_parts]
     whole_of = lambda shape, dtype: (sds(shape, dtype), whole(shape))
     y2, x2, x1, y3, qn, qc, oc, os_all, lse_c, lats = run_kernel(
@@ -1135,11 +1214,11 @@
 
     dy_own, dy_in = ring_total(dys, "tensor")
     feed_out, dy_in = seal(feed_out, dy_in)
-    line = Line() if groups == 4 else None
+    line = Line(meta, tc) if groups == 4 else None
     if line:
         for r in range(groups):
-            line.add(feed_out[r * tc : (r + 1) * tc])
-        line.send()
+            line.add(feed_out, r, "output", r)
+        line.start()
     else:
         result = lax.psum(feed_out, "tensor")
     *dos, dx1, g_own, g_oth, g_rup, g_split, g_cqdn = run_kernel(
@@ -1166,9 +1245,7 @@
     back_shift = lambda arrays: [send(a, "tensor", shift(groups, -r)) if r else a for r, a in enumerate(arrays)]
     moving = lambda: line.moving if line else []
     chains = Chains()
-    dos[0], g_oth, g_cqdn, *tied = seal(dos[0], g_oth, g_cqdn, *moving())
-    if line:
-        line.receive(tied)
+    dos[0], g_oth, g_cqdn, *arrived_line = seal(dos[0], g_oth, g_cqdn, *moving())
     dos_first = back_shift(dos[:groups])
     packed = jnp.concatenate([g_cqdn, g_dn1, g_rup[:rank], g_rup[rank:], g_up2, g_up1, g_dn2], axis=1)
     early_at = chains.add(adapter_steps(packed, 5 * d))
@@ -1187,16 +1264,16 @@
         lane = 0 if h == 0 else h - 1
         kv_at = lambda lane: block((tl, HEAD_DIM), lambda r, m: (0, lane))
         if h:
-            tied = seal(*dos_rest, *chains.arrived(), *back[-1][:1])
-            dos_rest = tied[: len(dos_rest)]
-            chains.put(tied[len(dos_rest) : -1])
-            dkv_in.append(send(back[-1][2], "seq", pair))
             if h == 1:
-                chains.step([early_at])
+                tied = seal(*dos_rest, *chains.arrived(), back[-1][0], back[-1][2])
+                dos_rest = tied[: len(dos_rest)]
+                chains.put(tied[len(dos_rest) : -2])
+                chains.step()
                 if line:
-                    line.send()
+                    line.advance(arrived_line)
             else:
-                chains.step()
+                tied = seal(back[-1][0], back[-1][2])
+            dkv_in.append(send(tied[-1], "seq", pair))
             grads = dos_rest
         back.append(
             run_kernel(
@@ -1233,32 +1310,93 @@
                     pltpu.VMEM((tc, HEAD_DIM), BF16),
                 ],
                 us=12.5,
-                after=list(tied[-1:]) if h else [],
+                after=list(tied[-2:-1]) if h else [],
             )
         )
     dq, dkv, dkv_out = zip(*[b[:3] for b in back])
     stat, cross = back[-1][3:]
-    stat, cross, *tied = seal(stat, cross, *chains.arrived(), *moving())
+    last_dkv = dkv_out[-1]
+    stat, cross, last_dkv, *tied = seal(stat, cross, last_dkv, *chains.arrived(), *moving())
     count = len(chains.arrived())
     chains.put(tied[:count])
+    arrived_line = tied[count:]
+    dkv_in.append(send(last_dkv, "seq", pair))
+    stat = stat + send(cross, "seq", pair)
+    chains.step([group_at])
+    for step in powers(groups):
+        (other,) = seal(send(stat, "tensor", flip(groups, step)))
+        stat = stat + other
+    st_back = st_own * st_own * st_own * stat / d
+    st_back, *tied = seal(st_back, *chains.arrived())
+    chains.put(tied)
+    chains.step()
     if line:
-        line.receive(tied[count:])
-    cross = send(cross, "seq", pair)
-    dkv_in.append(send(dkv_out[-1], "seq", pair))
-    chains.step([early_at])
-    to_group = chains.result(group_at)
-    g_ctx, split = to_group[:ctx_len], to_group[ctx_len:]
-    ctx_gain = jnp.where(is_key, cross_gain[1:2].astype(F32), 1.0)
-    ctx_stat = jnp.sum(g_ctx * ctx_gain * ctx_pre, axis=1)
-    stat = stat + cross
-    for step in powers(groups):
-        other, ctx_other, *tied = seal(*send((stat, ctx_stat), "tensor", flip(groups, step)), *chains.arrived())
-        chains.put(tied)
-        stat, ctx_stat = stat + other, ctx_stat + ctx_other
-    if line:
-        line.send()
-    chains.step()
-    st_back = st_own * st_own * st_own * stat / d
+        line.advance(arrived_line)
+
+    q_parts, late = [], None
+    calls = 2
+    for call in range(calls):
+        steps = groups // calls
+        in_d = block((tc, d), lambda b, m, c=call * steps: (c + b, 0))
+        in_w = block((tc, width), lambda b, m, c=call * steps: (c + b, 0))
+        in_h = block((tc, HEAD_DIM), lambda b, m, c=call * steps: (c + b, 0))
+        in_2h = block((tc, 2 * HEAD_DIM), lambda b, m, c=call * steps: (c + b, 0))
+        in_8 = block((8, tc), lambda b, m, c=call * steps: (0, c + b))
+        size = (rank, 3 * (d + width))
+        part, late = run_kernel(
+            functools.partial(qkv_back_kernel, hc, call),
+            meta,
+            [(a, in_h) for a in dq]
+            + [(a, in_2h) for a in list(dkv) + dkv_in]
+            + [
+                (pre_q, in_w),
+                (pre_k, in_w),
+                (st_own, in_8),
+                (st_back, in_8),
+                (self_gain, whole(self_gain.shape)),
+                (cos, in_h),
+                (sin, in_h),
+                (self_qkv, hbm),
+            ]
+            + self_tables
+            + [
+                (tok, in_d),
+                (vec, vspec),
+                (y1, in_d),
+                (lat_t, block((3 * rank, tc), lambda b, m, c=call * steps: (0, c + b))),
+                (dx1, whole((tc, d))),
+            ]
+            + ([(late, whole(size))] if call else []),
+            [(sds((steps * tc, d), BF16), block((tc, d), lambda b, m: (b, 0))), whole_of(size, F32)],
+            grid=(steps,),
+            scratch=[
+                pltpu.VMEM((3 * rank, 3 * width), BF16),
+                pltpu.VMEM(self_qkv.shape, BF16),
+                pltpu.SemaphoreType.DMA(()),
+            ],
+            us=14,
+        )
+        q_parts.append(part)
+        if line:
+            for r in range(steps):
+                line.add(part, r, "input_grad", call * steps + r)
+        late, *tied = seal(late, *chains.arrived(), *moving())
+        count = len(chains.arrived())
+        chains.put(tied[:count])
+        chains.step()
+        if call == 0:
+            to_group = chains.result(group_at)
+            g_ctx, split = to_group[:ctx_len], to_group[ctx_len:]
+            ctx_gain = jnp.where(is_key, cross_gain[1:2].astype(F32), 1.0)
+            ctx_stat = jnp.sum(g_ctx * ctx_gain * ctx_pre, axis=1)
+            stat_at = chains.add(total_steps(ctx_stat, "tensor"))
+            chains.advance(stat_at)
+        if line:
+            line.advance(tied[count:])
+    while not chains.done(stat_at):
+        chains.put(seal(*chains.arrived()))
+        chains.step()
+    ctx_stat = chains.result(stat_at)
 
     ctx_inverse = jnp.concatenate([st_own[2, j * tc : j * tc + ctx_len // groups] for j in range(groups)])
     ctx_cubed = ctx_inverse * ctx_inverse * ctx_inverse * ctx_stat / d
@@ -1277,57 +1415,9 @@
         ],
         [whole_of((ctx_len, d), F32), whole_of((rank, width), F32), whole_of((rank, d), F32)],
         us=6,
+        after=[line.acc[max(line.acc)]] if line else [],
     )
 
-    q_parts, late = [], None
-    for r in range(groups):
-        in_d = block((tc, d), lambda b, m, r=r: (r, 0))
-        in_w = block((tc, width), lambda b, m, r=r: (r, 0))
-        in_h = block((tc, HEAD_DIM), lambda b, m, r=r: (r, 0))
-        in_2h = block((tc, 2 * HEAD_DIM), lambda b, m, r=r: (r, 0))
-        in_8 = block((8, tc), lambda b, m, r=r: (0, r))
-        size = (rank, 3 * (d + width))
-        part, late = run_kernel(
-            functools.partial(qkv_back_kernel, hc, r),
-            meta,
-            [(a, in_h) for a in dq]
-            + [(a, in_2h) for a in list(dkv) + dkv_in]
-            + [
-                (pre_q, in_w),
-                (pre_k, in_w),
-                (st_own, in_8),
-                (st_back, in_8),
-                (self_gain, whole(self_gain.shape)),
-                (cos, in_h),
-                (sin, in_h),
-                (self_qkv, whole(self_qkv.shape)),
-            ]
-            + self_tables
-            + [
-                (tok, in_d),
-                (vec, vspec),
-                (y1, in_d),
-                (lat_t, block((3 * rank, tc), lambda b, m, r=r: (0, r))),
-                (dx1, whole((tc, d))),
-            ]
-            + ([(late, whole(size))] if r else []),
-            [whole_of((tc, d), BF16), whole_of(size, F32)],
-            scratch=[pltpu.VMEM((3 * rank, 3 * width), BF16)],
-            us=8.5,
-        )
-        q_parts.append(part)
-        if line:
-            line.add(part)
-        if r != 1:
-            late, *tied = seal(late, *chains.arrived(), *moving())
-            count = len(chains.arrived())
-            chains.put(tied[:count])
-            if r == 0:
-                ctx_at = chains.add(context_grad_steps(ctx_part))
-            chains.step()
-            if line:
-                line.receive(tied[count:])
-                line.send()
     pick = lambda g: [jnp.where(is_key, g, 0.0), jnp.where(is_key, 0.0, g)]
     late = jnp.concatenate(
         [late[:, : 3 * d]]
@@ -1338,20 +1428,24 @@
         + [jnp.broadcast_to(adapter_index[0].astype(F32) / seq, (rank, HEAD_DIM))],
         axis=1,
     )
+    ctx_at = chains.add(context_grad_steps(ctx_part))
     late_at = chains.add(adapter_steps(late, 5 * d))
-    chains.start(late_at)
-    while chains.live() or (line and line.live()):
-        tied = seal(*chains.arrived(), *(line.moving if line else []))
+    chains.advance(ctx_at)
+    chains.advance(late_at)
+    while line and line.at < len(line.parts):
+        tied = seal(*chains.arrived(), *moving())
         count = len(chains.arrived())
         chains.put(tied[:count])
         chains.step()
-        if line and line.moving:
-            line.receive(tied[count:])
-            if line.live():
-                line.send()
+        line.advance(tied[count:])
+    while line and line.live():
+        line.advance(line.moving)
+    while chains.live():
+        chains.put(seal(*chains.arrived()))
+        chains.step()
     early, late, context_grad = chains.result(early_at), chains.result(late_at), chains.result(ctx_at).astype(F32)
     if line:
-        result, input_grad = jnp.concatenate(line.out[:groups]), jnp.concatenate(line.out[groups:])
+        result, input_grad = line.outs["output"], line.outs["input_grad"]
     else:
         input_grad = lax.psum(jnp.concatenate(q_parts), "tensor")
 

time: 651 us -> 624 us (0.959)
  waiting for transfers between devices: 173 us -> 128 us
  Pallas kernels: 253 us -> 290 us
  other arithmetic: 57.2 us -> 28.2 us
  starting transfers between devices: 112 us -> 136 us
  between operations: 16.7 us -> 3.32 us
    ppermute x85 -> x92, waiting for transfers between devices: 173 us -> 128 us  [send(): return jax.tree.map(lambda v: lax.ppermute(v, axis, pairs), values)]
    pallas_call x20 -> x28, Pallas kernels: 253 us -> 290 us  [run_kernel(): pl.pallas_call(reading, grid_spec=pltpu.PrefetchScalarGridSpec(num_scalar...]
    ppermute x85 -> x92, starting transfers between devices: 112 us -> 136 us  [send(): return jax.tree.map(lambda v: lax.ppermute(v, axis, pairs), values)]
    select_n x13 -> x0, other arithmetic: 13.4 us -> none  [the longest x6 6.88 us: send(): mine = jnp.where(self.inner, outward, inward)]
    convert_element_type x10 -> x0, other arithmetic: 7.52 us -> none  [receive(): add_low = lambda a, b: (a.astype(F32) + b.astype(F32)).astype(BF16)]
    unnamed x174 -> x168, local copies, waits for them, and re-layouts: 13.1 us -> 16 us
  transfers between devices with their start and end apart: 86 -> 92, of which waited for: 32 -> 30; matrix products, arithmetic and copies ran while one was open for 9% -> 6% of each run, Pallas kernels for 36% -> 43%
where the time goes in v2:
time: 624 us; the launch traced here: 613 us
  Pallas kernels  290 us (46%)
  starting transfers between devices  136 us (22%)
  waiting for transfers between devices  128 us (21%)
  other arithmetic  28.2 us (5%)
  local copies, waits for them, and re-layouts  28.1 us (5%)
    pallas_call x28, Pallas kernels, run_kernel(): pl.pallas_call(reading, grid_spec=pltpu.PrefetchScalarGridSpec(num_scalar...  290 us
    ppermute x92, starting transfers between devices, send(): return jax.tree.map(lambda v: lax.ppermute(v, axis, pairs), values)  136 us
    ppermute x92, waiting for transfers between devices, send(): return jax.tree.map(lambda v: lax.ppermute(v, axis, pairs), values)  128 us
    unnamed x168, local copies, waits for them, and re-layouts  16 us
  transfers between devices with their start and end apart: 92, of which 30 were waited for; matrix products, arithmetic and copies ran while one was open for 6% of the time, Pallas kernels for 43%

profile of v2, /device:TPU:9, one launch (start us, length us, event | category | flops | bytes accessed | tf_op | source)
XLA Modules:
  0.0 613.5 jit_solution(3248621405190549219)
XLA Ops:
  1.9 2.6 shard_map.392.refs_8_
  10.2 5.6 shard_map.393
  15.8 3.3 sine_multiply_fusion
  19.1 15.7 %shard_map.394 = (bf16[1024,1536]{1,0:T(8,128)(2,1)}, bf16[48,1024]{1,0:T(8,128)(2,1)}, bf16[1024,384]{1,0:T(8,128)(2,1)}, bf16[1024,384]{1,0:T(8,128)(2,1)}, bf...) custom-call(s32[12]{0:T(128)} %stack.104.meta_ref, ...), custom_call_target="tpu_custom_call" | custom-call | flops 17250000896 | bytes 18121472 | tf_op jit(solution)/shard_map/pallas_call | solution.py:85
  38.9 4.6 collective-permute-done.2.refs_1_
  43.4 2.7 collective-permute-done.3.refs_2_
  46.9 3.2 shard_map.395.refs_8_.refs_25_.refs_28_
  50.6 3.3 collective-permute-start.4
  60.7 16.8 %shard_map.396 = (bf16[256,256]{1,0:T(8,128)(2,1)}, bf16[256,256]{1,0:T(8,128)(2,1)}, bf16[256,256]{1,0:T(8,128)(2,1)}, bf16[256,256]{1,0:T(8,128)(2,1)}, bf16[1024,256]{1,0:T(8,128)(2,1)}, /*index=5*/f32[16,1024]{1,0:T(8,128)}) custom-call(s32[12]{0:T(128)} %stack.104.meta_ref, bf16[1024,384]{1,0:T(8,128)(2,1)} %get-tuple-element.226.refs_0_, ...), custom_call_target="tpu_custom_call" | custom-call | flops 21849999360 | bytes 8290304 | tf_op jit(solution)/shard_map/pallas_call | solution.py:85
  79.7 9.8 %shard_map.397 = (bf16[256,128]{1,0:T(8,128)(2,1)}, bf16[256,128]{1,0:T(8,128)(2,1)}, bf16[256,128]{1,0:T(8,128)(2,1)}, bf16[256,128]{1,0:T(8,128)(2,1)}, bf16[1024,128]{1,0:T(8,128)(2,1)}, /*index=5*/f32[8,1024]{1,0:T(8,128)}) custom-call(s32[12]{0:T(128)} %stack.104.meta_ref, bf16[1024,384]{1,0:T(8,128)(2,1)} %get-tuple-element.226.refs_0_, ...), custom_call_target="tpu_custom_call" | custom-call | flops 10924999680 | bytes 7733248 | tf_op jit(solution)/shard_map/pallas_call | solution.py:85
  91.9 2.6 collective-permute-start.10
  96.6 6.8 %collective-permute-done.10.refs_2_ = bf16[256,256]{1,0:T(8,128)(2,1)S(1)} collective-permute-done((bf16[256,256]{1,0:T(8,128)(2,1)S(1)}, bf16[256,256]{1,0:T(8,128)(2,1)S(1)}, u32[]{:S(2)}, u32[]{:S(2)}) %collective-permute-start.10) | collective-permute-done | bytes 131104 | tf_op jit(solution)/shard_map/ppermute | solution.py:593
  103.4 2.5 collective-permute-done.11.refs_3_
  106.5 3.3 collective-permute-start.21
  110.8 3.1 collective-permute-start.25
  114.8 4.0 collective-permute-done.22.refs_17_.refs_20_
  119.1 9.0 %collective-permute-done.20.refs_15_.refs_18_ = bf16[576,384]{1,0:T(8,128)(2,1)S(1)} collective-permute-done((bf16[576,384]{1,0:T(8,128)(2,1)}, bf16[576,384]{1,0:T(8,128)(2,1)S(1)}, u32[]{:S(2)}, u32[]{:S(2)}) %collective-permute-start.20) | collective-permute-done | bytes 442400 | tf_op jit(solution)/shard_map/ppermute | solution.py:593
  133.4 20.7 %shard_map.398 = (bf16[256,1536]{1,0:T(8,128)(2,1)}, f32[256,1536]{1,0:T(8,128)}, f32[256,1536]{1,0:T(8,128)}, bf16[256,1536]{1,0:T(8,128)(2,1)}, bf16[256,1536]...) custom-call(s32[12]{0:T(128)} %stack.104.meta_ref, ...), custom_call_target="tpu_custom_call" | custom-call | flops 23000000512 | bytes 35987456 | tf_op jit(solution)/shard_map/pallas_call | solution.py:85
  154.4 18.6 %shard_map.399 = (bf16[1024,1536]{1,0:T(8,128)(2,1)}, f32[256,1536]{1,0:T(8,128)}, f32[16,2240]{1,0:T(8,128)}, f32[16,1536]{1,0:T(8,128)}, f32[16,1536]{1,0:T(8,128)}, /*index=5*/f32[16,2240]{1,0:T(8,128)}) custom-call(s32[12]{0:T(128)} %stack.104.meta_ref, bf16[256,1536]{1,0:T(8,128)(2,1)} %get-tuple-element.262.refs_0_, bf16[1024,1536]{1,0:T(8,128)(2,1)} %bitcast.176, ...), custom_call_target="tpu_custom_call" | custom-call | flops 20700000256 | bytes 26510080 | tf_op jit(solution)/shard_map/pallas_call | solution.py:85
  173.0 2.5 collective-permute-done.29.refs_0_
  176.4 17.9 %shard_map.400 = (bf16[1024,1536]{1,0:T(8,128)(2,1)}, bf16[256,1536]{1,0:T(8,128)(2,1)}, f32[16,2240]{1,0:T(8,128)}, f32[16,1536]{1,0:T(8,128)}, f32[16,1536]{1,0:T(8,128)}, /*index=5*/f32[16,2240]{1,0:T(8,128)}) custom-call(s32[12]{0:T(128)} %stack.104.meta_ref, bf16[256,1536]{1,0:T(8,128)(2,1)} %copy-done.44, ...), custom_call_target="tpu_custom_call", output_to_operand_aliasing={{0}: (15, {})} | custom-call | flops 20700000256 | bytes 27779840 | tf_op jit(solution)/shard_map/pallas_call | solution.py:85
  194.3 2.8 collective-permute-start.32
  199.3 17.9 %shard_map.401 = (bf16[1024,1536]{1,0:T(8,128)(2,1)}, bf16[256,1536]{1,0:T(8,128)(2,1)}, f32[16,2240]{1,0:T(8,128)}, f32[16,1536]{1,0:T(8,128)}, f32[16,1536]{1,0:T(8,128)}, /*index=5*/f32[16,2240]{1,0:T(8,128)}) custom-call(s32[12]{0:T(128)} %stack.104.meta_ref, bf16[256,1536]{1,0:T(8,128)(2,1)} %copy-done.40, ...), custom_call_target="tpu_custom_call", output_to_operand_aliasing={{0}: (15, {})} | custom-call | flops 20700000256 | bytes 27779840 | tf_op jit(solution)/shard_map/pallas_call | solution.py:85
  219.6 11.4 %collective-permute-done.31.refs_0_ = bf16[256,1536]{1,0:T(8,128)(2,1)S(1)} collective-permute-done((bf16[256,1536]{1,0:T(8,128)(2,1)S(1)}, bf16[256,1536]{1,0:T(8,128)(2,1)S(1)}, u32[]{:S(2)}, u32[]{:S(2)}) %collective-permute-start.31) | collective-permute-done | bytes 786464 | tf_op jit(solution)/shard_map/ppermute | solution.py:593
  231.9 18.1 %shard_map.402 = (bf16[1024,1536]{1,0:T(8,128)(2,1)}, bf16[256,1536]{1,0:T(8,128)(2,1)}, f32[16,2240]{1,0:T(8,128)}, f32[16,1536]{1,0:T(8,128)}, f32[16,1536]{1,0:T(8,128)}, /*index=5*/f32[16,2240]{1,0:T(8,128)}) custom-call(s32[12]{0:T(128)} %stack.104.meta_ref, bf16[256,1536]{1,0:T(8,128)(2,1)} %copy-done.43, ...), custom_call_target="tpu_custom_call", output_to_operand_aliasing={{0}: (15, {})} | custom-call | flops 20700000256 | bytes 27779840 | tf_op jit(solution)/shard_map/pallas_call | solution.py:85
  253.4 15.0 %collective-permute-done.34.refs_1_ = bf16[256,1536]{1,0:T(8,128)(2,1)S(1)} collective-permute-done((bf16[256,1536]{1,0:T(8,128)(2,1)S(1)}, bf16[256,1536]{1,0:T(8,128)(2,1)S(1)}, u32[]{:S(2)}, u32[]{:S(2)}) %collective-permute-start.34) | collective-permute-done | bytes 786464 | tf_op jit(solution)/shard_map/ppermute | solution.py:593
  268.4 2.6 fusion.52
  272.8 26.6 %shard_map.403 = (bf16[256,128]{1,0:T(8,128)(2,1)}, bf16[256,128]{1,0:T(8,128)(2,1)}, bf16[256,128]{1,0:T(8,128)(2,1)}, bf16[256,128]{1,0:T(8,128)(2,1)}, bf16[2...) custom-call(s32[12]{0:T(128)} %stack.104.meta_ref, ...), custom_call_target="tpu_custom_call" | custom-call | flops 29899999232 | bytes 42868736 | tf_op jit(solution)/shard_map/pallas_call | solution.py:85
  299.3 3.1 collective-permute-start.37
  306.1 5.7 collective-permute-start.43
  311.8 4.2 shard_map.407.refs_2_
  316.4 2.7 collective-permute-start.41
  322.4 12.6 %shard_map.404 = (f32[1024,128]{1,0:T(8,128)}, f32[1024,256]{1,0:T(8,128)}, bf16[1024,256]{1,0:T(8,128)(2,1)}, f32[8,1024]{1,0:T(8,128)}, f32[8,1024]{1,0:T(8,128)}) custom-call(s32[12]{0:T(128)} %stack.104.meta_ref, bf16[1024,384]{1,0:T(8,128)(2,1)} %get-tuple-element.226.refs_0_, f32[8,1024]{1,0:T(8,128)} %copy-done.15, f32[8,1024]{1,0:T(8,128)} %copy-done.15, ...), custom_call_target="tpu_custom_call" | custom-call | flops 14375000064 | bytes 10190848 | tf_op jit(solution)/shard_map/pallas_call | solution.py:85
  336.4 3.0 collective-permute-start.51
  339.4 12.5 %shard_map.405 = (f32[1024,128]{1,0:T(8,128)}, f32[1024,256]{1,0:T(8,128)}, bf16[1024,256]{1,0:T(8,128)(2,1)}, f32[8,1024]{1,0:T(8,128)}, f32[8,1024]{1,0:T(8,128)}) custom-call(s32[12]{0:T(128)} %stack.104.meta_ref, bf16[1024,384]{1,0:T(8,128)(2,1)} %get-tuple-element.226.refs_0_, f32[8,1024]{1,0:T(8,128)} %copy-done.15, f32[8,1024]{1,0:T(8,128)} %copy-done.15, ...), custom_call_target="tpu_custom_call" | custom-call | flops 14375000064 | bytes 10518528 | tf_op jit(solution)/shard_map/pallas_call | solution.py:85
  356.9 12.6 %shard_map.406 = (f32[1024,128]{1,0:T(8,128)}, f32[1024,256]{1,0:T(8,128)}, bf16[1024,256]{1,0:T(8,128)(2,1)}, f32[8,1024]{1,0:T(8,128)}, f32[8,1024]{1,0:T(8,128)}) custom-call(s32[12]{0:T(128)} %stack.104.meta_ref, bf16[1024,384]{1,0:T(8,128)(2,1)} %get-tuple-element.226.refs_0_, f32[8,1024]{1,0:T(8,128)} %copy-done.15, f32[8,1024]{1,0:T(8,128)} %copy-done.15, ...), custom_call_target="tpu_custom_call" | custom-call | flops 14375000064 | bytes 10223616 | tf_op jit(solution)/shard_map/pallas_call | solution.py:85
  379.3 4.8 shard_map.409
  390.6 12.3 %shard_map.408 = (bf16[512,1536]{1,0:T(8,128)(2,1)}, f32[16,5760]{1,0:T(8,128)}) custom-call(s32[12]{0:T(128)} %stack.104.meta_ref, f32[1024,128]{1,0:T(8,128)} %get-tuple-element.328.refs_16_.refs_0_, f32[1024,128]{1,0:T(8,128)} %get-tuple-element.335.refs_16_.refs_1_, f32[1024,128]{1,0:T(8,128)} %get-tuple-element.336.refs_2_, ...), custom_call_target="tpu_custom_call" | custom-call | flops 16099999744 | bytes 25470464 | tf_op jit(solution)/shard_map/pallas_call | solution.py:85
  403.0 10.2 %collective-permute-done.58 = bf16[560,384]{1,0:T(8,128)(2,1)S(1)} collective-permute-done((bf16[560,384]{1,0:T(8,128)(2,1)S(1)}, bf16[560,384]{1,0:T(8,128)(2,1)S(1)}, u32[]{:S(2)}, u32[]{:S(2)}) %collective-permute-start.58) | collective-permute-done | bytes 430112 | tf_op jit(solution)/shard_map/ppermute | solution.py:593
  415.7 2.8 collective-permute-start.61
  418.8 5.1 shard_map.411
  425.3 3.0 collective-permute-start.64
  428.3 12.5 %shard_map.410 = (bf16[512,1536]{1,0:T(8,128)(2,1)}, f32[16,5760]{1,0:T(8,128)}) custom-call(s32[12]{0:T(128)} %stack.104.meta_ref, f32[1024,128]{1,0:T(8,128)} %get-tuple-element.328.refs_16_.refs_0_, f32[1024,128]{1,0:T(8,128)} %get-tuple-element.335.refs_16_.refs_1_, f32[1024,128]{1,0:T(8,128)} %get-tuple-element.336.refs_2_, ...), custom_call_target="tpu_custom_call" | custom-call | flops 16099999744 | bytes 25839104 | tf_op jit(solution)/shard_map/pallas_call | solution.py:85
  443.2 2.7 collective-permute-done.64.refs_3_
  447.1 5.1 shard_map.412
  454.3 2.5 collective-permute-start.69
  457.9 5.8 shard_map.413
  474.3 5.3 shard_map.414
  489.9 3.2 collective-permute-done.71
  493.0 3.0 collective-permute-done.74.refs_0_
  496.0 2.8 collective-permute-done.75.refs_3_
  499.9 5.1 shard_map.415
  508.8 16.8 %collective-permute-done.77 = bf16[8,7680]{1,0:T(8,128)(2,1)S(1)} collective-permute-done((bf16[8,7680]{1,0:T(8,128)(2,1)S(1)}, bf16[8,7680]{1,0:T(8,128)(2,1)S(1)}, u32[]{:S(2)}, u32[]{:S(2)}) %collective-permute-start.77) | collective-permute-done | bytes 122912 | tf_op jit(solution)/shard_map/ppermute | solution.py:593
  528.7 5.0 shard_map.416
  534.3 2.6 collective-permute-start.83
  537.2 9.7 %collective-permute-done.82.refs_0_ = bf16[256,1536]{1,0:T(8,128)(2,1)S(1)} collective-permute-done((bf16[256,1536]{1,0:T(8,128)(2,1)}, bf16[256,1536]{1,0:T(8,128)(2,1)S(1)}, u32[]{:S(2)}, u32[]{:S(2)}) %collective-permute-start.82) | collective-permute-done | bytes 786464 | tf_op jit(solution)/shard_map/ppermute | solution.py:593
  546.9 4.9 collective-permute-done.83.refs_3_
  552.9 4.9 shard_map.417
  560.0 2.6 collective-permute-start.85
  564.7 10.1 %collective-permute-start.90 = (bf16[4,8,10880]{2,1,0:T(8,128)(2,1)}, bf16[4,8,10880]{2,1,0:T(8,128)(2,1)}, u32[]{:S(2)}, u32[]{:S(2)}) collective-permute-start(bf16[4,8,10880]{2,1,0:T(8,128)(2,1)} %pad_maximum_fusion.4), channel_id=1, source_target_pairs={{0,4},{4,0},{1,5},{5,1},{2,6},{6,2},{3,7},{7,3},{8,12},{12,8},{9,1... | collective-permute-start | bytes 2088968 | tf_op jit(solution)/shard_map/ppermute | solution.py:593
  575.0 4.7 shard_map.418
  586.6 8.6 %collective-permute-start.91 = (bf16[256,1536]{1,0:T(8,128)(2,1)S(1)}, bf16[256,1536]{1,0:T(8,128)(2,1)S(1)}, u32[]{:S(2)}, u32[]{:S(2)}) collective-permute-start(bf16[256,1536]{1,0:T(8,128)(2,1)S(1)} %pad_maximum_fusion.2), channel_id=1, source_target_pairs={{0,4},{4,0},{1,5},{5,1},{2,6},{6,2},{3,7},{7,3},{8,12},{12,8},{9,1... | collective-permute-start | bytes 2359304 | tf_op jit(solution)/shard_map/ppermute | solution.py:593
  598.6 2.6 copy.57
  606.5 4.2 shard_map.419
  (398 shorter events, 138.0 us)
Async XLA Ops:
  4.5 34.3 %collective-permute-start.1 = (bf16[144,1536]{1,0:T(8,128)(2,1)}, bf16[144,1536]{1,0:T(8,128)(2,1)S(1)}, u32[]{:S(2)}, u32[]{:S(2)}) collective-permute-start(bf16[144,1536]{1,0:T(8,128)(2,1)} %shard_map.392.refs_8_), channel_id=1, source_target_pairs={{0,1},{1,2},{2,3},{3,0},{4,5},{5,6},{6,7},{7,4},{8,9},{9,10},{10,1... | collective-permute-start | bytes 1327112 | tf_op jit(solution)/shard_map/ppermute | solution.py:593
  5.8 37.6 %collective-permute-start.2 = (bf16[144,1536]{1,0:T(8,128)(2,1)}, bf16[144,1536]{1,0:T(8,128)(2,1)S(1)}, u32[]{:S(2)}, u32[]{:S(2)}) collective-permute-start(bf16[144,1536]{1,0:T(8,128)(2,1)} %shard_map.392.refs_8_), channel_id=1, source_target_pairs={{0,2},{1,3},{2,0},{3,1},{4,6},{5,7},{6,4},{7,5},{8,10},{9,11},{10,... | collective-permute-start | bytes 1327112 | tf_op jit(solution)/shard_map/ppermute | solution.py:593
  6.9 39.3 %collective-permute-start.3 = (bf16[144,1536]{1,0:T(8,128)(2,1)}, bf16[144,1536]{1,0:T(8,128)(2,1)S(1)}, u32[]{:S(2)}, u32[]{:S(2)}) collective-permute-start(bf16[144,1536]{1,0:T(8,128)(2,1)} %shard_map.392.refs_8_), channel_id=1, source_target_pairs={{0,3},{1,0},{2,1},{3,2},{4,7},{5,4},{6,5},{7,6},{8,11},{9,8},{10,9... | collective-permute-start | bytes 1327112 | tf_op jit(solution)/shard_map/ppermute | solution.py:593
  35.9 23.6 %collective-permute-start.7 = (bf16[1024,768]{1,0:T(8,128)(2,1)}, bf16[1024,768]{1,0:T(8,128)(2,1)S(1)}, u32[]{:S(2)}, u32[]{:S(2)}) collective-permute-start(bf16[1024,768]{1,0:T(8,128)(2,1)} %get-tuple-element.229.refs_4_.refs_6_), channel_id=1, source_target_pairs={{0,4},{4,0},{1,5},{5,1},{2,6},{6,2},{3,7},{7,3},{8,12},{12,8},{9,1... | collective-permute-start | bytes 4718600 | tf_op jit(solution)/shard_map/ppermute | solution.py:593
  56.4 33.1 %collective-permute-start.13 = (bf16[3,144,1536]{2,1,0:T(8,128)(2,1)}, bf16[3,144,1536]{2,1,0:T(8,128)(2,1)S(1)}, u32[]{:S(2)}, u32[]{:S(2)}) collective-permute-start(bf16[3,144,1536]{2,1,0:T(8,128)(2,1)} %shard_map.395.refs_8_.refs_25_.refs_28_), channel_id=1, source_target_pairs={{0,8},{8,0},{16,24},{24,16},{1,9},{9,1},{17,25},{25,17},{2,10},{10... | collective-permute-start | bytes 3981320 | tf_op jit(solution)/shard_map/ppermute | solution.py:593
  57.6 31.9 %collective-permute-start.14 = (bf16[3,144,1536]{2,1,0:T(8,128)(2,1)}, bf16[3,144,1536]{2,1,0:T(8,128)(2,1)S(1)}, u32[]{:S(2)}, u32[]{:S(2)}) collective-permute-start(bf16[3,144,1536]{2,1,0:T(8,128)(2,1)} %shard_map.395.refs_8_.refs_25_.refs_28_), channel_id=1, source_target_pairs={{0,16},{8,24},{16,0},{24,8},{1,17},{9,25},{17,1},{25,9},{2,18},{10... | collective-permute-start | bytes 3981320 | tf_op jit(solution)/shard_map/ppermute | solution.py:593
  58.8 18.7 %collective-permute-start.8 = (bf16[576,384]{1,0:T(8,128)(2,1)}, bf16[576,384]{1,0:T(8,128)(2,1)S(1)}, u32[]{:S(2)}, u32[]{:S(2)}) collective-permute-start(bf16[576,384]{1,0:T(8,128)(2,1)} %get-tuple-element.234.refs_12_.refs_15_), channel_id=1, source_target_pairs={{0,1},{1,2},{2,3},{3,0},{4,5},{5,6},{6,7},{7,4},{8,9},{9,10},{10,1... | collective-permute-start | bytes 1327112 | tf_op jit(solution)/shard_map/ppermute | solution.py:593
  77.6 12.0 %collective-permute-start.12 = (bf16[576,384]{1,0:T(8,128)(2,1)S(1)}, bf16[576,384]{1,0:T(8,128)(2,1)S(1)}, u32[]{:S(2)}, u32[]{:S(2)}) collective-permute-start(bf16[576,384]{1,0:T(8,128)(2,1)S(1)} %collective-permute-done.8.refs_13_.refs_16_), channel_id=1, source_target_pairs={{0,1},{1,2},{2,3},{3,0},{4,5},{5,6},{6,7},{7,4},{8,9},{9,10},{10,1... | collective-permute-start | bytes 1327112 | tf_op jit(solution)/shard_map/ppermute | solution.py:593
  89.6 21.2 %collective-permute-start.18 = (bf16[3,80,1536]{2,1,0:T(8,128)(2,1)S(1)}, bf16[3,80,1536]{2,1,0:T(8,128)(2,1)S(1)}, u32[]{:S(2)}, u32[]{:S(2)}) collective-permute-start(bf16[3,80,1536]{2,1,0:T(8,128)(2,1)S(1)} %slice.230), channel_id=1, source_target_pairs={{0,8},{8,0},{16,24},{24,16},{1,9},{9,1},{17,25},{25,17},{2,10},{10... | collective-permute-start | bytes 2211848 | tf_op jit(solution)/shard_map/ppermute | solution.py:593
  90.0 20.8 %collective-permute-start.19 = (bf16[3,64,1536]{2,1,0:T(8,128)(2,1)S(1)}, bf16[3,64,1536]{2,1,0:T(8,128)(2,1)S(1)}, u32[]{:S(2)}, u32[]{:S(2)}) collective-permute-start(bf16[3,64,1536]{2,1,0:T(8,128)(2,1)S(1)} %slice.231), channel_id=1, source_target_pairs={{0,16},{8,24},{16,0},{24,8},{1,17},{9,25},{17,1},{25,9},{2,18},{10... | collective-permute-start | bytes 1769480 | tf_op jit(solution)/shard_map/ppermute | solution.py:593
  91.9 11.5 %collective-permute-start.10 = (bf16[256,256]{1,0:T(8,128)(2,1)S(1)}, bf16[256,256]{1,0:T(8,128)(2,1)S(1)}, u32[]{:S(2)}, u32[]{:S(2)}) collective-permute-start(bf16[256,256]{1,0:T(8,128)(2,1)S(1)} %copy-done.66), channel_id=1, source_target_pairs={{0,2},{1,3},{2,0},{3,1},{4,6},{5,7},{6,4},{7,5},{8,10},{9,11},{10,... | collective-permute-start | bytes 393224 | tf_op jit(solution)/shard_map/ppermute | solution.py:593
  95.0 11.5 %collective-permute-start.16 = (bf16[256,128]{1,0:T(8,128)(2,1)}, bf16[256,128]{1,0:T(8,128)(2,1)S(1)}, u32[]{:S(2)}, u32[]{:S(2)}) collective-permute-start(bf16[256,128]{1,0:T(8,128)(2,1)} %get-tuple-element.247), channel_id=1, source_target_pairs={{0,2},{1,3},{2,0},{3,1},{4,6},{5,7},{6,4},{7,5},{8,10},{9,11},{10,... | collective-permute-start | bytes 196616 | tf_op jit(solution)/shard_map/ppermute | solution.py:593
  110.8 20.2 %collective-permute-start.25 = (bf16[3,144,1536]{2,1,0:T(8,128)(2,1)S(1)}, bf16[3,144,1536]{2,1,0:T(8,128)(2,1)S(1)}, u32[]{:S(2)}, u32[]{:S(2)}) collective-permute-start(bf16[3,144,1536]{2,1,0:T(8,128)(2,1)S(1)} %collective-permute-done.13.refs_26_.refs_29_), channel_id=1, source_target_pairs={{0,4},{4,0},{1,5},{5,1},{2,6},{6,2},{3,7},{7,3},{8,12},{12,8},{9,1... | collective-permute-start | bytes 3981320 | tf_op jit(solution)/shard_map/ppermute | solution.py:593
  113.9 17.2 %collective-permute-start.26 = (bf16[3,144,1536]{2,1,0:T(8,128)(2,1)S(1)}, bf16[3,144,1536]{2,1,0:T(8,128)(2,1)S(1)}, u32[]{:S(2)}, u32[]{:S(2)}) collective-permute-start(bf16[3,144,1536]{2,1,0:T(8,128)(2,1)S(1)} %collective-permute-done.14.refs_27_.refs_30_), channel_id=1, source_target_pairs={{0,4},{4,0},{1,5},{5,1},{2,6},{6,2},{3,7},{7,3},{8,12},{12,8},{9,1... | collective-permute-start | bytes 3981320 | tf_op jit(solution)/shard_map/ppermute | solution.py:593
  114.5 13.7 %collective-permute-start.20 = (bf16[576,384]{1,0:T(8,128)(2,1)}, bf16[576,384]{1,0:T(8,128)(2,1)S(1)}, u32[]{:S(2)}, u32[]{:S(2)}) collective-permute-start(bf16[576,384]{1,0:T(8,128)(2,1)} %copy-done.51), channel_id=1, source_target_pairs={{0,1},{1,2},{2,3},{3,0},{4,5},{5,6},{6,7},{7,4},{8,9},{9,10},{10,1... | collective-permute-start | bytes 1327112 | tf_op jit(solution)/shard_map/ppermute | solution.py:593
  114.6 14.2 %collective-permute-start.23 = (bf16[576,384]{1,0:T(8,128)(2,1)}, bf16[576,384]{1,0:T(8,128)(2,1)}, u32[]{:S(2)}, u32[]{:S(2)}) collective-permute-start(bf16[576,384]{1,0:T(8,128)(2,1)} %copy-done.51), channel_id=1, source_target_pairs={{0,4},{4,0},{1,5},{5,1},{2,6},{6,2},{3,7},{7,3},{8,12},{12,8},{9,1... | collective-permute-start | bytes 1327112 | tf_op jit(solution)/shard_map/ppermute | solution.py:593
  118.7 12.3 %collective-permute-start.27 = (bf16[3,80,1536]{2,1,0:T(8,128)(2,1)S(1)}, bf16[3,80,1536]{2,1,0:T(8,128)(2,1)S(1)}, u32[]{:S(2)}, u32[]{:S(2)}) collective-permute-start(bf16[3,80,1536]{2,1,0:T(8,128)(2,1)S(1)} %collective-permute-done.18.refs_28_.refs_31_), channel_id=1, source_target_pairs={{0,4},{4,0},{1,5},{5,1},{2,6},{6,2},{3,7},{7,3},{8,12},{12,8},{9,1... | collective-permute-start | bytes 2211848 | tf_op jit(solution)/shard_map/ppermute | solution.py:593
  154.1 21.4 %collective-permute-start.29 = (bf16[256,1536]{1,0:T(8,128)(2,1)}, bf16[256,1536]{1,0:T(8,128)(2,1)S(1)}, u32[]{:S(2)}, u32[]{:S(2)}) collective-permute-start(bf16[256,1536]{1,0:T(8,128)(2,1)} %get-tuple-element.262.refs_0_), channel_id=1, source_target_pairs={{0,1},{1,2},{2,3},{3,0},{4,5},{5,6},{6,7},{7,4},{8,9},{9,10},{10,1... | collective-permute-start | bytes 2359304 | tf_op jit(solution)/shard_map/ppermute | solution.py:593
  175.5 21.6 %collective-permute-start.30 = (bf16[256,1536]{1,0:T(8,128)(2,1)S(1)}, bf16[256,1536]{1,0:T(8,128)(2,1)S(1)}, u32[]{:S(2)}, u32[]{:S(2)}) collective-permute-start(bf16[256,1536]{1,0:T(8,128)(2,1)S(1)} %collective-permute-done.29.refs_0_), channel_id=1, source_target_pairs={{0,1},{1,2},{2,3},{3,0},{4,5},{5,6},{6,7},{7,4},{8,9},{9,10},{10,1... | collective-permute-start | bytes 2359304 | tf_op jit(solution)/shard_map/ppermute | solution.py:593
  194.3 23.0 %collective-permute-start.32 = (bf16[256,1536]{1,0:T(8,128)(2,1)}, bf16[256,1536]{1,0:T(8,128)(2,1)S(1)}, u32[]{:S(2)}, u32[]{:S(2)}) collective-permute-start(bf16[256,1536]{1,0:T(8,128)(2,1)} %get-tuple-element.281), channel_id=1, source_target_pairs={{0,1},{1,2},{2,3},{3,0},{4,5},{5,6},{6,7},{7,4},{8,9},{9,10},{10,1... | collective-permute-start | bytes 2359304 | tf_op jit(solution)/shard_map/ppermute | solution.py:593
  197.1 33.9 %collective-permute-start.31 = (bf16[256,1536]{1,0:T(8,128)(2,1)S(1)}, bf16[256,1536]{1,0:T(8,128)(2,1)S(1)}, u32[]{:S(2)}, u32[]{:S(2)}) collective-permute-start(bf16[256,1536]{1,0:T(8,128)(2,1)S(1)} %collective-permute-done.30.refs_0_), channel_id=1, source_target_pairs={{0,1},{1,2},{2,3},{3,0},{4,5},{5,6},{6,7},{7,4},{8,9},{9,10},{10,1... | collective-permute-start | bytes 2359304 | tf_op jit(solution)/shard_map/ppermute | solution.py:593
  218.6 31.4 %collective-permute-start.33 = (bf16[256,1536]{1,0:T(8,128)(2,1)S(1)}, bf16[256,1536]{1,0:T(8,128)(2,1)S(1)}, u32[]{:S(2)}, u32[]{:S(2)}) collective-permute-start(bf16[256,1536]{1,0:T(8,128)(2,1)S(1)} %add_convert_fusion.1), channel_id=1, source_target_pairs={{0,1},{1,2},{2,3},{3,0},{4,5},{5,6},{6,7},{7,4},{8,9},{9,10},{10,1... | collective-permute-start | bytes 2359304 | tf_op jit(solution)/shard_map/ppermute | solution.py:593
  251.4 17.0 %collective-permute-start.34 = (bf16[256,1536]{1,0:T(8,128)(2,1)S(1)}, bf16[256,1536]{1,0:T(8,128)(2,1)S(1)}, u32[]{:S(2)}, u32[]{:S(2)}) collective-permute-start(bf16[256,1536]{1,0:T(8,128)(2,1)S(1)} %add_convert_fusion), channel_id=1, source_target_pairs={{0,1},{1,2},{2,3},{3,0},{4,5},{5,6},{6,7},{7,4},{8,9},{9,10},{10,1... | collective-permute-start | bytes 2359304 | tf_op jit(solution)/shard_map/ppermute | solution.py:593
  271.0 33.8 %collective-permute-start.35 = (bf16[256,1536]{1,0:T(8,128)(2,1)S(1)}, bf16[256,1536]{1,0:T(8,128)(2,1)S(1)}, u32[]{:S(2)}, u32[]{:S(2)}) collective-permute-start(bf16[256,1536]{1,0:T(8,128)(2,1)S(1)} %get-tuple-element.456), channel_id=1, source_target_pairs={{0,1},{3,2},{4,5},{7,6},{8,9},{11,10},{12,13},{15,14},{16,17},{19,... | collective-permute-start | bytes 2359304 | tf_op jit(solution)/shard_map/ppermute | solution.py:593
  299.3 17.0 %collective-permute-start.37 = (bf16[256,128]{1,0:T(8,128)(2,1)}, bf16[256,128]{1,0:T(8,128)(2,1)S(1)}, u32[]{:S(2)}, u32[]{:S(2)}) collective-permute-start(bf16[256,128]{1,0:T(8,128)(2,1)} %get-tuple-element.300), channel_id=1, source_target_pairs={{0,3},{1,0},{2,1},{3,2},{4,7},{5,4},{6,5},{7,6},{8,11},{9,8},{10,9... | collective-permute-start | bytes 196616 | tf_op jit(solution)/shard_map/ppermute | solution.py:593
  302.4 16.7 %collective-permute-start.38 = (bf16[256,128]{1,0:T(8,128)(2,1)}, bf16[256,128]{1,0:T(8,128)(2,1)S(1)}, u32[]{:S(2)}, u32[]{:S(2)}) collective-permute-start(bf16[256,128]{1,0:T(8,128)(2,1)} %get-tuple-element.301), channel_id=1, source_target_pairs={{0,2},{1,3},{2,0},{3,1},{4,6},{5,7},{6,4},{7,5},{8,10},{9,11},{10,... | collective-permute-start | bytes 196616 | tf_op jit(solution)/shard_map/ppermute | solution.py:593
  302.4 17.4 %collective-permute-start.39 = (bf16[256,128]{1,0:T(8,128)(2,1)}, bf16[256,128]{1,0:T(8,128)(2,1)}, u32[]{:S(2)}, u32[]{:S(2)}) collective-permute-start(bf16[256,128]{1,0:T(8,128)(2,1)} %get-tuple-element.302), channel_id=1, source_target_pairs={{0,1},{1,2},{2,3},{3,0},{4,5},{5,6},{6,7},{7,4},{8,9},{9,10},{10,1... | collective-permute-start | bytes 196616 | tf_op jit(solution)/shard_map/ppermute | solution.py:593
  303.7 31.3 %collective-permute-start.40 = (bf16[256,256]{1,0:T(8,128)(2,1)}, bf16[256,256]{1,0:T(8,128)(2,1)S(1)}, u32[]{:S(2)}, u32[]{:S(2)}) collective-permute-start(bf16[256,256]{1,0:T(8,128)(2,1)} %get-tuple-element.312), channel_id=1, source_target_pairs={{0,3},{1,0},{2,1},{3,2},{4,7},{5,4},{6,5},{7,6},{8,11},{9,8},{10,9... | collective-permute-start | bytes 393224 | tf_op jit(solution)/shard_map/ppermute | solution.py:593
  316.4 19.9 %collective-permute-start.41 = (bf16[256,256]{1,0:T(8,128)(2,1)}, bf16[256,256]{1,0:T(8,128)(2,1)S(1)}, u32[]{:S(2)}, u32[]{:S(2)}) collective-permute-start(bf16[256,256]{1,0:T(8,128)(2,1)} %get-tuple-element.313), channel_id=1, source_target_pairs={{0,2},{1,3},{2,0},{3,1},{4,6},{5,7},{6,4},{7,5},{8,10},{9,11},{10,... | collective-permute-start | bytes 393224 | tf_op jit(solution)/shard_map/ppermute | solution.py:593
  319.1 20.2 %collective-permute-start.42 = (bf16[256,256]{1,0:T(8,128)(2,1)S(1)}, bf16[256,256]{1,0:T(8,128)(2,1)}, u32[]{:S(2)}, u32[]{:S(2)}) collective-permute-start(bf16[256,256]{1,0:T(8,128)(2,1)S(1)} %copy-done.60), channel_id=1, source_target_pairs={{0,1},{1,2},{2,3},{3,0},{4,5},{5,6},{6,7},{7,4},{8,9},{9,10},{10,1... | collective-permute-start | bytes 393224 | tf_op jit(solution)/shard_map/ppermute | solution.py:593
  319.8 19.6 %collective-permute-start.44 = (bf16[8,7680]{1,0:T(8,128)(2,1)S(1)}, bf16[8,7680]{1,0:T(8,128)(2,1)S(1)}, u32[]{:S(2)}, u32[]{:S(2)}) collective-permute-start(bf16[8,7680]{1,0:T(8,128)(2,1)S(1)} %slice.300), channel_id=1, source_target_pairs={{0,1},{1,0},{2,3},{3,2},{4,5},{5,4},{6,7},{7,6},{8,9},{9,8},{10,11... | collective-permute-start | bytes 368648 | tf_op jit(solution)/shard_map/ppermute | solution.py:593
  321.7 17.7 %collective-permute-start.45 = (bf16[560,384]{1,0:T(8,128)(2,1)S(1)}, bf16[560,384]{1,0:T(8,128)(2,1)S(1)}, u32[]{:S(2)}, u32[]{:S(2)}) collective-permute-start(bf16[560,384]{1,0:T(8,128)(2,1)S(1)} %fusion.19), channel_id=1, source_target_pairs={{0,1},{1,2},{2,3},{3,0},{4,5},{5,6},{6,7},{7,4},{8,9},{9,10},{10,1... | collective-permute-start | bytes 1290248 | tf_op jit(solution)/shard_map/ppermute | solution.py:593
  335.0 34.4 %collective-permute-start.50 = (bf16[256,1536]{1,0:T(8,128)(2,1)S(1)}, bf16[256,1536]{1,0:T(8,128)(2,1)}, u32[]{:S(2)}, u32[]{:S(2)}) collective-permute-start(bf16[256,1536]{1,0:T(8,128)(2,1)S(1)} %copy-done.7), channel_id=1, source_target_pairs={{0,1},{3,2},{4,5},{7,6},{8,9},{11,10},{12,13},{15,14},{16,17},{19,... | collective-permute-start | bytes 2359304 | tf_op jit(solution)/shard_map/ppermute | solution.py:593
  336.4 33.8 %collective-permute-start.51 = (bf16[256,1536]{1,0:T(8,128)(2,1)}, bf16[256,1536]{1,0:T(8,128)(2,1)}, u32[]{:S(2)}, u32[]{:S(2)}) collective-permute-start(bf16[256,1536]{1,0:T(8,128)(2,1)} %shard_map.407.refs_2_), channel_id=1, source_target_pairs={{1,2},{2,1},{5,6},{6,5},{9,10},{10,9},{13,14},{14,13},{17,18},{18,... | collective-permute-start | bytes 2359304 | tf_op jit(solution)/shard_map/ppermute | solution.py:593
  351.9 37.2 %collective-permute-start.46 = (bf16[1024,256]{1,0:T(8,128)(2,1)}, bf16[1024,256]{1,0:T(8,128)(2,1)}, u32[]{:S(2)}, u32[]{:S(2)}) collective-permute-start(bf16[1024,256]{1,0:T(8,128)(2,1)} %get-tuple-element.340), channel_id=1, source_target_pairs={{0,4},{4,0},{1,5},{5,1},{2,6},{6,2},{3,7},{7,3},{8,12},{12,8},{9,1... | collective-permute-start | bytes 1572872 | tf_op jit(solution)/shard_map/ppermute | solution.py:593
  352.8 17.4 %collective-permute-start.48 = (bf16[8,7680]{1,0:T(8,128)(2,1)S(1)}, bf16[8,7680]{1,0:T(8,128)(2,1)S(1)}, u32[]{:S(2)}, u32[]{:S(2)}) collective-permute-start(bf16[8,7680]{1,0:T(8,128)(2,1)S(1)} %add_convert_fusion.10), channel_id=1, source_target_pairs={{0,2},{1,3},{2,0},{3,1},{4,6},{5,7},{6,4},{7,5},{8,10},{9,11},{10,... | collective-permute-start | bytes 368648 | tf_op jit(solution)/shard_map/ppermute | solution.py:593
  355.3 15.1 %collective-permute-start.49 = (bf16[560,384]{1,0:T(8,128)(2,1)S(1)}, bf16[560,384]{1,0:T(8,128)(2,1)S(1)}, u32[]{:S(2)}, u32[]{:S(2)}) collective-permute-start(bf16[560,384]{1,0:T(8,128)(2,1)S(1)} %fusion.3), channel_id=1, source_target_pairs={{0,1},{1,2},{2,3},{3,0},{4,5},{5,6},{6,7},{7,4},{8,9},{9,10},{10,1... | collective-permute-start | bytes 1290248 | tf_op jit(solution)/shard_map/ppermute | solution.py:593
  369.5 20.1 %collective-permute-start.47 = (bf16[1024,256]{1,0:T(8,128)(2,1)}, bf16[1024,256]{1,0:T(8,128)(2,1)S(1)}, u32[]{:S(2)}, u32[]{:S(2)}) collective-permute-start(bf16[1024,256]{1,0:T(8,128)(2,1)} %get-tuple-element.341), channel_id=1, source_target_pairs={{0,4},{4,0},{1,5},{5,1},{2,6},{6,2},{3,7},{7,3},{8,12},{12,8},{9,1... | collective-permute-start | bytes 1572872 | tf_op jit(solution)/shard_map/ppermute | solution.py:593
  370.4 20.2 %collective-permute-start.52 = (bf16[1024,256]{1,0:T(8,128)(2,1)}, bf16[1024,256]{1,0:T(8,128)(2,1)}, u32[]{:S(2)}, u32[]{:S(2)}) collective-permute-start(bf16[1024,256]{1,0:T(8,128)(2,1)} %get-tuple-element.348), channel_id=1, source_target_pairs={{0,4},{4,0},{1,5},{5,1},{2,6},{6,2},{3,7},{7,3},{8,12},{12,8},{9,1... | collective-permute-start | bytes 1572872 | tf_op jit(solution)/shard_map/ppermute | solution.py:593
  384.1 29.2 %collective-permute-start.59 = (bf16[256,1536]{1,0:T(8,128)(2,1)}, bf16[256,1536]{1,0:T(8,128)(2,1)}, u32[]{:S(2)}, u32[]{:S(2)}) collective-permute-start(bf16[256,1536]{1,0:T(8,128)(2,1)} %get-tuple-element.364.refs_5_), channel_id=1, source_target_pairs={{0,1},{3,2},{1,0},{2,3},{4,5},{7,6},{5,4},{6,7},{8,9},{11,10},{9,8... | collective-permute-start | bytes 2359304 | tf_op jit(solution)/shard_map/ppermute | solution.py:593
  385.9 28.6 %collective-permute-start.60 = (bf16[256,1536]{1,0:T(8,128)(2,1)}, bf16[256,1536]{1,0:T(8,128)(2,1)}, u32[]{:S(2)}, u32[]{:S(2)}) collective-permute-start(bf16[256,1536]{1,0:T(8,128)(2,1)} %get-tuple-element.365.refs_2_), channel_id=1, source_target_pairs={{1,2},{2,1},{5,6},{6,5},{9,10},{10,9},{13,14},{14,13},{17,18},{18,... | collective-permute-start | bytes 2359304 | tf_op jit(solution)/shard_map/ppermute | solution.py:593
  389.1 13.8 %collective-permute-start.57 = (bf16[2,8,12160]{2,1,0:T(8,128)(2,1)}, bf16[2,8,12160]{2,1,0:T(8,128)(2,1)S(1)}, u32[]{:S(2)}, u32[]{:S(2)}) collective-permute-start(bf16[2,8,12160]{2,1,0:T(8,128)(2,1)} %pad_maximum_fusion.7), channel_id=1, source_target_pairs={{0,16},{8,24},{16,0},{24,8},{1,17},{9,25},{17,1},{25,9},{2,18},{10... | collective-permute-start | bytes 1167368 | tf_op jit(solution)/shard_map/ppermute | solution.py:593
  389.6 23.6 %collective-permute-start.58 = (bf16[560,384]{1,0:T(8,128)(2,1)S(1)}, bf16[560,384]{1,0:T(8,128)(2,1)S(1)}, u32[]{:S(2)}, u32[]{:S(2)}) collective-permute-start(bf16[560,384]{1,0:T(8,128)(2,1)S(1)} %fusion.11), channel_id=1, source_target_pairs={{0,1},{1,2},{2,3},{3,0},{4,5},{5,6},{6,7},{7,4},{8,9},{9,10},{10,1... | collective-permute-start | bytes 1290248 | tf_op jit(solution)/shard_map/ppermute | solution.py:593
  415.7 25.1 %collective-permute-start.61 = (bf16[4,8,12160]{2,1,0:T(8,128)(2,1)S(1)}, bf16[4,8,12160]{2,1,0:T(8,128)(2,1)S(1)}, u32[]{:S(2)}, u32[]{:S(2)}) collective-permute-start(bf16[4,8,12160]{2,1,0:T(8,128)(2,1)S(1)} %pad_maximum_fusion.3), channel_id=1, source_target_pairs={{0,4},{4,0},{1,5},{5,1},{2,6},{6,2},{3,7},{7,3},{8,12},{12,8},{9,1... | collective-permute-start | bytes 2334728 | tf_op jit(solution)/shard_map/ppermute | solution.py:593
  418.7 22.1 %collective-permute-start.62 = (f32[512]{0:T(512)S(1)}, f32[512]{0:T(512)S(1)}, u32[]{:S(2)}, u32[]{:S(2)}) collective-permute-start(f32[512]{0:T(512)S(1)} %multiply_reduce_fusion), channel_id=1, source_target_pairs={{0,1},{1,0},{2,3},{3,2},{4,5},{5,4},{6,7},{7,6},{8,9},{9,8},{10,11... | collective-permute-start | bytes 6152 | tf_op jit(solution)/shard_map/ppermute | solution.py:593
  423.8 19.4 %collective-permute-start.63 = (bf16[256,1536]{1,0:T(8,128)(2,1)}, bf16[256,1536]{1,0:T(8,128)(2,1)S(1)}, u32[]{:S(2)}, u32[]{:S(2)}) collective-permute-start(bf16[256,1536]{1,0:T(8,128)(2,1)} %get-tuple-element.373.refs_5_), channel_id=1, source_target_pairs={{0,1},{3,2},{1,0},{2,3},{4,5},{7,6},{5,4},{6,7},{8,9},{11,10},{9,8... | collective-permute-start | bytes 2359304 | tf_op jit(solution)/shard_map/ppermute | solution.py:593
  425.3 20.6 %collective-permute-start.64 = (bf16[256,1536]{1,0:T(8,128)(2,1)}, bf16[256,1536]{1,0:T(8,128)(2,1)S(1)}, u32[]{:S(2)}, u32[]{:S(2)}) collective-permute-start(bf16[256,1536]{1,0:T(8,128)(2,1)} %get-tuple-element.374.refs_2_), channel_id=1, source_target_pairs={{1,2},{2,1},{5,6},{6,5},{9,10},{10,9},{13,14},{14,13},{17,18},{18,... | collective-permute-start | bytes 2359304 | tf_op jit(solution)/shard_map/ppermute | solution.py:593
  452.2 19.9 %collective-permute-start.68 = (bf16[256,1536]{1,0:T(8,128)(2,1)}, bf16[256,1536]{1,0:T(8,128)(2,1)}, u32[]{:S(2)}, u32[]{:S(2)}) collective-permute-start(bf16[256,1536]{1,0:T(8,128)(2,1)} %get-tuple-element.385.refs_5_), channel_id=1, source_target_pairs={{0,1},{3,2},{1,0},{2,3},{4,5},{7,6},{5,4},{6,7},{8,9},{11,10},{9,8... | collective-permute-start | bytes 2359304 | tf_op jit(solution)/shard_map/ppermute | solution.py:593
  454.3 19.2 %collective-permute-start.69 = (bf16[256,1536]{1,0:T(8,128)(2,1)}, bf16[256,1536]{1,0:T(8,128)(2,1)}, u32[]{:S(2)}, u32[]{:S(2)}) collective-permute-start(bf16[256,1536]{1,0:T(8,128)(2,1)} %get-tuple-element.380.refs_6_.refs_2_), channel_id=1, source_target_pairs={{1,2},{2,1},{5,6},{6,5},{9,10},{10,9},{13,14},{14,13},{17,18},{18,... | collective-permute-start | bytes 2359304 | tf_op jit(solution)/shard_map/ppermute | solution.py:593
  474.3 12.3 %collective-permute-start.73 = (bf16[8,7680]{1,0:T(8,128)(2,1)}, bf16[8,7680]{1,0:T(8,128)(2,1)S(1)}, u32[]{:S(2)}, u32[]{:S(2)}) collective-permute-start(bf16[8,7680]{1,0:T(8,128)(2,1)} %slice.312), channel_id=1, source_target_pairs={{0,1},{1,0},{2,3},{3,2},{4,5},{5,4},{6,7},{7,6},{8,9},{9,8},{10,11... | collective-permute-start | bytes 368648 | tf_op jit(solution)/shard_map/ppermute | solution.py:593
  479.6 16.4 %collective-permute-start.74 = (bf16[256,1536]{1,0:T(8,128)(2,1)}, bf16[256,1536]{1,0:T(8,128)(2,1)}, u32[]{:S(2)}, u32[]{:S(2)}) collective-permute-start(bf16[256,1536]{1,0:T(8,128)(2,1)} %get-tuple-element.391.refs_5_), channel_id=1, source_target_pairs={{0,1},{3,2},{1,0},{2,3},{4,5},{7,6},{5,4},{6,7},{8,9},{11,10},{9,8... | collective-permute-start | bytes 2359304 | tf_op jit(solution)/shard_map/ppermute | solution.py:593
  481.1 17.8 %collective-permute-start.75 = (bf16[256,1536]{1,0:T(8,128)(2,1)}, bf16[256,1536]{1,0:T(8,128)(2,1)}, u32[]{:S(2)}, u32[]{:S(2)}) collective-permute-start(bf16[256,1536]{1,0:T(8,128)(2,1)} %get-tuple-element.392.refs_2_), channel_id=1, source_target_pairs={{1,2},{2,1},{5,6},{6,5},{9,10},{10,9},{13,14},{14,13},{17,18},{18,... | collective-permute-start | bytes 2359304 | tf_op jit(solution)/shard_map/ppermute | solution.py:593
  499.8 25.8 %collective-permute-start.76 = (bf16[64,1536]{1,0:T(8,128)(2,1)S(1)}, bf16[64,1536]{1,0:T(8,128)(2,1)S(1)}, u32[]{:S(2)}, u32[]{:S(2)}) collective-permute-start(bf16[64,1536]{1,0:T(8,128)(2,1)S(1)} %add_convert_fusion.4), channel_id=1, source_target_pairs={{0,1},{1,0},{2,3},{3,2},{4,5},{5,4},{6,7},{7,6},{8,9},{9,8},{10,11... | collective-permute-start | bytes 589832 | tf_op jit(solution)/shard_map/ppermute | solution.py:593
  505.0 20.6 %collective-permute-start.78 = (bf16[256,1536]{1,0:T(8,128)(2,1)}, bf16[256,1536]{1,0:T(8,128)(2,1)S(1)}, u32[]{:S(2)}, u32[]{:S(2)}) collective-permute-start(bf16[256,1536]{1,0:T(8,128)(2,1)} %get-tuple-element.402.refs_5_), channel_id=1, source_target_pairs={{0,1},{3,2},{1,0},{2,3},{4,5},{7,6},{5,4},{6,7},{8,9},{11,10},{9,8... | collective-permute-start | bytes 2359304 | tf_op jit(solution)/shard_map/ppermute | solution.py:593
  506.4 19.2 %collective-permute-start.79 = (bf16[256,1536]{1,0:T(8,128)(2,1)}, bf16[256,1536]{1,0:T(8,128)(2,1)S(1)}, u32[]{:S(2)}, u32[]{:S(2)}) collective-permute-start(bf16[256,1536]{1,0:T(8,128)(2,1)} %get-tuple-element.403.refs_2_), channel_id=1, source_target_pairs={{1,2},{2,1},{5,6},{6,5},{9,10},{10,9},{13,14},{14,13},{17,18},{18,... | collective-permute-start | bytes 2359304 | tf_op jit(solution)/shard_map/ppermute | solution.py:593
  508.7 16.9 %collective-permute-start.77 = (bf16[8,7680]{1,0:T(8,128)(2,1)S(1)}, bf16[8,7680]{1,0:T(8,128)(2,1)S(1)}, u32[]{:S(2)}, u32[]{:S(2)}) collective-permute-start(bf16[8,7680]{1,0:T(8,128)(2,1)S(1)} %add_convert_fusion.8), channel_id=1, source_target_pairs={{0,2},{1,3},{2,0},{3,1},{4,6},{5,7},{6,4},{7,5},{8,10},{9,11},{10,... | collective-permute-start | bytes 368648 | tf_op jit(solution)/shard_map/ppermute | solution.py:593
  533.8 13.2 %collective-permute-start.82 = (bf16[256,1536]{1,0:T(8,128)(2,1)}, bf16[256,1536]{1,0:T(8,128)(2,1)S(1)}, u32[]{:S(2)}, u32[]{:S(2)}) collective-permute-start(bf16[256,1536]{1,0:T(8,128)(2,1)} %get-tuple-element.408.refs_4_), channel_id=1, source_target_pairs={{0,1},{3,2},{1,0},{2,3},{4,5},{7,6},{5,4},{6,7},{8,9},{11,10},{9,8... | collective-permute-start | bytes 2359304 | tf_op jit(solution)/shard_map/ppermute | solution.py:593
  534.3 17.6 %collective-permute-start.83 = (bf16[256,1536]{1,0:T(8,128)(2,1)}, bf16[256,1536]{1,0:T(8,128)(2,1)S(1)}, u32[]{:S(2)}, u32[]{:S(2)}) collective-permute-start(bf16[256,1536]{1,0:T(8,128)(2,1)} %get-tuple-element.409.refs_2_), channel_id=1, source_target_pairs={{1,2},{2,1},{5,6},{6,5},{9,10},{10,9},{13,14},{14,13},{17,18},{18,... | collective-permute-start | bytes 2359304 | tf_op jit(solution)/shard_map/ppermute | solution.py:593
  557.8 17.2 %collective-permute-start.84 = (bf16[256,1536]{1,0:T(8,128)(2,1)}, bf16[256,1536]{1,0:T(8,128)(2,1)}, u32[]{:S(2)}, u32[]{:S(2)}) collective-permute-start(bf16[256,1536]{1,0:T(8,128)(2,1)} %get-tuple-element.413.refs_3_), channel_id=1, source_target_pairs={{1,0},{2,3},{5,4},{6,7},{9,8},{10,11},{13,12},{14,15},{17,16},{18,... | collective-permute-start | bytes 2359304 | tf_op jit(solution)/shard_map/ppermute | solution.py:593
  560.0 15.0 %collective-permute-start.85 = (bf16[256,1536]{1,0:T(8,128)(2,1)}, bf16[256,1536]{1,0:T(8,128)(2,1)}, u32[]{:S(2)}, u32[]{:S(2)}) collective-permute-start(bf16[256,1536]{1,0:T(8,128)(2,1)} %get-tuple-element.414.refs_1_), channel_id=1, source_target_pairs={{1,2},{2,1},{5,6},{6,5},{9,10},{10,9},{13,14},{14,13},{17,18},{18,... | collective-permute-start | bytes 2359304 | tf_op jit(solution)/shard_map/ppermute | solution.py:593
  562.7 19.4 %collective-permute-start.89 = (bf16[128,1536]{1,0:T(8,128)(2,1)S(1)}, bf16[128,1536]{1,0:T(8,128)(2,1)}, u32[]{:S(2)}, u32[]{:S(2)}) collective-permute-start(bf16[128,1536]{1,0:T(8,128)(2,1)S(1)} %pad_maximum_fusion.5), channel_id=1, source_target_pairs={{0,16},{8,24},{16,0},{24,8},{1,17},{9,25},{17,1},{25,9},{2,18},{10... | collective-permute-start | bytes 1179656 | tf_op jit(solution)/shard_map/ppermute | solution.py:593
  564.7 17.5 %collective-permute-start.90 = (bf16[4,8,10880]{2,1,0:T(8,128)(2,1)}, bf16[4,8,10880]{2,1,0:T(8,128)(2,1)}, u32[]{:S(2)}, u32[]{:S(2)}) collective-permute-start(bf16[4,8,10880]{2,1,0:T(8,128)(2,1)} %pad_maximum_fusion.4), channel_id=1, source_target_pairs={{0,4},{4,0},{1,5},{5,1},{2,6},{6,2},{3,7},{7,3},{8,12},{12,8},{9,1... | collective-permute-start | bytes 2088968 | tf_op jit(solution)/shard_map/ppermute | solution.py:593
  579.7 26.8 %collective-permute-start.86 = (bf16[256,1536]{1,0:T(8,128)(2,1)}, bf16[256,1536]{1,0:T(8,128)(2,1)}, u32[]{:S(2)}, u32[]{:S(2)}) collective-permute-start(bf16[256,1536]{1,0:T(8,128)(2,1)} %get-tuple-element.416.refs_1_), channel_id=1, source_target_pairs={{1,0},{2,3},{5,4},{6,7},{9,8},{10,11},{13,12},{14,15},{17,16},{18,... | collective-permute-start | bytes 2359304 | tf_op jit(solution)/shard_map/ppermute | solution.py:593
  586.6 24.0 %collective-permute-start.91 = (bf16[256,1536]{1,0:T(8,128)(2,1)S(1)}, bf16[256,1536]{1,0:T(8,128)(2,1)S(1)}, u32[]{:S(2)}, u32[]{:S(2)}) collective-permute-start(bf16[256,1536]{1,0:T(8,128)(2,1)S(1)} %pad_maximum_fusion.2), channel_id=1, source_target_pairs={{0,4},{4,0},{1,5},{5,1},{2,6},{6,2},{3,7},{7,3},{8,12},{12,8},{9,1... | collective-permute-start | bytes 2359304 | tf_op jit(solution)/shard_map/ppermute | solution.py:593
  (103 other events, 974.0 us)

commit v3 on v2

--- a/solution.py
+++ b/solution.py
@@ -143,42 +143,9 @@
 
 
 def attention_kernel(groups, meta, raw_q, st, st_own, st_sib, k_own, k_sib, v_own, v_sib, *outs):
-    blocks, out, lse, kn, vt = outs[:groups], outs[groups], outs[groups + 1], outs[groups + 2], outs[groups + 3]
+    blocks, (out, lse, kn, knt, vn, qn, vt) = outs[:groups], outs[groups:]
     count = k_own.shape[0]
     step = pl.program_id(1)
-
-    @pl.when(step == 0)
-    def _():
-        for at, (k, s, v) in enumerate(((k_own, st_own, v_own), (k_sib, st_sib, v_sib))):
-            rows = slice(at * count, (at + 1) * count)
-            kn[rows, :] = (k[...].astype(F32) * s[...].T[:, 1:2]).astype(BF16)
-            vt[:, rows] = v[...].astype(F32).T.astype(BF16)
-
-    q = (raw_q[...].astype(F32) * (st[...].T[:, 0:1] * (SCALE * LOG2E))).astype(BF16)
-    scores = nt(kn[...], q)
-    highest = jnp.max(scores, axis=0, keepdims=True)
-    e = jnp.exp2(scores - highest)
-    total = jnp.sum(e, axis=0, keepdims=True)
-    mixed = (nn(vt[...], e.astype(BF16)) / total).T.astype(BF16)
-    out[...] = mixed
-    for r in range(groups):
-
-        @pl.when(step == r)
-        def _(r=r):
-            blocks[r][...] = mixed
-
-    lse[...] = jnp.broadcast_to(highest + jnp.log2(total), lse.shape)
-
-
-def attention_back_kernel(groups, first, meta, raw_q, st, st_own, st_sib, k_own, k_sib, v_own, v_sib, out, lse, *rest):
-    grads, rest = rest[:groups], rest[groups:]
-    if not first:
-        stat_in, cross_in = rest[:2]
-        rest = rest[2:]
-    dq, dkv_own, dkv_sib, stat, cross, kn, knt, vn, dk_acc, dv_acc, g_s = rest
-    count = k_own.shape[0]
-    size = raw_q.shape[0]
-    step = pl.program_id(0)
 
     @pl.when(step == 0)
     def _():
@@ -188,6 +155,37 @@
             kn[rows, :] = scaled.astype(BF16)
             knt[:, rows] = scaled.T.astype(BF16)
             vn[rows, :] = v[...]
+            vt[:, rows] = v[...].astype(F32).T.astype(BF16)
+
+    q = (raw_q[...].astype(F32) * (st[...].T[:, 0:1] * (SCALE * LOG2E))).astype(BF16)
+    qn[...] = q
+    scores = nt(kn[...], q)
+    highest = jnp.max(scores, axis=0, keepdims=True)
+    e = jnp.exp2(scores - highest)
+    total = jnp.sum(e, axis=0, keepdims=True)
+    mixed = (nn(vt[...], e.astype(BF16)) / total).T.astype(BF16)
+    out[...] = mixed
+    for r in range(groups):
+
+        @pl.when(step == r)
+        def _(r=r):
+            blocks[r][...] = mixed
+
+    lse[...] = jnp.broadcast_to(highest + jnp.log2(total), lse.shape)
+
+
+def attention_back_kernel(groups, first, meta, qn, st, st_own, st_sib, kn, knt, vn, out, lse, *rest):
+    grads, rest = rest[:groups], rest[groups:]
+    if not first:
+        stat_in, cross_in = rest[:2]
+        rest = rest[2:]
+    dq, dkv_own, dkv_sib, stat, cross, dk_acc, dv_acc, g_s = rest
+    count = kn.shape[0] // 2
+    size = qn.shape[0]
+    step = pl.program_id(0)
+
+    @pl.when(step == 0)
+    def _():
         dk_acc[...] = jnp.zeros_like(dk_acc)
         dv_acc[...] = jnp.zeros_like(dv_acc)
         stat[...] = jnp.zeros_like(stat) if first else stat_in[...]
@@ -199,8 +197,7 @@
         def _(r=r):
             g_s[...] = grads[r][...]
 
-    raw = raw_q[...].astype(F32)
-    q = (raw * (st[...].T[:, 0:1] * (SCALE * LOG2E))).astype(BF16)
+    q = qn[...]
     g = g_s[...]
     delta = row_total(g.astype(F32) * out[...].astype(F32))[0:1, :]
     p = jnp.exp2(nt(kn[...], q) - lse[0:1, :])
@@ -210,17 +207,17 @@
     dqs = nn(knt[...], ds).T * SCALE
     dq[...] = dqs
     lanes = pl.ds(pl.multiple_of(lax.rem(meta[AT_T] + step, groups) * size, size), size)
-    total = row_total(dqs * raw)
+    total = row_total(dqs * q.astype(F32)) / (st[0:1, :] * (SCALE * LOG2E))
     stat[:, lanes] += jnp.where(lax.broadcasted_iota(jnp.int32, total.shape, 0) == 0, total, 0.0)
 
     @pl.when(step == pl.num_programs(0) - 1)
     def _():
-        for at, (k, dkv, sums) in enumerate(((k_own, dkv_own, stat), (k_sib, dkv_sib, cross))):
+        for at, (s, dkv, sums) in enumerate(((st_own, dkv_own, stat), (st_sib, dkv_sib, cross))):
             rows = slice(at * count, (at + 1) * count)
             dk = dk_acc[rows, :] * (1.0 / LOG2E)
             dkv[:, :HEAD_DIM] = dk.astype(dkv.dtype)
             dkv[:, HEAD_DIM:] = dv_acc[rows, :].astype(dkv.dtype)
-            all_k = row_total(dk * k[...].astype(F32))
+            all_k = row_total(dk * kn[rows, :].astype(F32)) / s[1:2, :]
             sums[...] += jnp.where(lax.broadcasted_iota(jnp.int32, all_k.shape, 0) == 1, all_k, 0.0)
 
 
@@ -368,7 +365,7 @@
 
 def cross_kernel(groups, head_count, plan, meta, *refs):
     n = groups * head_count
-    os_first, os_rest, refs = refs[:groups], refs[groups : 2 * groups], refs[2 * groups :]
+    os_in, refs = refs[:groups], refs[groups:]
     tok, vec, up, dn3 = refs[:4]
     ctx_own, ctx_sib, refs = refs[4 : 4 + groups], refs[4 + groups : 4 + 2 * groups], refs[4 + 2 * groups :]
     st_own, st_sib, wo_own, wq_own, wc_own = refs[:5]
@@ -387,9 +384,7 @@
     ctx_inverse = jnp.broadcast_to(key_row, (8, ctx_len)).T[:, 0:1]
     width = head_count * HEAD_DIM
     for r in range(groups):
-        middle = r * width + os_first[r].shape[1]
-        os_all[:, r * width : middle] = os_first[r][...]
-        os_all[:, middle : (r + 1) * width] = os_rest[r][...]
+        os_all[:, r * width : (r + 1) * width] = os_in[r][...]
     os_v = os_all[...]
     down0, down1 = small[rank : 2 * rank, :], small[2 * rank : 3 * rank, :]
     lat = nt(os_v, down0).astype(BF16)
@@ -1091,50 +1086,44 @@
     st_own = lax.rsqrt((ssq + send(ssq, "tensor", flip(groups, last_step))) / d + EPS)
     st_sib = send(st_own, "seq", pair)
     by_group_sib = send(by_group, "seq", pair)
-    st_sib, by_group_sib = seal(st_sib, by_group_sib)
+    st_sib, by_group_sib, kv_sib = seal(st_sib, by_group_sib, kv_sib)
     ctx_low, _ = seal(ctx_low, st_own)
-    ctx_pieces = [ctx_low, send(ctx_low, "tensor", shift(groups, 1))]
+    ctx_pieces = gather_direct(ctx_low, "tensor")
 
     all_8 = whole((8, tl))
     turned = lambda r, m: lax.rem(m[AT_T] + r, groups)
-    parts = [(0, hc - 1), (hc - 1, 1)]
-    mixed, lses, os_pieces = [], [], []
-    for first, count in parts:
-        kv_at = lambda lane: block((tl, HEAD_DIM), lambda h, r, m: (0, lane + h))
-        own_rows = block((tc, HEAD_DIM), lambda h, r, m: (0, h))
-        *blocks, out, lse = run_kernel(
-            functools.partial(attention_kernel, groups),
-            meta,
-            [
-                (raw_q, block((tc, HEAD_DIM), lambda h, r, m, first=first: (turned(r, m), first + h))),
-                (st_own, block((8, tc), lambda h, r, m: (0, turned(r, m)))),
-                (st_own, all_8),
-                (st_sib, all_8),
-                (kv, kv_at(first)),
-                (kv_sib, kv_at(first)),
-                (kv, kv_at(hc + first)),
-                (kv_sib, kv_at(hc + first)),
-            ],
-            [(sds((tc, count * HEAD_DIM), BF16), own_rows)] * groups
-            + [
-                (sds((tl, count * HEAD_DIM), BF16), block((tc, HEAD_DIM), lambda h, r, m: (r, h))),
-                (sds((8 * count, tl), F32), block((8, tc), lambda h, r, m: (h, r))),
-            ],
-            grid=(count, groups),
-            scratch=[pltpu.VMEM((2 * tl, HEAD_DIM), BF16), pltpu.VMEM((HEAD_DIM, 2 * tl), BF16)],
-            us=9.5 * count,
-            after=[by_group] if first == 0 else [out],
-        )
-        mixed.append(out)
-        lses.append(lse)
-        if first:
-            blocks[0], ctx_pieces[-1], *along = seal(blocks[0], ctx_pieces[-1], *along)
-            ctx_pieces.append(send(ctx_pieces[-1], "tensor", shift(groups, 1)))
-            blocks[1], *os_pieces = seal(blocks[1], *os_pieces)
-        else:
-            blocks[0], ctx_pieces[-1] = seal(blocks[0], ctx_pieces[-1])
-            ctx_pieces.append(send(ctx_pieces[-1], "tensor", shift(groups, 1)))
-        os_pieces += [send(a, "tensor", shift(groups, r)) if r else a for r, a in enumerate(blocks)]
+    kv_at = lambda lane: block((tl, HEAD_DIM), lambda h, r, m: (0, lane + h))
+    own_rows = block((tc, HEAD_DIM), lambda h, r, m: (0, h))
+    *blocks, mixed, lses, kn, knt, vn, qn_self = run_kernel(
+        functools.partial(attention_kernel, groups),
+        meta,
+        [
+            (raw_q, block((tc, HEAD_DIM), lambda h, r, m: (turned(r, m), h))),
+            (st_own, block((8, tc), lambda h, r, m: (0, turned(r, m)))),
+            (st_own, all_8),
+            (st_sib, all_8),
+            (kv, kv_at(0)),
+            (kv_sib, kv_at(0)),
+            (kv, kv_at(hc)),
+            (kv_sib, kv_at(hc)),
+        ],
+        [(sds((tc, width), BF16), own_rows)] * groups
+        + [
+            (sds((tl, width), BF16), block((tc, HEAD_DIM), lambda h, r, m: (r, h))),
+            (sds((8 * hc, tl), F32), block((8, tc), lambda h, r, m: (h, r))),
+            (sds((2 * tl, width), BF16), block((2 * tl, HEAD_DIM), lambda h, r, m: (0, h))),
+            (sds((width, 2 * tl), BF16), block((HEAD_DIM, 2 * tl), lambda h, r, m: (h, 0))),
+            (sds((2 * tl, width), BF16), block((2 * tl, HEAD_DIM), lambda h, r, m: (0, h))),
+            (sds((tl, width), BF16), block((tc, HEAD_DIM), lambda h, r, m: (r, h))),
+        ],
+        grid=(hc, groups),
+        scratch=[pltpu.VMEM((HEAD_DIM, 2 * tl), BF16)],
+        us=25,
+        after=[by_group],
+    )
+    tied = seal(*blocks, *along, *ctx_pieces[1:])
+    blocks, along, ctx_pieces[1:] = tied[:groups], tied[groups : groups + len(along)], tied[groups + len(along) :]
+    os_pieces = [send(a, "tensor", shift(groups, r)) if r else a for r, a in enumerate(blocks)]
     weight_parts = [by_group] + along
     if share > 1:
         middle = far_cut(by_group.shape[1])
@@ -1142,8 +1131,9 @@
             send(along[1][:, :middle], "dp", flip(share, 1)),
             send(along[0][:, middle:], "dp", flip(share, 2)),
         ]
-    near = seal(*os_pieces[-groups + 1 :], *weight_parts)
-    os_pieces[-groups + 1 :], weight_parts = near[: groups - 1], near[groups - 1 :]
+    tied = seal(*os_pieces[1:], *along, *ctx_pieces)
+    os_pieces[1:], tied = tied[: groups - 1], tied[groups - 1 :]
+    weight_parts[1 : 1 + len(along)], ctx_pieces = tied[: len(along)], tied[len(along) :]
     weight_parts = weight_parts + [by_group_sib] + [send(p, "seq", pair) for p in weight_parts[1:]]
     ctx_sib = [send(p, "seq", pair) for p in ctx_pieces]
 
@@ -1259,10 +1249,8 @@
 
     back, dkv_in = [], []
     for h in range(hc):
-        of, at = (0, h) if h < parts[1][0] else (1, h - parts[1][0])
         grads = dos_first if h == 0 else dos_rest
         lane = 0 if h == 0 else h - 1
-        kv_at = lambda lane: block((tl, HEAD_DIM), lambda r, m: (0, lane))
         if h:
             if h == 1:
                 tied = seal(*dos_rest, *chains.arrived(), back[-1][0], back[-1][2])
@@ -1280,16 +1268,15 @@
                 functools.partial(attention_back_kernel, groups, h == 0),
                 meta,
                 [
-                    (raw_q, block((tc, HEAD_DIM), lambda r, m, h=h: (turned(r, m), h))),
+                    (qn_self, block((tc, HEAD_DIM), lambda r, m, h=h: (r, h))),
                     (st_own, block((8, tc), lambda r, m: (0, turned(r, m)))),
                     (st_own, all_8),
                     (st_sib, all_8),
-                    (kv, kv_at(h)),
-                    (kv_sib, kv_at(h)),
-                    (kv, kv_at(hc + h)),
-                    (kv_sib, kv_at(hc + h)),
-                    (mixed[of], block((tc, HEAD_DIM), lambda r, m, at=at: (r, at))),
-                    (lses[of], block((8, tc), lambda r, m, at=at: (at, r))),
+                    (kn, block((2 * tl, HEAD_DIM), lambda r, m, h=h: (0, h))),
+                    (knt, block((HEAD_DIM, 2 * tl), lambda r, m, h=h: (h, 0))),
+                    (vn, block((2 * tl, HEAD_DIM), lambda r, m, h=h: (0, h))),
+                    (mixed, block((tc, HEAD_DIM), lambda r, m, h=h: (r, h))),
+                    (lses, block((8, tc), lambda r, m, h=h: (h, r))),
                 ]
                 + [(g, block((tc, HEAD_DIM), lambda r, m, lane=lane: (0, lane))) for g in grads]
                 + ([(a, all_8) for a in back[-1][3:]] if h else []),
@@ -1302,9 +1289,6 @@
                 ],
                 grid=(groups,),
                 scratch=[
-                    pltpu.VMEM((2 * tl, HEAD_DIM), BF16),
-                    pltpu.VMEM((HEAD_DIM, 2 * tl), BF16),
-                    pltpu.VMEM((2 * tl, HEAD_DIM), BF16),
                     pltpu.VMEM((2 * tl, HEAD_DIM), F32),
                     pltpu.VMEM((2 * tl, HEAD_DIM), F32),
                     pltpu.VMEM((tc, HEAD_DIM), BF16),

time: 624 us -> 617 us (0.989)
  waiting for transfers between devices: 128 us -> 140 us
  starting transfers between devices: 136 us -> 126 us
    ppermute x92 -> x89, waiting for transfers between devices: 128 us -> 140 us  [send(): return jax.tree.map(lambda v: lax.ppermute(v, axis, pairs), values)]
    ppermute x92 -> x89, starting transfers between devices: 136 us -> 126 us  [send(): return jax.tree.map(lambda v: lax.ppermute(v, axis, pairs), values)]
    pallas_call x28 -> x27, Pallas kernels: 290 us -> 284 us  [run_kernel(): pl.pallas_call(reading, grid_spec=pltpu.PrefetchScalarGridSpec(num_scalar...]
    unnamed x168 -> x154, local copies, waits for them, and re-layouts: 16 us -> 13.9 us
  transfers between devices with their start and end apart: 92 -> 89, of which waited for: 30 -> 33; matrix products, arithmetic and copies ran while one was open for 6% -> 6% of each run, Pallas kernels for 43% -> 43%
where the time goes in v3:
time: 617 us; the launch traced here: 607 us
  Pallas kernels  284 us (46%)
  waiting for transfers between devices  140 us (23%)
  starting transfers between devices  126 us (20%)
  other arithmetic  28.2 us (5%)
  local copies, waits for them, and re-layouts  26.1 us (4%)
    pallas_call x27, Pallas kernels, run_kernel(): pl.pallas_call(reading, grid_spec=pltpu.PrefetchScalarGridSpec(num_scalar...  284 us
    ppermute x89, waiting for transfers between devices, send(): return jax.tree.map(lambda v: lax.ppermute(v, axis, pairs), values)  140 us
    ppermute x89, starting transfers between devices, send(): return jax.tree.map(lambda v: lax.ppermute(v, axis, pairs), values)  126 us
    unnamed x154, local copies, waits for them, and re-layouts  13.9 us
  transfers between devices with their start and end apart: 89, of which 33 were waited for; matrix products, arithmetic and copies ran while one was open for 6% of the time, Pallas kernels for 43%

profile of v3, /device:TPU:9, one launch (start us, length us, event | category | flops | bytes accessed | tf_op | source)
XLA Modules:
  0.0 607.5 jit_solution(154110305925477709)
XLA Ops:
  2.0 2.6 shard_map.392.refs_8_
  10.3 5.6 shard_map.393
  15.9 3.3 sine_multiply_fusion
  19.2 15.7 %shard_map.394 = (bf16[1024,1536]{1,0:T(8,128)(2,1)}, bf16[48,1024]{1,0:T(8,128)(2,1)}, bf16[1024,384]{1,0:T(8,128)(2,1)}, bf16[1024,384]{1,0:T(8,128)(2,1)}, bf...) custom-call(s32[12]{0:T(128)} %stack.104.meta_ref, ...), custom_call_target="tpu_custom_call" | custom-call | flops 17250000896 | bytes 18121472 | tf_op jit(solution)/shard_map/pallas_call | solution.py:85
  38.9 4.6 collective-permute-done.2.refs_1_
  43.5 2.7 collective-permute-done.3.refs_2_
  47.0 3.1 shard_map.395.refs_8_.refs_21_.refs_28_
  50.6 3.3 collective-permute-start.4
  62.9 25.3 %shard_map.396 = (bf16[256,384]{1,0:T(8,128)(2,1)}, bf16[256,384]{1,0:T(8,128)(2,1)}, bf16[256,384]{1,0:T(8,128)(2,1)}, bf16[256,384]{1,0:T(8,128)(2,1)}, bf16[1...) custom-call(s32[12]{0:T(128)} %stack.104.meta_ref, ...), custom_call_target="tpu_custom_call" | custom-call | flops 28750000128 | bytes 14352384 | tf_op jit(solution)/shard_map/pallas_call | solution.py:85
  88.2 8.8 %collective-permute-done.11.refs_10_.refs_17_ = bf16[576,384]{1,0:T(8,128)(2,1)} collective-permute-done((bf16[576,384]{1,0:T(8,128)(2,1)S(1)}, bf16[576,384]{1,0:T(8,128)(2,1)}, u32[]{:S(2)}, u32[]{:S(2)}) %collective-permute-start.11) | collective-permute-done | bytes 442400 | tf_op jit(solution)/shard_map/ppermute | solution.py:588
  96.9 3.7 collective-permute-done.12.refs_11_.refs_18_
  103.3 3.6 collective-permute-done.13.refs_1_
  106.8 10.9 %collective-permute-done.14.refs_2_ = bf16[256,384]{1,0:T(8,128)(2,1)S(1)} collective-permute-done((bf16[256,384]{1,0:T(8,128)(2,1)}, bf16[256,384]{1,0:T(8,128)(2,1)S(1)}, u32[]{:S(2)}, u32[]{:S(2)}) %collective-permute-start.14) | collective-permute-done | bytes 196640 | tf_op jit(solution)/shard_map/ppermute | solution.py:588
  125.9 2.3 collective-permute-done.19.refs_15_.refs_22_
  130.5 20.7 %shard_map.397 = (bf16[256,1536]{1,0:T(8,128)(2,1)}, f32[256,1536]{1,0:T(8,128)}, f32[256,1536]{1,0:T(8,128)}, bf16[256,1536]{1,0:T(8,128)(2,1)}, bf16[256,1536]...) custom-call(s32[12]{0:T(128)} %stack.104.meta_ref, ...), custom_call_target="tpu_custom_call" | custom-call | flops 23000000512 | bytes 35987456 | tf_op jit(solution)/shard_map/pallas_call | solution.py:85
  151.5 18.6 %shard_map.398 = (bf16[1024,1536]{1,0:T(8,128)(2,1)}, f32[256,1536]{1,0:T(8,128)}, f32[16,2240]{1,0:T(8,128)}, f32[16,1536]{1,0:T(8,128)}, f32[16,1536]{1,0:T(8,128)}, /*index=5*/f32[16,2240]{1,0:T(8,128)}) custom-call(s32[12]{0:T(128)} %stack.104.meta_ref, bf16[256,1536]{1,0:T(8,128)(2,1)} %get-tuple-element.255.refs_0_, bf16[1024,1536]{1,0:T(8,128)(2,1)} %bitcast.176, ...), custom_call_target="tpu_custom_call" | custom-call | flops 20700000256 | bytes 26510080 | tf_op jit(solution)/shard_map/pallas_call | solution.py:85
  170.4 3.3 collective-permute-start.27
  173.7 18.0 %shard_map.399 = (bf16[1024,1536]{1,0:T(8,128)(2,1)}, bf16[256,1536]{1,0:T(8,128)(2,1)}, f32[16,2240]{1,0:T(8,128)}, f32[16,1536]{1,0:T(8,128)}, f32[16,1536]{1,0:T(8,128)}, /*index=5*/f32[16,2240]{1,0:T(8,128)}) custom-call(s32[12]{0:T(128)} %stack.104.meta_ref, bf16[256,1536]{1,0:T(8,128)(2,1)} %copy-done.44, ...), custom_call_target="tpu_custom_call", output_to_operand_aliasing={{0}: (15, {})} | custom-call | flops 20700000256 | bytes 27779840 | tf_op jit(solution)/shard_map/pallas_call | solution.py:85
  194.3 17.9 %shard_map.400 = (bf16[1024,1536]{1,0:T(8,128)(2,1)}, bf16[256,1536]{1,0:T(8,128)(2,1)}, f32[16,2240]{1,0:T(8,128)}, f32[16,1536]{1,0:T(8,128)}, f32[16,1536]{1,0:T(8,128)}, /*index=5*/f32[16,2240]{1,0:T(8,128)}) custom-call(s32[12]{0:T(128)} %stack.104.meta_ref, bf16[256,1536]{1,0:T(8,128)(2,1)} %copy-done.40, ...), custom_call_target="tpu_custom_call", output_to_operand_aliasing={{0}: (15, {})} | custom-call | flops 20700000256 | bytes 27779840 | tf_op jit(solution)/shard_map/pallas_call | solution.py:85
  214.6 12.4 %collective-permute-done.28.refs_0_ = bf16[256,1536]{1,0:T(8,128)(2,1)S(1)} collective-permute-done((bf16[256,1536]{1,0:T(8,128)(2,1)S(1)}, bf16[256,1536]{1,0:T(8,128)(2,1)S(1)}, u32[]{:S(2)}, u32[]{:S(2)}) %collective-permute-start.28) | collective-permute-done | bytes 786464 | tf_op jit(solution)/shard_map/ppermute | solution.py:588
  227.8 18.1 %shard_map.401 = (bf16[1024,1536]{1,0:T(8,128)(2,1)}, bf16[256,1536]{1,0:T(8,128)(2,1)}, f32[16,2240]{1,0:T(8,128)}, f32[16,1536]{1,0:T(8,128)}, f32[16,1536]{1,0:T(8,128)}, /*index=5*/f32[16,2240]{1,0:T(8,128)}) custom-call(s32[12]{0:T(128)} %stack.104.meta_ref, bf16[256,1536]{1,0:T(8,128)(2,1)} %copy-done.43, ...), custom_call_target="tpu_custom_call", output_to_operand_aliasing={{0}: (15, {})} | custom-call | flops 20700000256 | bytes 27779840 | tf_op jit(solution)/shard_map/pallas_call | solution.py:85
  248.0 16.2 %collective-permute-done.31.refs_1_ = bf16[256,1536]{1,0:T(8,128)(2,1)S(1)} collective-permute-done((bf16[256,1536]{1,0:T(8,128)(2,1)S(1)}, bf16[256,1536]{1,0:T(8,128)(2,1)S(1)}, u32[]{:S(2)}, u32[]{:S(2)}) %collective-permute-start.31) | collective-permute-done | bytes 786464 | tf_op jit(solution)/shard_map/ppermute | solution.py:588
  264.3 2.6 fusion.52
  268.6 26.6 %shard_map.402 = (bf16[256,128]{1,0:T(8,128)(2,1)}, bf16[256,128]{1,0:T(8,128)(2,1)}, bf16[256,128]{1,0:T(8,128)(2,1)}, bf16[256,128]{1,0:T(8,128)(2,1)}, bf16[2...) custom-call(s32[12]{0:T(128)} %stack.104.meta_ref, ...), custom_call_target="tpu_custom_call" | custom-call | flops 29899999232 | bytes 42868736 | tf_op jit(solution)/shard_map/pallas_call | solution.py:85
  295.2 3.1 collective-permute-start.34
  302.0 5.0 collective-permute-start.40
  307.1 4.2 shard_map.406.refs_2_
  311.7 2.7 collective-permute-start.38
  317.7 11.0 %shard_map.403 = (f32[1024,128]{1,0:T(8,128)}, f32[1024,256]{1,0:T(8,128)}, bf16[1024,256]{1,0:T(8,128)(2,1)}, f32[8,1024]{1,0:T(8,128)}, f32[8,1024]{1,0:T(8,128)}) custom-call(s32[12]{0:T(128)} %stack.104.meta_ref, bf16[1024,384]{1,0:T(8,128)(2,1)} %get-tuple-element.298.refs_0_, f32[8,1024]{1,0:T(8,128)} %copy-done.15, f32[8,1024]{1,0:T(8,128)} %copy-done.15, ...), custom_call_target="tpu_custom_call" | custom-call | flops 14375000064 | bytes 8912896 | tf_op jit(solution)/shard_map/pallas_call | solution.py:85
  330.0 3.0 collective-permute-start.48
  333.0 10.9 %shard_map.404 = (f32[1024,128]{1,0:T(8,128)}, f32[1024,256]{1,0:T(8,128)}, bf16[1024,256]{1,0:T(8,128)(2,1)}, f32[8,1024]{1,0:T(8,128)}, f32[8,1024]{1,0:T(8,128)}) custom-call(s32[12]{0:T(128)} %stack.104.meta_ref, bf16[1024,384]{1,0:T(8,128)(2,1)} %get-tuple-element.298.refs_0_, f32[8,1024]{1,0:T(8,128)} %copy-done.15, f32[8,1024]{1,0:T(8,128)} %copy-done.15, ...), custom_call_target="tpu_custom_call" | custom-call | flops 14375000064 | bytes 9240576 | tf_op jit(solution)/shard_map/pallas_call | solution.py:85
  349.2 11.0 %shard_map.405 = (f32[1024,128]{1,0:T(8,128)}, f32[1024,256]{1,0:T(8,128)}, bf16[1024,256]{1,0:T(8,128)(2,1)}, f32[8,1024]{1,0:T(8,128)}, f32[8,1024]{1,0:T(8,128)}) custom-call(s32[12]{0:T(128)} %stack.104.meta_ref, bf16[1024,384]{1,0:T(8,128)(2,1)} %get-tuple-element.298.refs_0_, f32[8,1024]{1,0:T(8,128)} %copy-done.15, f32[8,1024]{1,0:T(8,128)} %copy-done.15, ...), custom_call_target="tpu_custom_call" | custom-call | flops 14375000064 | bytes 9240576 | tf_op jit(solution)/shard_map/pallas_call | solution.py:85
  360.8 3.2 collective-permute-done.46
  367.8 2.3 collective-permute-start.51
  372.9 4.8 shard_map.408
  379.5 2.3 collective-permute-start.57
  385.3 12.3 %shard_map.407 = (bf16[512,1536]{1,0:T(8,128)(2,1)}, f32[16,5760]{1,0:T(8,128)}) custom-call(s32[12]{0:T(128)} %stack.104.meta_ref, f32[1024,128]{1,0:T(8,128)} %get-tuple-element.326.refs_15_.refs_0_, f32[1024,128]{1,0:T(8,128)} %get-tuple-element.331.refs_15_.refs_1_, f32[1024,128]{1,0:T(8,128)} %get-tuple-element.332.refs_2_, ...), custom_call_target="tpu_custom_call" | custom-call | flops 16099999744 | bytes 25470464 | tf_op jit(solution)/shard_map/pallas_call | solution.py:85
  397.7 9.2 %collective-permute-done.55 = bf16[560,384]{1,0:T(8,128)(2,1)S(1)} collective-permute-done((bf16[560,384]{1,0:T(8,128)(2,1)S(1)}, bf16[560,384]{1,0:T(8,128)(2,1)S(1)}, u32[]{:S(2)}, u32[]{:S(2)}) %collective-permute-start.55) | collective-permute-done | bytes 430112 | tf_op jit(solution)/shard_map/ppermute | solution.py:588
  409.3 2.8 collective-permute-start.58
  412.4 5.1 shard_map.410
  418.9 3.0 collective-permute-start.61
  421.9 12.5 %shard_map.409 = (bf16[512,1536]{1,0:T(8,128)(2,1)}, f32[16,5760]{1,0:T(8,128)}) custom-call(s32[12]{0:T(128)} %stack.104.meta_ref, f32[1024,128]{1,0:T(8,128)} %get-tuple-element.326.refs_15_.refs_0_, f32[1024,128]{1,0:T(8,128)} %get-tuple-element.331.refs_15_.refs_1_, f32[1024,128]{1,0:T(8,128)} %get-tuple-element.332.refs_2_, ...), custom_call_target="tpu_custom_call" | custom-call | flops 16099999744 | bytes 25839104 | tf_op jit(solution)/shard_map/pallas_call | solution.py:85
  434.5 2.4 collective-permute-done.60.refs_0_
  436.9 2.7 collective-permute-done.61.refs_3_
  440.8 5.1 shard_map.411
  451.3 5.8 shard_map.412
  459.0 2.3 collective-permute-start.63
  467.9 5.3 shard_map.413
  481.3 2.3 collective-permute-done.67
  486.3 3.3 collective-permute-done.71.refs_0_
  489.7 2.8 collective-permute-done.72.refs_3_
  493.6 5.1 shard_map.414
  502.5 16.8 %collective-permute-done.74 = bf16[8,7680]{1,0:T(8,128)(2,1)S(1)} collective-permute-done((bf16[8,7680]{1,0:T(8,128)(2,1)S(1)}, bf16[8,7680]{1,0:T(8,128)(2,1)S(1)}, u32[]{:S(2)}, u32[]{:S(2)}) %collective-permute-start.74) | collective-permute-done | bytes 122912 | tf_op jit(solution)/shard_map/ppermute | solution.py:588
  521.9 5.0 shard_map.415
  527.5 2.9 collective-permute-start.80
  530.6 9.5 %collective-permute-done.79.refs_0_ = bf16[256,1536]{1,0:T(8,128)(2,1)S(1)} collective-permute-done((bf16[256,1536]{1,0:T(8,128)(2,1)}, bf16[256,1536]{1,0:T(8,128)(2,1)S(1)}, u32[]{:S(2)}, u32[]{:S(2)}) %collective-permute-start.79) | collective-permute-done | bytes 786464 | tf_op jit(solution)/shard_map/ppermute | solution.py:588
  540.1 4.9 collective-permute-done.80.refs_3_
  547.4 4.9 shard_map.416
  554.5 2.5 collective-permute-start.82
  558.3 10.1 %collective-permute-start.87 = (bf16[4,8,10880]{2,1,0:T(8,128)(2,1)}, bf16[4,8,10880]{2,1,0:T(8,128)(2,1)}, u32[]{:S(2)}, u32[]{:S(2)}) collective-permute-start(bf16[4,8,10880]{2,1,0:T(8,128)(2,1)} %pad_maximum_fusion.4), channel_id=1, source_target_pairs={{0,4},{4,0},{1,5},{5,1},{2,6},{6,2},{3,7},{7,3},{8,12},{12,8},{9,1... | collective-permute-start | bytes 2088968 | tf_op jit(solution)/shard_map/ppermute | solution.py:588
  568.7 4.7 shard_map.417
  579.9 9.3 %collective-permute-start.88 = (bf16[256,1536]{1,0:T(8,128)(2,1)S(1)}, bf16[256,1536]{1,0:T(8,128)(2,1)S(1)}, u32[]{:S(2)}, u32[]{:S(2)}) collective-permute-start(bf16[256,1536]{1,0:T(8,128)(2,1)S(1)} %pad_maximum_fusion.2), channel_id=1, source_target_pairs={{0,4},{4,0},{1,5},{5,1},{2,6},{6,2},{3,7},{7,3},{8,12},{12,8},{9,1... | collective-permute-start | bytes 2359304 | tf_op jit(solution)/shard_map/ppermute | solution.py:588
  592.7 2.6 copy.57
  600.6 4.2 shard_map.418
  (377 shorter events, 131.8 us)
Async XLA Ops:
  4.6 34.3 %collective-permute-start.1 = (bf16[144,1536]{1,0:T(8,128)(2,1)}, bf16[144,1536]{1,0:T(8,128)(2,1)S(1)}, u32[]{:S(2)}, u32[]{:S(2)}) collective-permute-start(bf16[144,1536]{1,0:T(8,128)(2,1)} %shard_map.392.refs_8_), channel_id=1, source_target_pairs={{0,1},{1,2},{2,3},{3,0},{4,5},{5,6},{6,7},{7,4},{8,9},{9,10},{10,1... | collective-permute-start | bytes 1327112 | tf_op jit(solution)/shard_map/ppermute | solution.py:588
  5.9 37.6 %collective-permute-start.2 = (bf16[144,1536]{1,0:T(8,128)(2,1)}, bf16[144,1536]{1,0:T(8,128)(2,1)S(1)}, u32[]{:S(2)}, u32[]{:S(2)}) collective-permute-start(bf16[144,1536]{1,0:T(8,128)(2,1)} %shard_map.392.refs_8_), channel_id=1, source_target_pairs={{0,2},{1,3},{2,0},{3,1},{4,6},{5,7},{6,4},{7,5},{8,10},{9,11},{10,... | collective-permute-start | bytes 1327112 | tf_op jit(solution)/shard_map/ppermute | solution.py:588
  6.9 39.3 %collective-permute-start.3 = (bf16[144,1536]{1,0:T(8,128)(2,1)}, bf16[144,1536]{1,0:T(8,128)(2,1)S(1)}, u32[]{:S(2)}, u32[]{:S(2)}) collective-permute-start(bf16[144,1536]{1,0:T(8,128)(2,1)} %shard_map.392.refs_8_), channel_id=1, source_target_pairs={{0,3},{1,0},{2,1},{3,2},{4,7},{5,4},{6,5},{7,6},{8,11},{9,8},{10,9... | collective-permute-start | bytes 1327112 | tf_op jit(solution)/shard_map/ppermute | solution.py:588
  36.0 23.6 %collective-permute-start.7 = (bf16[1024,768]{1,0:T(8,128)(2,1)}, bf16[1024,768]{1,0:T(8,128)(2,1)S(1)}, u32[]{:S(2)}, u32[]{:S(2)}) collective-permute-start(bf16[1024,768]{1,0:T(8,128)(2,1)} %get-tuple-element.226.refs_4_.refs_6_), channel_id=1, source_target_pairs={{0,4},{4,0},{1,5},{5,1},{2,6},{6,2},{3,7},{7,3},{8,12},{12,8},{9,1... | collective-permute-start | bytes 4718600 | tf_op jit(solution)/shard_map/ppermute | solution.py:588
  50.1 11.4 %collective-permute-start.6 = (bf16[3,144,1536]{2,1,0:T(8,128)(2,1)}, bf16[3,144,1536]{2,1,0:T(8,128)(2,1)S(1)}, u32[]{:S(2)}, u32[]{:S(2)}) collective-permute-start(bf16[3,144,1536]{2,1,0:T(8,128)(2,1)} %shard_map.395.refs_8_.refs_21_.refs_28_), channel_id=1, source_target_pairs={{0,4},{4,0},{1,5},{5,1},{2,6},{6,2},{3,7},{7,3},{8,12},{12,8},{9,1... | collective-permute-start | bytes 3981320 | tf_op jit(solution)/shard_map/ppermute | solution.py:588
  56.4 44.2 %collective-permute-start.8 = (bf16[3,144,1536]{2,1,0:T(8,128)(2,1)}, bf16[3,144,1536]{2,1,0:T(8,128)(2,1)S(1)}, u32[]{:S(2)}, u32[]{:S(2)}) collective-permute-start(bf16[3,144,1536]{2,1,0:T(8,128)(2,1)} %shard_map.395.refs_8_.refs_21_.refs_28_), channel_id=1, source_target_pairs={{0,8},{8,0},{16,24},{24,16},{1,9},{9,1},{17,25},{25,17},{2,10},{10... | collective-permute-start | bytes 3981320 | tf_op jit(solution)/shard_map/ppermute | solution.py:588
  57.6 43.0 %collective-permute-start.9 = (bf16[3,144,1536]{2,1,0:T(8,128)(2,1)}, bf16[3,144,1536]{2,1,0:T(8,128)(2,1)S(1)}, u32[]{:S(2)}, u32[]{:S(2)}) collective-permute-start(bf16[3,144,1536]{2,1,0:T(8,128)(2,1)} %shard_map.395.refs_8_.refs_21_.refs_28_), channel_id=1, source_target_pairs={{0,16},{8,24},{16,0},{24,8},{1,17},{9,25},{17,1},{25,9},{2,18},{10... | collective-permute-start | bytes 3981320 | tf_op jit(solution)/shard_map/ppermute | solution.py:588
  58.8 29.3 %collective-permute-start.10 = (bf16[576,384]{1,0:T(8,128)(2,1)S(1)}, bf16[576,384]{1,0:T(8,128)(2,1)}, u32[]{:S(2)}, u32[]{:S(2)}) collective-permute-start(bf16[576,384]{1,0:T(8,128)(2,1)S(1)} %copy-done.50), channel_id=1, source_target_pairs={{0,1},{1,2},{2,3},{3,0},{4,5},{5,6},{6,7},{7,4},{8,9},{9,10},{10,1... | collective-permute-start | bytes 1327112 | tf_op jit(solution)/shard_map/ppermute | solution.py:588
  59.6 37.3 %collective-permute-start.11 = (bf16[576,384]{1,0:T(8,128)(2,1)S(1)}, bf16[576,384]{1,0:T(8,128)(2,1)}, u32[]{:S(2)}, u32[]{:S(2)}) collective-permute-start(bf16[576,384]{1,0:T(8,128)(2,1)S(1)} %copy-done.50), channel_id=1, source_target_pairs={{0,2},{1,3},{2,0},{3,1},{4,6},{5,7},{6,4},{7,5},{8,10},{9,11},{10,... | collective-permute-start | bytes 1327112 | tf_op jit(solution)/shard_map/ppermute | solution.py:588
  61.5 39.1 %collective-permute-start.12 = (bf16[576,384]{1,0:T(8,128)(2,1)S(1)}, bf16[576,384]{1,0:T(8,128)(2,1)}, u32[]{:S(2)}, u32[]{:S(2)}) collective-permute-start(bf16[576,384]{1,0:T(8,128)(2,1)S(1)} %copy-done.50), channel_id=1, source_target_pairs={{0,3},{1,0},{2,1},{3,2},{4,7},{5,4},{6,5},{7,6},{8,11},{9,8},{10,9... | collective-permute-start | bytes 1327112 | tf_op jit(solution)/shard_map/ppermute | solution.py:588
  100.6 19.1 %collective-permute-start.21 = (bf16[3,64,1536]{2,1,0:T(8,128)(2,1)S(1)}, bf16[3,64,1536]{2,1,0:T(8,128)(2,1)S(1)}, u32[]{:S(2)}, u32[]{:S(2)}) collective-permute-start(bf16[3,64,1536]{2,1,0:T(8,128)(2,1)S(1)} %slice.231), channel_id=1, source_target_pairs={{0,16},{8,24},{16,0},{24,8},{1,17},{9,25},{17,1},{25,9},{2,18},{10... | collective-permute-start | bytes 1769480 | tf_op jit(solution)/shard_map/ppermute | solution.py:588
  100.9 16.7 %collective-permute-start.14 = (bf16[256,384]{1,0:T(8,128)(2,1)}, bf16[256,384]{1,0:T(8,128)(2,1)S(1)}, u32[]{:S(2)}, u32[]{:S(2)}) collective-permute-start(bf16[256,384]{1,0:T(8,128)(2,1)} %get-tuple-element.237), channel_id=1, source_target_pairs={{0,2},{1,3},{2,0},{3,1},{4,6},{5,7},{6,4},{7,5},{8,10},{9,11},{10,... | collective-permute-start | bytes 589832 | tf_op jit(solution)/shard_map/ppermute | solution.py:588
  100.9 17.8 %collective-permute-start.15 = (bf16[256,384]{1,0:T(8,128)(2,1)}, bf16[256,384]{1,0:T(8,128)(2,1)S(1)}, u32[]{:S(2)}, u32[]{:S(2)}) collective-permute-start(bf16[256,384]{1,0:T(8,128)(2,1)} %get-tuple-element.238), channel_id=1, source_target_pairs={{0,3},{1,0},{2,1},{3,2},{4,7},{5,4},{6,5},{7,6},{8,11},{9,8},{10,9... | collective-permute-start | bytes 589832 | tf_op jit(solution)/shard_map/ppermute | solution.py:588
  102.6 19.0 %collective-permute-start.20 = (bf16[3,80,1536]{2,1,0:T(8,128)(2,1)S(1)}, bf16[3,80,1536]{2,1,0:T(8,128)(2,1)S(1)}, u32[]{:S(2)}, u32[]{:S(2)}) collective-permute-start(bf16[3,80,1536]{2,1,0:T(8,128)(2,1)S(1)} %slice.230), channel_id=1, source_target_pairs={{0,8},{8,0},{16,24},{24,16},{1,9},{9,1},{17,25},{25,17},{2,10},{10... | collective-permute-start | bytes 2211848 | tf_op jit(solution)/shard_map/ppermute | solution.py:588
  151.2 19.2 %collective-permute-start.26 = (bf16[256,1536]{1,0:T(8,128)(2,1)}, bf16[256,1536]{1,0:T(8,128)(2,1)S(1)}, u32[]{:S(2)}, u32[]{:S(2)}) collective-permute-start(bf16[256,1536]{1,0:T(8,128)(2,1)} %get-tuple-element.255.refs_0_), channel_id=1, source_target_pairs={{0,1},{1,2},{2,3},{3,0},{4,5},{5,6},{6,7},{7,4},{8,9},{9,10},{10,1... | collective-permute-start | bytes 2359304 | tf_op jit(solution)/shard_map/ppermute | solution.py:588
  170.4 21.7 %collective-permute-start.27 = (bf16[256,1536]{1,0:T(8,128)(2,1)S(1)}, bf16[256,1536]{1,0:T(8,128)(2,1)S(1)}, u32[]{:S(2)}, u32[]{:S(2)}) collective-permute-start(bf16[256,1536]{1,0:T(8,128)(2,1)S(1)} %collective-permute-done.26.refs_0_), channel_id=1, source_target_pairs={{0,1},{1,2},{2,3},{3,0},{4,5},{5,6},{6,7},{7,4},{8,9},{9,10},{10,1... | collective-permute-start | bytes 2359304 | tf_op jit(solution)/shard_map/ppermute | solution.py:588
  191.7 20.5 %collective-permute-start.29 = (bf16[256,1536]{1,0:T(8,128)(2,1)}, bf16[256,1536]{1,0:T(8,128)(2,1)S(1)}, u32[]{:S(2)}, u32[]{:S(2)}) collective-permute-start(bf16[256,1536]{1,0:T(8,128)(2,1)} %get-tuple-element.274), channel_id=1, source_target_pairs={{0,1},{1,2},{2,3},{3,0},{4,5},{5,6},{6,7},{7,4},{8,9},{9,10},{10,1... | collective-permute-start | bytes 2359304 | tf_op jit(solution)/shard_map/ppermute | solution.py:588
  192.2 34.8 %collective-permute-start.28 = (bf16[256,1536]{1,0:T(8,128)(2,1)S(1)}, bf16[256,1536]{1,0:T(8,128)(2,1)S(1)}, u32[]{:S(2)}, u32[]{:S(2)}) collective-permute-start(bf16[256,1536]{1,0:T(8,128)(2,1)S(1)} %collective-permute-done.27.refs_0_), channel_id=1, source_target_pairs={{0,1},{1,2},{2,3},{3,0},{4,5},{5,6},{6,7},{7,4},{8,9},{9,10},{10,1... | collective-permute-start | bytes 2359304 | tf_op jit(solution)/shard_map/ppermute | solution.py:588
  213.6 32.3 %collective-permute-start.30 = (bf16[256,1536]{1,0:T(8,128)(2,1)S(1)}, bf16[256,1536]{1,0:T(8,128)(2,1)S(1)}, u32[]{:S(2)}, u32[]{:S(2)}) collective-permute-start(bf16[256,1536]{1,0:T(8,128)(2,1)S(1)} %add_convert_fusion.1), channel_id=1, source_target_pairs={{0,1},{1,2},{2,3},{3,0},{4,5},{5,6},{6,7},{7,4},{8,9},{9,10},{10,1... | collective-permute-start | bytes 2359304 | tf_op jit(solution)/shard_map/ppermute | solution.py:588
  247.2 17.0 %collective-permute-start.31 = (bf16[256,1536]{1,0:T(8,128)(2,1)S(1)}, bf16[256,1536]{1,0:T(8,128)(2,1)S(1)}, u32[]{:S(2)}, u32[]{:S(2)}) collective-permute-start(bf16[256,1536]{1,0:T(8,128)(2,1)S(1)} %add_convert_fusion), channel_id=1, source_target_pairs={{0,1},{1,2},{2,3},{3,0},{4,5},{5,6},{6,7},{7,4},{8,9},{9,10},{10,1... | collective-permute-start | bytes 2359304 | tf_op jit(solution)/shard_map/ppermute | solution.py:588
  266.9 33.8 %collective-permute-start.32 = (bf16[256,1536]{1,0:T(8,128)(2,1)S(1)}, bf16[256,1536]{1,0:T(8,128)(2,1)S(1)}, u32[]{:S(2)}, u32[]{:S(2)}) collective-permute-start(bf16[256,1536]{1,0:T(8,128)(2,1)S(1)} %get-tuple-element.452), channel_id=1, source_target_pairs={{0,1},{3,2},{4,5},{7,6},{8,9},{11,10},{12,13},{15,14},{16,17},{19,... | collective-permute-start | bytes 2359304 | tf_op jit(solution)/shard_map/ppermute | solution.py:588
  295.2 16.4 %collective-permute-start.34 = (bf16[256,128]{1,0:T(8,128)(2,1)}, bf16[256,128]{1,0:T(8,128)(2,1)S(1)}, u32[]{:S(2)}, u32[]{:S(2)}) collective-permute-start(bf16[256,128]{1,0:T(8,128)(2,1)} %get-tuple-element.293), channel_id=1, source_target_pairs={{0,3},{1,0},{2,1},{3,2},{4,7},{5,4},{6,5},{7,6},{8,11},{9,8},{10,9... | collective-permute-start | bytes 196616 | tf_op jit(solution)/shard_map/ppermute | solution.py:588
  298.3 16.1 %collective-permute-start.35 = (bf16[256,128]{1,0:T(8,128)(2,1)}, bf16[256,128]{1,0:T(8,128)(2,1)S(1)}, u32[]{:S(2)}, u32[]{:S(2)}) collective-permute-start(bf16[256,128]{1,0:T(8,128)(2,1)} %get-tuple-element.294), channel_id=1, source_target_pairs={{0,2},{1,3},{2,0},{3,1},{4,6},{5,7},{6,4},{7,5},{8,10},{9,11},{10,... | collective-permute-start | bytes 196616 | tf_op jit(solution)/shard_map/ppermute | solution.py:588
  298.3 16.7 %collective-permute-start.36 = (bf16[256,128]{1,0:T(8,128)(2,1)}, bf16[256,128]{1,0:T(8,128)(2,1)}, u32[]{:S(2)}, u32[]{:S(2)}) collective-permute-start(bf16[256,128]{1,0:T(8,128)(2,1)} %get-tuple-element.295), channel_id=1, source_target_pairs={{0,1},{1,2},{2,3},{3,0},{4,5},{5,6},{6,7},{7,4},{8,9},{9,10},{10,1... | collective-permute-start | bytes 196616 | tf_op jit(solution)/shard_map/ppermute | solution.py:588
  299.6 29.1 %collective-permute-start.37 = (bf16[256,256]{1,0:T(8,128)(2,1)}, bf16[256,256]{1,0:T(8,128)(2,1)S(1)}, u32[]{:S(2)}, u32[]{:S(2)}) collective-permute-start(bf16[256,256]{1,0:T(8,128)(2,1)} %get-tuple-element.310), channel_id=1, source_target_pairs={{0,3},{1,0},{2,1},{3,2},{4,7},{5,4},{6,5},{7,6},{8,11},{9,8},{10,9... | collective-permute-start | bytes 393224 | tf_op jit(solution)/shard_map/ppermute | solution.py:588
  311.7 18.3 %collective-permute-start.38 = (bf16[256,256]{1,0:T(8,128)(2,1)}, bf16[256,256]{1,0:T(8,128)(2,1)S(1)}, u32[]{:S(2)}, u32[]{:S(2)}) collective-permute-start(bf16[256,256]{1,0:T(8,128)(2,1)} %get-tuple-element.311), channel_id=1, source_target_pairs={{0,2},{1,3},{2,0},{3,1},{4,6},{5,7},{6,4},{7,5},{8,10},{9,11},{10,... | collective-permute-start | bytes 393224 | tf_op jit(solution)/shard_map/ppermute | solution.py:588
  314.4 18.6 %collective-permute-start.39 = (bf16[256,256]{1,0:T(8,128)(2,1)S(1)}, bf16[256,256]{1,0:T(8,128)(2,1)}, u32[]{:S(2)}, u32[]{:S(2)}) collective-permute-start(bf16[256,256]{1,0:T(8,128)(2,1)S(1)} %copy-done.62), channel_id=1, source_target_pairs={{0,1},{1,2},{2,3},{3,0},{4,5},{5,6},{6,7},{7,4},{8,9},{9,10},{10,1... | collective-permute-start | bytes 393224 | tf_op jit(solution)/shard_map/ppermute | solution.py:588
  315.0 17.9 %collective-permute-start.41 = (bf16[8,7680]{1,0:T(8,128)(2,1)S(1)}, bf16[8,7680]{1,0:T(8,128)(2,1)S(1)}, u32[]{:S(2)}, u32[]{:S(2)}) collective-permute-start(bf16[8,7680]{1,0:T(8,128)(2,1)S(1)} %slice.300), channel_id=1, source_target_pairs={{0,1},{1,0},{2,3},{3,2},{4,5},{5,4},{6,7},{7,6},{8,9},{9,8},{10,11... | collective-permute-start | bytes 368648 | tf_op jit(solution)/shard_map/ppermute | solution.py:588
  316.9 16.1 %collective-permute-start.42 = (bf16[560,384]{1,0:T(8,128)(2,1)S(1)}, bf16[560,384]{1,0:T(8,128)(2,1)S(1)}, u32[]{:S(2)}, u32[]{:S(2)}) collective-permute-start(bf16[560,384]{1,0:T(8,128)(2,1)S(1)} %fusion.19), channel_id=1, source_target_pairs={{0,1},{1,2},{2,3},{3,0},{4,5},{5,6},{6,7},{7,4},{8,9},{9,10},{10,1... | collective-permute-start | bytes 1290248 | tf_op jit(solution)/shard_map/ppermute | solution.py:588
  328.7 31.5 %collective-permute-start.47 = (bf16[256,1536]{1,0:T(8,128)(2,1)S(1)}, bf16[256,1536]{1,0:T(8,128)(2,1)}, u32[]{:S(2)}, u32[]{:S(2)}) collective-permute-start(bf16[256,1536]{1,0:T(8,128)(2,1)S(1)} %copy-done.7), channel_id=1, source_target_pairs={{0,1},{3,2},{4,5},{7,6},{8,9},{11,10},{12,13},{15,14},{16,17},{19,... | collective-permute-start | bytes 2359304 | tf_op jit(solution)/shard_map/ppermute | solution.py:588
  330.0 30.8 %collective-permute-start.48 = (bf16[256,1536]{1,0:T(8,128)(2,1)}, bf16[256,1536]{1,0:T(8,128)(2,1)}, u32[]{:S(2)}, u32[]{:S(2)}) collective-permute-start(bf16[256,1536]{1,0:T(8,128)(2,1)} %shard_map.406.refs_2_), channel_id=1, source_target_pairs={{1,2},{2,1},{5,6},{6,5},{9,10},{10,9},{13,14},{14,13},{17,18},{18,... | collective-permute-start | bytes 2359304 | tf_op jit(solution)/shard_map/ppermute | solution.py:588
  344.0 38.8 %collective-permute-start.43 = (bf16[1024,256]{1,0:T(8,128)(2,1)}, bf16[1024,256]{1,0:T(8,128)(2,1)}, u32[]{:S(2)}, u32[]{:S(2)}) collective-permute-start(bf16[1024,256]{1,0:T(8,128)(2,1)} %get-tuple-element.336), channel_id=1, source_target_pairs={{0,4},{4,0},{1,5},{5,1},{2,6},{6,2},{3,7},{7,3},{8,12},{12,8},{9,1... | collective-permute-start | bytes 1572872 | tf_op jit(solution)/shard_map/ppermute | solution.py:588
  345.2 15.6 %collective-permute-start.45 = (bf16[8,7680]{1,0:T(8,128)(2,1)S(1)}, bf16[8,7680]{1,0:T(8,128)(2,1)S(1)}, u32[]{:S(2)}, u32[]{:S(2)}) collective-permute-start(bf16[8,7680]{1,0:T(8,128)(2,1)S(1)} %add_convert_fusion.10), channel_id=1, source_target_pairs={{0,2},{1,3},{2,0},{3,1},{4,6},{5,7},{6,4},{7,5},{8,10},{9,11},{10,... | collective-permute-start | bytes 368648 | tf_op jit(solution)/shard_map/ppermute | solution.py:588
  347.3 16.8 %collective-permute-start.46 = (bf16[560,384]{1,0:T(8,128)(2,1)S(1)}, bf16[560,384]{1,0:T(8,128)(2,1)S(1)}, u32[]{:S(2)}, u32[]{:S(2)}) collective-permute-start(bf16[560,384]{1,0:T(8,128)(2,1)S(1)} %fusion.3), channel_id=1, source_target_pairs={{0,1},{1,2},{2,3},{3,0},{4,5},{5,6},{6,7},{7,4},{8,9},{9,10},{10,1... | collective-permute-start | bytes 1290248 | tf_op jit(solution)/shard_map/ppermute | solution.py:588
  360.2 23.9 %collective-permute-start.44 = (bf16[1024,256]{1,0:T(8,128)(2,1)}, bf16[1024,256]{1,0:T(8,128)(2,1)S(1)}, u32[]{:S(2)}, u32[]{:S(2)}) collective-permute-start(bf16[1024,256]{1,0:T(8,128)(2,1)} %get-tuple-element.337), channel_id=1, source_target_pairs={{0,4},{4,0},{1,5},{5,1},{2,6},{6,2},{3,7},{7,3},{8,12},{12,8},{9,1... | collective-permute-start | bytes 1572872 | tf_op jit(solution)/shard_map/ppermute | solution.py:588
  364.1 21.3 %collective-permute-start.49 = (bf16[1024,256]{1,0:T(8,128)(2,1)}, bf16[1024,256]{1,0:T(8,128)(2,1)}, u32[]{:S(2)}, u32[]{:S(2)}) collective-permute-start(bf16[1024,256]{1,0:T(8,128)(2,1)} %get-tuple-element.344), channel_id=1, source_target_pairs={{0,4},{4,0},{1,5},{5,1},{2,6},{6,2},{3,7},{7,3},{8,12},{12,8},{9,1... | collective-permute-start | bytes 1572872 | tf_op jit(solution)/shard_map/ppermute | solution.py:588
  377.7 29.1 %collective-permute-start.56 = (bf16[256,1536]{1,0:T(8,128)(2,1)}, bf16[256,1536]{1,0:T(8,128)(2,1)}, u32[]{:S(2)}, u32[]{:S(2)}) collective-permute-start(bf16[256,1536]{1,0:T(8,128)(2,1)} %get-tuple-element.360.refs_5_), channel_id=1, source_target_pairs={{0,1},{3,2},{1,0},{2,3},{4,5},{7,6},{5,4},{6,7},{8,9},{11,10},{9,8... | collective-permute-start | bytes 2359304 | tf_op jit(solution)/shard_map/ppermute | solution.py:588
  379.5 28.6 %collective-permute-start.57 = (bf16[256,1536]{1,0:T(8,128)(2,1)}, bf16[256,1536]{1,0:T(8,128)(2,1)}, u32[]{:S(2)}, u32[]{:S(2)}) collective-permute-start(bf16[256,1536]{1,0:T(8,128)(2,1)} %get-tuple-element.361.refs_2_), channel_id=1, source_target_pairs={{1,2},{2,1},{5,6},{6,5},{9,10},{10,9},{13,14},{14,13},{17,18},{18,... | collective-permute-start | bytes 2359304 | tf_op jit(solution)/shard_map/ppermute | solution.py:588
  382.8 14.9 %collective-permute-start.54 = (bf16[2,8,12160]{2,1,0:T(8,128)(2,1)}, bf16[2,8,12160]{2,1,0:T(8,128)(2,1)S(1)}, u32[]{:S(2)}, u32[]{:S(2)}) collective-permute-start(bf16[2,8,12160]{2,1,0:T(8,128)(2,1)} %pad_maximum_fusion.7), channel_id=1, source_target_pairs={{0,16},{8,24},{16,0},{24,8},{1,17},{9,25},{17,1},{25,9},{2,18},{10... | collective-permute-start | bytes 1167368 | tf_op jit(solution)/shard_map/ppermute | solution.py:588
  384.1 22.7 %collective-permute-start.55 = (bf16[560,384]{1,0:T(8,128)(2,1)S(1)}, bf16[560,384]{1,0:T(8,128)(2,1)S(1)}, u32[]{:S(2)}, u32[]{:S(2)}) collective-permute-start(bf16[560,384]{1,0:T(8,128)(2,1)S(1)} %fusion.11), channel_id=1, source_target_pairs={{0,1},{1,2},{2,3},{3,0},{4,5},{5,6},{6,7},{7,4},{8,9},{9,10},{10,1... | collective-permute-start | bytes 1290248 | tf_op jit(solution)/shard_map/ppermute | solution.py:588
  409.3 25.1 %collective-permute-start.58 = (bf16[4,8,12160]{2,1,0:T(8,128)(2,1)S(1)}, bf16[4,8,12160]{2,1,0:T(8,128)(2,1)S(1)}, u32[]{:S(2)}, u32[]{:S(2)}) collective-permute-start(bf16[4,8,12160]{2,1,0:T(8,128)(2,1)S(1)} %pad_maximum_fusion.3), channel_id=1, source_target_pairs={{0,4},{4,0},{1,5},{5,1},{2,6},{6,2},{3,7},{7,3},{8,12},{12,8},{9,1... | collective-permute-start | bytes 2334728 | tf_op jit(solution)/shard_map/ppermute | solution.py:588
  412.4 22.1 %collective-permute-start.59 = (f32[512]{0:T(512)S(1)}, f32[512]{0:T(512)S(1)}, u32[]{:S(2)}, u32[]{:S(2)}) collective-permute-start(f32[512]{0:T(512)S(1)} %multiply_reduce_fusion), channel_id=1, source_target_pairs={{0,1},{1,0},{2,3},{3,2},{4,5},{5,4},{6,7},{7,6},{8,9},{9,8},{10,11... | collective-permute-start | bytes 6152 | tf_op jit(solution)/shard_map/ppermute | solution.py:588
  417.5 19.4 %collective-permute-start.60 = (bf16[256,1536]{1,0:T(8,128)(2,1)}, bf16[256,1536]{1,0:T(8,128)(2,1)S(1)}, u32[]{:S(2)}, u32[]{:S(2)}) collective-permute-start(bf16[256,1536]{1,0:T(8,128)(2,1)} %get-tuple-element.369.refs_5_), channel_id=1, source_target_pairs={{0,1},{3,2},{1,0},{2,3},{4,5},{7,6},{5,4},{6,7},{8,9},{11,10},{9,8... | collective-permute-start | bytes 2359304 | tf_op jit(solution)/shard_map/ppermute | solution.py:588
  418.9 20.6 %collective-permute-start.61 = (bf16[256,1536]{1,0:T(8,128)(2,1)}, bf16[256,1536]{1,0:T(8,128)(2,1)S(1)}, u32[]{:S(2)}, u32[]{:S(2)}) collective-permute-start(bf16[256,1536]{1,0:T(8,128)(2,1)} %get-tuple-element.370.refs_2_), channel_id=1, source_target_pairs={{1,2},{2,1},{5,6},{6,5},{9,10},{10,9},{13,14},{14,13},{17,18},{18,... | collective-permute-start | bytes 2359304 | tf_op jit(solution)/shard_map/ppermute | solution.py:588
  445.8 19.7 %collective-permute-start.65 = (bf16[256,1536]{1,0:T(8,128)(2,1)}, bf16[256,1536]{1,0:T(8,128)(2,1)}, u32[]{:S(2)}, u32[]{:S(2)}) collective-permute-start(bf16[256,1536]{1,0:T(8,128)(2,1)} %get-tuple-element.381.refs_5_), channel_id=1, source_target_pairs={{0,1},{3,2},{1,0},{2,3},{4,5},{7,6},{5,4},{6,7},{8,9},{11,10},{9,8... | collective-permute-start | bytes 2359304 | tf_op jit(solution)/shard_map/ppermute | solution.py:588
  448.0 19.2 %collective-permute-start.66 = (bf16[256,1536]{1,0:T(8,128)(2,1)}, bf16[256,1536]{1,0:T(8,128)(2,1)}, u32[]{:S(2)}, u32[]{:S(2)}) collective-permute-start(bf16[256,1536]{1,0:T(8,128)(2,1)} %get-tuple-element.376.refs_6_.refs_2_), channel_id=1, source_target_pairs={{1,2},{2,1},{5,6},{6,5},{9,10},{10,9},{13,14},{14,13},{17,18},{18,... | collective-permute-start | bytes 2359304 | tf_op jit(solution)/shard_map/ppermute | solution.py:588
  467.9 12.2 %collective-permute-start.70 = (bf16[8,7680]{1,0:T(8,128)(2,1)}, bf16[8,7680]{1,0:T(8,128)(2,1)S(1)}, u32[]{:S(2)}, u32[]{:S(2)}) collective-permute-start(bf16[8,7680]{1,0:T(8,128)(2,1)} %slice.312), channel_id=1, source_target_pairs={{0,1},{1,0},{2,3},{3,2},{4,5},{5,4},{6,7},{7,6},{8,9},{9,8},{10,11... | collective-permute-start | bytes 368648 | tf_op jit(solution)/shard_map/ppermute | solution.py:588
  473.2 16.4 %collective-permute-start.71 = (bf16[256,1536]{1,0:T(8,128)(2,1)}, bf16[256,1536]{1,0:T(8,128)(2,1)}, u32[]{:S(2)}, u32[]{:S(2)}) collective-permute-start(bf16[256,1536]{1,0:T(8,128)(2,1)} %get-tuple-element.387.refs_5_), channel_id=1, source_target_pairs={{0,1},{3,2},{1,0},{2,3},{4,5},{7,6},{5,4},{6,7},{8,9},{11,10},{9,8... | collective-permute-start | bytes 2359304 | tf_op jit(solution)/shard_map/ppermute | solution.py:588
  474.7 17.8 %collective-permute-start.72 = (bf16[256,1536]{1,0:T(8,128)(2,1)}, bf16[256,1536]{1,0:T(8,128)(2,1)}, u32[]{:S(2)}, u32[]{:S(2)}) collective-permute-start(bf16[256,1536]{1,0:T(8,128)(2,1)} %get-tuple-element.388.refs_2_), channel_id=1, source_target_pairs={{1,2},{2,1},{5,6},{6,5},{9,10},{10,9},{13,14},{14,13},{17,18},{18,... | collective-permute-start | bytes 2359304 | tf_op jit(solution)/shard_map/ppermute | solution.py:588
  493.5 25.8 %collective-permute-start.73 = (bf16[64,1536]{1,0:T(8,128)(2,1)S(1)}, bf16[64,1536]{1,0:T(8,128)(2,1)S(1)}, u32[]{:S(2)}, u32[]{:S(2)}) collective-permute-start(bf16[64,1536]{1,0:T(8,128)(2,1)S(1)} %add_convert_fusion.4), channel_id=1, source_target_pairs={{0,1},{1,0},{2,3},{3,2},{4,5},{5,4},{6,7},{7,6},{8,9},{9,8},{10,11... | collective-permute-start | bytes 589832 | tf_op jit(solution)/shard_map/ppermute | solution.py:588
  498.6 20.7 %collective-permute-start.75 = (bf16[256,1536]{1,0:T(8,128)(2,1)}, bf16[256,1536]{1,0:T(8,128)(2,1)S(1)}, u32[]{:S(2)}, u32[]{:S(2)}) collective-permute-start(bf16[256,1536]{1,0:T(8,128)(2,1)} %get-tuple-element.398.refs_5_), channel_id=1, source_target_pairs={{0,1},{3,2},{1,0},{2,3},{4,5},{7,6},{5,4},{6,7},{8,9},{11,10},{9,8... | collective-permute-start | bytes 2359304 | tf_op jit(solution)/shard_map/ppermute | solution.py:588
  500.1 19.2 %collective-permute-start.76 = (bf16[256,1536]{1,0:T(8,128)(2,1)}, bf16[256,1536]{1,0:T(8,128)(2,1)S(1)}, u32[]{:S(2)}, u32[]{:S(2)}) collective-permute-start(bf16[256,1536]{1,0:T(8,128)(2,1)} %get-tuple-element.399.refs_2_), channel_id=1, source_target_pairs={{1,2},{2,1},{5,6},{6,5},{9,10},{10,9},{13,14},{14,13},{17,18},{18,... | collective-permute-start | bytes 2359304 | tf_op jit(solution)/shard_map/ppermute | solution.py:588
  502.4 16.9 %collective-permute-start.74 = (bf16[8,7680]{1,0:T(8,128)(2,1)S(1)}, bf16[8,7680]{1,0:T(8,128)(2,1)S(1)}, u32[]{:S(2)}, u32[]{:S(2)}) collective-permute-start(bf16[8,7680]{1,0:T(8,128)(2,1)S(1)} %add_convert_fusion.8), channel_id=1, source_target_pairs={{0,2},{1,3},{2,0},{3,1},{4,6},{5,7},{6,4},{7,5},{8,10},{9,11},{10,... | collective-permute-start | bytes 368648 | tf_op jit(solution)/shard_map/ppermute | solution.py:588
  519.3 11.2 %collective-permute-start.77 = (bf16[64,1536]{1,0:T(8,128)(2,1)S(1)}, bf16[64,1536]{1,0:T(8,128)(2,1)S(1)}, u32[]{:S(2)}, u32[]{:S(2)}) collective-permute-start(bf16[64,1536]{1,0:T(8,128)(2,1)S(1)} %add_convert_fusion.3), channel_id=1, source_target_pairs={{0,2},{1,3},{2,0},{3,1},{4,6},{5,7},{6,4},{7,5},{8,10},{9,11},{10,... | collective-permute-start | bytes 589832 | tf_op jit(solution)/shard_map/ppermute | solution.py:588
  527.0 13.2 %collective-permute-start.79 = (bf16[256,1536]{1,0:T(8,128)(2,1)}, bf16[256,1536]{1,0:T(8,128)(2,1)S(1)}, u32[]{:S(2)}, u32[]{:S(2)}) collective-permute-start(bf16[256,1536]{1,0:T(8,128)(2,1)} %get-tuple-element.404.refs_4_), channel_id=1, source_target_pairs={{0,1},{3,2},{1,0},{2,3},{4,5},{7,6},{5,4},{6,7},{8,9},{11,10},{9,8... | collective-permute-start | bytes 2359304 | tf_op jit(solution)/shard_map/ppermute | solution.py:588
  527.5 17.6 %collective-permute-start.80 = (bf16[256,1536]{1,0:T(8,128)(2,1)}, bf16[256,1536]{1,0:T(8,128)(2,1)S(1)}, u32[]{:S(2)}, u32[]{:S(2)}) collective-permute-start(bf16[256,1536]{1,0:T(8,128)(2,1)} %get-tuple-element.405.refs_2_), channel_id=1, source_target_pairs={{1,2},{2,1},{5,6},{6,5},{9,10},{10,9},{13,14},{14,13},{17,18},{18,... | collective-permute-start | bytes 2359304 | tf_op jit(solution)/shard_map/ppermute | solution.py:588
  545.1 11.9 %collective-permute-start.85 = (bf16[2,8,10880]{2,1,0:T(8,128)(2,1)S(1)}, bf16[2,8,10880]{2,1,0:T(8,128)(2,1)S(1)}, u32[]{:S(2)}, u32[]{:S(2)}) collective-permute-start(bf16[2,8,10880]{2,1,0:T(8,128)(2,1)S(1)} %pad_maximum_fusion.8), channel_id=1, source_target_pairs={{0,16},{8,24},{16,0},{24,8},{1,17},{9,25},{17,1},{25,9},{2,18},{10... | collective-permute-start | bytes 1044488 | tf_op jit(solution)/shard_map/ppermute | solution.py:588
  546.1 10.9 %collective-permute-start.84 = (bf16[64,1536]{1,0:T(8,128)(2,1)S(1)}, bf16[64,1536]{1,0:T(8,128)(2,1)S(1)}, u32[]{:S(2)}, u32[]{:S(2)}) collective-permute-start(bf16[64,1536]{1,0:T(8,128)(2,1)S(1)} %add_convert_fusion.2), channel_id=1, source_target_pairs={{0,8},{8,0},{16,24},{24,16},{1,9},{9,1},{17,25},{25,17},{2,10},{10... | collective-permute-start | bytes 589832 | tf_op jit(solution)/shard_map/ppermute | solution.py:588
  552.3 16.4 %collective-permute-start.81 = (bf16[256,1536]{1,0:T(8,128)(2,1)}, bf16[256,1536]{1,0:T(8,128)(2,1)}, u32[]{:S(2)}, u32[]{:S(2)}) collective-permute-start(bf16[256,1536]{1,0:T(8,128)(2,1)} %get-tuple-element.409.refs_3_), channel_id=1, source_target_pairs={{1,0},{2,3},{5,4},{6,7},{9,8},{10,11},{13,12},{14,15},{17,16},{18,... | collective-permute-start | bytes 2359304 | tf_op jit(solution)/shard_map/ppermute | solution.py:588
  554.5 14.2 %collective-permute-start.82 = (bf16[256,1536]{1,0:T(8,128)(2,1)}, bf16[256,1536]{1,0:T(8,128)(2,1)}, u32[]{:S(2)}, u32[]{:S(2)}) collective-permute-start(bf16[256,1536]{1,0:T(8,128)(2,1)} %get-tuple-element.410.refs_1_), channel_id=1, source_target_pairs={{1,2},{2,1},{5,6},{6,5},{9,10},{10,9},{13,14},{14,13},{17,18},{18,... | collective-permute-start | bytes 2359304 | tf_op jit(solution)/shard_map/ppermute | solution.py:588
  557.1 18.4 %collective-permute-start.86 = (bf16[128,1536]{1,0:T(8,128)(2,1)S(1)}, bf16[128,1536]{1,0:T(8,128)(2,1)}, u32[]{:S(2)}, u32[]{:S(2)}) collective-permute-start(bf16[128,1536]{1,0:T(8,128)(2,1)S(1)} %pad_maximum_fusion.5), channel_id=1, source_target_pairs={{0,16},{8,24},{16,0},{24,8},{1,17},{9,25},{17,1},{25,9},{2,18},{10... | collective-permute-start | bytes 1179656 | tf_op jit(solution)/shard_map/ppermute | solution.py:588
  558.3 17.2 %collective-permute-start.87 = (bf16[4,8,10880]{2,1,0:T(8,128)(2,1)}, bf16[4,8,10880]{2,1,0:T(8,128)(2,1)}, u32[]{:S(2)}, u32[]{:S(2)}) collective-permute-start(bf16[4,8,10880]{2,1,0:T(8,128)(2,1)} %pad_maximum_fusion.4), channel_id=1, source_target_pairs={{0,4},{4,0},{1,5},{5,1},{2,6},{6,2},{3,7},{7,3},{8,12},{12,8},{9,1... | collective-permute-start | bytes 2088968 | tf_op jit(solution)/shard_map/ppermute | solution.py:588
  573.3 27.2 %collective-permute-start.83 = (bf16[256,1536]{1,0:T(8,128)(2,1)}, bf16[256,1536]{1,0:T(8,128)(2,1)}, u32[]{:S(2)}, u32[]{:S(2)}) collective-permute-start(bf16[256,1536]{1,0:T(8,128)(2,1)} %get-tuple-element.412.refs_1_), channel_id=1, source_target_pairs={{1,0},{2,3},{5,4},{6,7},{9,8},{10,11},{13,12},{14,15},{17,16},{18,... | collective-permute-start | bytes 2359304 | tf_op jit(solution)/shard_map/ppermute | solution.py:588
  579.9 24.8 %collective-permute-start.88 = (bf16[256,1536]{1,0:T(8,128)(2,1)S(1)}, bf16[256,1536]{1,0:T(8,128)(2,1)S(1)}, u32[]{:S(2)}, u32[]{:S(2)}) collective-permute-start(bf16[256,1536]{1,0:T(8,128)(2,1)S(1)} %pad_maximum_fusion.2), channel_id=1, source_target_pairs={{0,4},{4,0},{1,5},{5,1},{2,6},{6,2},{3,7},{7,3},{8,12},{12,8},{9,1... | collective-permute-start | bytes 2359304 | tf_op jit(solution)/shard_map/ppermute | solution.py:588
  (93 other events, 830.4 us)

commit v4 on v3

--- a/solution.py
+++ b/solution.py
@@ -27,6 +27,10 @@
 
 def nt(left, right):
     return lax.dot_general(left, right, (((1,), (1,)), ((), ())), preferred_element_type=F32)
+
+
+def both_ways(values):
+    return values.astype(BF16), values.T.astype(BF16)
 
 
 def row_total(values):
@@ -536,11 +540,9 @@
         copies.append(pair)
     y = y2[...]
     dff = (og[...].astype(F32) * vec[M5 : M5 + 1, :]).astype(BF16)
-    lat = nt(y, dn1[...]).astype(BF16)
-    lat_t = nt(dn1[...], y).astype(BF16)
-    drl = nt(dff, up2[...]).astype(BF16)
-    drl_t = nt(up2[...], dff).astype(BF16)
-    part = grad = rl = rl_t = d_lat = d_lat_t = 0.0
+    lat, lat_t = both_ways(nt(y, dn1[...]))
+    drl, drl_t = both_ways(nt(dff, up2[...]))
+    part = grad = rl = d_lat = 0.0
     for (start, size), pair in zip(tiles, copies):
         cols = slice(start, start + size)
         finish(pair)
@@ -554,15 +556,15 @@
         part = part + nn(act, w2[cols, :])
         grad = grad + nn(dh, w1[cols, :])
         rl = rl + nt(act, dn2[:, cols])
-        rl_t = rl_t + nt(dn2[:, cols], act)
         d_lat = d_lat + nt(dh, up1[:, cols])
-        d_lat_t = d_lat_t + nt(up1[:, cols], dh)
         new_up1, new_dn2 = nn(lat_t, dh), nn(drl_t, act)
         g_up1[:, cols] = new_up1 if first else new_up1 + acc[0][:, cols]
         g_dn2[:, cols] = new_dn2 if first else new_dn2 + acc[3][:, cols]
-    part = part + nn(rl.astype(BF16), up2[...])
-    grad = grad + nn(d_lat.astype(BF16), dn1[...])
-    new_dn1, new_up2 = nn(d_lat_t.astype(BF16), y), nn(rl_t.astype(BF16), dff)
+    rl, rl_t = both_ways(rl)
+    d_lat, d_lat_t = both_ways(d_lat)
+    part = part + nn(rl, up2[...])
+    grad = grad + nn(d_lat, dn1[...])
+    new_dn1, new_up2 = nn(d_lat_t, y), nn(rl_t, dff)
     g_dn1[...] = new_dn1 if first else new_dn1 + acc[1][...]
     g_up2[...] = new_up2 if first else new_up2 + acc[2][...]
     part = part * vec[M5 : M5 + 1, :]
@@ -753,7 +755,7 @@
         if inward and outward:
             mine = self.total[self.at - 2]
         elif inward:
-            mine = array[block * self.size : (block + 1) * self.size]
+            mine = array if array.shape[0] == self.size else array[block * self.size : (block + 1) * self.size]
         else:
             mine = self.total.get(self.at - 2)
         self.moving = [send(mine, "tensor", pairs)] if pairs else []
@@ -768,7 +770,7 @@
         first = moving.pop(0) if inward or outward else None
         second = moving.pop(0) if across else None
         both = across and at + 1 < len(self.parts)
-        grid = 4
+        grid = 2
         rows = lambda block: pl.BlockSpec((self.size // grid, width), lambda b, m: (block * grid + b, 0))
         width = (second if first is None else first).shape[1]
         kind = sds((self.size, width), BF16)
@@ -1203,11 +1205,12 @@
     g_up1, g_dn1, g_up2, g_dn2 = acc
 
     dy_own, dy_in = ring_total(dys, "tensor")
-    feed_out, dy_in = seal(feed_out, dy_in)
+    feed_first = [feed_out[r * tc : (r + 1) * tc] for r in range(2)]
+    feed_out, dy_in, *feed_first = seal(feed_out, dy_in, *feed_first)
     line = Line(meta, tc) if groups == 4 else None
     if line:
         for r in range(groups):
-            line.add(feed_out, r, "output", r)
+            line.add(*((feed_first[r], 0) if r < 2 else (feed_out, r)), "output", r)
         line.start()
     else:
         result = lax.psum(feed_out, "tensor")

time: 617 us -> 601 us (0.974)
  Pallas kernels: 284 us -> 269 us
    pallas_call x27, Pallas kernels: 284 us -> 269 us  [run_kernel(): pl.pallas_call(reading, grid_spec=pltpu.PrefetchScalarGridSpec(num_scalar...]
    unnamed x154 -> x148, local copies, waits for them, and re-layouts: 13.9 us -> 13.9 us
  transfers between devices with their start and end apart: 89 -> 89, of which waited for: 33 -> 33; matrix products, arithmetic and copies ran while one was open for 6% -> 7% of each run, Pallas kernels for 43% -> 41%
where the time goes in v4:
time: 601 us; the launch traced here: 593 us
  Pallas kernels  269 us (45%)
  waiting for transfers between devices  141 us (23%)
  starting transfers between devices  127 us (21%)
  other arithmetic  28.2 us (5%)
  local copies, waits for them, and re-layouts  25.9 us (4%)
    pallas_call x27, Pallas kernels, run_kernel(): pl.pallas_call(reading, grid_spec=pltpu.PrefetchScalarGridSpec(num_scalar...  269 us
    ppermute x89, waiting for transfers between devices, send(): return jax.tree.map(lambda v: lax.ppermute(v, axis, pairs), values)  141 us
    ppermute x89, starting transfers between devices, send(): return jax.tree.map(lambda v: lax.ppermute(v, axis, pairs), values)  127 us
    unnamed x148, local copies, waits for them, and re-layouts  13.9 us
  transfers between devices with their start and end apart: 89, of which 33 were waited for; matrix products, arithmetic and copies ran while one was open for 7% of the time, Pallas kernels for 41%

profile of v4, /device:TPU:9, one launch (start us, length us, event | category | flops | bytes accessed | tf_op | source)
XLA Modules:
  0.0 593.0 jit_solution(13616582730591505893)
XLA Ops:
  2.0 2.6 shard_map.392.refs_8_
  10.3 5.6 shard_map.393
  15.9 3.3 sine_multiply_fusion
  19.2 15.7 %shard_map.394 = (bf16[1024,1536]{1,0:T(8,128)(2,1)}, bf16[48,1024]{1,0:T(8,128)(2,1)}, bf16[1024,384]{1,0:T(8,128)(2,1)}, bf16[1024,384]{1,0:T(8,128)(2,1)}, bf...) custom-call(s32[12]{0:T(128)} %stack.104.meta_ref, ...), custom_call_target="tpu_custom_call" | custom-call | flops 17250000896 | bytes 18121472 | tf_op jit(solution)/shard_map/pallas_call | solution.py:89
  39.0 4.6 collective-permute-done.2.refs_1_
  43.5 2.7 collective-permute-done.3.refs_2_
  47.0 3.1 shard_map.395.refs_8_.refs_21_.refs_28_
  50.6 3.3 collective-permute-start.4
  62.9 25.3 %shard_map.396 = (bf16[256,384]{1,0:T(8,128)(2,1)}, bf16[256,384]{1,0:T(8,128)(2,1)}, bf16[256,384]{1,0:T(8,128)(2,1)}, bf16[256,384]{1,0:T(8,128)(2,1)}, bf16[1...) custom-call(s32[12]{0:T(128)} %stack.104.meta_ref, ...), custom_call_target="tpu_custom_call" | custom-call | flops 28750000128 | bytes 14352384 | tf_op jit(solution)/shard_map/pallas_call | solution.py:89
  88.2 8.7 %collective-permute-done.11.refs_10_.refs_17_ = bf16[576,384]{1,0:T(8,128)(2,1)S(1)} collective-permute-done((bf16[576,384]{1,0:T(8,128)(2,1)S(1)}, bf16[576,384]{1,0:T(8,128)(2,1)S(1)}, u32[]{:S(2)}, u32[]{:S(2)}) %collective-permute-start.11) | collective-permute-done | bytes 442400 | tf_op jit(solution)/shard_map/ppermute | solution.py:590
  97.0 3.7 collective-permute-done.12.refs_11_.refs_18_
  103.3 3.7 collective-permute-done.13.refs_1_
  107.0 10.8 %collective-permute-done.14.refs_2_ = bf16[256,384]{1,0:T(8,128)(2,1)S(1)} collective-permute-done((bf16[256,384]{1,0:T(8,128)(2,1)}, bf16[256,384]{1,0:T(8,128)(2,1)S(1)}, u32[]{:S(2)}, u32[]{:S(2)}) %collective-permute-start.14) | collective-permute-done | bytes 196640 | tf_op jit(solution)/shard_map/ppermute | solution.py:590
  121.6 2.6 collective-permute-done.17.refs_13_.refs_20_
  128.5 20.8 %shard_map.397 = (bf16[256,1536]{1,0:T(8,128)(2,1)}, f32[256,1536]{1,0:T(8,128)}, f32[256,1536]{1,0:T(8,128)}, bf16[256,1536]{1,0:T(8,128)(2,1)}, bf16[256,1536]...) custom-call(s32[12]{0:T(128)} %stack.104.meta_ref, ...), custom_call_target="tpu_custom_call" | custom-call | flops 23000000512 | bytes 35987456 | tf_op jit(solution)/shard_map/pallas_call | solution.py:89
  149.6 17.5 %shard_map.398 = (bf16[1024,1536]{1,0:T(8,128)(2,1)}, f32[256,1536]{1,0:T(8,128)}, f32[16,2240]{1,0:T(8,128)}, f32[16,1536]{1,0:T(8,128)}, f32[16,1536]{1,0:T(8,128)}, /*index=5*/f32[16,2240]{1,0:T(8,128)}) custom-call(s32[12]{0:T(128)} %stack.104.meta_ref, bf16[256,1536]{1,0:T(8,128)(2,1)} %get-tuple-element.257.refs_0_, bf16[1024,1536]{1,0:T(8,128)(2,1)} %bitcast.176, ...), custom_call_target="tpu_custom_call" | custom-call | flops 20700000256 | bytes 26510080 | tf_op jit(solution)/shard_map/pallas_call | solution.py:89
  170.8 16.8 %shard_map.399 = (bf16[1024,1536]{1,0:T(8,128)(2,1)}, bf16[256,1536]{1,0:T(8,128)(2,1)}, f32[16,2240]{1,0:T(8,128)}, f32[16,1536]{1,0:T(8,128)}, f32[16,1536]{1,0:T(8,128)}, /*index=5*/f32[16,2240]{1,0:T(8,128)}) custom-call(s32[12]{0:T(128)} %stack.104.meta_ref, bf16[256,1536]{1,0:T(8,128)(2,1)} %copy-done.43, ...), custom_call_target="tpu_custom_call", output_to_operand_aliasing={{0}: (15, {})} | custom-call | flops 20700000256 | bytes 27779840 | tf_op jit(solution)/shard_map/pallas_call | solution.py:89
  189.1 2.3 collective-permute-start.28
  191.4 16.8 %shard_map.400 = (bf16[1024,1536]{1,0:T(8,128)(2,1)}, bf16[256,1536]{1,0:T(8,128)(2,1)}, f32[16,2240]{1,0:T(8,128)}, f32[16,1536]{1,0:T(8,128)}, f32[16,1536]{1,0:T(8,128)}, /*index=5*/f32[16,2240]{1,0:T(8,128)}) custom-call(s32[12]{0:T(128)} %stack.104.meta_ref, bf16[256,1536]{1,0:T(8,128)(2,1)} %copy-done.39, ...), custom_call_target="tpu_custom_call", output_to_operand_aliasing={{0}: (15, {})} | custom-call | flops 20700000256 | bytes 27779840 | tf_op jit(solution)/shard_map/pallas_call | solution.py:89
  210.5 12.8 %collective-permute-done.28.refs_0_ = bf16[256,1536]{1,0:T(8,128)(2,1)S(1)} collective-permute-done((bf16[256,1536]{1,0:T(8,128)(2,1)S(1)}, bf16[256,1536]{1,0:T(8,128)(2,1)S(1)}, u32[]{:S(2)}, u32[]{:S(2)}) %collective-permute-start.28) | collective-permute-done | bytes 786464 | tf_op jit(solution)/shard_map/ppermute | solution.py:590
  224.2 16.9 %shard_map.401 = (bf16[1024,1536]{1,0:T(8,128)(2,1)}, bf16[256,1536]{1,0:T(8,128)(2,1)}, f32[16,2240]{1,0:T(8,128)}, f32[16,1536]{1,0:T(8,128)}, f32[16,1536]{1,0:T(8,128)}, /*index=5*/f32[16,2240]{1,0:T(8,128)}) custom-call(s32[12]{0:T(128)} %stack.104.meta_ref, bf16[256,1536]{1,0:T(8,128)(2,1)} %copy-done.42, ...), custom_call_target="tpu_custom_call", output_to_operand_aliasing={{0}: (15, {})} | custom-call | flops 20700000256 | bytes 27779840 | tf_op jit(solution)/shard_map/pallas_call | solution.py:89
  243.9 2.4 fusion.52
  246.2 14.0 %collective-permute-done.31.refs_1_ = bf16[256,1536]{1,0:T(8,128)(2,1)S(1)} collective-permute-done((bf16[256,1536]{1,0:T(8,128)(2,1)S(1)}, bf16[256,1536]{1,0:T(8,128)(2,1)S(1)}, u32[]{:S(2)}, u32[]{:S(2)}) %collective-permute-start.31) | collective-permute-done | bytes 786464 | tf_op jit(solution)/shard_map/ppermute | solution.py:590
  262.9 26.7 %shard_map.402 = (bf16[256,128]{1,0:T(8,128)(2,1)}, bf16[256,128]{1,0:T(8,128)(2,1)}, bf16[256,128]{1,0:T(8,128)(2,1)}, bf16[256,128]{1,0:T(8,128)(2,1)}, bf16[2...) custom-call(s32[12]{0:T(128)} %stack.104.meta_ref, ...), custom_call_target="tpu_custom_call" | custom-call | flops 29899999232 | bytes 42868736 | tf_op jit(solution)/shard_map/pallas_call | solution.py:89
  289.5 3.0 collective-permute-start.34
  296.3 5.9 %collective-permute-start.40 = (bf16[8,12160]{1,0:T(8,128)(2,1)S(1)}, bf16[8,12160]{1,0:T(8,128)(2,1)S(1)}, u32[]{:S(2)}, u32[]{:S(2)}) collective-permute-start(bf16[8,12160]{1,0:T(8,128)(2,1)S(1)} %select_convert_fusion.2), channel_id=1, source_target_pairs={{0,4},{4,0},{1,5},{5,1},{2,6},{6,2},{3,7},{7,3},{8,12},{12,8},{9,1... | collective-permute-start | bytes 583688 | tf_op jit(solution)/shard_map/ppermute | solution.py:590
  302.2 2.9 shard_map.406.refs_2_
  305.5 2.7 collective-permute-start.38
  311.5 11.0 %shard_map.403 = (f32[1024,128]{1,0:T(8,128)}, f32[1024,256]{1,0:T(8,128)}, bf16[1024,256]{1,0:T(8,128)(2,1)}, f32[8,1024]{1,0:T(8,128)}, f32[8,1024]{1,0:T(8,128)}) custom-call(s32[12]{0:T(128)} %stack.104.meta_ref, bf16[1024,384]{1,0:T(8,128)(2,1)} %get-tuple-element.300.refs_0_, f32[8,1024]{1,0:T(8,128)} %copy-done.16, f32[8,1024]{1,0:T(8,128)} %copy-done.16, ...), custom_call_target="tpu_custom_call" | custom-call | flops 14375000064 | bytes 8912896 | tf_op jit(solution)/shard_map/pallas_call | solution.py:89
  323.8 3.0 collective-permute-start.48
  326.9 10.9 %shard_map.404 = (f32[1024,128]{1,0:T(8,128)}, f32[1024,256]{1,0:T(8,128)}, bf16[1024,256]{1,0:T(8,128)(2,1)}, f32[8,1024]{1,0:T(8,128)}, f32[8,1024]{1,0:T(8,128)}) custom-call(s32[12]{0:T(128)} %stack.104.meta_ref, bf16[1024,384]{1,0:T(8,128)(2,1)} %get-tuple-element.300.refs_0_, f32[8,1024]{1,0:T(8,128)} %copy-done.16, f32[8,1024]{1,0:T(8,128)} %copy-done.16, ...), custom_call_target="tpu_custom_call" | custom-call | flops 14375000064 | bytes 9240576 | tf_op jit(solution)/shard_map/pallas_call | solution.py:89
  343.0 11.0 %shard_map.405 = (f32[1024,128]{1,0:T(8,128)}, f32[1024,256]{1,0:T(8,128)}, bf16[1024,256]{1,0:T(8,128)(2,1)}, f32[8,1024]{1,0:T(8,128)}, f32[8,1024]{1,0:T(8,128)}) custom-call(s32[12]{0:T(128)} %stack.104.meta_ref, bf16[1024,384]{1,0:T(8,128)(2,1)} %get-tuple-element.300.refs_0_, f32[8,1024]{1,0:T(8,128)} %copy-done.16, f32[8,1024]{1,0:T(8,128)} %copy-done.16, ...), custom_call_target="tpu_custom_call" | custom-call | flops 14375000064 | bytes 9240576 | tf_op jit(solution)/shard_map/pallas_call | solution.py:89
  354.7 3.2 collective-permute-done.46
  361.7 2.3 collective-permute-start.51
  366.8 3.7 shard_map.408
  372.3 2.3 collective-permute-start.57
  378.2 12.3 %shard_map.407 = (bf16[512,1536]{1,0:T(8,128)(2,1)}, f32[16,5760]{1,0:T(8,128)}) custom-call(s32[12]{0:T(128)} %stack.104.meta_ref, f32[1024,128]{1,0:T(8,128)} %get-tuple-element.328.refs_15_.refs_0_, f32[1024,128]{1,0:T(8,128)} %get-tuple-element.333.refs_15_.refs_1_, f32[1024,128]{1,0:T(8,128)} %get-tuple-element.334.refs_2_, ...), custom_call_target="tpu_custom_call" | custom-call | flops 16099999744 | bytes 25470464 | tf_op jit(solution)/shard_map/pallas_call | solution.py:89
  390.5 9.1 %collective-permute-done.55 = bf16[560,384]{1,0:T(8,128)(2,1)S(1)} collective-permute-done((bf16[560,384]{1,0:T(8,128)(2,1)S(1)}, bf16[560,384]{1,0:T(8,128)(2,1)S(1)}, u32[]{:S(2)}, u32[]{:S(2)}) %collective-permute-start.55) | collective-permute-done | bytes 430112 | tf_op jit(solution)/shard_map/ppermute | solution.py:590
  402.1 2.8 collective-permute-start.58
  405.2 4.1 shard_map.410
  410.8 3.0 collective-permute-start.61
  413.8 12.5 %shard_map.409 = (bf16[512,1536]{1,0:T(8,128)(2,1)}, f32[16,5760]{1,0:T(8,128)}) custom-call(s32[12]{0:T(128)} %stack.104.meta_ref, f32[1024,128]{1,0:T(8,128)} %get-tuple-element.328.refs_15_.refs_0_, f32[1024,128]{1,0:T(8,128)} %get-tuple-element.333.refs_15_.refs_1_, f32[1024,128]{1,0:T(8,128)} %get-tuple-element.334.refs_2_, ...), custom_call_target="tpu_custom_call" | custom-call | flops 16099999744 | bytes 25839104 | tf_op jit(solution)/shard_map/pallas_call | solution.py:89
  426.3 2.4 collective-permute-done.60.refs_0_
  428.7 2.7 collective-permute-done.61.refs_3_
  432.6 4.1 shard_map.411
  438.9 2.3 collective-permute-start.66
  442.2 5.8 shard_map.412
  450.0 2.3 collective-permute-start.63
  458.8 4.4 shard_map.413
  464.7 2.3 collective-permute-start.72
  471.2 2.3 collective-permute-done.67
  476.4 3.9 collective-permute-done.71.refs_0_
  483.5 4.1 shard_map.414
  489.1 2.5 collective-permute-start.76
  491.8 17.4 %collective-permute-done.74 = bf16[8,7680]{1,0:T(8,128)(2,1)S(1)} collective-permute-done((bf16[8,7680]{1,0:T(8,128)(2,1)S(1)}, bf16[8,7680]{1,0:T(8,128)(2,1)S(1)}, u32[]{:S(2)}, u32[]{:S(2)}) %collective-permute-start.74) | collective-permute-done | bytes 122912 | tf_op jit(solution)/shard_map/ppermute | solution.py:590
  510.3 4.1 shard_map.415
  518.9 10.0 %collective-permute-done.79.refs_0_ = bf16[256,1536]{1,0:T(8,128)(2,1)S(1)} collective-permute-done((bf16[256,1536]{1,0:T(8,128)(2,1)}, bf16[256,1536]{1,0:T(8,128)(2,1)S(1)}, u32[]{:S(2)}, u32[]{:S(2)}) %collective-permute-start.79) | collective-permute-done | bytes 786464 | tf_op jit(solution)/shard_map/ppermute | solution.py:590
  528.9 5.8 collective-permute-done.80.refs_3_
  537.2 3.9 shard_map.416
  546.5 9.4 %collective-permute-start.87 = (bf16[4,8,10880]{2,1,0:T(8,128)(2,1)}, bf16[4,8,10880]{2,1,0:T(8,128)(2,1)}, u32[]{:S(2)}, u32[]{:S(2)}) collective-permute-start(bf16[4,8,10880]{2,1,0:T(8,128)(2,1)} %pad_maximum_fusion.4), channel_id=1, source_target_pairs={{0,4},{4,0},{1,5},{5,1},{2,6},{6,2},{3,7},{7,3},{8,12},{12,8},{9,1... | collective-permute-start | bytes 2088968 | tf_op jit(solution)/shard_map/ppermute | solution.py:590
  556.3 3.5 shard_map.417
  566.5 9.7 %collective-permute-start.88 = (bf16[256,1536]{1,0:T(8,128)(2,1)S(1)}, bf16[256,1536]{1,0:T(8,128)(2,1)S(1)}, u32[]{:S(2)}, u32[]{:S(2)}) collective-permute-start(bf16[256,1536]{1,0:T(8,128)(2,1)S(1)} %pad_maximum_fusion.2), channel_id=1, source_target_pairs={{0,4},{4,0},{1,5},{5,1},{2,6},{6,2},{3,7},{7,3},{8,12},{12,8},{9,1... | collective-permute-start | bytes 2359304 | tf_op jit(solution)/shard_map/ppermute | solution.py:590
  579.5 2.6 copy.57
  587.4 2.8 shard_map.418
  (371 shorter events, 133.4 us)
Async XLA Ops:
  4.7 34.3 %collective-permute-start.1 = (bf16[144,1536]{1,0:T(8,128)(2,1)}, bf16[144,1536]{1,0:T(8,128)(2,1)S(1)}, u32[]{:S(2)}, u32[]{:S(2)}) collective-permute-start(bf16[144,1536]{1,0:T(8,128)(2,1)} %shard_map.392.refs_8_), channel_id=1, source_target_pairs={{0,1},{1,2},{2,3},{3,0},{4,5},{5,6},{6,7},{7,4},{8,9},{9,10},{10,1... | collective-permute-start | bytes 1327112 | tf_op jit(solution)/shard_map/ppermute | solution.py:590
  5.9 37.6 %collective-permute-start.2 = (bf16[144,1536]{1,0:T(8,128)(2,1)}, bf16[144,1536]{1,0:T(8,128)(2,1)S(1)}, u32[]{:S(2)}, u32[]{:S(2)}) collective-permute-start(bf16[144,1536]{1,0:T(8,128)(2,1)} %shard_map.392.refs_8_), channel_id=1, source_target_pairs={{0,2},{1,3},{2,0},{3,1},{4,6},{5,7},{6,4},{7,5},{8,10},{9,11},{10,... | collective-permute-start | bytes 1327112 | tf_op jit(solution)/shard_map/ppermute | solution.py:590
  7.0 39.3 %collective-permute-start.3 = (bf16[144,1536]{1,0:T(8,128)(2,1)}, bf16[144,1536]{1,0:T(8,128)(2,1)S(1)}, u32[]{:S(2)}, u32[]{:S(2)}) collective-permute-start(bf16[144,1536]{1,0:T(8,128)(2,1)} %shard_map.392.refs_8_), channel_id=1, source_target_pairs={{0,3},{1,0},{2,1},{3,2},{4,7},{5,4},{6,5},{7,6},{8,11},{9,8},{10,9... | collective-permute-start | bytes 1327112 | tf_op jit(solution)/shard_map/ppermute | solution.py:590
  36.0 23.6 %collective-permute-start.7 = (bf16[1024,768]{1,0:T(8,128)(2,1)}, bf16[1024,768]{1,0:T(8,128)(2,1)S(1)}, u32[]{:S(2)}, u32[]{:S(2)}) collective-permute-start(bf16[1024,768]{1,0:T(8,128)(2,1)} %get-tuple-element.228.refs_4_.refs_6_), channel_id=1, source_target_pairs={{0,4},{4,0},{1,5},{5,1},{2,6},{6,2},{3,7},{7,3},{8,12},{12,8},{9,1... | collective-permute-start | bytes 4718600 | tf_op jit(solution)/shard_map/ppermute | solution.py:590
  50.1 11.4 %collective-permute-start.6 = (bf16[3,144,1536]{2,1,0:T(8,128)(2,1)}, bf16[3,144,1536]{2,1,0:T(8,128)(2,1)S(1)}, u32[]{:S(2)}, u32[]{:S(2)}) collective-permute-start(bf16[3,144,1536]{2,1,0:T(8,128)(2,1)} %shard_map.395.refs_8_.refs_21_.refs_28_), channel_id=1, source_target_pairs={{0,4},{4,0},{1,5},{5,1},{2,6},{6,2},{3,7},{7,3},{8,12},{12,8},{9,1... | collective-permute-start | bytes 3981320 | tf_op jit(solution)/shard_map/ppermute | solution.py:590
  56.4 44.2 %collective-permute-start.8 = (bf16[3,144,1536]{2,1,0:T(8,128)(2,1)}, bf16[3,144,1536]{2,1,0:T(8,128)(2,1)S(1)}, u32[]{:S(2)}, u32[]{:S(2)}) collective-permute-start(bf16[3,144,1536]{2,1,0:T(8,128)(2,1)} %shard_map.395.refs_8_.refs_21_.refs_28_), channel_id=1, source_target_pairs={{0,8},{8,0},{16,24},{24,16},{1,9},{9,1},{17,25},{25,17},{2,10},{10... | collective-permute-start | bytes 3981320 | tf_op jit(solution)/shard_map/ppermute | solution.py:590
  57.6 43.0 %collective-permute-start.9 = (bf16[3,144,1536]{2,1,0:T(8,128)(2,1)}, bf16[3,144,1536]{2,1,0:T(8,128)(2,1)S(1)}, u32[]{:S(2)}, u32[]{:S(2)}) collective-permute-start(bf16[3,144,1536]{2,1,0:T(8,128)(2,1)} %shard_map.395.refs_8_.refs_21_.refs_28_), channel_id=1, source_target_pairs={{0,16},{8,24},{16,0},{24,8},{1,17},{9,25},{17,1},{25,9},{2,18},{10... | collective-permute-start | bytes 3981320 | tf_op jit(solution)/shard_map/ppermute | solution.py:590
  58.9 29.3 %collective-permute-start.10 = (bf16[576,384]{1,0:T(8,128)(2,1)S(1)}, bf16[576,384]{1,0:T(8,128)(2,1)S(1)}, u32[]{:S(2)}, u32[]{:S(2)}) collective-permute-start(bf16[576,384]{1,0:T(8,128)(2,1)S(1)} %copy-done.46), channel_id=1, source_target_pairs={{0,1},{1,2},{2,3},{3,0},{4,5},{5,6},{6,7},{7,4},{8,9},{9,10},{10,1... | collective-permute-start | bytes 1327112 | tf_op jit(solution)/shard_map/ppermute | solution.py:590
  59.6 37.3 %collective-permute-start.11 = (bf16[576,384]{1,0:T(8,128)(2,1)S(1)}, bf16[576,384]{1,0:T(8,128)(2,1)S(1)}, u32[]{:S(2)}, u32[]{:S(2)}) collective-permute-start(bf16[576,384]{1,0:T(8,128)(2,1)S(1)} %copy-done.46), channel_id=1, source_target_pairs={{0,2},{1,3},{2,0},{3,1},{4,6},{5,7},{6,4},{7,5},{8,10},{9,11},{10,... | collective-permute-start | bytes 1327112 | tf_op jit(solution)/shard_map/ppermute | solution.py:590
  61.5 39.1 %collective-permute-start.12 = (bf16[576,384]{1,0:T(8,128)(2,1)S(1)}, bf16[576,384]{1,0:T(8,128)(2,1)}, u32[]{:S(2)}, u32[]{:S(2)}) collective-permute-start(bf16[576,384]{1,0:T(8,128)(2,1)S(1)} %copy-done.46), channel_id=1, source_target_pairs={{0,3},{1,0},{2,1},{3,2},{4,7},{5,4},{6,5},{7,6},{8,11},{9,8},{10,9... | collective-permute-start | bytes 1327112 | tf_op jit(solution)/shard_map/ppermute | solution.py:590
  100.7 19.0 %collective-permute-start.21 = (bf16[3,64,1536]{2,1,0:T(8,128)(2,1)S(1)}, bf16[3,64,1536]{2,1,0:T(8,128)(2,1)}, u32[]{:S(2)}, u32[]{:S(2)}) collective-permute-start(bf16[3,64,1536]{2,1,0:T(8,128)(2,1)S(1)} %slice.231), channel_id=1, source_target_pairs={{0,16},{8,24},{16,0},{24,8},{1,17},{9,25},{17,1},{25,9},{2,18},{10... | collective-permute-start | bytes 1769480 | tf_op jit(solution)/shard_map/ppermute | solution.py:590
  101.0 16.7 %collective-permute-start.14 = (bf16[256,384]{1,0:T(8,128)(2,1)}, bf16[256,384]{1,0:T(8,128)(2,1)S(1)}, u32[]{:S(2)}, u32[]{:S(2)}) collective-permute-start(bf16[256,384]{1,0:T(8,128)(2,1)} %get-tuple-element.239), channel_id=1, source_target_pairs={{0,2},{1,3},{2,0},{3,1},{4,6},{5,7},{6,4},{7,5},{8,10},{9,11},{10,... | collective-permute-start | bytes 589832 | tf_op jit(solution)/shard_map/ppermute | solution.py:590
  101.0 17.7 %collective-permute-start.15 = (bf16[256,384]{1,0:T(8,128)(2,1)}, bf16[256,384]{1,0:T(8,128)(2,1)S(1)}, u32[]{:S(2)}, u32[]{:S(2)}) collective-permute-start(bf16[256,384]{1,0:T(8,128)(2,1)} %get-tuple-element.240), channel_id=1, source_target_pairs={{0,3},{1,0},{2,1},{3,2},{4,7},{5,4},{6,5},{7,6},{8,11},{9,8},{10,9... | collective-permute-start | bytes 589832 | tf_op jit(solution)/shard_map/ppermute | solution.py:590
  102.7 18.7 %collective-permute-start.20 = (bf16[3,80,1536]{2,1,0:T(8,128)(2,1)S(1)}, bf16[3,80,1536]{2,1,0:T(8,128)(2,1)S(1)}, u32[]{:S(2)}, u32[]{:S(2)}) collective-permute-start(bf16[3,80,1536]{2,1,0:T(8,128)(2,1)S(1)} %slice.230), channel_id=1, source_target_pairs={{0,8},{8,0},{16,24},{24,16},{1,9},{9,1},{17,25},{25,17},{2,10},{10... | collective-permute-start | bytes 2211848 | tf_op jit(solution)/shard_map/ppermute | solution.py:590
  149.3 19.2 %collective-permute-start.26 = (bf16[256,1536]{1,0:T(8,128)(2,1)}, bf16[256,1536]{1,0:T(8,128)(2,1)S(1)}, u32[]{:S(2)}, u32[]{:S(2)}) collective-permute-start(bf16[256,1536]{1,0:T(8,128)(2,1)} %get-tuple-element.257.refs_0_), channel_id=1, source_target_pairs={{0,1},{1,2},{2,3},{3,0},{4,5},{5,6},{6,7},{7,4},{8,9},{9,10},{10,1... | collective-permute-start | bytes 2359304 | tf_op jit(solution)/shard_map/ppermute | solution.py:590
  168.6 20.5 %collective-permute-start.27 = (bf16[256,1536]{1,0:T(8,128)(2,1)S(1)}, bf16[256,1536]{1,0:T(8,128)(2,1)S(1)}, u32[]{:S(2)}, u32[]{:S(2)}) collective-permute-start(bf16[256,1536]{1,0:T(8,128)(2,1)S(1)} %collective-permute-done.26.refs_0_), channel_id=1, source_target_pairs={{0,1},{1,2},{2,3},{3,0},{4,5},{5,6},{6,7},{7,4},{8,9},{9,10},{10,1... | collective-permute-start | bytes 2359304 | tf_op jit(solution)/shard_map/ppermute | solution.py:590
  187.6 20.6 %collective-permute-start.29 = (bf16[256,1536]{1,0:T(8,128)(2,1)}, bf16[256,1536]{1,0:T(8,128)(2,1)S(1)}, u32[]{:S(2)}, u32[]{:S(2)}) collective-permute-start(bf16[256,1536]{1,0:T(8,128)(2,1)} %get-tuple-element.276), channel_id=1, source_target_pairs={{0,1},{1,2},{2,3},{3,0},{4,5},{5,6},{6,7},{7,4},{8,9},{9,10},{10,1... | collective-permute-start | bytes 2359304 | tf_op jit(solution)/shard_map/ppermute | solution.py:590
  189.1 34.2 %collective-permute-start.28 = (bf16[256,1536]{1,0:T(8,128)(2,1)S(1)}, bf16[256,1536]{1,0:T(8,128)(2,1)S(1)}, u32[]{:S(2)}, u32[]{:S(2)}) collective-permute-start(bf16[256,1536]{1,0:T(8,128)(2,1)S(1)} %collective-permute-done.27.refs_0_), channel_id=1, source_target_pairs={{0,1},{1,2},{2,3},{3,0},{4,5},{5,6},{6,7},{7,4},{8,9},{9,10},{10,1... | collective-permute-start | bytes 2359304 | tf_op jit(solution)/shard_map/ppermute | solution.py:590
  209.5 31.6 %collective-permute-start.30 = (bf16[256,1536]{1,0:T(8,128)(2,1)S(1)}, bf16[256,1536]{1,0:T(8,128)(2,1)S(1)}, u32[]{:S(2)}, u32[]{:S(2)}) collective-permute-start(bf16[256,1536]{1,0:T(8,128)(2,1)S(1)} %add_convert_fusion.1), channel_id=1, source_target_pairs={{0,1},{1,2},{2,3},{3,0},{4,5},{5,6},{6,7},{7,4},{8,9},{9,10},{10,1... | collective-permute-start | bytes 2359304 | tf_op jit(solution)/shard_map/ppermute | solution.py:590
  242.4 17.8 %collective-permute-start.31 = (bf16[256,1536]{1,0:T(8,128)(2,1)S(1)}, bf16[256,1536]{1,0:T(8,128)(2,1)S(1)}, u32[]{:S(2)}, u32[]{:S(2)}) collective-permute-start(bf16[256,1536]{1,0:T(8,128)(2,1)S(1)} %add_convert_fusion), channel_id=1, source_target_pairs={{0,1},{1,2},{2,3},{3,0},{4,5},{5,6},{6,7},{7,4},{8,9},{9,10},{10,1... | collective-permute-start | bytes 2359304 | tf_op jit(solution)/shard_map/ppermute | solution.py:590
  261.1 33.9 %collective-permute-start.32 = (bf16[256,1536]{1,0:T(8,128)(2,1)S(1)}, bf16[256,1536]{1,0:T(8,128)(2,1)S(1)}, u32[]{:S(2)}, u32[]{:S(2)}) collective-permute-start(bf16[256,1536]{1,0:T(8,128)(2,1)S(1)} %get-tuple-element.292.refs_1_), channel_id=1, source_target_pairs={{0,1},{3,2},{4,5},{7,6},{8,9},{11,10},{12,13},{15,14},{16,17},{19,... | collective-permute-start | bytes 2359304 | tf_op jit(solution)/shard_map/ppermute | solution.py:590
  289.5 15.9 %collective-permute-start.34 = (bf16[256,128]{1,0:T(8,128)(2,1)}, bf16[256,128]{1,0:T(8,128)(2,1)S(1)}, u32[]{:S(2)}, u32[]{:S(2)}) collective-permute-start(bf16[256,128]{1,0:T(8,128)(2,1)} %get-tuple-element.295), channel_id=1, source_target_pairs={{0,3},{1,0},{2,1},{3,2},{4,7},{5,4},{6,5},{7,6},{8,11},{9,8},{10,9... | collective-permute-start | bytes 196616 | tf_op jit(solution)/shard_map/ppermute | solution.py:590
  292.6 15.6 %collective-permute-start.35 = (bf16[256,128]{1,0:T(8,128)(2,1)}, bf16[256,128]{1,0:T(8,128)(2,1)S(1)}, u32[]{:S(2)}, u32[]{:S(2)}) collective-permute-start(bf16[256,128]{1,0:T(8,128)(2,1)} %get-tuple-element.296), channel_id=1, source_target_pairs={{0,2},{1,3},{2,0},{3,1},{4,6},{5,7},{6,4},{7,5},{8,10},{9,11},{10,... | collective-permute-start | bytes 196616 | tf_op jit(solution)/shard_map/ppermute | solution.py:590
  292.6 16.3 %collective-permute-start.36 = (bf16[256,128]{1,0:T(8,128)(2,1)}, bf16[256,128]{1,0:T(8,128)(2,1)}, u32[]{:S(2)}, u32[]{:S(2)}) collective-permute-start(bf16[256,128]{1,0:T(8,128)(2,1)} %get-tuple-element.297), channel_id=1, source_target_pairs={{0,1},{1,2},{2,3},{3,0},{4,5},{5,6},{6,7},{7,4},{8,9},{9,10},{10,1... | collective-permute-start | bytes 196616 | tf_op jit(solution)/shard_map/ppermute | solution.py:590
  293.8 28.7 %collective-permute-start.37 = (bf16[256,256]{1,0:T(8,128)(2,1)}, bf16[256,256]{1,0:T(8,128)(2,1)S(1)}, u32[]{:S(2)}, u32[]{:S(2)}) collective-permute-start(bf16[256,256]{1,0:T(8,128)(2,1)} %get-tuple-element.312), channel_id=1, source_target_pairs={{0,3},{1,0},{2,1},{3,2},{4,7},{5,4},{6,5},{7,6},{8,11},{9,8},{10,9... | collective-permute-start | bytes 393224 | tf_op jit(solution)/shard_map/ppermute | solution.py:590
  305.5 18.3 %collective-permute-start.38 = (bf16[256,256]{1,0:T(8,128)(2,1)}, bf16[256,256]{1,0:T(8,128)(2,1)S(1)}, u32[]{:S(2)}, u32[]{:S(2)}) collective-permute-start(bf16[256,256]{1,0:T(8,128)(2,1)} %get-tuple-element.313), channel_id=1, source_target_pairs={{0,2},{1,3},{2,0},{3,1},{4,6},{5,7},{6,4},{7,5},{8,10},{9,11},{10,... | collective-permute-start | bytes 393224 | tf_op jit(solution)/shard_map/ppermute | solution.py:590
  308.2 18.6 %collective-permute-start.39 = (bf16[256,256]{1,0:T(8,128)(2,1)S(1)}, bf16[256,256]{1,0:T(8,128)(2,1)}, u32[]{:S(2)}, u32[]{:S(2)}) collective-permute-start(bf16[256,256]{1,0:T(8,128)(2,1)S(1)} %copy-done.59), channel_id=1, source_target_pairs={{0,1},{1,2},{2,3},{3,0},{4,5},{5,6},{6,7},{7,4},{8,9},{9,10},{10,1... | collective-permute-start | bytes 393224 | tf_op jit(solution)/shard_map/ppermute | solution.py:590
  308.9 17.9 %collective-permute-start.41 = (bf16[8,7680]{1,0:T(8,128)(2,1)S(1)}, bf16[8,7680]{1,0:T(8,128)(2,1)S(1)}, u32[]{:S(2)}, u32[]{:S(2)}) collective-permute-start(bf16[8,7680]{1,0:T(8,128)(2,1)S(1)} %slice.300), channel_id=1, source_target_pairs={{0,1},{1,0},{2,3},{3,2},{4,5},{5,4},{6,7},{7,6},{8,9},{9,8},{10,11... | collective-permute-start | bytes 368648 | tf_op jit(solution)/shard_map/ppermute | solution.py:590
  310.8 16.1 %collective-permute-start.42 = (bf16[560,384]{1,0:T(8,128)(2,1)S(1)}, bf16[560,384]{1,0:T(8,128)(2,1)S(1)}, u32[]{:S(2)}, u32[]{:S(2)}) collective-permute-start(bf16[560,384]{1,0:T(8,128)(2,1)S(1)} %fusion.19), channel_id=1, source_target_pairs={{0,1},{1,2},{2,3},{3,0},{4,5},{5,6},{6,7},{7,4},{8,9},{9,10},{10,1... | collective-permute-start | bytes 1290248 | tf_op jit(solution)/shard_map/ppermute | solution.py:590
  322.5 31.5 %collective-permute-start.47 = (bf16[256,1536]{1,0:T(8,128)(2,1)S(1)}, bf16[256,1536]{1,0:T(8,128)(2,1)}, u32[]{:S(2)}, u32[]{:S(2)}) collective-permute-start(bf16[256,1536]{1,0:T(8,128)(2,1)S(1)} %copy-done.7), channel_id=1, source_target_pairs={{0,1},{3,2},{4,5},{7,6},{8,9},{11,10},{12,13},{15,14},{16,17},{19,... | collective-permute-start | bytes 2359304 | tf_op jit(solution)/shard_map/ppermute | solution.py:590
  323.8 30.8 %collective-permute-start.48 = (bf16[256,1536]{1,0:T(8,128)(2,1)}, bf16[256,1536]{1,0:T(8,128)(2,1)}, u32[]{:S(2)}, u32[]{:S(2)}) collective-permute-start(bf16[256,1536]{1,0:T(8,128)(2,1)} %shard_map.406.refs_2_), channel_id=1, source_target_pairs={{1,2},{2,1},{5,6},{6,5},{9,10},{10,9},{13,14},{14,13},{17,18},{18,... | collective-permute-start | bytes 2359304 | tf_op jit(solution)/shard_map/ppermute | solution.py:590
  337.8 37.8 %collective-permute-start.43 = (bf16[1024,256]{1,0:T(8,128)(2,1)}, bf16[1024,256]{1,0:T(8,128)(2,1)}, u32[]{:S(2)}, u32[]{:S(2)}) collective-permute-start(bf16[1024,256]{1,0:T(8,128)(2,1)} %get-tuple-element.338), channel_id=1, source_target_pairs={{0,4},{4,0},{1,5},{5,1},{2,6},{6,2},{3,7},{7,3},{8,12},{12,8},{9,1... | collective-permute-start | bytes 1572872 | tf_op jit(solution)/shard_map/ppermute | solution.py:590
  339.1 15.6 %collective-permute-start.45 = (bf16[8,7680]{1,0:T(8,128)(2,1)S(1)}, bf16[8,7680]{1,0:T(8,128)(2,1)S(1)}, u32[]{:S(2)}, u32[]{:S(2)}) collective-permute-start(bf16[8,7680]{1,0:T(8,128)(2,1)S(1)} %add_convert_fusion.10), channel_id=1, source_target_pairs={{0,2},{1,3},{2,0},{3,1},{4,6},{5,7},{6,4},{7,5},{8,10},{9,11},{10,... | collective-permute-start | bytes 368648 | tf_op jit(solution)/shard_map/ppermute | solution.py:590
  341.1 16.8 %collective-permute-start.46 = (bf16[560,384]{1,0:T(8,128)(2,1)S(1)}, bf16[560,384]{1,0:T(8,128)(2,1)S(1)}, u32[]{:S(2)}, u32[]{:S(2)}) collective-permute-start(bf16[560,384]{1,0:T(8,128)(2,1)S(1)} %fusion.3), channel_id=1, source_target_pairs={{0,1},{1,2},{2,3},{3,0},{4,5},{5,6},{6,7},{7,4},{8,9},{9,10},{10,1... | collective-permute-start | bytes 1290248 | tf_op jit(solution)/shard_map/ppermute | solution.py:590
  354.0 22.9 %collective-permute-start.44 = (bf16[1024,256]{1,0:T(8,128)(2,1)}, bf16[1024,256]{1,0:T(8,128)(2,1)S(1)}, u32[]{:S(2)}, u32[]{:S(2)}) collective-permute-start(bf16[1024,256]{1,0:T(8,128)(2,1)} %get-tuple-element.339), channel_id=1, source_target_pairs={{0,4},{4,0},{1,5},{5,1},{2,6},{6,2},{3,7},{7,3},{8,12},{12,8},{9,1... | collective-permute-start | bytes 1572872 | tf_op jit(solution)/shard_map/ppermute | solution.py:590
  357.9 20.2 %collective-permute-start.49 = (bf16[1024,256]{1,0:T(8,128)(2,1)}, bf16[1024,256]{1,0:T(8,128)(2,1)}, u32[]{:S(2)}, u32[]{:S(2)}) collective-permute-start(bf16[1024,256]{1,0:T(8,128)(2,1)} %get-tuple-element.347), channel_id=1, source_target_pairs={{0,4},{4,0},{1,5},{5,1},{2,6},{6,2},{3,7},{7,3},{8,12},{12,8},{9,1... | collective-permute-start | bytes 1572872 | tf_op jit(solution)/shard_map/ppermute | solution.py:590
  370.5 29.1 %collective-permute-start.56 = (bf16[256,1536]{1,0:T(8,128)(2,1)}, bf16[256,1536]{1,0:T(8,128)(2,1)}, u32[]{:S(2)}, u32[]{:S(2)}) collective-permute-start(bf16[256,1536]{1,0:T(8,128)(2,1)} %get-tuple-element.364.refs_5_), channel_id=1, source_target_pairs={{0,1},{3,2},{1,0},{2,3},{4,5},{7,6},{5,4},{6,7},{8,9},{11,10},{9,8... | collective-permute-start | bytes 2359304 | tf_op jit(solution)/shard_map/ppermute | solution.py:590
  372.3 28.6 %collective-permute-start.57 = (bf16[256,1536]{1,0:T(8,128)(2,1)}, bf16[256,1536]{1,0:T(8,128)(2,1)}, u32[]{:S(2)}, u32[]{:S(2)}) collective-permute-start(bf16[256,1536]{1,0:T(8,128)(2,1)} %get-tuple-element.365.refs_2_), channel_id=1, source_target_pairs={{1,2},{2,1},{5,6},{6,5},{9,10},{10,9},{13,14},{14,13},{17,18},{18,... | collective-permute-start | bytes 2359304 | tf_op jit(solution)/shard_map/ppermute | solution.py:590
  375.6 14.9 %collective-permute-start.54 = (bf16[2,8,12160]{2,1,0:T(8,128)(2,1)}, bf16[2,8,12160]{2,1,0:T(8,128)(2,1)S(1)}, u32[]{:S(2)}, u32[]{:S(2)}) collective-permute-start(bf16[2,8,12160]{2,1,0:T(8,128)(2,1)} %pad_maximum_fusion.7), channel_id=1, source_target_pairs={{0,16},{8,24},{16,0},{24,8},{1,17},{9,25},{17,1},{25,9},{2,18},{10... | collective-permute-start | bytes 1167368 | tf_op jit(solution)/shard_map/ppermute | solution.py:590
  376.9 22.7 %collective-permute-start.55 = (bf16[560,384]{1,0:T(8,128)(2,1)S(1)}, bf16[560,384]{1,0:T(8,128)(2,1)S(1)}, u32[]{:S(2)}, u32[]{:S(2)}) collective-permute-start(bf16[560,384]{1,0:T(8,128)(2,1)S(1)} %fusion.11), channel_id=1, source_target_pairs={{0,1},{1,2},{2,3},{3,0},{4,5},{5,6},{6,7},{7,4},{8,9},{9,10},{10,1... | collective-permute-start | bytes 1290248 | tf_op jit(solution)/shard_map/ppermute | solution.py:590
  402.1 24.2 %collective-permute-start.58 = (bf16[4,8,12160]{2,1,0:T(8,128)(2,1)S(1)}, bf16[4,8,12160]{2,1,0:T(8,128)(2,1)S(1)}, u32[]{:S(2)}, u32[]{:S(2)}) collective-permute-start(bf16[4,8,12160]{2,1,0:T(8,128)(2,1)S(1)} %pad_maximum_fusion.3), channel_id=1, source_target_pairs={{0,4},{4,0},{1,5},{5,1},{2,6},{6,2},{3,7},{7,3},{8,12},{12,8},{9,1... | collective-permute-start | bytes 2334728 | tf_op jit(solution)/shard_map/ppermute | solution.py:590
  405.2 21.1 %collective-permute-start.59 = (f32[512]{0:T(512)S(1)}, f32[512]{0:T(512)S(1)}, u32[]{:S(2)}, u32[]{:S(2)}) collective-permute-start(f32[512]{0:T(512)S(1)} %multiply_reduce_fusion), channel_id=1, source_target_pairs={{0,1},{1,0},{2,3},{3,2},{4,5},{5,4},{6,7},{7,6},{8,9},{9,8},{10,11... | collective-permute-start | bytes 6152 | tf_op jit(solution)/shard_map/ppermute | solution.py:590
  409.4 19.4 %collective-permute-start.60 = (bf16[256,1536]{1,0:T(8,128)(2,1)}, bf16[256,1536]{1,0:T(8,128)(2,1)S(1)}, u32[]{:S(2)}, u32[]{:S(2)}) collective-permute-start(bf16[256,1536]{1,0:T(8,128)(2,1)} %get-tuple-element.373.refs_5_), channel_id=1, source_target_pairs={{0,1},{3,2},{1,0},{2,3},{4,5},{7,6},{5,4},{6,7},{8,9},{11,10},{9,8... | collective-permute-start | bytes 2359304 | tf_op jit(solution)/shard_map/ppermute | solution.py:590
  410.8 20.6 %collective-permute-start.61 = (bf16[256,1536]{1,0:T(8,128)(2,1)}, bf16[256,1536]{1,0:T(8,128)(2,1)S(1)}, u32[]{:S(2)}, u32[]{:S(2)}) collective-permute-start(bf16[256,1536]{1,0:T(8,128)(2,1)} %get-tuple-element.374.refs_2_), channel_id=1, source_target_pairs={{1,2},{2,1},{5,6},{6,5},{9,10},{10,9},{13,14},{14,13},{17,18},{18,... | collective-permute-start | bytes 2359304 | tf_op jit(solution)/shard_map/ppermute | solution.py:590
  431.4 9.8 %collective-permute-start.62 = (f32[512]{0:T(512)S(1)}, f32[512]{0:T(512)S(1)}, u32[]{:S(2)}, u32[]{:S(2)}) collective-permute-start(f32[512]{0:T(512)S(1)} %add.168), channel_id=1, source_target_pairs={{0,2},{1,3},{2,0},{3,1},{4,6},{5,7},{6,4},{7,5},{8,10},{9,11},{10,... | collective-permute-start | bytes 6152 | tf_op jit(solution)/shard_map/ppermute | solution.py:590
  436.8 19.7 %collective-permute-start.65 = (bf16[256,1536]{1,0:T(8,128)(2,1)}, bf16[256,1536]{1,0:T(8,128)(2,1)}, u32[]{:S(2)}, u32[]{:S(2)}) collective-permute-start(bf16[256,1536]{1,0:T(8,128)(2,1)} %get-tuple-element.385.refs_5_), channel_id=1, source_target_pairs={{0,1},{3,2},{1,0},{2,3},{4,5},{7,6},{5,4},{6,7},{8,9},{11,10},{9,8... | collective-permute-start | bytes 2359304 | tf_op jit(solution)/shard_map/ppermute | solution.py:590
  438.9 19.2 %collective-permute-start.66 = (bf16[256,1536]{1,0:T(8,128)(2,1)}, bf16[256,1536]{1,0:T(8,128)(2,1)}, u32[]{:S(2)}, u32[]{:S(2)}) collective-permute-start(bf16[256,1536]{1,0:T(8,128)(2,1)} %get-tuple-element.380.refs_6_.refs_2_), channel_id=1, source_target_pairs={{1,2},{2,1},{5,6},{6,5},{9,10},{10,9},{13,14},{14,13},{17,18},{18,... | collective-permute-start | bytes 2359304 | tf_op jit(solution)/shard_map/ppermute | solution.py:590
  458.8 11.3 %collective-permute-start.70 = (bf16[8,7680]{1,0:T(8,128)(2,1)}, bf16[8,7680]{1,0:T(8,128)(2,1)S(1)}, u32[]{:S(2)}, u32[]{:S(2)}) collective-permute-start(bf16[8,7680]{1,0:T(8,128)(2,1)} %slice.312), channel_id=1, source_target_pairs={{0,1},{1,0},{2,3},{3,2},{4,5},{5,4},{6,7},{7,6},{8,9},{9,8},{10,11... | collective-permute-start | bytes 368648 | tf_op jit(solution)/shard_map/ppermute | solution.py:590
  463.2 17.1 %collective-permute-start.71 = (bf16[256,1536]{1,0:T(8,128)(2,1)}, bf16[256,1536]{1,0:T(8,128)(2,1)}, u32[]{:S(2)}, u32[]{:S(2)}) collective-permute-start(bf16[256,1536]{1,0:T(8,128)(2,1)} %get-tuple-element.391.refs_5_), channel_id=1, source_target_pairs={{0,1},{3,2},{1,0},{2,3},{4,5},{7,6},{5,4},{6,7},{8,9},{11,10},{9,8... | collective-permute-start | bytes 2359304 | tf_op jit(solution)/shard_map/ppermute | solution.py:590
  464.7 17.8 %collective-permute-start.72 = (bf16[256,1536]{1,0:T(8,128)(2,1)}, bf16[256,1536]{1,0:T(8,128)(2,1)}, u32[]{:S(2)}, u32[]{:S(2)}) collective-permute-start(bf16[256,1536]{1,0:T(8,128)(2,1)} %get-tuple-element.392.refs_2_), channel_id=1, source_target_pairs={{1,2},{2,1},{5,6},{6,5},{9,10},{10,9},{13,14},{14,13},{17,18},{18,... | collective-permute-start | bytes 2359304 | tf_op jit(solution)/shard_map/ppermute | solution.py:590
  483.4 25.7 %collective-permute-start.73 = (bf16[64,1536]{1,0:T(8,128)(2,1)S(1)}, bf16[64,1536]{1,0:T(8,128)(2,1)S(1)}, u32[]{:S(2)}, u32[]{:S(2)}) collective-permute-start(bf16[64,1536]{1,0:T(8,128)(2,1)S(1)} %add_convert_fusion.4), channel_id=1, source_target_pairs={{0,1},{1,0},{2,3},{3,2},{4,5},{5,4},{6,7},{7,6},{8,9},{9,8},{10,11... | collective-permute-start | bytes 589832 | tf_op jit(solution)/shard_map/ppermute | solution.py:590
  487.7 21.5 %collective-permute-start.75 = (bf16[256,1536]{1,0:T(8,128)(2,1)}, bf16[256,1536]{1,0:T(8,128)(2,1)S(1)}, u32[]{:S(2)}, u32[]{:S(2)}) collective-permute-start(bf16[256,1536]{1,0:T(8,128)(2,1)} %get-tuple-element.402.refs_5_), channel_id=1, source_target_pairs={{0,1},{3,2},{1,0},{2,3},{4,5},{7,6},{5,4},{6,7},{8,9},{11,10},{9,8... | collective-permute-start | bytes 2359304 | tf_op jit(solution)/shard_map/ppermute | solution.py:590
  489.1 20.1 %collective-permute-start.76 = (bf16[256,1536]{1,0:T(8,128)(2,1)}, bf16[256,1536]{1,0:T(8,128)(2,1)S(1)}, u32[]{:S(2)}, u32[]{:S(2)}) collective-permute-start(bf16[256,1536]{1,0:T(8,128)(2,1)} %get-tuple-element.403.refs_2_), channel_id=1, source_target_pairs={{1,2},{2,1},{5,6},{6,5},{9,10},{10,9},{13,14},{14,13},{17,18},{18,... | collective-permute-start | bytes 2359304 | tf_op jit(solution)/shard_map/ppermute | solution.py:590
  491.7 17.5 %collective-permute-start.74 = (bf16[8,7680]{1,0:T(8,128)(2,1)S(1)}, bf16[8,7680]{1,0:T(8,128)(2,1)S(1)}, u32[]{:S(2)}, u32[]{:S(2)}) collective-permute-start(bf16[8,7680]{1,0:T(8,128)(2,1)S(1)} %add_convert_fusion.8), channel_id=1, source_target_pairs={{0,2},{1,3},{2,0},{3,1},{4,6},{5,7},{6,4},{7,5},{8,10},{9,11},{10,... | collective-permute-start | bytes 368648 | tf_op jit(solution)/shard_map/ppermute | solution.py:590
  509.2 9.7 %collective-permute-start.77 = (bf16[64,1536]{1,0:T(8,128)(2,1)S(1)}, bf16[64,1536]{1,0:T(8,128)(2,1)S(1)}, u32[]{:S(2)}, u32[]{:S(2)}) collective-permute-start(bf16[64,1536]{1,0:T(8,128)(2,1)S(1)} %add_convert_fusion.3), channel_id=1, source_target_pairs={{0,2},{1,3},{2,0},{3,1},{4,6},{5,7},{6,4},{7,5},{8,10},{9,11},{10,... | collective-permute-start | bytes 589832 | tf_op jit(solution)/shard_map/ppermute | solution.py:590
  514.4 14.5 %collective-permute-start.79 = (bf16[256,1536]{1,0:T(8,128)(2,1)}, bf16[256,1536]{1,0:T(8,128)(2,1)S(1)}, u32[]{:S(2)}, u32[]{:S(2)}) collective-permute-start(bf16[256,1536]{1,0:T(8,128)(2,1)} %get-tuple-element.408.refs_4_), channel_id=1, source_target_pairs={{0,1},{3,2},{1,0},{2,3},{4,5},{7,6},{5,4},{6,7},{8,9},{11,10},{9,8... | collective-permute-start | bytes 2359304 | tf_op jit(solution)/shard_map/ppermute | solution.py:590
  516.4 18.4 %collective-permute-start.80 = (bf16[256,1536]{1,0:T(8,128)(2,1)}, bf16[256,1536]{1,0:T(8,128)(2,1)S(1)}, u32[]{:S(2)}, u32[]{:S(2)}) collective-permute-start(bf16[256,1536]{1,0:T(8,128)(2,1)} %get-tuple-element.409.refs_2_), channel_id=1, source_target_pairs={{1,2},{2,1},{5,6},{6,5},{9,10},{10,9},{13,14},{14,13},{17,18},{18,... | collective-permute-start | bytes 2359304 | tf_op jit(solution)/shard_map/ppermute | solution.py:590
  534.8 10.4 %collective-permute-start.85 = (bf16[2,8,10880]{2,1,0:T(8,128)(2,1)S(1)}, bf16[2,8,10880]{2,1,0:T(8,128)(2,1)S(1)}, u32[]{:S(2)}, u32[]{:S(2)}) collective-permute-start(bf16[2,8,10880]{2,1,0:T(8,128)(2,1)S(1)} %pad_maximum_fusion.8), channel_id=1, source_target_pairs={{0,16},{8,24},{16,0},{24,8},{1,17},{9,25},{17,1},{25,9},{2,18},{10... | collective-permute-start | bytes 1044488 | tf_op jit(solution)/shard_map/ppermute | solution.py:590
  541.1 14.9 %collective-permute-start.81 = (bf16[256,1536]{1,0:T(8,128)(2,1)}, bf16[256,1536]{1,0:T(8,128)(2,1)}, u32[]{:S(2)}, u32[]{:S(2)}) collective-permute-start(bf16[256,1536]{1,0:T(8,128)(2,1)} %get-tuple-element.413.refs_3_), channel_id=1, source_target_pairs={{1,0},{2,3},{5,4},{6,7},{9,8},{10,11},{13,12},{14,15},{17,16},{18,... | collective-permute-start | bytes 2359304 | tf_op jit(solution)/shard_map/ppermute | solution.py:590
  543.3 13.0 %collective-permute-start.82 = (bf16[256,1536]{1,0:T(8,128)(2,1)}, bf16[256,1536]{1,0:T(8,128)(2,1)}, u32[]{:S(2)}, u32[]{:S(2)}) collective-permute-start(bf16[256,1536]{1,0:T(8,128)(2,1)} %get-tuple-element.414.refs_1_), channel_id=1, source_target_pairs={{1,2},{2,1},{5,6},{6,5},{9,10},{10,9},{13,14},{14,13},{17,18},{18,... | collective-permute-start | bytes 2359304 | tf_op jit(solution)/shard_map/ppermute | solution.py:590
  545.3 16.7 %collective-permute-start.86 = (bf16[128,1536]{1,0:T(8,128)(2,1)S(1)}, bf16[128,1536]{1,0:T(8,128)(2,1)}, u32[]{:S(2)}, u32[]{:S(2)}) collective-permute-start(bf16[128,1536]{1,0:T(8,128)(2,1)S(1)} %pad_maximum_fusion.5), channel_id=1, source_target_pairs={{0,16},{8,24},{16,0},{24,8},{1,17},{9,25},{17,1},{25,9},{2,18},{10... | collective-permute-start | bytes 1179656 | tf_op jit(solution)/shard_map/ppermute | solution.py:590
  546.5 15.5 %collective-permute-start.87 = (bf16[4,8,10880]{2,1,0:T(8,128)(2,1)}, bf16[4,8,10880]{2,1,0:T(8,128)(2,1)}, u32[]{:S(2)}, u32[]{:S(2)}) collective-permute-start(bf16[4,8,10880]{2,1,0:T(8,128)(2,1)} %pad_maximum_fusion.4), channel_id=1, source_target_pairs={{0,4},{4,0},{1,5},{5,1},{2,6},{6,2},{3,7},{7,3},{8,12},{12,8},{9,1... | collective-permute-start | bytes 2088968 | tf_op jit(solution)/shard_map/ppermute | solution.py:590
  559.8 27.6 %collective-permute-start.83 = (bf16[256,1536]{1,0:T(8,128)(2,1)}, bf16[256,1536]{1,0:T(8,128)(2,1)}, u32[]{:S(2)}, u32[]{:S(2)}) collective-permute-start(bf16[256,1536]{1,0:T(8,128)(2,1)} %get-tuple-element.416.refs_1_), channel_id=1, source_target_pairs={{1,0},{2,3},{5,4},{6,7},{9,8},{10,11},{13,12},{14,15},{17,16},{18,... | collective-permute-start | bytes 2359304 | tf_op jit(solution)/shard_map/ppermute | solution.py:590
  566.5 23.8 %collective-permute-start.88 = (bf16[256,1536]{1,0:T(8,128)(2,1)S(1)}, bf16[256,1536]{1,0:T(8,128)(2,1)S(1)}, u32[]{:S(2)}, u32[]{:S(2)}) collective-permute-start(bf16[256,1536]{1,0:T(8,128)(2,1)S(1)} %pad_maximum_fusion.2), channel_id=1, source_target_pairs={{0,4},{4,0},{1,5},{5,1},{2,6},{6,2},{3,7},{7,3},{8,12},{12,8},{9,1... | collective-permute-start | bytes 2359304 | tf_op jit(solution)/shard_map/ppermute | solution.py:590
  (90 other events, 846.8 us)

commit v5 on v4

--- a/solution.py
+++ b/solution.py
@@ -1178,7 +1178,7 @@
         us=20,
     )
 
-    tiles = [(a, min(768, ff - a)) for a in range(0, ff, 768)]
+    tiles = [(0, min(256, ff))] + [(a, min(1024, ff - a)) for a in range(256, ff, 1024)]
     w1t = ffn_in.T
     y2_pieces = ring_pieces(y2, "tensor")
     feed_bias = ffn_bias.astype(F32)[None]

time: 601 us -> 600 us (level)
  transfers between devices with their start and end apart: 89 -> 89, of which waited for: 33 -> 34; matrix products, arithmetic and copies ran while one was open for 7% -> 7% of each run, Pallas kernels for 41% -> 41%
where the time goes in v5:
time: 600 us; the launch traced here: 591 us
  Pallas kernels  266 us (44%)
  waiting for transfers between devices  142 us (24%)
  starting transfers between devices  126 us (21%)
  other arithmetic  28.2 us (5%)
  local copies, waits for them, and re-layouts  25.8 us (4%)
    pallas_call x27, Pallas kernels, run_kernel(): pl.pallas_call(reading, grid_spec=pltpu.PrefetchScalarGridSpec(num_scalar...  266 us
    ppermute x89, waiting for transfers between devices, send(): return jax.tree.map(lambda v: lax.ppermute(v, axis, pairs), values)  142 us
    ppermute x89, starting transfers between devices, send(): return jax.tree.map(lambda v: lax.ppermute(v, axis, pairs), values)  126 us
    unnamed x148, local copies, waits for them, and re-layouts  13.9 us
  transfers between devices with their start and end apart: 89, of which 34 were waited for; matrix products, arithmetic and copies ran while one was open for 7% of the time, Pallas kernels for 41%

profile of v5, /device:TPU:9, one launch (start us, length us, event | category | flops | bytes accessed | tf_op | source)
XLA Modules:
  0.0 591.1 jit_solution(12378789134618202496)
XLA Ops:
  2.0 2.6 shard_map.392.refs_8_
  10.3 5.6 shard_map.393
  15.9 3.3 sine_multiply_fusion
  19.2 15.7 %shard_map.394 = (bf16[1024,1536]{1,0:T(8,128)(2,1)}, bf16[48,1024]{1,0:T(8,128)(2,1)}, bf16[1024,384]{1,0:T(8,128)(2,1)}, bf16[1024,384]{1,0:T(8,128)(2,1)}, bf...) custom-call(s32[12]{0:T(128)} %stack.104.meta_ref, ...), custom_call_target="tpu_custom_call" | custom-call | flops 17250000896 | bytes 18121472 | tf_op jit(solution)/shard_map/pallas_call | solution.py:89
  39.0 4.6 collective-permute-done.2.refs_1_
  43.5 2.7 collective-permute-done.3.refs_2_
  47.0 3.1 shard_map.395.refs_8_.refs_21_.refs_28_
  50.6 3.3 collective-permute-start.4
  62.9 25.3 %shard_map.396 = (bf16[256,384]{1,0:T(8,128)(2,1)}, bf16[256,384]{1,0:T(8,128)(2,1)}, bf16[256,384]{1,0:T(8,128)(2,1)}, bf16[256,384]{1,0:T(8,128)(2,1)}, bf16[1...) custom-call(s32[12]{0:T(128)} %stack.104.meta_ref, ...), custom_call_target="tpu_custom_call" | custom-call | flops 28750000128 | bytes 14352384 | tf_op jit(solution)/shard_map/pallas_call | solution.py:89
  88.2 8.7 %collective-permute-done.11.refs_10_.refs_17_ = bf16[576,384]{1,0:T(8,128)(2,1)S(1)} collective-permute-done((bf16[576,384]{1,0:T(8,128)(2,1)S(1)}, bf16[576,384]{1,0:T(8,128)(2,1)S(1)}, u32[]{:S(2)}, u32[]{:S(2)}) %collective-permute-start.11) | collective-permute-done | bytes 442400 | tf_op jit(solution)/shard_map/ppermute | solution.py:590
  97.0 3.7 collective-permute-done.12.refs_11_.refs_18_
  103.6 3.4 collective-permute-done.13.refs_1_
  107.0 10.8 %collective-permute-done.14.refs_2_ = bf16[256,384]{1,0:T(8,128)(2,1)S(1)} collective-permute-done((bf16[256,384]{1,0:T(8,128)(2,1)}, bf16[256,384]{1,0:T(8,128)(2,1)S(1)}, u32[]{:S(2)}, u32[]{:S(2)}) %collective-permute-start.14) | collective-permute-done | bytes 196640 | tf_op jit(solution)/shard_map/ppermute | solution.py:590
  121.9 2.3 collective-permute-done.17.refs_13_.refs_20_
  128.5 20.8 %shard_map.397 = (bf16[256,1536]{1,0:T(8,128)(2,1)}, f32[256,1536]{1,0:T(8,128)}, f32[256,1536]{1,0:T(8,128)}, bf16[256,1536]{1,0:T(8,128)(2,1)}, bf16[256,1536]...) custom-call(s32[12]{0:T(128)} %stack.104.meta_ref, ...), custom_call_target="tpu_custom_call" | custom-call | flops 23000000512 | bytes 35987456 | tf_op jit(solution)/shard_map/pallas_call | solution.py:89
  149.6 16.8 %shard_map.398 = (bf16[1024,1536]{1,0:T(8,128)(2,1)}, f32[256,1536]{1,0:T(8,128)}, f32[16,2240]{1,0:T(8,128)}, f32[16,1536]{1,0:T(8,128)}, f32[16,1536]{1,0:T(8,128)}, /*index=5*/f32[16,2240]{1,0:T(8,128)}) custom-call(s32[12]{0:T(128)} %stack.104.meta_ref, bf16[256,1536]{1,0:T(8,128)(2,1)} %get-tuple-element.257.refs_0_, bf16[1024,1536]{1,0:T(8,128)(2,1)} %bitcast.176, ...), custom_call_target="tpu_custom_call" | custom-call | flops 20700000256 | bytes 26510080 | tf_op jit(solution)/shard_map/pallas_call | solution.py:89
  169.9 16.1 %shard_map.399 = (bf16[1024,1536]{1,0:T(8,128)(2,1)}, bf16[256,1536]{1,0:T(8,128)(2,1)}, f32[16,2240]{1,0:T(8,128)}, f32[16,1536]{1,0:T(8,128)}, f32[16,1536]{1,0:T(8,128)}, /*index=5*/f32[16,2240]{1,0:T(8,128)}) custom-call(s32[12]{0:T(128)} %stack.104.meta_ref, bf16[256,1536]{1,0:T(8,128)(2,1)} %copy-done.43, ...), custom_call_target="tpu_custom_call", output_to_operand_aliasing={{0}: (15, {})} | custom-call | flops 20700000256 | bytes 27779840 | tf_op jit(solution)/shard_map/pallas_call | solution.py:89
  190.5 16.1 %shard_map.400 = (bf16[1024,1536]{1,0:T(8,128)(2,1)}, bf16[256,1536]{1,0:T(8,128)(2,1)}, f32[16,2240]{1,0:T(8,128)}, f32[16,1536]{1,0:T(8,128)}, f32[16,1536]{1,0:T(8,128)}, /*index=5*/f32[16,2240]{1,0:T(8,128)}) custom-call(s32[12]{0:T(128)} %stack.104.meta_ref, bf16[256,1536]{1,0:T(8,128)(2,1)} %copy-done.39, ...), custom_call_target="tpu_custom_call", output_to_operand_aliasing={{0}: (15, {})} | custom-call | flops 20700000256 | bytes 27779840 | tf_op jit(solution)/shard_map/pallas_call | solution.py:89
  209.2 13.5 %collective-permute-done.28.refs_0_ = bf16[256,1536]{1,0:T(8,128)(2,1)S(1)} collective-permute-done((bf16[256,1536]{1,0:T(8,128)(2,1)S(1)}, bf16[256,1536]{1,0:T(8,128)(2,1)S(1)}, u32[]{:S(2)}, u32[]{:S(2)}) %collective-permute-start.28) | collective-permute-done | bytes 786464 | tf_op jit(solution)/shard_map/ppermute | solution.py:590
  223.5 16.2 %shard_map.401 = (bf16[1024,1536]{1,0:T(8,128)(2,1)}, bf16[256,1536]{1,0:T(8,128)(2,1)}, f32[16,2240]{1,0:T(8,128)}, f32[16,1536]{1,0:T(8,128)}, f32[16,1536]{1,0:T(8,128)}, /*index=5*/f32[16,2240]{1,0:T(8,128)}) custom-call(s32[12]{0:T(128)} %stack.104.meta_ref, bf16[256,1536]{1,0:T(8,128)(2,1)} %copy-done.42, ...), custom_call_target="tpu_custom_call", output_to_operand_aliasing={{0}: (15, {})} | custom-call | flops 20700000256 | bytes 27779840 | tf_op jit(solution)/shard_map/pallas_call | solution.py:89
  242.2 2.4 fusion.52
  244.6 14.1 %collective-permute-done.31.refs_1_ = bf16[256,1536]{1,0:T(8,128)(2,1)S(1)} collective-permute-done((bf16[256,1536]{1,0:T(8,128)(2,1)S(1)}, bf16[256,1536]{1,0:T(8,128)(2,1)S(1)}, u32[]{:S(2)}, u32[]{:S(2)}) %collective-permute-start.31) | collective-permute-done | bytes 786464 | tf_op jit(solution)/shard_map/ppermute | solution.py:590
  261.1 26.8 %shard_map.402 = (bf16[256,128]{1,0:T(8,128)(2,1)}, bf16[256,128]{1,0:T(8,128)(2,1)}, bf16[256,128]{1,0:T(8,128)(2,1)}, bf16[256,128]{1,0:T(8,128)(2,1)}, bf16[2...) custom-call(s32[12]{0:T(128)} %stack.104.meta_ref, ...), custom_call_target="tpu_custom_call" | custom-call | flops 29899999232 | bytes 42868736 | tf_op jit(solution)/shard_map/pallas_call | solution.py:89
  287.9 3.0 collective-permute-start.34
  294.6 6.1 %collective-permute-start.40 = (bf16[8,12160]{1,0:T(8,128)(2,1)S(1)}, bf16[8,12160]{1,0:T(8,128)(2,1)S(1)}, u32[]{:S(2)}, u32[]{:S(2)}) collective-permute-start(bf16[8,12160]{1,0:T(8,128)(2,1)S(1)} %select_convert_fusion.2), channel_id=1, source_target_pairs={{0,4},{4,0},{1,5},{5,1},{2,6},{6,2},{3,7},{7,3},{8,12},{12,8},{9,1... | collective-permute-start | bytes 583688 | tf_op jit(solution)/shard_map/ppermute | solution.py:590
  300.7 2.9 shard_map.406.refs_2_
  304.0 2.7 collective-permute-start.38
  310.0 11.0 %shard_map.403 = (f32[1024,128]{1,0:T(8,128)}, f32[1024,256]{1,0:T(8,128)}, bf16[1024,256]{1,0:T(8,128)(2,1)}, f32[8,1024]{1,0:T(8,128)}, f32[8,1024]{1,0:T(8,128)}) custom-call(s32[12]{0:T(128)} %stack.104.meta_ref, bf16[1024,384]{1,0:T(8,128)(2,1)} %get-tuple-element.300.refs_0_, f32[8,1024]{1,0:T(8,128)} %copy-done.16, f32[8,1024]{1,0:T(8,128)} %copy-done.16, ...), custom_call_target="tpu_custom_call" | custom-call | flops 14375000064 | bytes 8912896 | tf_op jit(solution)/shard_map/pallas_call | solution.py:89
  322.3 3.0 collective-permute-start.48
  325.3 10.9 %shard_map.404 = (f32[1024,128]{1,0:T(8,128)}, f32[1024,256]{1,0:T(8,128)}, bf16[1024,256]{1,0:T(8,128)(2,1)}, f32[8,1024]{1,0:T(8,128)}, f32[8,1024]{1,0:T(8,128)}) custom-call(s32[12]{0:T(128)} %stack.104.meta_ref, bf16[1024,384]{1,0:T(8,128)(2,1)} %get-tuple-element.300.refs_0_, f32[8,1024]{1,0:T(8,128)} %copy-done.16, f32[8,1024]{1,0:T(8,128)} %copy-done.16, ...), custom_call_target="tpu_custom_call" | custom-call | flops 14375000064 | bytes 9240576 | tf_op jit(solution)/shard_map/pallas_call | solution.py:89
  341.5 11.0 %shard_map.405 = (f32[1024,128]{1,0:T(8,128)}, f32[1024,256]{1,0:T(8,128)}, bf16[1024,256]{1,0:T(8,128)(2,1)}, f32[8,1024]{1,0:T(8,128)}, f32[8,1024]{1,0:T(8,128)}) custom-call(s32[12]{0:T(128)} %stack.104.meta_ref, bf16[1024,384]{1,0:T(8,128)(2,1)} %get-tuple-element.300.refs_0_, f32[8,1024]{1,0:T(8,128)} %copy-done.16, f32[8,1024]{1,0:T(8,128)} %copy-done.16, ...), custom_call_target="tpu_custom_call" | custom-call | flops 14375000064 | bytes 9240576 | tf_op jit(solution)/shard_map/pallas_call | solution.py:89
  353.2 3.2 collective-permute-done.46
  360.1 2.3 collective-permute-start.51
  365.2 3.7 shard_map.408
  370.8 2.3 collective-permute-start.57
  376.7 12.3 %shard_map.407 = (bf16[512,1536]{1,0:T(8,128)(2,1)}, f32[16,5760]{1,0:T(8,128)}) custom-call(s32[12]{0:T(128)} %stack.104.meta_ref, f32[1024,128]{1,0:T(8,128)} %get-tuple-element.328.refs_15_.refs_0_, f32[1024,128]{1,0:T(8,128)} %get-tuple-element.333.refs_15_.refs_1_, f32[1024,128]{1,0:T(8,128)} %get-tuple-element.334.refs_2_, ...), custom_call_target="tpu_custom_call" | custom-call | flops 16099999744 | bytes 25470464 | tf_op jit(solution)/shard_map/pallas_call | solution.py:89
  389.1 9.0 %collective-permute-done.55 = bf16[560,384]{1,0:T(8,128)(2,1)S(1)} collective-permute-done((bf16[560,384]{1,0:T(8,128)(2,1)S(1)}, bf16[560,384]{1,0:T(8,128)(2,1)S(1)}, u32[]{:S(2)}, u32[]{:S(2)}) %collective-permute-start.55) | collective-permute-done | bytes 430112 | tf_op jit(solution)/shard_map/ppermute | solution.py:590
  400.6 2.8 collective-permute-start.58
  403.7 4.1 shard_map.410
  409.3 3.0 collective-permute-start.61
  412.3 12.5 %shard_map.409 = (bf16[512,1536]{1,0:T(8,128)(2,1)}, f32[16,5760]{1,0:T(8,128)}) custom-call(s32[12]{0:T(128)} %stack.104.meta_ref, f32[1024,128]{1,0:T(8,128)} %get-tuple-element.328.refs_15_.refs_0_, f32[1024,128]{1,0:T(8,128)} %get-tuple-element.333.refs_15_.refs_1_, f32[1024,128]{1,0:T(8,128)} %get-tuple-element.334.refs_2_, ...), custom_call_target="tpu_custom_call" | custom-call | flops 16099999744 | bytes 25839104 | tf_op jit(solution)/shard_map/pallas_call | solution.py:89
  424.8 2.4 collective-permute-done.60.refs_0_
  427.2 2.7 collective-permute-done.61.refs_3_
  431.1 4.1 shard_map.411
  437.3 2.3 collective-permute-start.66
  440.6 5.8 shard_map.412
  448.4 2.3 collective-permute-start.63
  457.3 4.4 shard_map.413
  463.1 2.3 collective-permute-start.72
  469.7 2.3 collective-permute-done.67
  474.7 4.1 collective-permute-done.71.refs_0_
  482.0 4.1 shard_map.414
  487.6 2.4 collective-permute-start.76
  490.1 17.5 %collective-permute-done.74 = bf16[8,7680]{1,0:T(8,128)(2,1)S(1)} collective-permute-done((bf16[8,7680]{1,0:T(8,128)(2,1)S(1)}, bf16[8,7680]{1,0:T(8,128)(2,1)S(1)}, u32[]{:S(2)}, u32[]{:S(2)}) %collective-permute-start.74) | collective-permute-done | bytes 122912 | tf_op jit(solution)/shard_map/ppermute | solution.py:590
  508.7 4.1 shard_map.415
  514.9 2.3 collective-permute-start.80
  517.4 10.0 %collective-permute-done.79.refs_0_ = bf16[256,1536]{1,0:T(8,128)(2,1)S(1)} collective-permute-done((bf16[256,1536]{1,0:T(8,128)(2,1)}, bf16[256,1536]{1,0:T(8,128)(2,1)S(1)}, u32[]{:S(2)}, u32[]{:S(2)}) %collective-permute-start.79) | collective-permute-done | bytes 786464 | tf_op jit(solution)/shard_map/ppermute | solution.py:590
  527.4 5.8 collective-permute-done.80.refs_3_
  535.6 3.9 shard_map.416
  544.9 9.4 %collective-permute-start.87 = (bf16[4,8,10880]{2,1,0:T(8,128)(2,1)}, bf16[4,8,10880]{2,1,0:T(8,128)(2,1)}, u32[]{:S(2)}, u32[]{:S(2)}) collective-permute-start(bf16[4,8,10880]{2,1,0:T(8,128)(2,1)} %pad_maximum_fusion.4), channel_id=1, source_target_pairs={{0,4},{4,0},{1,5},{5,1},{2,6},{6,2},{3,7},{7,3},{8,12},{12,8},{9,1... | collective-permute-start | bytes 2088968 | tf_op jit(solution)/shard_map/ppermute | solution.py:590
  554.7 3.5 shard_map.417
  564.8 9.7 %collective-permute-start.88 = (bf16[256,1536]{1,0:T(8,128)(2,1)S(1)}, bf16[256,1536]{1,0:T(8,128)(2,1)S(1)}, u32[]{:S(2)}, u32[]{:S(2)}) collective-permute-start(bf16[256,1536]{1,0:T(8,128)(2,1)S(1)} %pad_maximum_fusion.2), channel_id=1, source_target_pairs={{0,4},{4,0},{1,5},{5,1},{2,6},{6,2},{3,7},{7,3},{8,12},{12,8},{9,1... | collective-permute-start | bytes 2359304 | tf_op jit(solution)/shard_map/ppermute | solution.py:590
  577.9 2.6 copy.57
  585.8 2.8 shard_map.418
  (371 shorter events, 134.0 us)
Async XLA Ops:
  4.7 34.3 %collective-permute-start.1 = (bf16[144,1536]{1,0:T(8,128)(2,1)}, bf16[144,1536]{1,0:T(8,128)(2,1)S(1)}, u32[]{:S(2)}, u32[]{:S(2)}) collective-permute-start(bf16[144,1536]{1,0:T(8,128)(2,1)} %shard_map.392.refs_8_), channel_id=1, source_target_pairs={{0,1},{1,2},{2,3},{3,0},{4,5},{5,6},{6,7},{7,4},{8,9},{9,10},{10,1... | collective-permute-start | bytes 1327112 | tf_op jit(solution)/shard_map/ppermute | solution.py:590
  5.9 37.6 %collective-permute-start.2 = (bf16[144,1536]{1,0:T(8,128)(2,1)}, bf16[144,1536]{1,0:T(8,128)(2,1)S(1)}, u32[]{:S(2)}, u32[]{:S(2)}) collective-permute-start(bf16[144,1536]{1,0:T(8,128)(2,1)} %shard_map.392.refs_8_), channel_id=1, source_target_pairs={{0,2},{1,3},{2,0},{3,1},{4,6},{5,7},{6,4},{7,5},{8,10},{9,11},{10,... | collective-permute-start | bytes 1327112 | tf_op jit(solution)/shard_map/ppermute | solution.py:590
  7.0 39.3 %collective-permute-start.3 = (bf16[144,1536]{1,0:T(8,128)(2,1)}, bf16[144,1536]{1,0:T(8,128)(2,1)S(1)}, u32[]{:S(2)}, u32[]{:S(2)}) collective-permute-start(bf16[144,1536]{1,0:T(8,128)(2,1)} %shard_map.392.refs_8_), channel_id=1, source_target_pairs={{0,3},{1,0},{2,1},{3,2},{4,7},{5,4},{6,5},{7,6},{8,11},{9,8},{10,9... | collective-permute-start | bytes 1327112 | tf_op jit(solution)/shard_map/ppermute | solution.py:590
  36.0 23.6 %collective-permute-start.7 = (bf16[1024,768]{1,0:T(8,128)(2,1)}, bf16[1024,768]{1,0:T(8,128)(2,1)S(1)}, u32[]{:S(2)}, u32[]{:S(2)}) collective-permute-start(bf16[1024,768]{1,0:T(8,128)(2,1)} %get-tuple-element.228.refs_4_.refs_6_), channel_id=1, source_target_pairs={{0,4},{4,0},{1,5},{5,1},{2,6},{6,2},{3,7},{7,3},{8,12},{12,8},{9,1... | collective-permute-start | bytes 4718600 | tf_op jit(solution)/shard_map/ppermute | solution.py:590
  50.1 11.4 %collective-permute-start.6 = (bf16[3,144,1536]{2,1,0:T(8,128)(2,1)}, bf16[3,144,1536]{2,1,0:T(8,128)(2,1)S(1)}, u32[]{:S(2)}, u32[]{:S(2)}) collective-permute-start(bf16[3,144,1536]{2,1,0:T(8,128)(2,1)} %shard_map.395.refs_8_.refs_21_.refs_28_), channel_id=1, source_target_pairs={{0,4},{4,0},{1,5},{5,1},{2,6},{6,2},{3,7},{7,3},{8,12},{12,8},{9,1... | collective-permute-start | bytes 3981320 | tf_op jit(solution)/shard_map/ppermute | solution.py:590
  56.4 44.2 %collective-permute-start.8 = (bf16[3,144,1536]{2,1,0:T(8,128)(2,1)}, bf16[3,144,1536]{2,1,0:T(8,128)(2,1)S(1)}, u32[]{:S(2)}, u32[]{:S(2)}) collective-permute-start(bf16[3,144,1536]{2,1,0:T(8,128)(2,1)} %shard_map.395.refs_8_.refs_21_.refs_28_), channel_id=1, source_target_pairs={{0,8},{8,0},{16,24},{24,16},{1,9},{9,1},{17,25},{25,17},{2,10},{10... | collective-permute-start | bytes 3981320 | tf_op jit(solution)/shard_map/ppermute | solution.py:590
  57.6 43.0 %collective-permute-start.9 = (bf16[3,144,1536]{2,1,0:T(8,128)(2,1)}, bf16[3,144,1536]{2,1,0:T(8,128)(2,1)S(1)}, u32[]{:S(2)}, u32[]{:S(2)}) collective-permute-start(bf16[3,144,1536]{2,1,0:T(8,128)(2,1)} %shard_map.395.refs_8_.refs_21_.refs_28_), channel_id=1, source_target_pairs={{0,16},{8,24},{16,0},{24,8},{1,17},{9,25},{17,1},{25,9},{2,18},{10... | collective-permute-start | bytes 3981320 | tf_op jit(solution)/shard_map/ppermute | solution.py:590
  58.9 29.3 %collective-permute-start.10 = (bf16[576,384]{1,0:T(8,128)(2,1)S(1)}, bf16[576,384]{1,0:T(8,128)(2,1)S(1)}, u32[]{:S(2)}, u32[]{:S(2)}) collective-permute-start(bf16[576,384]{1,0:T(8,128)(2,1)S(1)} %copy-done.46), channel_id=1, source_target_pairs={{0,1},{1,2},{2,3},{3,0},{4,5},{5,6},{6,7},{7,4},{8,9},{9,10},{10,1... | collective-permute-start | bytes 1327112 | tf_op jit(solution)/shard_map/ppermute | solution.py:590
  59.6 37.3 %collective-permute-start.11 = (bf16[576,384]{1,0:T(8,128)(2,1)S(1)}, bf16[576,384]{1,0:T(8,128)(2,1)S(1)}, u32[]{:S(2)}, u32[]{:S(2)}) collective-permute-start(bf16[576,384]{1,0:T(8,128)(2,1)S(1)} %copy-done.46), channel_id=1, source_target_pairs={{0,2},{1,3},{2,0},{3,1},{4,6},{5,7},{6,4},{7,5},{8,10},{9,11},{10,... | collective-permute-start | bytes 1327112 | tf_op jit(solution)/shard_map/ppermute | solution.py:590
  61.5 39.1 %collective-permute-start.12 = (bf16[576,384]{1,0:T(8,128)(2,1)S(1)}, bf16[576,384]{1,0:T(8,128)(2,1)}, u32[]{:S(2)}, u32[]{:S(2)}) collective-permute-start(bf16[576,384]{1,0:T(8,128)(2,1)S(1)} %copy-done.46), channel_id=1, source_target_pairs={{0,3},{1,0},{2,1},{3,2},{4,7},{5,4},{6,5},{7,6},{8,11},{9,8},{10,9... | collective-permute-start | bytes 1327112 | tf_op jit(solution)/shard_map/ppermute | solution.py:590
  100.7 19.0 %collective-permute-start.21 = (bf16[3,64,1536]{2,1,0:T(8,128)(2,1)S(1)}, bf16[3,64,1536]{2,1,0:T(8,128)(2,1)}, u32[]{:S(2)}, u32[]{:S(2)}) collective-permute-start(bf16[3,64,1536]{2,1,0:T(8,128)(2,1)S(1)} %slice.231), channel_id=1, source_target_pairs={{0,16},{8,24},{16,0},{24,8},{1,17},{9,25},{17,1},{25,9},{2,18},{10... | collective-permute-start | bytes 1769480 | tf_op jit(solution)/shard_map/ppermute | solution.py:590
  101.0 16.7 %collective-permute-start.14 = (bf16[256,384]{1,0:T(8,128)(2,1)}, bf16[256,384]{1,0:T(8,128)(2,1)S(1)}, u32[]{:S(2)}, u32[]{:S(2)}) collective-permute-start(bf16[256,384]{1,0:T(8,128)(2,1)} %get-tuple-element.239), channel_id=1, source_target_pairs={{0,2},{1,3},{2,0},{3,1},{4,6},{5,7},{6,4},{7,5},{8,10},{9,11},{10,... | collective-permute-start | bytes 589832 | tf_op jit(solution)/shard_map/ppermute | solution.py:590
  101.0 17.7 %collective-permute-start.15 = (bf16[256,384]{1,0:T(8,128)(2,1)}, bf16[256,384]{1,0:T(8,128)(2,1)S(1)}, u32[]{:S(2)}, u32[]{:S(2)}) collective-permute-start(bf16[256,384]{1,0:T(8,128)(2,1)} %get-tuple-element.240), channel_id=1, source_target_pairs={{0,3},{1,0},{2,1},{3,2},{4,7},{5,4},{6,5},{7,6},{8,11},{9,8},{10,9... | collective-permute-start | bytes 589832 | tf_op jit(solution)/shard_map/ppermute | solution.py:590
  103.0 18.4 %collective-permute-start.20 = (bf16[3,80,1536]{2,1,0:T(8,128)(2,1)S(1)}, bf16[3,80,1536]{2,1,0:T(8,128)(2,1)S(1)}, u32[]{:S(2)}, u32[]{:S(2)}) collective-permute-start(bf16[3,80,1536]{2,1,0:T(8,128)(2,1)S(1)} %slice.230), channel_id=1, source_target_pairs={{0,8},{8,0},{16,24},{24,16},{1,9},{9,1},{17,25},{25,17},{2,10},{10... | collective-permute-start | bytes 2211848 | tf_op jit(solution)/shard_map/ppermute | solution.py:590
  149.3 19.2 %collective-permute-start.26 = (bf16[256,1536]{1,0:T(8,128)(2,1)}, bf16[256,1536]{1,0:T(8,128)(2,1)S(1)}, u32[]{:S(2)}, u32[]{:S(2)}) collective-permute-start(bf16[256,1536]{1,0:T(8,128)(2,1)} %get-tuple-element.257.refs_0_), channel_id=1, source_target_pairs={{0,1},{1,2},{2,3},{3,0},{4,5},{5,6},{6,7},{7,4},{8,9},{9,10},{10,1... | collective-permute-start | bytes 2359304 | tf_op jit(solution)/shard_map/ppermute | solution.py:590
  168.5 20.2 %collective-permute-start.27 = (bf16[256,1536]{1,0:T(8,128)(2,1)S(1)}, bf16[256,1536]{1,0:T(8,128)(2,1)S(1)}, u32[]{:S(2)}, u32[]{:S(2)}) collective-permute-start(bf16[256,1536]{1,0:T(8,128)(2,1)S(1)} %collective-permute-done.26.refs_0_), channel_id=1, source_target_pairs={{0,1},{1,2},{2,3},{3,0},{4,5},{5,6},{6,7},{7,4},{8,9},{9,10},{10,1... | collective-permute-start | bytes 2359304 | tf_op jit(solution)/shard_map/ppermute | solution.py:590
  186.0 20.6 %collective-permute-start.29 = (bf16[256,1536]{1,0:T(8,128)(2,1)}, bf16[256,1536]{1,0:T(8,128)(2,1)S(1)}, u32[]{:S(2)}, u32[]{:S(2)}) collective-permute-start(bf16[256,1536]{1,0:T(8,128)(2,1)} %get-tuple-element.276), channel_id=1, source_target_pairs={{0,1},{1,2},{2,3},{3,0},{4,5},{5,6},{6,7},{7,4},{8,9},{9,10},{10,1... | collective-permute-start | bytes 2359304 | tf_op jit(solution)/shard_map/ppermute | solution.py:590
  188.8 33.9 %collective-permute-start.28 = (bf16[256,1536]{1,0:T(8,128)(2,1)S(1)}, bf16[256,1536]{1,0:T(8,128)(2,1)S(1)}, u32[]{:S(2)}, u32[]{:S(2)}) collective-permute-start(bf16[256,1536]{1,0:T(8,128)(2,1)S(1)} %collective-permute-done.27.refs_0_), channel_id=1, source_target_pairs={{0,1},{1,2},{2,3},{3,0},{4,5},{5,6},{6,7},{7,4},{8,9},{9,10},{10,1... | collective-permute-start | bytes 2359304 | tf_op jit(solution)/shard_map/ppermute | solution.py:590
  208.0 31.8 %collective-permute-start.30 = (bf16[256,1536]{1,0:T(8,128)(2,1)S(1)}, bf16[256,1536]{1,0:T(8,128)(2,1)S(1)}, u32[]{:S(2)}, u32[]{:S(2)}) collective-permute-start(bf16[256,1536]{1,0:T(8,128)(2,1)S(1)} %add_convert_fusion.1), channel_id=1, source_target_pairs={{0,1},{1,2},{2,3},{3,0},{4,5},{5,6},{6,7},{7,4},{8,9},{9,10},{10,1... | collective-permute-start | bytes 2359304 | tf_op jit(solution)/shard_map/ppermute | solution.py:590
  241.1 17.6 %collective-permute-start.31 = (bf16[256,1536]{1,0:T(8,128)(2,1)S(1)}, bf16[256,1536]{1,0:T(8,128)(2,1)S(1)}, u32[]{:S(2)}, u32[]{:S(2)}) collective-permute-start(bf16[256,1536]{1,0:T(8,128)(2,1)S(1)} %add_convert_fusion), channel_id=1, source_target_pairs={{0,1},{1,2},{2,3},{3,0},{4,5},{5,6},{6,7},{7,4},{8,9},{9,10},{10,1... | collective-permute-start | bytes 2359304 | tf_op jit(solution)/shard_map/ppermute | solution.py:590
  259.6 33.7 %collective-permute-start.32 = (bf16[256,1536]{1,0:T(8,128)(2,1)S(1)}, bf16[256,1536]{1,0:T(8,128)(2,1)S(1)}, u32[]{:S(2)}, u32[]{:S(2)}) collective-permute-start(bf16[256,1536]{1,0:T(8,128)(2,1)S(1)} %get-tuple-element.292.refs_1_), channel_id=1, source_target_pairs={{0,1},{3,2},{4,5},{7,6},{8,9},{11,10},{12,13},{15,14},{16,17},{19,... | collective-permute-start | bytes 2359304 | tf_op jit(solution)/shard_map/ppermute | solution.py:590
  287.9 16.1 %collective-permute-start.34 = (bf16[256,128]{1,0:T(8,128)(2,1)}, bf16[256,128]{1,0:T(8,128)(2,1)S(1)}, u32[]{:S(2)}, u32[]{:S(2)}) collective-permute-start(bf16[256,128]{1,0:T(8,128)(2,1)} %get-tuple-element.295), channel_id=1, source_target_pairs={{0,3},{1,0},{2,1},{3,2},{4,7},{5,4},{6,5},{7,6},{8,11},{9,8},{10,9... | collective-permute-start | bytes 196616 | tf_op jit(solution)/shard_map/ppermute | solution.py:590
  290.9 15.8 %collective-permute-start.35 = (bf16[256,128]{1,0:T(8,128)(2,1)}, bf16[256,128]{1,0:T(8,128)(2,1)S(1)}, u32[]{:S(2)}, u32[]{:S(2)}) collective-permute-start(bf16[256,128]{1,0:T(8,128)(2,1)} %get-tuple-element.296), channel_id=1, source_target_pairs={{0,2},{1,3},{2,0},{3,1},{4,6},{5,7},{6,4},{7,5},{8,10},{9,11},{10,... | collective-permute-start | bytes 196616 | tf_op jit(solution)/shard_map/ppermute | solution.py:590
  290.9 16.4 %collective-permute-start.36 = (bf16[256,128]{1,0:T(8,128)(2,1)}, bf16[256,128]{1,0:T(8,128)(2,1)}, u32[]{:S(2)}, u32[]{:S(2)}) collective-permute-start(bf16[256,128]{1,0:T(8,128)(2,1)} %get-tuple-element.297), channel_id=1, source_target_pairs={{0,1},{1,2},{2,3},{3,0},{4,5},{5,6},{6,7},{7,4},{8,9},{9,10},{10,1... | collective-permute-start | bytes 196616 | tf_op jit(solution)/shard_map/ppermute | solution.py:590
  292.2 28.8 %collective-permute-start.37 = (bf16[256,256]{1,0:T(8,128)(2,1)}, bf16[256,256]{1,0:T(8,128)(2,1)S(1)}, u32[]{:S(2)}, u32[]{:S(2)}) collective-permute-start(bf16[256,256]{1,0:T(8,128)(2,1)} %get-tuple-element.312), channel_id=1, source_target_pairs={{0,3},{1,0},{2,1},{3,2},{4,7},{5,4},{6,5},{7,6},{8,11},{9,8},{10,9... | collective-permute-start | bytes 393224 | tf_op jit(solution)/shard_map/ppermute | solution.py:590
  304.0 18.3 %collective-permute-start.38 = (bf16[256,256]{1,0:T(8,128)(2,1)}, bf16[256,256]{1,0:T(8,128)(2,1)S(1)}, u32[]{:S(2)}, u32[]{:S(2)}) collective-permute-start(bf16[256,256]{1,0:T(8,128)(2,1)} %get-tuple-element.313), channel_id=1, source_target_pairs={{0,2},{1,3},{2,0},{3,1},{4,6},{5,7},{6,4},{7,5},{8,10},{9,11},{10,... | collective-permute-start | bytes 393224 | tf_op jit(solution)/shard_map/ppermute | solution.py:590
  306.7 18.6 %collective-permute-start.39 = (bf16[256,256]{1,0:T(8,128)(2,1)S(1)}, bf16[256,256]{1,0:T(8,128)(2,1)}, u32[]{:S(2)}, u32[]{:S(2)}) collective-permute-start(bf16[256,256]{1,0:T(8,128)(2,1)S(1)} %copy-done.59), channel_id=1, source_target_pairs={{0,1},{1,2},{2,3},{3,0},{4,5},{5,6},{6,7},{7,4},{8,9},{9,10},{10,1... | collective-permute-start | bytes 393224 | tf_op jit(solution)/shard_map/ppermute | solution.py:590
  307.4 17.9 %collective-permute-start.41 = (bf16[8,7680]{1,0:T(8,128)(2,1)S(1)}, bf16[8,7680]{1,0:T(8,128)(2,1)S(1)}, u32[]{:S(2)}, u32[]{:S(2)}) collective-permute-start(bf16[8,7680]{1,0:T(8,128)(2,1)S(1)} %slice.300), channel_id=1, source_target_pairs={{0,1},{1,0},{2,3},{3,2},{4,5},{5,4},{6,7},{7,6},{8,9},{9,8},{10,11... | collective-permute-start | bytes 368648 | tf_op jit(solution)/shard_map/ppermute | solution.py:590
  309.2 16.1 %collective-permute-start.42 = (bf16[560,384]{1,0:T(8,128)(2,1)S(1)}, bf16[560,384]{1,0:T(8,128)(2,1)S(1)}, u32[]{:S(2)}, u32[]{:S(2)}) collective-permute-start(bf16[560,384]{1,0:T(8,128)(2,1)S(1)} %fusion.19), channel_id=1, source_target_pairs={{0,1},{1,2},{2,3},{3,0},{4,5},{5,6},{6,7},{7,4},{8,9},{9,10},{10,1... | collective-permute-start | bytes 1290248 | tf_op jit(solution)/shard_map/ppermute | solution.py:590
  321.0 31.5 %collective-permute-start.47 = (bf16[256,1536]{1,0:T(8,128)(2,1)S(1)}, bf16[256,1536]{1,0:T(8,128)(2,1)}, u32[]{:S(2)}, u32[]{:S(2)}) collective-permute-start(bf16[256,1536]{1,0:T(8,128)(2,1)S(1)} %copy-done.7), channel_id=1, source_target_pairs={{0,1},{3,2},{4,5},{7,6},{8,9},{11,10},{12,13},{15,14},{16,17},{19,... | collective-permute-start | bytes 2359304 | tf_op jit(solution)/shard_map/ppermute | solution.py:590
  322.3 30.8 %collective-permute-start.48 = (bf16[256,1536]{1,0:T(8,128)(2,1)}, bf16[256,1536]{1,0:T(8,128)(2,1)}, u32[]{:S(2)}, u32[]{:S(2)}) collective-permute-start(bf16[256,1536]{1,0:T(8,128)(2,1)} %shard_map.406.refs_2_), channel_id=1, source_target_pairs={{1,2},{2,1},{5,6},{6,5},{9,10},{10,9},{13,14},{14,13},{17,18},{18,... | collective-permute-start | bytes 2359304 | tf_op jit(solution)/shard_map/ppermute | solution.py:590
  336.3 37.8 %collective-permute-start.43 = (bf16[1024,256]{1,0:T(8,128)(2,1)}, bf16[1024,256]{1,0:T(8,128)(2,1)}, u32[]{:S(2)}, u32[]{:S(2)}) collective-permute-start(bf16[1024,256]{1,0:T(8,128)(2,1)} %get-tuple-element.338), channel_id=1, source_target_pairs={{0,4},{4,0},{1,5},{5,1},{2,6},{6,2},{3,7},{7,3},{8,12},{12,8},{9,1... | collective-permute-start | bytes 1572872 | tf_op jit(solution)/shard_map/ppermute | solution.py:590
  337.5 15.6 %collective-permute-start.45 = (bf16[8,7680]{1,0:T(8,128)(2,1)S(1)}, bf16[8,7680]{1,0:T(8,128)(2,1)S(1)}, u32[]{:S(2)}, u32[]{:S(2)}) collective-permute-start(bf16[8,7680]{1,0:T(8,128)(2,1)S(1)} %add_convert_fusion.10), channel_id=1, source_target_pairs={{0,2},{1,3},{2,0},{3,1},{4,6},{5,7},{6,4},{7,5},{8,10},{9,11},{10,... | collective-permute-start | bytes 368648 | tf_op jit(solution)/shard_map/ppermute | solution.py:590
  339.6 16.8 %collective-permute-start.46 = (bf16[560,384]{1,0:T(8,128)(2,1)S(1)}, bf16[560,384]{1,0:T(8,128)(2,1)S(1)}, u32[]{:S(2)}, u32[]{:S(2)}) collective-permute-start(bf16[560,384]{1,0:T(8,128)(2,1)S(1)} %fusion.3), channel_id=1, source_target_pairs={{0,1},{1,2},{2,3},{3,0},{4,5},{5,6},{6,7},{7,4},{8,9},{9,10},{10,1... | collective-permute-start | bytes 1290248 | tf_op jit(solution)/shard_map/ppermute | solution.py:590
  352.5 22.8 %collective-permute-start.44 = (bf16[1024,256]{1,0:T(8,128)(2,1)}, bf16[1024,256]{1,0:T(8,128)(2,1)S(1)}, u32[]{:S(2)}, u32[]{:S(2)}) collective-permute-start(bf16[1024,256]{1,0:T(8,128)(2,1)} %get-tuple-element.339), channel_id=1, source_target_pairs={{0,4},{4,0},{1,5},{5,1},{2,6},{6,2},{3,7},{7,3},{8,12},{12,8},{9,1... | collective-permute-start | bytes 1572872 | tf_op jit(solution)/shard_map/ppermute | solution.py:590
  356.4 20.3 %collective-permute-start.49 = (bf16[1024,256]{1,0:T(8,128)(2,1)}, bf16[1024,256]{1,0:T(8,128)(2,1)}, u32[]{:S(2)}, u32[]{:S(2)}) collective-permute-start(bf16[1024,256]{1,0:T(8,128)(2,1)} %get-tuple-element.347), channel_id=1, source_target_pairs={{0,4},{4,0},{1,5},{5,1},{2,6},{6,2},{3,7},{7,3},{8,12},{12,8},{9,1... | collective-permute-start | bytes 1572872 | tf_op jit(solution)/shard_map/ppermute | solution.py:590
  369.0 29.1 %collective-permute-start.56 = (bf16[256,1536]{1,0:T(8,128)(2,1)}, bf16[256,1536]{1,0:T(8,128)(2,1)}, u32[]{:S(2)}, u32[]{:S(2)}) collective-permute-start(bf16[256,1536]{1,0:T(8,128)(2,1)} %get-tuple-element.364.refs_5_), channel_id=1, source_target_pairs={{0,1},{3,2},{1,0},{2,3},{4,5},{7,6},{5,4},{6,7},{8,9},{11,10},{9,8... | collective-permute-start | bytes 2359304 | tf_op jit(solution)/shard_map/ppermute | solution.py:590
  370.8 28.6 %collective-permute-start.57 = (bf16[256,1536]{1,0:T(8,128)(2,1)}, bf16[256,1536]{1,0:T(8,128)(2,1)}, u32[]{:S(2)}, u32[]{:S(2)}) collective-permute-start(bf16[256,1536]{1,0:T(8,128)(2,1)} %get-tuple-element.365.refs_2_), channel_id=1, source_target_pairs={{1,2},{2,1},{5,6},{6,5},{9,10},{10,9},{13,14},{14,13},{17,18},{18,... | collective-permute-start | bytes 2359304 | tf_op jit(solution)/shard_map/ppermute | solution.py:590
  374.0 15.0 %collective-permute-start.54 = (bf16[2,8,12160]{2,1,0:T(8,128)(2,1)}, bf16[2,8,12160]{2,1,0:T(8,128)(2,1)S(1)}, u32[]{:S(2)}, u32[]{:S(2)}) collective-permute-start(bf16[2,8,12160]{2,1,0:T(8,128)(2,1)} %pad_maximum_fusion.7), channel_id=1, source_target_pairs={{0,16},{8,24},{16,0},{24,8},{1,17},{9,25},{17,1},{25,9},{2,18},{10... | collective-permute-start | bytes 1167368 | tf_op jit(solution)/shard_map/ppermute | solution.py:590
  375.3 22.8 %collective-permute-start.55 = (bf16[560,384]{1,0:T(8,128)(2,1)S(1)}, bf16[560,384]{1,0:T(8,128)(2,1)S(1)}, u32[]{:S(2)}, u32[]{:S(2)}) collective-permute-start(bf16[560,384]{1,0:T(8,128)(2,1)S(1)} %fusion.11), channel_id=1, source_target_pairs={{0,1},{1,2},{2,3},{3,0},{4,5},{5,6},{6,7},{7,4},{8,9},{9,10},{10,1... | collective-permute-start | bytes 1290248 | tf_op jit(solution)/shard_map/ppermute | solution.py:590
  400.6 24.2 %collective-permute-start.58 = (bf16[4,8,12160]{2,1,0:T(8,128)(2,1)S(1)}, bf16[4,8,12160]{2,1,0:T(8,128)(2,1)S(1)}, u32[]{:S(2)}, u32[]{:S(2)}) collective-permute-start(bf16[4,8,12160]{2,1,0:T(8,128)(2,1)S(1)} %pad_maximum_fusion.3), channel_id=1, source_target_pairs={{0,4},{4,0},{1,5},{5,1},{2,6},{6,2},{3,7},{7,3},{8,12},{12,8},{9,1... | collective-permute-start | bytes 2334728 | tf_op jit(solution)/shard_map/ppermute | solution.py:590
  403.6 21.1 %collective-permute-start.59 = (f32[512]{0:T(512)S(1)}, f32[512]{0:T(512)S(1)}, u32[]{:S(2)}, u32[]{:S(2)}) collective-permute-start(f32[512]{0:T(512)S(1)} %multiply_reduce_fusion), channel_id=1, source_target_pairs={{0,1},{1,0},{2,3},{3,2},{4,5},{5,4},{6,7},{7,6},{8,9},{9,8},{10,11... | collective-permute-start | bytes 6152 | tf_op jit(solution)/shard_map/ppermute | solution.py:590
  407.8 19.4 %collective-permute-start.60 = (bf16[256,1536]{1,0:T(8,128)(2,1)}, bf16[256,1536]{1,0:T(8,128)(2,1)S(1)}, u32[]{:S(2)}, u32[]{:S(2)}) collective-permute-start(bf16[256,1536]{1,0:T(8,128)(2,1)} %get-tuple-element.373.refs_5_), channel_id=1, source_target_pairs={{0,1},{3,2},{1,0},{2,3},{4,5},{7,6},{5,4},{6,7},{8,9},{11,10},{9,8... | collective-permute-start | bytes 2359304 | tf_op jit(solution)/shard_map/ppermute | solution.py:590
  409.3 20.6 %collective-permute-start.61 = (bf16[256,1536]{1,0:T(8,128)(2,1)}, bf16[256,1536]{1,0:T(8,128)(2,1)S(1)}, u32[]{:S(2)}, u32[]{:S(2)}) collective-permute-start(bf16[256,1536]{1,0:T(8,128)(2,1)} %get-tuple-element.374.refs_2_), channel_id=1, source_target_pairs={{1,2},{2,1},{5,6},{6,5},{9,10},{10,9},{13,14},{14,13},{17,18},{18,... | collective-permute-start | bytes 2359304 | tf_op jit(solution)/shard_map/ppermute | solution.py:590
  429.9 9.8 %collective-permute-start.62 = (f32[512]{0:T(512)S(1)}, f32[512]{0:T(512)S(1)}, u32[]{:S(2)}, u32[]{:S(2)}) collective-permute-start(f32[512]{0:T(512)S(1)} %add.168), channel_id=1, source_target_pairs={{0,2},{1,3},{2,0},{3,1},{4,6},{5,7},{6,4},{7,5},{8,10},{9,11},{10,... | collective-permute-start | bytes 6152 | tf_op jit(solution)/shard_map/ppermute | solution.py:590
  435.2 19.7 %collective-permute-start.65 = (bf16[256,1536]{1,0:T(8,128)(2,1)}, bf16[256,1536]{1,0:T(8,128)(2,1)}, u32[]{:S(2)}, u32[]{:S(2)}) collective-permute-start(bf16[256,1536]{1,0:T(8,128)(2,1)} %get-tuple-element.385.refs_5_), channel_id=1, source_target_pairs={{0,1},{3,2},{1,0},{2,3},{4,5},{7,6},{5,4},{6,7},{8,9},{11,10},{9,8... | collective-permute-start | bytes 2359304 | tf_op jit(solution)/shard_map/ppermute | solution.py:590
  437.3 19.2 %collective-permute-start.66 = (bf16[256,1536]{1,0:T(8,128)(2,1)}, bf16[256,1536]{1,0:T(8,128)(2,1)}, u32[]{:S(2)}, u32[]{:S(2)}) collective-permute-start(bf16[256,1536]{1,0:T(8,128)(2,1)} %get-tuple-element.380.refs_6_.refs_2_), channel_id=1, source_target_pairs={{1,2},{2,1},{5,6},{6,5},{9,10},{10,9},{13,14},{14,13},{17,18},{18,... | collective-permute-start | bytes 2359304 | tf_op jit(solution)/shard_map/ppermute | solution.py:590
  457.3 11.3 %collective-permute-start.70 = (bf16[8,7680]{1,0:T(8,128)(2,1)}, bf16[8,7680]{1,0:T(8,128)(2,1)S(1)}, u32[]{:S(2)}, u32[]{:S(2)}) collective-permute-start(bf16[8,7680]{1,0:T(8,128)(2,1)} %slice.312), channel_id=1, source_target_pairs={{0,1},{1,0},{2,3},{3,2},{4,5},{5,4},{6,7},{7,6},{8,9},{9,8},{10,11... | collective-permute-start | bytes 368648 | tf_op jit(solution)/shard_map/ppermute | solution.py:590
  461.7 17.1 %collective-permute-start.71 = (bf16[256,1536]{1,0:T(8,128)(2,1)}, bf16[256,1536]{1,0:T(8,128)(2,1)}, u32[]{:S(2)}, u32[]{:S(2)}) collective-permute-start(bf16[256,1536]{1,0:T(8,128)(2,1)} %get-tuple-element.391.refs_5_), channel_id=1, source_target_pairs={{0,1},{3,2},{1,0},{2,3},{4,5},{7,6},{5,4},{6,7},{8,9},{11,10},{9,8... | collective-permute-start | bytes 2359304 | tf_op jit(solution)/shard_map/ppermute | solution.py:590
  463.1 17.8 %collective-permute-start.72 = (bf16[256,1536]{1,0:T(8,128)(2,1)}, bf16[256,1536]{1,0:T(8,128)(2,1)}, u32[]{:S(2)}, u32[]{:S(2)}) collective-permute-start(bf16[256,1536]{1,0:T(8,128)(2,1)} %get-tuple-element.392.refs_2_), channel_id=1, source_target_pairs={{1,2},{2,1},{5,6},{6,5},{9,10},{10,9},{13,14},{14,13},{17,18},{18,... | collective-permute-start | bytes 2359304 | tf_op jit(solution)/shard_map/ppermute | solution.py:590
  481.9 25.7 %collective-permute-start.73 = (bf16[64,1536]{1,0:T(8,128)(2,1)S(1)}, bf16[64,1536]{1,0:T(8,128)(2,1)S(1)}, u32[]{:S(2)}, u32[]{:S(2)}) collective-permute-start(bf16[64,1536]{1,0:T(8,128)(2,1)S(1)} %add_convert_fusion.4), channel_id=1, source_target_pairs={{0,1},{1,0},{2,3},{3,2},{4,5},{5,4},{6,7},{7,6},{8,9},{9,8},{10,11... | collective-permute-start | bytes 589832 | tf_op jit(solution)/shard_map/ppermute | solution.py:590
  486.1 21.5 %collective-permute-start.75 = (bf16[256,1536]{1,0:T(8,128)(2,1)}, bf16[256,1536]{1,0:T(8,128)(2,1)S(1)}, u32[]{:S(2)}, u32[]{:S(2)}) collective-permute-start(bf16[256,1536]{1,0:T(8,128)(2,1)} %get-tuple-element.402.refs_5_), channel_id=1, source_target_pairs={{0,1},{3,2},{1,0},{2,3},{4,5},{7,6},{5,4},{6,7},{8,9},{11,10},{9,8... | collective-permute-start | bytes 2359304 | tf_op jit(solution)/shard_map/ppermute | solution.py:590
  487.6 20.1 %collective-permute-start.76 = (bf16[256,1536]{1,0:T(8,128)(2,1)}, bf16[256,1536]{1,0:T(8,128)(2,1)S(1)}, u32[]{:S(2)}, u32[]{:S(2)}) collective-permute-start(bf16[256,1536]{1,0:T(8,128)(2,1)} %get-tuple-element.403.refs_2_), channel_id=1, source_target_pairs={{1,2},{2,1},{5,6},{6,5},{9,10},{10,9},{13,14},{14,13},{17,18},{18,... | collective-permute-start | bytes 2359304 | tf_op jit(solution)/shard_map/ppermute | solution.py:590
  490.0 17.5 %collective-permute-start.74 = (bf16[8,7680]{1,0:T(8,128)(2,1)S(1)}, bf16[8,7680]{1,0:T(8,128)(2,1)S(1)}, u32[]{:S(2)}, u32[]{:S(2)}) collective-permute-start(bf16[8,7680]{1,0:T(8,128)(2,1)S(1)} %add_convert_fusion.8), channel_id=1, source_target_pairs={{0,2},{1,3},{2,0},{3,1},{4,6},{5,7},{6,4},{7,5},{8,10},{9,11},{10,... | collective-permute-start | bytes 368648 | tf_op jit(solution)/shard_map/ppermute | solution.py:590
  507.7 9.7 %collective-permute-start.77 = (bf16[64,1536]{1,0:T(8,128)(2,1)S(1)}, bf16[64,1536]{1,0:T(8,128)(2,1)S(1)}, u32[]{:S(2)}, u32[]{:S(2)}) collective-permute-start(bf16[64,1536]{1,0:T(8,128)(2,1)S(1)} %add_convert_fusion.3), channel_id=1, source_target_pairs={{0,2},{1,3},{2,0},{3,1},{4,6},{5,7},{6,4},{7,5},{8,10},{9,11},{10,... | collective-permute-start | bytes 589832 | tf_op jit(solution)/shard_map/ppermute | solution.py:590
  512.9 14.6 %collective-permute-start.79 = (bf16[256,1536]{1,0:T(8,128)(2,1)}, bf16[256,1536]{1,0:T(8,128)(2,1)S(1)}, u32[]{:S(2)}, u32[]{:S(2)}) collective-permute-start(bf16[256,1536]{1,0:T(8,128)(2,1)} %get-tuple-element.408.refs_4_), channel_id=1, source_target_pairs={{0,1},{3,2},{1,0},{2,3},{4,5},{7,6},{5,4},{6,7},{8,9},{11,10},{9,8... | collective-permute-start | bytes 2359304 | tf_op jit(solution)/shard_map/ppermute | solution.py:590
  514.9 18.4 %collective-permute-start.80 = (bf16[256,1536]{1,0:T(8,128)(2,1)}, bf16[256,1536]{1,0:T(8,128)(2,1)S(1)}, u32[]{:S(2)}, u32[]{:S(2)}) collective-permute-start(bf16[256,1536]{1,0:T(8,128)(2,1)} %get-tuple-element.409.refs_2_), channel_id=1, source_target_pairs={{1,2},{2,1},{5,6},{6,5},{9,10},{10,9},{13,14},{14,13},{17,18},{18,... | collective-permute-start | bytes 2359304 | tf_op jit(solution)/shard_map/ppermute | solution.py:590
  533.3 10.3 %collective-permute-start.85 = (bf16[2,8,10880]{2,1,0:T(8,128)(2,1)S(1)}, bf16[2,8,10880]{2,1,0:T(8,128)(2,1)S(1)}, u32[]{:S(2)}, u32[]{:S(2)}) collective-permute-start(bf16[2,8,10880]{2,1,0:T(8,128)(2,1)S(1)} %pad_maximum_fusion.8), channel_id=1, source_target_pairs={{0,16},{8,24},{16,0},{24,8},{1,17},{9,25},{17,1},{25,9},{2,18},{10... | collective-permute-start | bytes 1044488 | tf_op jit(solution)/shard_map/ppermute | solution.py:590
  539.5 15.0 %collective-permute-start.81 = (bf16[256,1536]{1,0:T(8,128)(2,1)}, bf16[256,1536]{1,0:T(8,128)(2,1)}, u32[]{:S(2)}, u32[]{:S(2)}) collective-permute-start(bf16[256,1536]{1,0:T(8,128)(2,1)} %get-tuple-element.413.refs_3_), channel_id=1, source_target_pairs={{1,0},{2,3},{5,4},{6,7},{9,8},{10,11},{13,12},{14,15},{17,16},{18,... | collective-permute-start | bytes 2359304 | tf_op jit(solution)/shard_map/ppermute | solution.py:590
  541.7 13.0 %collective-permute-start.82 = (bf16[256,1536]{1,0:T(8,128)(2,1)}, bf16[256,1536]{1,0:T(8,128)(2,1)}, u32[]{:S(2)}, u32[]{:S(2)}) collective-permute-start(bf16[256,1536]{1,0:T(8,128)(2,1)} %get-tuple-element.414.refs_1_), channel_id=1, source_target_pairs={{1,2},{2,1},{5,6},{6,5},{9,10},{10,9},{13,14},{14,13},{17,18},{18,... | collective-permute-start | bytes 2359304 | tf_op jit(solution)/shard_map/ppermute | solution.py:590
  543.7 16.7 %collective-permute-start.86 = (bf16[128,1536]{1,0:T(8,128)(2,1)S(1)}, bf16[128,1536]{1,0:T(8,128)(2,1)}, u32[]{:S(2)}, u32[]{:S(2)}) collective-permute-start(bf16[128,1536]{1,0:T(8,128)(2,1)S(1)} %pad_maximum_fusion.5), channel_id=1, source_target_pairs={{0,16},{8,24},{16,0},{24,8},{1,17},{9,25},{17,1},{25,9},{2,18},{10... | collective-permute-start | bytes 1179656 | tf_op jit(solution)/shard_map/ppermute | solution.py:590
  544.9 15.4 %collective-permute-start.87 = (bf16[4,8,10880]{2,1,0:T(8,128)(2,1)}, bf16[4,8,10880]{2,1,0:T(8,128)(2,1)}, u32[]{:S(2)}, u32[]{:S(2)}) collective-permute-start(bf16[4,8,10880]{2,1,0:T(8,128)(2,1)} %pad_maximum_fusion.4), channel_id=1, source_target_pairs={{0,4},{4,0},{1,5},{5,1},{2,6},{6,2},{3,7},{7,3},{8,12},{12,8},{9,1... | collective-permute-start | bytes 2088968 | tf_op jit(solution)/shard_map/ppermute | solution.py:590
  558.2 27.6 %collective-permute-start.83 = (bf16[256,1536]{1,0:T(8,128)(2,1)}, bf16[256,1536]{1,0:T(8,128)(2,1)}, u32[]{:S(2)}, u32[]{:S(2)}) collective-permute-start(bf16[256,1536]{1,0:T(8,128)(2,1)} %get-tuple-element.416.refs_1_), channel_id=1, source_target_pairs={{1,0},{2,3},{5,4},{6,7},{9,8},{10,11},{13,12},{14,15},{17,16},{18,... | collective-permute-start | bytes 2359304 | tf_op jit(solution)/shard_map/ppermute | solution.py:590
  564.8 23.8 %collective-permute-start.88 = (bf16[256,1536]{1,0:T(8,128)(2,1)S(1)}, bf16[256,1536]{1,0:T(8,128)(2,1)S(1)}, u32[]{:S(2)}, u32[]{:S(2)}) collective-permute-start(bf16[256,1536]{1,0:T(8,128)(2,1)S(1)} %pad_maximum_fusion.2), channel_id=1, source_target_pairs={{0,4},{4,0},{1,5},{5,1},{2,6},{6,2},{3,7},{7,3},{8,12},{12,8},{9,1... | collective-permute-start | bytes 2359304 | tf_op jit(solution)/shard_map/ppermute | solution.py:590
  (90 other events, 845.4 us)
